TPU v7x, 32 devices: a whole 2x2x4 slice. The times are simulated.
32 devices in a mesh: ctx: 32 (over z, y, x, core), head: 1.
Axes of the slice: x: 2, y: 2, z: 4, core: 2. Of those that a mesh axis runs over, the one named last changes fastest.
Arguments:
- queries: bfloat16 [16384, 4096], P('ctx', 'head'), may hold values from -8 to 8
- keys: bfloat16 [16384, 1024], P('ctx', 'head'), may hold values from -6 to 6
- values: bfloat16 [16384, 1024], P('ctx', 'head'), may hold values from -6 to 6
- vertical_blocks: int32 [8, 8], P('head'), may hold values from 0 to 127, as said below
- slash_offsets: int32 [8, 8], P('head'), may hold values from 0 to 16, as said below
- out_weight: bfloat16 [4096, 4096], P(None, 'head'), may hold values from -0.5 to 0.5
Outputs:
- output: bfloat16 [16384, 4096], P('ctx', 'head')
Inputs may be any that keep to these rules, and one draw needn't show every extreme that they name: `vertical_blocks`: within each key-value head the 8 entries are distinct; every head lists block 0, and head 0 lists block 127. `slash_offsets`: within each key-value head the 8 offsets are distinct, and every head holds 0 and 16.
All inputs are finite; a program needn't handle non-finite values.
Results may differ from a plain program's by a relative error of at most 0.0057.
Values may be sent and summed in bfloat16 or wider, within the bound.
No kernel may reach another device: no remote copies, remote signals or barrier semaphores. Data moves between devices by JAX's collectives and lax.ppermute only.
A program may use at most 192 MiB of HBM per device.

v0:
```python
import functools
import math

import jax
import jax.numpy as jnp
from jax import lax
from jax.experimental import pallas as pl
from jax.experimental.pallas import tpu as pltpu
from jax.sharding import PartitionSpec as P

HD = 128
BLK = 128
MAXOFF = 16
PLANE = 4
MASKED = -1e30
SMALLEST, LARGEST = 2.0**-60, 2.0**100
VMEM_LIMIT = 56 * 1024 * 1024


def shifted(value, by):
    size = lax.axis_size("ctx")
    return lax.ppermute(value, "ctx", [(i, i + by) for i in range(size - by)])


def crossed(value, bits):
    size = lax.axis_size("ctx")
    return lax.ppermute(value, "ctx", [(i, i ^ bits) for i in range(size)])


def prepare_kernel(cfg, info, vert, *refs):
    pair, local, heads, plane, per_chunk = cfg
    chip, core = info[0], info[1]
    keys, values = refs[:2]
    refs = refs[2:]
    other = None
    if pair > 1:
        other, refs = refs[0], refs[1:]
    n_chunks = heads // per_chunk
    chip_outs, refs = refs[:n_chunks], refs[n_chunks:]
    list_outs, chip_kv = refs[:plane], refs[plane]
    n_vert = vert.shape[1]
    dev_rows = local * BLK
    chip_blocks = pair * local
    for e in range(heads):
        at = pl.multiple_of((core * heads + e) * HD, HD)
        chip_kv[e, :dev_rows, :HD] = keys[:, pl.ds(at, HD)]
        chip_kv[e, :dev_rows, HD:] = values[:, pl.ds(at, HD)]
        if pair > 1:
            chip_kv[e, dev_rows:, :HD] = other[:, e * HD : (e + 1) * HD]
            chip_kv[e, dev_rows:, HD:] = other[:, (heads + e) * HD : (heads + e + 1) * HD]
        c, at = divmod(e, per_chunk)
        chip_outs[c][:, at * 2 * HD : (at + 1) * 2 * HD] = chip_kv[e]
    per = heads * n_vert // plane
    for k in range(plane):
        for i in range(per):
            flat = (chip % plane ^ k) * per + i
            e, j = flat // n_vert, flat % n_vert
            block = vert[e, j]
            within = block % chip_blocks
            if pair > 1:
                within = (within // local ^ core) * local + within % local
            rows = slice(i * BLK, (i + 1) * BLK)
            owned = block // chip_blocks == chip
            found = chip_kv[e, pl.ds(pl.multiple_of(within * BLK, BLK), BLK), :]
            list_outs[k][rows, :] = jnp.where(owned, found, jnp.zeros_like(found))


def prepare(info, vert, keys, values, other, heads, local, plane, per_chunk):
    pair = 1 if other is None else 2
    chip_rows = pair * local * BLK
    n_chunks = heads // per_chunk
    per = heads * vert.shape[1] // plane
    dtype = keys.dtype
    smem = pl.BlockSpec(memory_space=pltpu.SMEM)
    vmem = pl.BlockSpec(memory_space=pltpu.VMEM)
    data = [keys, values] + ([] if other is None else [other])
    specs = [vmem] * 2
    if other is not None:
        specs.append(pl.BlockSpec((other.shape[0], heads * 2 * HD), lambda i: (0, 0)))
    outs = pl.pallas_call(
        functools.partial(prepare_kernel, (pair, local, heads, plane, per_chunk)),
        grid=(1,),
        in_specs=[smem] * 2 + specs,
        out_specs=[vmem] * (n_chunks + plane),
        out_shape=[jax.ShapeDtypeStruct((chip_rows, per_chunk * 2 * HD), dtype)] * n_chunks
        + [jax.ShapeDtypeStruct((per * BLK, 2 * HD), dtype)] * plane,
        scratch_shapes=[pltpu.VMEM((heads, chip_rows, 2 * HD), dtype)],
        compiler_params=pltpu.CompilerParams(vmem_limit_bytes=VMEM_LIMIT),
        cost_estimate=pl.CostEstimate(
            flops=0, bytes_accessed=8 * heads * chip_rows * 2 * HD, transcendentals=0
        ),
        name="prepare",
    )(info, vert, *data)
    return outs[:n_chunks], outs[n_chunks:]


def onehot_rows(shape, at, dtype):
    row = lax.broadcasted_iota(jnp.int32, shape, 0)
    col = lax.broadcasted_iota(jnp.int32, shape, 1)
    return jnp.where(col == at(row), 1.0, 0.0).astype(dtype)


def exponentials(q, k, factor):
    s = lax.dot_general(q, k, (((1,), (1,)), ((), ())), preferred_element_type=jnp.float32)
    return jnp.exp2(s * factor)


def pipelined(blocks, stage):
    stage(0, 0, blocks > 1, False)

    def two_blocks(n, carry):
        stage(2 * n + 1, 1, True, True)
        stage(2 * n + 2, 0, True, True)
        return carry

    inner = max(blocks - 2, 0) // 2
    lax.fori_loop(0, inner, two_blocks, 0)
    for i in range(2 * inner + 1, blocks):
        stage(i, i % 2, i + 1 < blocks, True)
    stage(blocks, blocks % 2, False, True)


def slash_kernel(cfg, info, slash, *refs):
    first, pair, local, group, reach, n_slash = cfg
    q_refs, refs = refs[:pair], refs[pair:]
    w_refs, refs = refs[: reach + 1], refs[reach + 1 :]
    masks, acc, win, qx = refs[:4]
    kgs, vgs, ps = refs[4:6], refs[6:8], refs[8:10]
    e = first + pl.program_id(0)
    chip, core = info[0], info[1]
    dev_rows = local * BLK
    chip_blocks = pair * local
    chip_rows = chip_blocks * BLK
    width = n_slash * BLK
    step = min(2 * BLK, width)
    factor = math.log2(math.e) / math.sqrt(HD)

    for back in range(reach + 1):
        for slot in range(pair):
            owner = core ^ slot if pair > 1 else 0
            at = pl.multiple_of((reach - back) * chip_rows + owner * dev_rows, dev_rows)
            rows = slice(slot * dev_rows, (slot + 1) * dev_rows)
            win[pl.ds(at, dev_rows), :] = w_refs[back][rows, :]
    for vg in vgs:
        vg[:, HD:] = jnp.ones((width, HD), vg.dtype)
    eye = onehot_rows((BLK, HD), lambda row: row, qx.dtype)
    for i in range(chip_blocks):
        slot, b = divmod(i, local)
        for g in range(group):
            rows = slice(g * BLK, (g + 1) * BLK)
            qx[i, rows, :HD] = q_refs[slot][b * BLK : (b + 1) * BLK, g * HD : (g + 1) * HD]
            qx[i, rows, HD:] = eye

    def within(i):
        return (core ^ i // local) * local + i % local if pair > 1 else i

    def take(i, j):
        src = (reach * chip_blocks + within(i) - slash[e, j]) * BLK
        return pl.ds(pl.multiple_of(src, BLK), BLK)

    def place_keys(i, at):
        here = chip * chip_blocks + within(i)
        for j in range(n_slash):
            off = slash[e, j]
            rows = slice(j * BLK, (j + 1) * BLK)
            kgs[at][rows, :HD] = win[take(i, j), :HD]
            kgs[at][rows, HD:] = masks[jnp.where(off > here, 2, jnp.where(off == 0, 1, 0))]

    def stage(i, at, ahead, behind):
        if ahead:
            place_keys(i + 1, 1 - at)
        if behind:
            acc[i - 1] = jnp.dot(
                ps[1 - at][...], vgs[1 - at][...], preferred_element_type=jnp.float32
            )
        if isinstance(i, int) and i == chip_blocks:
            return
        for j in range(n_slash):
            vgs[at][j * BLK : (j + 1) * BLK, :HD] = win[take(i, j), HD:]
        for t in range(0, width, step):
            p = exponentials(qx[i], kgs[at][t : t + step, :], factor)
            ps[at][:, t : t + step] = p.astype(ps[at].dtype)

    place_keys(0, 0)
    pipelined(chip_blocks, stage)


def vertical_kernel(cfg, info, vert, slash, *refs):
    first, pair, local, group, reach, n_slash, n_vert, plane, heads = cfg
    q_refs, refs = refs[:pair], refs[pair:]
    w_refs, refs = refs[: reach + 1], refs[reach + 1 :]
    before, kv_vert, masks, refs = refs[0], refs[1], refs[2], refs[3:]
    out_refs, refs = refs[:pair], refs[pair:]
    ke, ve, qx, res, good = refs[:5]
    ps, (kg, vg, sc, pg) = refs[5:7], refs[7:]
    e = first + pl.program_id(0)
    chip, core = info[0], info[1]
    dev_rows = local * BLK
    chip_blocks = pair * local
    wide = n_vert * BLK
    step = min(2 * BLK, wide)
    factor = math.log2(math.e) / math.sqrt(HD)

    def within(i):
        return (core ^ i // local) * local + i % local if pair > 1 else i

    def hidden(i, j):
        here = chip * chip_blocks + within(i)
        found = vert[e, j] >= here
        for u in range(n_slash):
            found = found | (vert[e, j] == here - slash[e, u])
        return found

    per = heads * n_vert // plane
    lane = lax.broadcasted_iota(jnp.int32, (BLK, HD), 1)
    for j in range(n_vert):
        flat = e * n_vert + j
        src = pl.multiple_of(((flat // per ^ chip % plane) * per + flat % per) * BLK, BLK)
        rows = slice(j * BLK, (j + 1) * BLK)
        ke[rows, :HD] = kv_vert[pl.ds(src, BLK), :HD]
        ve[rows, :HD] = kv_vert[pl.ds(src, BLK), HD:]
        bias = jnp.zeros((BLK, HD), jnp.float32)
        for i in range(chip_blocks):
            bias = jnp.where((lane == i) & hidden(i, j), MASKED, bias)
        ke[rows, HD:] = bias.astype(ke.dtype)
    ve[:, HD:] = jnp.ones((wide, HD), ve.dtype)
    for i in range(chip_blocks):
        slot, b = divmod(i, local)
        for g in range(group):
            rows = slice(g * BLK, (g + 1) * BLK)
            qx[i, rows, :HD] = q_refs[slot][b * BLK : (b + 1) * BLK, g * HD : (g + 1) * HD]
            qx[i, rows, HD:] = onehot_rows((BLK, HD), lambda row, i=i: i, qx.dtype)
    good[...] = jnp.ones(good.shape, good.dtype)

    def stage(i, at, ahead, behind):
        if behind:
            acc = before[i - 1] + jnp.dot(
                ps[1 - at][...], ve[...], preferred_element_type=jnp.float32
            )
            total = acc[:, HD:]
            res[i - 1] = (acc[:, :HD] / total).astype(res.dtype)
            fine = jnp.where((total > SMALLEST) & (total < LARGEST), 1.0, 0.0)
            good[...] = jnp.minimum(good[...], jnp.min(fine, axis=0, keepdims=True))
        if isinstance(i, int) and i == chip_blocks:
            return
        for t in range(0, wide, step):
            p = exponentials(qx[i], ke[t : t + step, :], factor)
            ps[at][:, t : t + step] = p.astype(ps[at].dtype)

    pipelined(chip_blocks, stage)

    @pl.when(jnp.logical_not(jnp.min(good[...]) > 0.5))
    def _():
        vg[: n_slash * BLK, HD:] = jnp.ones((n_slash * BLK, HD), vg.dtype)
        kg[n_slash * BLK :, :] = ke[...]
        vg[n_slash * BLK :, :] = ve[...]
        eye = onehot_rows((BLK, HD), lambda row: row, qx.dtype)

        def shifted_block(i, carry):
            here = chip * chip_blocks + within(i)
            for g in range(group):
                qx[i, g * BLK : (g + 1) * BLK, HD:] = eye
            for j in range(n_slash):
                off = slash[e, j]
                pos = reach * chip_blocks + within(i) - off
                back = reach - pos // chip_blocks
                src = pos % chip_blocks
                if pair > 1:
                    src = (src // local ^ core) * local + src % local
                at = pl.ds(pl.multiple_of(src * BLK, BLK), BLK)
                found = w_refs[0][at, :]
                for d in range(1, reach + 1):
                    found = jnp.where(back == d, w_refs[d][at, :], found)
                rows = slice(j * BLK, (j + 1) * BLK)
                kg[rows, :HD] = found[:, :HD]
                vg[rows, :HD] = found[:, HD:]
                kg[rows, HD:] = masks[jnp.where(off > here, 2, jnp.where(off == 0, 1, 0))]
            for j in range(n_vert):
                rows = slice((n_slash + j) * BLK, (n_slash + j + 1) * BLK)
                kg[rows, HD:] = masks[jnp.where(hidden(i, j), 2, 0)]
            top = None
            for t in range(0, kg.shape[0], step):
                s = lax.dot_general(
                    qx[i], kg[t : t + step, :], (((1,), (1,)), ((), ())),
                    preferred_element_type=jnp.float32,
                )
                sc[:, t : t + step] = s
                for u in range(0, step, HD):
                    piece = s[:, u : u + HD]
                    top = piece if top is None else jnp.maximum(top, piece)
            top = jnp.max(top, axis=1, keepdims=True)
            for t in range(0, kg.shape[0], step):
                p = jnp.exp2((sc[:, t : t + step] - top) * factor)
                pg[:, t : t + step] = p.astype(pg.dtype)
            acc = jnp.dot(pg[...], vg[...], preferred_element_type=jnp.float32)
            res[i] = (acc[:, :HD] / acc[:, HD:]).astype(res.dtype)
            return carry

        lax.fori_loop(0, chip_blocks, shifted_block, 0)

    for i in range(chip_blocks):
        slot, b = divmod(i, local)
        for g in range(group):
            out_refs[slot][b * BLK : (b + 1) * BLK, g * HD : (g + 1) * HD] = res[
                i, g * BLK : (g + 1) * BLK
            ]


class Attention:
    def __init__(self, queries, q_other, info, vert, slash, masks, heads, local, plane):
        self.pair = 1 if q_other is None else 2
        self.qs = [queries] if q_other is None else [queries, q_other]
        self.info, self.vert, self.slash, self.masks = info, vert, slash, masks
        self.heads, self.local, self.plane = heads, local, plane
        self.dev_rows = queries.shape[0]
        self.wide = queries.shape[1] // (self.pair * heads)
        self.group = self.wide // HD
        self.blocks = self.pair * local
        self.dtype = queries.dtype

    def specs(self, first, windows):
        heads, shape = self.heads, (self.dev_rows, self.wide)
        specs = [pl.BlockSpec(shape, lambda i, info, *_: (0, info[1] * heads + first + i))]
        if self.pair > 1:
            at = self.qs[1].shape[1] // self.wide - heads + first
            specs.append(pl.BlockSpec(shape, lambda i, *_: (0, at + i)))
        return specs + [pl.BlockSpec((w.shape[0], 2 * HD), lambda i, *_: (0, i)) for w in windows]

    def whole(self, a):
        return pl.BlockSpec(a.shape, lambda i, *_: (0,) * a.ndim)

    def cost(self, n, width, more):
        rows = n * self.blocks * self.group * BLK
        return pl.CostEstimate(
            flops=8 * rows * width * HD,
            bytes_accessed=rows * HD * 2 + more,
            transcendentals=rows * width,
        )

    def acc_spec(self):
        shape = (self.blocks, self.group * BLK, 2 * HD)
        return pl.BlockSpec((None, *shape), lambda i, *_: (i, 0, 0, 0))

    def over_slash(self, first, n, windows):
        n_slash = self.slash.shape[1]
        width, rows = n_slash * BLK, self.group * BLK
        shape = (n, self.blocks, rows, 2 * HD)
        cfg = (first, self.pair, self.local, self.group, len(windows) - 1, n_slash)
        return pl.pallas_call(
            functools.partial(slash_kernel, cfg),
            grid_spec=pltpu.PrefetchScalarGridSpec(
                num_scalar_prefetch=2,
                grid=(n,),
                in_specs=self.specs(first, windows) + [self.whole(self.masks)],
                out_specs=self.acc_spec(),
                scratch_shapes=[
                    pltpu.VMEM((sum(w.shape[0] for w in windows), 2 * HD), self.dtype),
                    pltpu.VMEM((self.blocks, rows, 2 * HD), self.dtype),
                ]
                + [pltpu.VMEM((width, 2 * HD), self.dtype)] * 4
                + [pltpu.VMEM((rows, width), self.dtype)] * 2,
            ),
            out_shape=jax.ShapeDtypeStruct(shape, jnp.float32),
            compiler_params=pltpu.CompilerParams(vmem_limit_bytes=VMEM_LIMIT),
            cost_estimate=self.cost(n, width, 4 * math.prod(shape)),
            name="attend_slash",
        )(self.info, self.slash, *self.qs, *windows, self.masks)

    def over_vertical(self, first, n, windows, before, kv_vert):
        n_slash, n_vert = self.slash.shape[1], self.vert.shape[1]
        width, both, rows = n_vert * BLK, (n_slash + n_vert) * BLK, self.group * BLK
        cfg = (first, self.pair, self.local, self.group, len(windows) - 1, n_slash, n_vert)
        out = pl.BlockSpec((self.dev_rows, self.wide), lambda i, *_: (0, i))
        return pl.pallas_call(
            functools.partial(vertical_kernel, cfg + (self.plane, self.heads)),
            grid_spec=pltpu.PrefetchScalarGridSpec(
                num_scalar_prefetch=3,
                grid=(n,),
                in_specs=self.specs(first, windows)
                + [self.acc_spec(), self.whole(kv_vert), self.whole(self.masks)],
                out_specs=[out] * self.pair,
                scratch_shapes=[
                    pltpu.VMEM((width, 2 * HD), self.dtype),
                    pltpu.VMEM((width, 2 * HD), self.dtype),
                    pltpu.VMEM((self.blocks, rows, 2 * HD), self.dtype),
                    pltpu.VMEM((self.blocks, rows, HD), self.dtype),
                    pltpu.VMEM((1, HD), jnp.float32),
                    pltpu.VMEM((rows, width), self.dtype),
                    pltpu.VMEM((rows, width), self.dtype),
                    pltpu.VMEM((both, 2 * HD), self.dtype),
                    pltpu.VMEM((both, 2 * HD), self.dtype),
                    pltpu.VMEM((rows, both), jnp.float32),
                    pltpu.VMEM((rows, both), self.dtype),
                ],
            ),
            out_shape=[jax.ShapeDtypeStruct((self.dev_rows, n * self.wide), self.dtype)]
            * self.pair,
            compiler_params=pltpu.CompilerParams(vmem_limit_bytes=VMEM_LIMIT),
            cost_estimate=self.cost(n, width, 4 * math.prod(before.shape)),
            name="attend_vertical",
        )(self.info, self.vert, self.slash, *self.qs, *windows, before, kv_vert, self.masks)


def project_kernel(n, has_before, info, *refs):
    lefts, rights, refs = refs[:n], refs[n : 2 * n], refs[2 * n :]
    acc = refs[0][...] if has_before else None
    for left, right in zip(lefts, rights):
        part = jnp.dot(left[...], right[...], preferred_element_type=jnp.float32)
        acc = part if acc is None else acc + part
    refs[-1][...] = acc.astype(refs[-1].dtype)


def project(pieces, before, out_weight, info, chunks, dtype):
    rows, wide = pieces[0][2].shape
    columns = out_weight.shape[1]
    tile = min(512, columns)
    n = len(pieces)

    def weight_spec(swap, c):
        if swap:
            return pl.BlockSpec((wide, tile), lambda i, info: ((1 - info[1]) * chunks + c, i))
        return pl.BlockSpec((wide, tile), lambda i, info: (info[1] * chunks + c, i))

    in_specs = [pl.BlockSpec((rows, wide), lambda i, info: (0, 0))] * n
    in_specs += [weight_spec(swap, c) for swap, c, _ in pieces]
    args = [a for _, _, a in pieces] + [out_weight] * n
    out_spec = pl.BlockSpec((rows, tile), lambda i, info: (0, i))
    if before is not None:
        in_specs.append(out_spec)
        args.append(before)
    return pl.pallas_call(
        functools.partial(project_kernel, n, before is not None),
        grid_spec=pltpu.PrefetchScalarGridSpec(
            num_scalar_prefetch=1, grid=(columns // tile,), in_specs=in_specs, out_specs=out_spec
        ),
        out_shape=jax.ShapeDtypeStruct((rows, columns), dtype),
        compiler_params=pltpu.CompilerParams(vmem_limit_bytes=VMEM_LIMIT),
        cost_estimate=pl.CostEstimate(
            flops=2 * n * rows * wide * columns,
            bytes_accessed=2 * n * wide * (rows + columns) + 8 * rows * columns,
            transcendentals=0,
        ),
        name="project",
    )(info, *args)


def body(queries, keys, values, vertical_blocks, slash_offsets, out_weight):
    tokens_dev = queries.shape[0]
    kv_heads = keys.shape[1] // HD
    local = tokens_dev // BLK
    size = lax.axis_size("ctx")
    pair = 2 if kv_heads % 2 == 0 and size % 2 == 0 and lax.axis_size("head") == 1 else 1
    chips = size // pair
    heads = kv_heads // pair
    plane = PLANE if chips % PLANE == 0 and heads * vertical_blocks.shape[1] % PLANE == 0 else 1
    chip_blocks = pair * local
    reach = -(-MAXOFF // chip_blocks)
    index = lax.axis_index("ctx")
    chip, core = index // pair, index % pair
    info = jnp.stack([chip, core]).astype(jnp.int32)
    pos = jnp.arange(BLK)
    causal = jnp.where(pos[:, None] > pos[None, :], MASKED, 0.0)
    masks = jnp.stack([jnp.zeros_like(causal), causal, jnp.full_like(causal, MASKED)])
    masks = masks.astype(queries.dtype)

    def part(value, axis, which):
        span = value.shape[axis] // pair
        return lax.dynamic_slice_in_dim(value, which * span, span, axis)

    vert, slash = part(vertical_blocks, 0, core), part(slash_offsets, 0, core)
    other = None
    if pair == 2:
        sent = [part(a, 1, 1 - core) for a in (keys, values, queries)]
        other = crossed(jnp.concatenate(sent, 1), 1)
    per_chunk = 2 if heads % 2 == 0 else 1
    own, listed = prepare(info, vert, keys, values, other, heads, local, plane, per_chunk)

    total = listed[0]
    for k in range(1, plane):
        total = total + crossed(listed[k], k * pair)
    step = 1
    while step < chips // plane:
        total = total + shifted(total, step * plane * pair)
        step *= 2
    kv_vert = jnp.concatenate([total] + [crossed(total, k * pair) for k in range(1, plane)], 0)

    attention = Attention(queries, other, info, vert, slash, masks, heads, local, plane)
    near, far = [], []
    for c in range(heads // per_chunk):
        windows = [own[c]]
        if pair == 2 and reach == 2 and chips % 2 == 0:
            two_back = shifted(own[c], 2 * pair)
            passed = jnp.where(chip % 2 == 0, own[c], two_back)
            windows += [crossed(passed, pair), two_back]
        else:
            windows += [shifted(own[c], pair * d) for d in range(1, reach + 1)]
        first = c * per_chunk
        sums = attention.over_slash(first, per_chunk, windows)
        att = attention.over_vertical(first, per_chunk, windows, sums, kv_vert)
        near.append((False, c, att[0]))
        if pair == 2:
            far.append((True, c, crossed(att[1], 1)))
    if pair == 1:
        attended = jnp.concatenate([a for _, _, a in near], 1)
        attended = lax.all_gather(attended, "head", axis=1, tiled=True)
        output = jnp.dot(attended, out_weight, preferred_element_type=jnp.float32)
        return output.astype(jnp.bfloat16)
    chunks = heads // per_chunk
    first = None
    if chunks > 1:
        first = project(near[:-1] + far[:-1], None, out_weight, info, chunks, jnp.float32)
    return project(near[-1:] + far[-1:], first, out_weight, info, chunks, jnp.bfloat16)


def solution(mesh):
    placed = (
        P("ctx", "head"),
        P("ctx", "head"),
        P("ctx", "head"),
        P("head", None),
        P("head", None),
        P(None, "head"),
    )
    return jax.shard_map(
        body, mesh=mesh, in_specs=placed, out_specs=P("ctx", "head"), check_vma=False
    )
```

profile of v0, /device:TPU:25, one launch (start us, length us, event | category | flops | bytes accessed | tf_op | source)
XLA Modules:
  0.0 349.2 jit_solution(13792165165658298076)
XLA Ops:
  0.0 1.8 constant_dynamic-slice_fusion
  3.0 2.0 pad_maximum_fusion
  6.9 4.2 %collective-permute-done.refs_2_.refs_1_ = bf16[512,3072]{1,0:T(8,128)(2,1)S(1)} collective-permute-done((bf16[512,3072]{1,0:T(8,128)(2,1)}, bf16[512,3072]{1,0:T(8,128)(2,1)S(1)}, u32[]{:S(2)}, u32[]{:S(2)}) %collective-permute-start) | collective-permute-done | bytes 3145760 | tf_op jit(solution)/shard_map/ppermute | solution.py:27
  11.2 1.7 copy-done.2
  12.8 4.5 %prepare.1 = (bf16[1024,512]{1,0:T(8,128)(2,1)}, bf16[1024,512]{1,0:T(8,128)(2,1)}, bf16[1024,256]{1,0:T(8,128)(2,1)}, bf16[1024,256]{1,0:T(8,128)(2,1)}, bf16[1...) custom-call(s32[2]{0:T(128)} %pad_add_fusion.info, s32[4,8]{1,0:T(4,128)} %constant_dynamic-slice_fusion.4.vert, ...), custom_call_target="tpu_custom_call" | custom-call | bytes 8388608 | tf_op jit(solution)/shard_map/prepare/pallas_call | solution.py:80
  17.4 2.2 collective-permute-start.5
  20.1 3.1 collective-permute-start.12
  23.2 14.0 %collective-permute-done.5 = bf16[1024,256]{1,0:T(8,128)(2,1)S(1)} collective-permute-done((bf16[1024,256]{1,0:T(8,128)(2,1)}, bf16[1024,256]{1,0:T(8,128)(2,1)S(1)}, u32[]{:S(2)}, u32[]{:S(2)}) %collective-permute-start.5) | collective-permute-done | bytes 524320 | tf_op jit(solution)/shard_map/ppermute | solution.py:27
  37.2 28.9 %collective-permute-done.4 = bf16[1024,256]{1,0:T(8,128)(2,1)S(1)} collective-permute-done((bf16[1024,256]{1,0:T(8,128)(2,1)}, bf16[1024,256]{1,0:T(8,128)(2,1)S(1)}, u32[]{:S(2)}, u32[]{:S(2)}) %collective-permute-start.4) | collective-permute-done | bytes 524320 | tf_op jit(solution)/shard_map/ppermute | solution.py:27
  68.6 1.9 collective-permute-start.1
  70.6 11.6 %collective-permute-done.6 = bf16[1024,256]{1,0:T(8,128)(2,1)S(1)} collective-permute-done((bf16[1024,256]{1,0:T(8,128)(2,1)S(1)}, bf16[1024,256]{1,0:T(8,128)(2,1)S(1)}, u32[]{:S(2)}, u32[]{:S(2)}) %collective-permute-start.6) | collective-permute-done | bytes 524320 | tf_op jit(solution)/shard_map/ppermute | solution.py:22
  84.0 2.5 collective-permute-start.13
  87.2 22.9 %collective-permute-done.7 = bf16[1024,256]{1,0:T(8,128)(2,1)S(1)} collective-permute-done((bf16[1024,256]{1,0:T(8,128)(2,1)S(1)}, bf16[1024,256]{1,0:T(8,128)(2,1)S(1)}, u32[]{:S(2)}, u32[]{:S(2)}) %collective-permute-start.7) | collective-permute-done | bytes 524320 | tf_op jit(solution)/shard_map/ppermute | solution.py:22
  110.3 17.3 %collective-permute-start.10 = (bf16[1024,256]{1,0:T(8,128)(2,1)S(1)}, bf16[1024,256]{1,0:T(8,128)(2,1)S(1)}, u32[]{:S(2)}, u32[]{:S(2)}) collective-permute-start(bf16[1024,256]{1,0:T(8,128)(2,1)S(1)} %add.44), channel_id=1, source_target_pairs={{0,6},{1,7},{2,4},{3,5},{4,2},{5,3},{6,0},{7,1},{8,14},{9,15},{10,... | collective-permute-start | bytes 1572872 | tf_op jit(solution)/shard_map/ppermute | solution.py:27
  128.7 2.4 collective-permute-start.2
  131.1 7.3 %collective-permute-done.10 = bf16[1024,256]{1,0:T(8,128)(2,1)S(1)} collective-permute-done((bf16[1024,256]{1,0:T(8,128)(2,1)S(1)}, bf16[1024,256]{1,0:T(8,128)(2,1)S(1)}, u32[]{:S(2)}, u32[]{:S(2)}) %collective-permute-start.10) | collective-permute-done | bytes 524320 | tf_op jit(solution)/shard_map/ppermute | solution.py:27
  138.5 12.7 %collective-permute-done.9 = bf16[1024,256]{1,0:T(8,128)(2,1)S(1)} collective-permute-done((bf16[1024,256]{1,0:T(8,128)(2,1)S(1)}, bf16[1024,256]{1,0:T(8,128)(2,1)S(1)}, u32[]{:S(2)}, u32[]{:S(2)}) %collective-permute-start.9) | collective-permute-done | bytes 524320 | tf_op jit(solution)/shard_map/ppermute | solution.py:27
  153.7 17.7 %attend_slash.3.refs_5_ = f32[2,8,512,256]{3,2,1,0:T(8,128)} custom-call(s32[2]{0:T(128)} %pad_add_fusion.info, s32[4,8]{1,0:T(4,128)} %constant_dynamic-slice_fusion.3.slash, bf16[512,4096]{1,0:T(8,128)(2,1)} %refs_0_.9, bf16[512,3072]{1,0:T(8,128)(2,1)} %copy-done.2, bf16[1024,512]{1,0:T(8,128)(2,1)} %get-tuple-element.22.refs_2_, ...), custom_call_target="tpu_custom_call" | custom-call | flops 8589934592 | bytes 10485760 | tf_op jit(solution)/shard_map/attend_slash/pallas_call | solution.py:349
  171.3 60.2 %attend_vertical.3 = (bf16[512,1024]{1,0:T(8,128)(2,1)}, bf16[512,1024]{1,0:T(8,128)(2,1)}) custom-call(s32[2]{0:T(128)} %pad_add_fusion.info, s32[4,8]{1,0:T(4,128)} %constant_dynamic-slice_fusion.4.vert, s32[4,8]{1,0:T(4,128)} %constant_dynamic-slice_fusion.3.slash, bf16[512,4096]{1,0:T(8,128)(2,1)} %refs_0_.9, bf16[512,3072]{1,0:T(8,128)(2,1)} %copy-done.2, ...), custom_call_target="tpu_custom_call" | custom-call | flops 8589934592 | bytes 10485760 | tf_op jit(solution)/shard_map/attend_vertical/pallas_call | solution.py:374
  231.6 2.6 collective-permute-start.14
  235.2 17.9 %attend_slash.2.refs_5_ = f32[2,8,512,256]{3,2,1,0:T(8,128)} custom-call(s32[2]{0:T(128)} %pad_add_fusion.info, s32[4,8]{1,0:T(4,128)} %constant_dynamic-slice_fusion.3.slash, bf16[512,4096]{1,0:T(8,128)(2,1)} %refs_0_.9, bf16[512,3072]{1,0:T(8,128)(2,1)} %copy-done.2, bf16[1024,512]{1,0:T(8,128)(2,1)} %get-tuple-element.15.refs_2_, ...), custom_call_target="tpu_custom_call" | custom-call | flops 8589934592 | bytes 10485760 | tf_op jit(solution)/shard_map/attend_slash/pallas_call | solution.py:349
  253.1 60.2 %attend_vertical.2 = (bf16[512,1024]{1,0:T(8,128)(2,1)}, bf16[512,1024]{1,0:T(8,128)(2,1)}) custom-call(s32[2]{0:T(128)} %pad_add_fusion.info, s32[4,8]{1,0:T(4,128)} %constant_dynamic-slice_fusion.4.vert, s32[4,8]{1,0:T(4,128)} %constant_dynamic-slice_fusion.3.slash, bf16[512,4096]{1,0:T(8,128)(2,1)} %refs_0_.9, bf16[512,3072]{1,0:T(8,128)(2,1)} %copy-done.2, ...), custom_call_target="tpu_custom_call" | custom-call | flops 8589934592 | bytes 10485760 | tf_op jit(solution)/shard_map/attend_vertical/pallas_call | solution.py:374
  314.3 16.4 %project.2.refs_4_ = f32[512,4096]{1,0:T(8,128)} custom-call(s32[2]{0:T(128)} %pad_add_fusion.info, bf16[512,1024]{1,0:T(8,128)(2,1)} %get-tuple-element.23.refs_0_, bf16[512,1024]{1,0:T(8,128)(2,1)} %copy-done.4, bf16[4096,4096]{1,0:T(8,128)(2,1)} %refs_3_.3, bf16[4096,4096]{1,0:T(8,128)(2,1)} %refs_3_.3), custom_call_target="tpu_custom_call" | custom-call | flops 8589934592 | bytes 35651584 | tf_op jit(solution)/shard_map/project/pallas_call | solution.py:431
  331.7 17.4 %project.3 = bf16[512,4096]{1,0:T(8,128)(2,1)} custom-call(s32[2]{0:T(128)} %pad_add_fusion.info, bf16[512,1024]{1,0:T(8,128)(2,1)} %get-tuple-element.20.refs_0_, bf16[512,1024]{1,0:T(8,128)(2,1)} %copy-done.5, bf16[4096,4096]{1,0:T(8,128)(2,1)} %refs_3_.3, bf16[4096,4096]{1,0:T(8,128)(2,1)} %refs_3_.3, f32[512,4096]{1,0:T(8,128)} %project.2.refs_4_), custom_call_target="tpu_custom_call" | custom-call | flops 8589934592 | bytes 35651584 | tf_op jit(solution)/shard_map/project/pallas_call | solution.py:431
  (51 shorter events, 15.4 us)
Async XLA Ops:
  0.0 6.3 %copy-start = (s32[8,8]{1,0:T(8,128)S(1)}, s32[8,8]{1,0:T(8,128)}, u32[]{:S(2)}) copy-start(s32[8,8]{1,0:T(8,128)} %param.9) | copy-start | bytes 772
  0.0 1.9 copy-start.3
  5.0 6.2 %collective-permute-start = (bf16[512,3072]{1,0:T(8,128)(2,1)}, bf16[512,3072]{1,0:T(8,128)(2,1)S(1)}, u32[]{:S(2)}, u32[]{:S(2)}) collective-permute-start(bf16[512,3072]{1,0:T(8,128)(2,1)} %pad_maximum_fusion), channel_id=1, source_target_pairs={{0,1},{1,0},{2,3},{3,2},{4,5},{5,4},{6,7},{7,6},{8,9},{9,8},{10,11... | collective-permute-start | bytes 9437192 | tf_op jit(solution)/shard_map/ppermute | solution.py:27
  11.2 1.7 copy-start.2
  17.4 66.5 %copy-start.7 = (bf16[1024,512]{1,0:T(8,128)(2,1)S(1)}, bf16[1024,512]{1,0:T(8,128)(2,1)}, u32[]{:S(2)}) copy-start(bf16[1024,512]{1,0:T(8,128)(2,1)} %get-tuple-element.22.refs_2_) | copy-start | bytes 3145732
  17.4 69.2 %copy-start.8 = (s32[8,8]{1,0:T(8,128)S(1)}, s32[8,8]{1,0:T(8,128)}, u32[]{:S(2)}) copy-start(s32[8,8]{1,0:T(8,128)} %param.10) | copy-start | bytes 772
  17.4 19.9 %collective-permute-start.5 = (bf16[1024,256]{1,0:T(8,128)(2,1)}, bf16[1024,256]{1,0:T(8,128)(2,1)S(1)}, u32[]{:S(2)}, u32[]{:S(2)}) collective-permute-start(bf16[1024,256]{1,0:T(8,128)(2,1)} %get-tuple-element.19), channel_id=1, source_target_pairs={{0,6},{1,7},{2,4},{3,5},{4,2},{5,3},{6,0},{7,1},{8,14},{9,15},{10,... | collective-permute-start | bytes 1572872 | tf_op jit(solution)/shard_map/ppermute | solution.py:27
  19.6 46.5 %collective-permute-start.4 = (bf16[1024,256]{1,0:T(8,128)(2,1)}, bf16[1024,256]{1,0:T(8,128)(2,1)S(1)}, u32[]{:S(2)}, u32[]{:S(2)}) collective-permute-start(bf16[1024,256]{1,0:T(8,128)(2,1)} %get-tuple-element.18), channel_id=1, source_target_pairs={{0,4},{1,5},{2,6},{3,7},{4,0},{5,1},{6,2},{7,3},{8,12},{9,13},{10,... | collective-permute-start | bytes 1572872 | tf_op jit(solution)/shard_map/ppermute | solution.py:27
  19.8 46.3 %collective-permute-start.3 = (bf16[1024,256]{1,0:T(8,128)(2,1)}, bf16[1024,256]{1,0:T(8,128)(2,1)S(1)}, u32[]{:S(2)}, u32[]{:S(2)}) collective-permute-start(bf16[1024,256]{1,0:T(8,128)(2,1)} %get-tuple-element.17), channel_id=1, source_target_pairs={{0,2},{1,3},{2,0},{3,1},{4,6},{5,7},{6,4},{7,5},{8,10},{9,11},{10,... | collective-permute-start | bytes 1572872 | tf_op jit(solution)/shard_map/ppermute | solution.py:27
  20.1 63.8 %collective-permute-start.12 = (bf16[1024,512]{1,0:T(8,128)(2,1)}, bf16[1024,512]{1,0:T(8,128)(2,1)}, u32[]{:S(2)}, u32[]{:S(2)}) collective-permute-start(bf16[1024,512]{1,0:T(8,128)(2,1)} %get-tuple-element.22.refs_2_), channel_id=1, source_target_pairs={{0,4},{1,5},{2,6},{3,7},{4,8},{5,9},{6,10},{7,11},{8,12},{9,13},{1... | collective-permute-start | bytes 3145736 | tf_op jit(solution)/shard_map/ppermute | solution.py:22
  66.1 62.5 %copy-start.6 = (bf16[1024,512]{1,0:T(8,128)(2,1)S(1)}, bf16[1024,512]{1,0:T(8,128)(2,1)}, u32[]{:S(2)}) copy-start(bf16[1024,512]{1,0:T(8,128)(2,1)} %get-tuple-element.15.refs_2_) | copy-start | bytes 3145732
  67.3 14.9 %collective-permute-start.6 = (bf16[1024,256]{1,0:T(8,128)(2,1)S(1)}, bf16[1024,256]{1,0:T(8,128)(2,1)S(1)}, u32[]{:S(2)}, u32[]{:S(2)}) collective-permute-start(bf16[1024,256]{1,0:T(8,128)(2,1)S(1)} %add_add_fusion), channel_id=1, source_target_pairs={{0,8},{1,9},{2,10},{3,11},{4,12},{5,13},{6,14},{7,15},{8,16},{9,17... | collective-permute-start | bytes 1572872 | tf_op jit(solution)/shard_map/ppermute | solution.py:22
  68.6 60.0 %collective-permute-start.1 = (bf16[1024,512]{1,0:T(8,128)(2,1)}, bf16[1024,512]{1,0:T(8,128)(2,1)}, u32[]{:S(2)}, u32[]{:S(2)}) collective-permute-start(bf16[1024,512]{1,0:T(8,128)(2,1)} %get-tuple-element.15.refs_2_), channel_id=1, source_target_pairs={{0,4},{1,5},{2,6},{3,7},{4,8},{5,9},{6,10},{7,11},{8,12},{9,13},{1... | collective-permute-start | bytes 3145736 | tf_op jit(solution)/shard_map/ppermute | solution.py:22
  82.4 27.8 %collective-permute-start.7 = (bf16[1024,256]{1,0:T(8,128)(2,1)S(1)}, bf16[1024,256]{1,0:T(8,128)(2,1)S(1)}, u32[]{:S(2)}, u32[]{:S(2)}) collective-permute-start(bf16[1024,256]{1,0:T(8,128)(2,1)S(1)} %add.43), channel_id=1, source_target_pairs={{0,16},{1,17},{2,18},{3,19},{4,20},{5,21},{6,22},{7,23},{8,24},{9,... | collective-permute-start | bytes 1572872 | tf_op jit(solution)/shard_map/ppermute | solution.py:22
  84.0 68.6 %collective-permute-start.13 = (bf16[1024,512]{1,0:T(8,128)(2,1)S(1)}, bf16[1024,512]{1,0:T(8,128)(2,1)S(1)}, u32[]{:S(2)}, u32[]{:S(2)}) collective-permute-start(bf16[1024,512]{1,0:T(8,128)(2,1)S(1)} %broadcast_select_fusion), channel_id=1, source_target_pairs={{0,2},{1,3},{2,0},{3,1},{4,6},{5,7},{6,4},{7,5},{8,10},{9,11},{10,... | collective-permute-start | bytes 3145736 | tf_op jit(solution)/shard_map/ppermute | solution.py:27
  110.3 28.2 %collective-permute-start.10 = (bf16[1024,256]{1,0:T(8,128)(2,1)S(1)}, bf16[1024,256]{1,0:T(8,128)(2,1)S(1)}, u32[]{:S(2)}, u32[]{:S(2)}) collective-permute-start(bf16[1024,256]{1,0:T(8,128)(2,1)S(1)} %add.44), channel_id=1, source_target_pairs={{0,6},{1,7},{2,4},{3,5},{4,2},{5,3},{6,0},{7,1},{8,14},{9,15},{10,... | collective-permute-start | bytes 1572872 | tf_op jit(solution)/shard_map/ppermute | solution.py:27
  127.5 23.6 %collective-permute-start.9 = (bf16[1024,256]{1,0:T(8,128)(2,1)S(1)}, bf16[1024,256]{1,0:T(8,128)(2,1)S(1)}, u32[]{:S(2)}, u32[]{:S(2)}) collective-permute-start(bf16[1024,256]{1,0:T(8,128)(2,1)S(1)} %add.44), channel_id=1, source_target_pairs={{0,4},{1,5},{2,6},{3,7},{4,0},{5,1},{6,2},{7,3},{8,12},{9,13},{10,... | collective-permute-start | bytes 1572872 | tf_op jit(solution)/shard_map/ppermute | solution.py:27
  127.5 23.6 %collective-permute-start.8 = (bf16[1024,256]{1,0:T(8,128)(2,1)S(1)}, bf16[1024,256]{1,0:T(8,128)(2,1)S(1)}, u32[]{:S(2)}, u32[]{:S(2)}) collective-permute-start(bf16[1024,256]{1,0:T(8,128)(2,1)S(1)} %add.44), channel_id=1, source_target_pairs={{0,2},{1,3},{2,0},{3,1},{4,6},{5,7},{6,4},{7,5},{8,10},{9,11},{10,... | collective-permute-start | bytes 1572872 | tf_op jit(solution)/shard_map/ppermute | solution.py:27
  128.7 105.5 %collective-permute-start.2 = (bf16[1024,512]{1,0:T(8,128)(2,1)S(1)}, bf16[1024,512]{1,0:T(8,128)(2,1)S(1)}, u32[]{:S(2)}, u32[]{:S(2)}) collective-permute-start(bf16[1024,512]{1,0:T(8,128)(2,1)S(1)} %broadcast_select_fusion.1), channel_id=1, source_target_pairs={{0,2},{1,3},{2,0},{3,1},{4,6},{5,7},{6,4},{7,5},{8,10},{9,11},{10,... | collective-permute-start | bytes 3145736 | tf_op jit(solution)/shard_map/ppermute | solution.py:27
  152.7 1.0 copy-start.9
  231.6 81.8 %collective-permute-start.14 = (bf16[512,1024]{1,0:T(8,128)(2,1)}, bf16[512,1024]{1,0:T(8,128)(2,1)S(1)}, u32[]{:S(2)}, u32[]{:S(2)}) collective-permute-start(bf16[512,1024]{1,0:T(8,128)(2,1)} %get-tuple-element.24), channel_id=1, source_target_pairs={{0,1},{1,0},{2,3},{3,2},{4,5},{5,4},{6,7},{7,6},{8,9},{9,8},{10,11... | collective-permute-start | bytes 3145736 | tf_op jit(solution)/shard_map/ppermute | solution.py:27
  313.3 17.4 %collective-permute-start.11 = (bf16[512,1024]{1,0:T(8,128)(2,1)}, bf16[512,1024]{1,0:T(8,128)(2,1)S(1)}, u32[]{:S(2)}, u32[]{:S(2)}) collective-permute-start(bf16[512,1024]{1,0:T(8,128)(2,1)} %get-tuple-element.21), channel_id=1, source_target_pairs={{0,1},{1,0},{2,3},{3,2},{4,5},{5,4},{6,7},{7,6},{8,9},{9,8},{10,11... | collective-permute-start | bytes 3145736 | tf_op jit(solution)/shard_map/ppermute | solution.py:27
  330.7 1.1 copy-start.5
  331.7 17.4 %copy-start.1 = (s32[8,8]{1,0:T(8,128)S(1)}, s32[8,8]{1,0:T(8,128)}, u32[]{:S(2)}) copy-start(s32[8,8]{1,0:T(8,128)} %param.9) | copy-start | bytes 772
  (2 other events, 2.0 us)
where the time goes:
time: 350 us; the launch traced here: 349 us
  Pallas kernels  194 us (55%)
  waiting for transfers between devices  102 us (29%)
  starting transfers between devices  36.4 us (10%)
  local copies, waits for them, and re-layouts  9.95 us (3%)
  other arithmetic  6.62 us (2%)
    pallas_call x2, Pallas kernels, over_vertical(): pl.pallas_call(functools.partial(vertical_kernel, cfg + (self.plane, self...  120 us
    ppermute x11, waiting for transfers between devices, crossed(): return lax.ppermute(value, 'ctx', [(i, i ^ bits) for i in range(size)])  67.1 us
    pallas_call x2, Pallas kernels, over_slash(): pl.pallas_call(functools.partial(slash_kernel, cfg), grid_spec=pltpu.Pref...  35.6 us
    ppermute x4, waiting for transfers between devices, shifted(): return lax.ppermute(value, 'ctx', [(i, i + by) for i in range(size - by)])  34.6 us
    pallas_call x2, Pallas kernels, project(): pl.pallas_call(functools.partial(project_kernel, n, before is not None),...  33.8 us
    ppermute x11, starting transfers between devices, crossed(): return lax.ppermute(value, 'ctx', [(i, i ^ bits) for i in range(size)])  28.6 us
    ppermute x4, starting transfers between devices, shifted(): return lax.ppermute(value, 'ctx', [(i, i + by) for i in range(size - by)])  7.82 us
  transfers between devices with their start and end apart: 15, of which 7 were waited for; matrix products, arithmetic and copies ran while one was open for 2% of the time, Pallas kernels for 49%

commit v1 on v0

--- a/solution.py
+++ b/solution.py
@@ -91,7 +91,7 @@
         ),
         name="prepare",
     )(info, vert, *data)
-    return outs[:n_chunks], outs[n_chunks:]
+    return list(outs[:n_chunks]), list(outs[n_chunks:])
 
 
 def onehot_rows(shape, at, dtype):
@@ -132,7 +132,6 @@
     chip_blocks = pair * local
     chip_rows = chip_blocks * BLK
     width = n_slash * BLK
-    step = min(2 * BLK, width)
     factor = math.log2(math.e) / math.sqrt(HD)
 
     for back in range(reach + 1):
@@ -177,9 +176,7 @@
             return
         for j in range(n_slash):
             vgs[at][j * BLK : (j + 1) * BLK, :HD] = win[take(i, j), HD:]
-        for t in range(0, width, step):
-            p = exponentials(qx[i], kgs[at][t : t + step, :], factor)
-            ps[at][:, t : t + step] = p.astype(ps[at].dtype)
+        ps[at][...] = exponentials(qx[i], kgs[at][...], factor).astype(ps[at].dtype)
 
     place_keys(0, 0)
     pipelined(chip_blocks, stage)
@@ -243,9 +240,7 @@
             good[...] = jnp.minimum(good[...], jnp.min(fine, axis=0, keepdims=True))
         if isinstance(i, int) and i == chip_blocks:
             return
-        for t in range(0, wide, step):
-            p = exponentials(qx[i], ke[t : t + step, :], factor)
-            ps[at][:, t : t + step] = p.astype(ps[at].dtype)
+        ps[at][...] = exponentials(qx[i], ke[...], factor).astype(ps[at].dtype)
 
     pipelined(chip_blocks, stage)
 
@@ -413,7 +408,7 @@
 def project(pieces, before, out_weight, info, chunks, dtype):
     rows, wide = pieces[0][2].shape
     columns = out_weight.shape[1]
-    tile = min(512, columns)
+    tile = min(1024, columns)
     n = len(pieces)
 
     def weight_spec(swap, c):
@@ -478,15 +473,16 @@
     total = listed[0]
     for k in range(1, plane):
         total = total + crossed(listed[k], k * pair)
+    total, own[1:] = lax.optimization_barrier((total, own[1:]))
     step = 1
     while step < chips // plane:
         total = total + shifted(total, step * plane * pair)
         step *= 2
-    kv_vert = jnp.concatenate([total] + [crossed(total, k * pair) for k in range(1, plane)], 0)
 
     attention = Attention(queries, other, info, vert, slash, masks, heads, local, plane)
-    near, far = [], []
-    for c in range(heads // per_chunk):
+    chunks = heads // per_chunk
+    all_windows, sums = [], []
+    for c in range(chunks):
         windows = [own[c]]
         if pair == 2 and reach == 2 and chips % 2 == 0:
             two_back = shifted(own[c], 2 * pair)
@@ -494,9 +490,14 @@
             windows += [crossed(passed, pair), two_back]
         else:
             windows += [shifted(own[c], pair * d) for d in range(1, reach + 1)]
-        first = c * per_chunk
-        sums = attention.over_slash(first, per_chunk, windows)
-        att = attention.over_vertical(first, per_chunk, windows, sums, kv_vert)
+        all_windows.append(windows)
+        sums.append(attention.over_slash(c * per_chunk, per_chunk, windows))
+    gathered = [total] + [crossed(total, k * pair) for k in range(1, plane)]
+    gathered, sums = lax.optimization_barrier((gathered, sums))
+    kv_vert = jnp.concatenate(gathered, 0)
+    near, far = [], []
+    for c in range(chunks):
+        att = attention.over_vertical(c * per_chunk, per_chunk, all_windows[c], sums[c], kv_vert)
         near.append((False, c, att[0]))
         if pair == 2:
             far.append((True, c, crossed(att[1], 1)))
@@ -505,7 +506,6 @@
         attended = lax.all_gather(attended, "head", axis=1, tiled=True)
         output = jnp.dot(attended, out_weight, preferred_element_type=jnp.float32)
         return output.astype(jnp.bfloat16)
-    chunks = heads // per_chunk
     first = None
     if chunks > 1:
         first = project(near[:-1] + far[:-1], None, out_weight, info, chunks, jnp.float32)

time: 350 us -> 328 us (0.937)
  waiting for transfers between devices: 102 us -> 80.5 us
    ppermute x11, waiting for transfers between devices: 67.1 us -> 46.3 us  [crossed(): return lax.ppermute(value, 'ctx', [(i, i ^ bits) for i in range(size)])]
    unnamed x22 -> x29, local copies, waits for them, and re-layouts: 5.72 us -> 7.37 us
  transfers between devices with their start and end apart: 15 -> 15, of which waited for: 7 -> 6; matrix products, arithmetic and copies ran while one was open for 2% -> 1% of each run, Pallas kernels for 49% -> 34%
where the time goes in v1:
time: 328 us; the launch traced here: 327 us
  Pallas kernels  192 us (59%)
  waiting for transfers between devices  80.5 us (25%)
  starting transfers between devices  38.2 us (12%)
  local copies, waits for them, and re-layouts  10.7 us (3%)
  other arithmetic  5.16 us (2%)
    pallas_call x2, Pallas kernels, over_vertical(): pl.pallas_call(functools.partial(vertical_kernel, cfg + (self.plane, self...  121 us
    ppermute x11, waiting for transfers between devices, crossed(): return lax.ppermute(value, 'ctx', [(i, i ^ bits) for i in range(size)])  46.3 us
    pallas_call x2, Pallas kernels, over_slash(): pl.pallas_call(functools.partial(slash_kernel, cfg), grid_spec=pltpu.Pref...  35.2 us
    ppermute x4, waiting for transfers between devices, shifted(): return lax.ppermute(value, 'ctx', [(i, i + by) for i in range(size - by)])  34.2 us
    pallas_call x2, Pallas kernels, project(): pl.pallas_call(functools.partial(project_kernel, n, before is not None),...  31.3 us
    ppermute x11, starting transfers between devices, crossed(): return lax.ppermute(value, 'ctx', [(i, i ^ bits) for i in range(size)])  30.5 us
    ppermute x4, starting transfers between devices, shifted(): return lax.ppermute(value, 'ctx', [(i, i + by) for i in range(size - by)])  7.64 us
    unnamed x29, local copies, waits for them, and re-layouts  7.37 us
  transfers between devices with their start and end apart: 15, of which 6 were waited for; matrix products, arithmetic and copies ran while one was open for 1% of the time, Pallas kernels for 34%

profile of v1, /device:TPU:25, one launch (start us, length us, event | category | flops | bytes accessed | tf_op | source)
XLA Modules:
  0.0 326.6 jit_solution(1651973219700242811)
XLA Ops:
  0.0 2.0 constant_dynamic-slice_fusion
  2.3 2.0 pad_maximum_fusion
  6.2 4.3 %collective-permute-done.refs_2_.refs_1_ = bf16[512,3072]{1,0:T(8,128)(2,1)S(1)} collective-permute-done((bf16[512,3072]{1,0:T(8,128)(2,1)}, bf16[512,3072]{1,0:T(8,128)(2,1)S(1)}, u32[]{:S(2)}, u32[]{:S(2)}) %collective-permute-start) | collective-permute-done | bytes 3145760 | tf_op jit(solution)/shard_map/ppermute | solution.py:27
  10.5 1.7 copy-done.2
  12.1 4.5 %prepare.1 = (bf16[1024,512]{1,0:T(8,128)(2,1)}, bf16[1024,512]{1,0:T(8,128)(2,1)}, bf16[1024,256]{1,0:T(8,128)(2,1)}, bf16[1024,256]{1,0:T(8,128)(2,1)}, bf16[1...) custom-call(s32[2]{0:T(128)} %pad_add_fusion.info, s32[4,8]{1,0:T(4,128)} %constant_dynamic-slice_fusion.4.vert, ...), custom_call_target="tpu_custom_call" | custom-call | bytes 8388608 | tf_op jit(solution)/shard_map/prepare/pallas_call | solution.py:80
  19.3 3.1 collective-permute-start.11
  22.4 7.6 %collective-permute-done.1 = bf16[1024,256]{1,0:T(8,128)(2,1)S(1)} collective-permute-done((bf16[1024,256]{1,0:T(8,128)(2,1)}, bf16[1024,256]{1,0:T(8,128)(2,1)S(1)}, u32[]{:S(2)}, u32[]{:S(2)}) %collective-permute-start.1) | collective-permute-done | bytes 524320 | tf_op jit(solution)/shard_map/ppermute | solution.py:27
  30.0 34.5 %collective-permute-done.2 = bf16[1024,256]{1,0:T(8,128)(2,1)S(1)} collective-permute-done((bf16[1024,256]{1,0:T(8,128)(2,1)}, bf16[1024,256]{1,0:T(8,128)(2,1)S(1)}, u32[]{:S(2)}, u32[]{:S(2)}) %collective-permute-start.2) | collective-permute-done | bytes 524320 | tf_op jit(solution)/shard_map/ppermute | solution.py:27
  65.7 1.9 collective-permute-start.4
  67.6 1.3 collective-permute-start.6
  69.1 1.5 collective-permute-start.12
  70.7 10.8 %collective-permute-done.6 = bf16[1024,256]{1,0:T(8,128)(2,1)S(1)} collective-permute-done((bf16[1024,256]{1,0:T(8,128)(2,1)S(1)}, bf16[1024,256]{1,0:T(8,128)(2,1)S(1)}, u32[]{:S(2)}, u32[]{:S(2)}) %collective-permute-start.6) | collective-permute-done | bytes 524320 | tf_op jit(solution)/shard_map/ppermute | solution.py:22
  81.6 1.3 collective-permute-start.7
  82.9 8.9 %collective-permute-done.4.refs_4_ = bf16[1024,512]{1,0:T(8,128)(2,1)} collective-permute-done((bf16[1024,512]{1,0:T(8,128)(2,1)}, bf16[1024,512]{1,0:T(8,128)(2,1)}, u32[]{:S(2)}, u32[]{:S(2)}) %collective-permute-start.4) | collective-permute-done | bytes 1048608 | tf_op jit(solution)/shard_map/ppermute | solution.py:22
  92.0 1.5 collective-permute-start.5
  94.9 14.5 %collective-permute-done.7 = bf16[1024,256]{1,0:T(8,128)(2,1)S(1)} collective-permute-done((bf16[1024,256]{1,0:T(8,128)(2,1)S(1)}, bf16[1024,256]{1,0:T(8,128)(2,1)S(1)}, u32[]{:S(2)}, u32[]{:S(2)}) %collective-permute-start.7) | collective-permute-done | bytes 524320 | tf_op jit(solution)/shard_map/ppermute | solution.py:22
  109.5 21.8 %collective-permute-start.10 = (bf16[1024,256]{1,0:T(8,128)(2,1)S(1)}, bf16[1024,256]{1,0:T(8,128)(2,1)S(1)}, u32[]{:S(2)}, u32[]{:S(2)}) collective-permute-start(bf16[1024,256]{1,0:T(8,128)(2,1)S(1)} %add.44), channel_id=1, source_target_pairs={{0,6},{1,7},{2,4},{3,5},{4,2},{5,3},{6,0},{7,1},{8,14},{9,15},{10,... | collective-permute-start | bytes 1572872 | tf_op jit(solution)/shard_map/ppermute | solution.py:27
  133.6 17.5 %attend_slash.2.refs_5_ = f32[2,8,512,256]{3,2,1,0:T(8,128)} custom-call(s32[2]{0:T(128)} %pad_add_fusion.info, s32[4,8]{1,0:T(4,128)} %constant_dynamic-slice_fusion.3.slash, bf16[512,4096]{1,0:T(8,128)(2,1)} %refs_0_.9, bf16[512,3072]{1,0:T(8,128)(2,1)} %copy-done.2, bf16[1024,512]{1,0:T(8,128)(2,1)} %get-tuple-element.30.refs_2_, ...), custom_call_target="tpu_custom_call" | custom-call | flops 8589934592 | bytes 10485760 | tf_op jit(solution)/shard_map/attend_slash/pallas_call | solution.py:344
  152.2 17.6 %attend_slash.3.refs_5_ = f32[2,8,512,256]{3,2,1,0:T(8,128)} custom-call(s32[2]{0:T(128)} %pad_add_fusion.info, s32[4,8]{1,0:T(4,128)} %constant_dynamic-slice_fusion.3.slash, bf16[512,4096]{1,0:T(8,128)(2,1)} %refs_0_.9, bf16[512,3072]{1,0:T(8,128)(2,1)} %copy-done.2, bf16[1024,512]{1,0:T(8,128)(2,1)} %get-tuple-element.28.refs_2_, ...), custom_call_target="tpu_custom_call" | custom-call | flops 8589934592 | bytes 10485760 | tf_op jit(solution)/shard_map/attend_slash/pallas_call | solution.py:344
  170.0 1.3 copy-done.9
  171.4 60.4 %attend_vertical.3 = (bf16[512,1024]{1,0:T(8,128)(2,1)}, bf16[512,1024]{1,0:T(8,128)(2,1)}) custom-call(s32[2]{0:T(128)} %pad_add_fusion.info, s32[4,8]{1,0:T(4,128)} %constant_dynamic-slice_fusion.4.vert, s32[4,8]{1,0:T(4,128)} %constant_dynamic-slice_fusion.3.slash, bf16[512,4096]{1,0:T(8,128)(2,1)} %refs_0_.9, bf16[512,3072]{1,0:T(8,128)(2,1)} %copy-done.2, ...), custom_call_target="tpu_custom_call" | custom-call | flops 8589934592 | bytes 10485760 | tf_op jit(solution)/shard_map/attend_vertical/pallas_call | solution.py:369
  232.8 60.5 %attend_vertical.2 = (bf16[512,1024]{1,0:T(8,128)(2,1)}, bf16[512,1024]{1,0:T(8,128)(2,1)}) custom-call(s32[2]{0:T(128)} %pad_add_fusion.info, s32[4,8]{1,0:T(4,128)} %constant_dynamic-slice_fusion.4.vert, s32[4,8]{1,0:T(4,128)} %constant_dynamic-slice_fusion.3.slash, bf16[512,4096]{1,0:T(8,128)(2,1)} %refs_0_.9, bf16[512,3072]{1,0:T(8,128)(2,1)} %copy-done.2, ...), custom_call_target="tpu_custom_call" | custom-call | flops 8589934592 | bytes 10485760 | tf_op jit(solution)/shard_map/attend_vertical/pallas_call | solution.py:369
  294.3 15.0 %project.2.refs_4_ = f32[512,4096]{1,0:T(8,128)} custom-call(s32[2]{0:T(128)} %pad_add_fusion.info, bf16[512,1024]{1,0:T(8,128)(2,1)} %get-tuple-element.39.refs_0_, bf16[512,1024]{1,0:T(8,128)(2,1)} %copy-done.5, bf16[4096,4096]{1,0:T(8,128)(2,1)} %refs_3_.3, bf16[4096,4096]{1,0:T(8,128)(2,1)} %refs_3_.3), custom_call_target="tpu_custom_call" | custom-call | flops 8589934592 | bytes 35651584 | tf_op jit(solution)/shard_map/project/pallas_call | solution.py:426
  310.4 16.3 %project.3 = bf16[512,4096]{1,0:T(8,128)(2,1)} custom-call(s32[2]{0:T(128)} %pad_add_fusion.info, bf16[512,1024]{1,0:T(8,128)(2,1)} %get-tuple-element.36.refs_0_, bf16[512,1024]{1,0:T(8,128)(2,1)} %copy-done.6, bf16[4096,4096]{1,0:T(8,128)(2,1)} %refs_3_.3, bf16[4096,4096]{1,0:T(8,128)(2,1)} %refs_3_.3, f32[512,4096]{1,0:T(8,128)} %project.2.refs_4_), custom_call_target="tpu_custom_call" | custom-call | flops 8589934592 | bytes 35651584 | tf_op jit(solution)/shard_map/project/pallas_call | solution.py:426
  (58 shorter events, 14.5 us)
Async XLA Ops:
  0.0 5.6 %copy-start = (s32[8,8]{1,0:T(8,128)S(1)}, s32[8,8]{1,0:T(8,128)}, u32[]{:S(2)}) copy-start(s32[8,8]{1,0:T(8,128)} %param.9) | copy-start | bytes 772
  0.0 2.0 copy-start.3
  0.0 2.2 copy-start.4
  4.3 6.2 %collective-permute-start = (bf16[512,3072]{1,0:T(8,128)(2,1)}, bf16[512,3072]{1,0:T(8,128)(2,1)S(1)}, u32[]{:S(2)}, u32[]{:S(2)}) collective-permute-start(bf16[512,3072]{1,0:T(8,128)(2,1)} %pad_maximum_fusion), channel_id=1, source_target_pairs={{0,1},{1,0},{2,3},{3,2},{4,5},{5,4},{6,7},{7,6},{8,9},{9,8},{10,11... | collective-permute-start | bytes 9437192 | tf_op jit(solution)/shard_map/ppermute | solution.py:27
  10.5 1.7 copy-start.2
  16.6 52.4 %copy-start.8 = (bf16[1024,512]{1,0:T(8,128)(2,1)S(1)}, bf16[1024,512]{1,0:T(8,128)(2,1)}, u32[]{:S(2)}) copy-start(bf16[1024,512]{1,0:T(8,128)(2,1)} %get-tuple-element.30.refs_2_) | copy-start | bytes 3145732
  16.6 13.4 %collective-permute-start.1 = (bf16[1024,256]{1,0:T(8,128)(2,1)}, bf16[1024,256]{1,0:T(8,128)(2,1)S(1)}, u32[]{:S(2)}, u32[]{:S(2)}) collective-permute-start(bf16[1024,256]{1,0:T(8,128)(2,1)} %get-tuple-element.24), channel_id=1, source_target_pairs={{0,2},{1,3},{2,0},{3,1},{4,6},{5,7},{6,4},{7,5},{8,10},{9,11},{10,... | collective-permute-start | bytes 1572872 | tf_op jit(solution)/shard_map/ppermute | solution.py:27
  17.8 46.6 %collective-permute-start.2 = (bf16[1024,256]{1,0:T(8,128)(2,1)}, bf16[1024,256]{1,0:T(8,128)(2,1)S(1)}, u32[]{:S(2)}, u32[]{:S(2)}) collective-permute-start(bf16[1024,256]{1,0:T(8,128)(2,1)} %get-tuple-element.25), channel_id=1, source_target_pairs={{0,4},{1,5},{2,6},{3,7},{4,0},{5,1},{6,2},{7,3},{8,12},{9,13},{10,... | collective-permute-start | bytes 1572872 | tf_op jit(solution)/shard_map/ppermute | solution.py:27
  19.1 45.4 %collective-permute-start.3 = (bf16[1024,256]{1,0:T(8,128)(2,1)}, bf16[1024,256]{1,0:T(8,128)(2,1)S(1)}, u32[]{:S(2)}, u32[]{:S(2)}) collective-permute-start(bf16[1024,256]{1,0:T(8,128)(2,1)} %get-tuple-element.26), channel_id=1, source_target_pairs={{0,6},{1,7},{2,4},{3,5},{4,2},{5,3},{6,0},{7,1},{8,14},{9,15},{10,... | collective-permute-start | bytes 1572872 | tf_op jit(solution)/shard_map/ppermute | solution.py:27
  19.3 49.7 %collective-permute-start.11 = (bf16[1024,512]{1,0:T(8,128)(2,1)}, bf16[1024,512]{1,0:T(8,128)(2,1)}, u32[]{:S(2)}, u32[]{:S(2)}) collective-permute-start(bf16[1024,512]{1,0:T(8,128)(2,1)} %get-tuple-element.30.refs_2_), channel_id=1, source_target_pairs={{0,4},{1,5},{2,6},{3,7},{4,8},{5,9},{6,10},{7,11},{8,12},{9,13},{1... | collective-permute-start | bytes 3145736 | tf_op jit(solution)/shard_map/ppermute | solution.py:22
  64.5 27.4 %copy-start.7 = (bf16[1024,512]{1,0:T(8,128)(2,1)S(1)}, bf16[1024,512]{1,0:T(8,128)(2,1)}, u32[]{:S(2)}) copy-start(bf16[1024,512]{1,0:T(8,128)(2,1)} %get-tuple-element.28.refs_2_) | copy-start | bytes 3145732
  65.7 26.1 %collective-permute-start.4 = (bf16[1024,512]{1,0:T(8,128)(2,1)}, bf16[1024,512]{1,0:T(8,128)(2,1)}, u32[]{:S(2)}, u32[]{:S(2)}) collective-permute-start(bf16[1024,512]{1,0:T(8,128)(2,1)} %get-tuple-element.28.refs_2_), channel_id=1, source_target_pairs={{0,4},{1,5},{2,6},{3,7},{4,8},{5,9},{6,10},{7,11},{8,12},{9,13},{1... | collective-permute-start | bytes 3145736 | tf_op jit(solution)/shard_map/ppermute | solution.py:22
  67.6 13.8 %collective-permute-start.6 = (bf16[1024,256]{1,0:T(8,128)(2,1)S(1)}, bf16[1024,256]{1,0:T(8,128)(2,1)S(1)}, u32[]{:S(2)}, u32[]{:S(2)}) collective-permute-start(bf16[1024,256]{1,0:T(8,128)(2,1)S(1)} %add_add_fusion), channel_id=1, source_target_pairs={{0,8},{1,9},{2,10},{3,11},{4,12},{5,13},{6,14},{7,15},{8,16},{9,17... | collective-permute-start | bytes 1572872 | tf_op jit(solution)/shard_map/ppermute | solution.py:22
  69.1 24.4 %copy-start.10 = (s32[8,8]{1,0:T(8,128)S(1)}, s32[8,8]{1,0:T(8,128)}, u32[]{:S(2)}) copy-start(s32[8,8]{1,0:T(8,128)} %param.10) | copy-start | bytes 772
  69.1 63.5 %collective-permute-start.12 = (bf16[1024,512]{1,0:T(8,128)(2,1)S(1)}, bf16[1024,512]{1,0:T(8,128)(2,1)S(1)}, u32[]{:S(2)}, u32[]{:S(2)}) collective-permute-start(bf16[1024,512]{1,0:T(8,128)(2,1)S(1)} %broadcast_select_fusion), channel_id=1, source_target_pairs={{0,2},{1,3},{2,0},{3,1},{4,6},{5,7},{6,4},{7,5},{8,10},{9,11},{10,... | collective-permute-start | bytes 3145736 | tf_op jit(solution)/shard_map/ppermute | solution.py:27
  81.6 27.8 %collective-permute-start.7 = (bf16[1024,256]{1,0:T(8,128)(2,1)S(1)}, bf16[1024,256]{1,0:T(8,128)(2,1)S(1)}, u32[]{:S(2)}, u32[]{:S(2)}) collective-permute-start(bf16[1024,256]{1,0:T(8,128)(2,1)S(1)} %add.43), channel_id=1, source_target_pairs={{0,16},{1,17},{2,18},{3,19},{4,20},{5,21},{6,22},{7,23},{8,24},{9,... | collective-permute-start | bytes 1572872 | tf_op jit(solution)/shard_map/ppermute | solution.py:22
  92.0 59.2 %collective-permute-start.5 = (bf16[1024,512]{1,0:T(8,128)(2,1)S(1)}, bf16[1024,512]{1,0:T(8,128)(2,1)S(1)}, u32[]{:S(2)}, u32[]{:S(2)}) collective-permute-start(bf16[1024,512]{1,0:T(8,128)(2,1)S(1)} %broadcast_select_fusion.1), channel_id=1, source_target_pairs={{0,2},{1,3},{2,0},{3,1},{4,6},{5,7},{6,4},{7,5},{8,10},{9,11},{10,... | collective-permute-start | bytes 3145736 | tf_op jit(solution)/shard_map/ppermute | solution.py:27
  109.5 60.3 %collective-permute-start.10 = (bf16[1024,256]{1,0:T(8,128)(2,1)S(1)}, bf16[1024,256]{1,0:T(8,128)(2,1)S(1)}, u32[]{:S(2)}, u32[]{:S(2)}) collective-permute-start(bf16[1024,256]{1,0:T(8,128)(2,1)S(1)} %add.44), channel_id=1, source_target_pairs={{0,6},{1,7},{2,4},{3,5},{4,2},{5,3},{6,0},{7,1},{8,14},{9,15},{10,... | collective-permute-start | bytes 1572872 | tf_op jit(solution)/shard_map/ppermute | solution.py:27
  131.4 38.5 %collective-permute-start.9 = (bf16[1024,256]{1,0:T(8,128)(2,1)S(1)}, bf16[1024,256]{1,0:T(8,128)(2,1)S(1)}, u32[]{:S(2)}, u32[]{:S(2)}) collective-permute-start(bf16[1024,256]{1,0:T(8,128)(2,1)S(1)} %add.44), channel_id=1, source_target_pairs={{0,4},{1,5},{2,6},{3,7},{4,0},{5,1},{6,2},{7,3},{8,12},{9,13},{10,... | collective-permute-start | bytes 1572872 | tf_op jit(solution)/shard_map/ppermute | solution.py:27
  131.5 38.4 %collective-permute-start.8 = (bf16[1024,256]{1,0:T(8,128)(2,1)S(1)}, bf16[1024,256]{1,0:T(8,128)(2,1)S(1)}, u32[]{:S(2)}, u32[]{:S(2)}) collective-permute-start(bf16[1024,256]{1,0:T(8,128)(2,1)S(1)} %add.44), channel_id=1, source_target_pairs={{0,2},{1,3},{2,0},{3,1},{4,6},{5,7},{6,4},{7,5},{8,10},{9,11},{10,... | collective-permute-start | bytes 1572872 | tf_op jit(solution)/shard_map/ppermute | solution.py:27
  170.0 1.3 copy-start.9
  231.8 61.6 %collective-permute-start.14 = (bf16[512,1024]{1,0:T(8,128)(2,1)}, bf16[512,1024]{1,0:T(8,128)(2,1)S(1)}, u32[]{:S(2)}, u32[]{:S(2)}) collective-permute-start(bf16[512,1024]{1,0:T(8,128)(2,1)} %get-tuple-element.40), channel_id=1, source_target_pairs={{0,1},{1,0},{2,3},{3,2},{4,5},{5,4},{6,7},{7,6},{8,9},{9,8},{10,11... | collective-permute-start | bytes 3145736 | tf_op jit(solution)/shard_map/ppermute | solution.py:27
  293.3 16.0 %collective-permute-start.13 = (bf16[512,1024]{1,0:T(8,128)(2,1)}, bf16[512,1024]{1,0:T(8,128)(2,1)S(1)}, u32[]{:S(2)}, u32[]{:S(2)}) collective-permute-start(bf16[512,1024]{1,0:T(8,128)(2,1)} %get-tuple-element.37), channel_id=1, source_target_pairs={{0,1},{1,0},{2,3},{3,2},{4,5},{5,4},{6,7},{7,6},{8,9},{9,8},{10,11... | collective-permute-start | bytes 3145736 | tf_op jit(solution)/shard_map/ppermute | solution.py:27
  310.4 16.3 %copy-start.1 = (s32[8,8]{1,0:T(8,128)S(1)}, s32[8,8]{1,0:T(8,128)}, u32[]{:S(2)}) copy-start(s32[8,8]{1,0:T(8,128)} %param.9) | copy-start | bytes 772
  (4 other events, 4.1 us)

commit v2 on v1

--- a/solution.py
+++ b/solution.py
@@ -43,11 +43,13 @@
     chip_blocks = pair * local
     for e in range(heads):
         at = pl.multiple_of((core * heads + e) * HD, HD)
-        chip_kv[e, :dev_rows, :HD] = keys[:, pl.ds(at, HD)]
         chip_kv[e, :dev_rows, HD:] = values[:, pl.ds(at, HD)]
         if pair > 1:
-            chip_kv[e, dev_rows:, :HD] = other[:, e * HD : (e + 1) * HD]
             chip_kv[e, dev_rows:, HD:] = other[:, (heads + e) * HD : (heads + e + 1) * HD]
+        for b in range(pair * local):
+            rows = slice(b % local * BLK, (b % local + 1) * BLK)
+            block = keys[rows, pl.ds(at, HD)] if b < local else other[rows, e * HD : (e + 1) * HD]
+            chip_kv[e, b * BLK : (b + 1) * BLK, :HD] = block.T
         c, at = divmod(e, per_chunk)
         chip_outs[c][:, at * 2 * HD : (at + 1) * 2 * HD] = chip_kv[e]
     per = heads * n_vert // plane
@@ -101,8 +103,7 @@
 
 
 def exponentials(q, k, factor):
-    s = lax.dot_general(q, k, (((1,), (1,)), ((), ())), preferred_element_type=jnp.float32)
-    return jnp.exp2(s * factor)
+    return jnp.exp2(jnp.dot(q, k, preferred_element_type=jnp.float32) * factor)
 
 
 def pipelined(blocks, stage):
@@ -161,9 +162,9 @@
         here = chip * chip_blocks + within(i)
         for j in range(n_slash):
             off = slash[e, j]
-            rows = slice(j * BLK, (j + 1) * BLK)
-            kgs[at][rows, :HD] = win[take(i, j), :HD]
-            kgs[at][rows, HD:] = masks[jnp.where(off > here, 2, jnp.where(off == 0, 1, 0))]
+            cols = slice(j * BLK, (j + 1) * BLK)
+            kgs[at][:HD, cols] = win[take(i, j), :HD]
+            kgs[at][HD:, cols] = masks[jnp.where(off > here, 2, jnp.where(off == 0, 1, 0))]
 
     def stage(i, at, ahead, behind):
         if ahead:
@@ -209,17 +210,17 @@
         return found
 
     per = heads * n_vert // plane
-    lane = lax.broadcasted_iota(jnp.int32, (BLK, HD), 1)
+    row = lax.broadcasted_iota(jnp.int32, (HD, BLK), 0)
     for j in range(n_vert):
         flat = e * n_vert + j
         src = pl.multiple_of(((flat // per ^ chip % plane) * per + flat % per) * BLK, BLK)
         rows = slice(j * BLK, (j + 1) * BLK)
-        ke[rows, :HD] = kv_vert[pl.ds(src, BLK), :HD]
+        ke[:HD, rows] = kv_vert[pl.ds(src, BLK), :HD]
         ve[rows, :HD] = kv_vert[pl.ds(src, BLK), HD:]
-        bias = jnp.zeros((BLK, HD), jnp.float32)
+        bias = jnp.zeros((HD, BLK), jnp.float32)
         for i in range(chip_blocks):
-            bias = jnp.where((lane == i) & hidden(i, j), MASKED, bias)
-        ke[rows, HD:] = bias.astype(ke.dtype)
+            bias = jnp.where((row == i) & hidden(i, j), MASKED, bias)
+        ke[HD:, rows] = bias.astype(ke.dtype)
     ve[:, HD:] = jnp.ones((wide, HD), ve.dtype)
     for i in range(chip_blocks):
         slot, b = divmod(i, local)
@@ -247,7 +248,7 @@
     @pl.when(jnp.logical_not(jnp.min(good[...]) > 0.5))
     def _():
         vg[: n_slash * BLK, HD:] = jnp.ones((n_slash * BLK, HD), vg.dtype)
-        kg[n_slash * BLK :, :] = ke[...]
+        kg[:, n_slash * BLK :] = ke[...]
         vg[n_slash * BLK :, :] = ve[...]
         eye = onehot_rows((BLK, HD), lambda row: row, qx.dtype)
 
@@ -267,24 +268,21 @@
                 for d in range(1, reach + 1):
                     found = jnp.where(back == d, w_refs[d][at, :], found)
                 rows = slice(j * BLK, (j + 1) * BLK)
-                kg[rows, :HD] = found[:, :HD]
+                kg[:HD, rows] = found[:, :HD]
                 vg[rows, :HD] = found[:, HD:]
-                kg[rows, HD:] = masks[jnp.where(off > here, 2, jnp.where(off == 0, 1, 0))]
+                kg[HD:, rows] = masks[jnp.where(off > here, 2, jnp.where(off == 0, 1, 0))]
             for j in range(n_vert):
                 rows = slice((n_slash + j) * BLK, (n_slash + j + 1) * BLK)
-                kg[rows, HD:] = masks[jnp.where(hidden(i, j), 2, 0)]
+                kg[HD:, rows] = masks[jnp.where(hidden(i, j), 2, 0)]
             top = None
-            for t in range(0, kg.shape[0], step):
-                s = lax.dot_general(
-                    qx[i], kg[t : t + step, :], (((1,), (1,)), ((), ())),
-                    preferred_element_type=jnp.float32,
-                )
+            for t in range(0, kg.shape[1], step):
+                s = jnp.dot(qx[i], kg[:, t : t + step], preferred_element_type=jnp.float32)
                 sc[:, t : t + step] = s
                 for u in range(0, step, HD):
                     piece = s[:, u : u + HD]
                     top = piece if top is None else jnp.maximum(top, piece)
             top = jnp.max(top, axis=1, keepdims=True)
-            for t in range(0, kg.shape[0], step):
+            for t in range(0, kg.shape[1], step):
                 p = jnp.exp2((sc[:, t : t + step] - top) * factor)
                 pg[:, t : t + step] = p.astype(pg.dtype)
             acc = jnp.dot(pg[...], vg[...], preferred_element_type=jnp.float32)
@@ -352,7 +350,8 @@
                     pltpu.VMEM((sum(w.shape[0] for w in windows), 2 * HD), self.dtype),
                     pltpu.VMEM((self.blocks, rows, 2 * HD), self.dtype),
                 ]
-                + [pltpu.VMEM((width, 2 * HD), self.dtype)] * 4
+                + [pltpu.VMEM((2 * HD, width), self.dtype)] * 2
+                + [pltpu.VMEM((width, 2 * HD), self.dtype)] * 2
                 + [pltpu.VMEM((rows, width), self.dtype)] * 2,
             ),
             out_shape=jax.ShapeDtypeStruct(shape, jnp.float32),
@@ -375,14 +374,14 @@
                 + [self.acc_spec(), self.whole(kv_vert), self.whole(self.masks)],
                 out_specs=[out] * self.pair,
                 scratch_shapes=[
-                    pltpu.VMEM((width, 2 * HD), self.dtype),
+                    pltpu.VMEM((2 * HD, width), self.dtype),
                     pltpu.VMEM((width, 2 * HD), self.dtype),
                     pltpu.VMEM((self.blocks, rows, 2 * HD), self.dtype),
                     pltpu.VMEM((self.blocks, rows, HD), self.dtype),
                     pltpu.VMEM((1, HD), jnp.float32),
                     pltpu.VMEM((rows, width), self.dtype),
                     pltpu.VMEM((rows, width), self.dtype),
-                    pltpu.VMEM((both, 2 * HD), self.dtype),
+                    pltpu.VMEM((2 * HD, both), self.dtype),
                     pltpu.VMEM((both, 2 * HD), self.dtype),
                     pltpu.VMEM((rows, both), jnp.float32),
                     pltpu.VMEM((rows, both), self.dtype),
@@ -454,7 +453,7 @@
     chip, core = index // pair, index % pair
     info = jnp.stack([chip, core]).astype(jnp.int32)
     pos = jnp.arange(BLK)
-    causal = jnp.where(pos[:, None] > pos[None, :], MASKED, 0.0)
+    causal = jnp.where(pos[:, None] < pos[None, :], MASKED, 0.0)
     masks = jnp.stack([jnp.zeros_like(causal), causal, jnp.full_like(causal, MASKED)])
     masks = masks.astype(queries.dtype)
 
@@ -463,23 +462,26 @@
         return lax.dynamic_slice_in_dim(value, which * span, span, axis)
 
     vert, slash = part(vertical_blocks, 0, core), part(slash_offsets, 0, core)
-    other = None
+    kv_other = None
     if pair == 2:
-        sent = [part(a, 1, 1 - core) for a in (keys, values, queries)]
-        other = crossed(jnp.concatenate(sent, 1), 1)
+        kv_other = crossed(jnp.concatenate([part(a, 1, 1 - core) for a in (keys, values)], 1), 1)
     per_chunk = 2 if heads % 2 == 0 else 1
-    own, listed = prepare(info, vert, keys, values, other, heads, local, plane, per_chunk)
+    own, listed = prepare(info, vert, keys, values, kv_other, heads, local, plane, per_chunk)
 
     total = listed[0]
     for k in range(1, plane):
         total = total + crossed(listed[k], k * pair)
-    total, own[1:] = lax.optimization_barrier((total, own[1:]))
+    q_sent = part(queries, 1, 1 - core) if pair == 2 else None
+    total, own[0], q_sent = lax.optimization_barrier((total, own[0], q_sent))
+    q_other = crossed(q_sent, 1) if pair == 2 else None
     step = 1
     while step < chips // plane:
         total = total + shifted(total, step * plane * pair)
+        total, q_other = lax.optimization_barrier((total, q_other))
         step *= 2
-
-    attention = Attention(queries, other, info, vert, slash, masks, heads, local, plane)
+    total, own[1:] = lax.optimization_barrier((total, own[1:]))
+
+    attention = Attention(queries, q_other, info, vert, slash, masks, heads, local, plane)
     chunks = heads // per_chunk
     all_windows, sums = [], []
     for c in range(chunks):
@@ -493,7 +495,7 @@
         all_windows.append(windows)
         sums.append(attention.over_slash(c * per_chunk, per_chunk, windows))
     gathered = [total] + [crossed(total, k * pair) for k in range(1, plane)]
-    gathered, sums = lax.optimization_barrier((gathered, sums))
+    gathered, sums[0] = lax.optimization_barrier((gathered, sums[0]))
     kv_vert = jnp.concatenate(gathered, 0)
     near, far = [], []
     for c in range(chunks):

time: 328 us -> 330 us (level)
  waiting for transfers between devices: 80.5 us -> 93.7 us
  starting transfers between devices: 38.2 us -> 27.6 us
    ppermute x4, waiting for transfers between devices: 34.2 us -> 48.4 us  [shifted(): return lax.ppermute(value, 'ctx', [(i, i + by) for i in range(size - by)])]
    ppermute x11 -> x12, starting transfers between devices: 30.5 us -> 18.4 us  [crossed(): return lax.ppermute(value, 'ctx', [(i, i ^ bits) for i in range(size)])]
    unnamed x29 -> x25, local copies, waits for them, and re-layouts: 7.37 us -> 4.93 us
    ppermute x11 -> x12, waiting for transfers between devices: 46.3 us -> 45.3 us  [crossed(): return lax.ppermute(value, 'ctx', [(i, i ^ bits) for i in range(size)])]
  transfers between devices with their start and end apart: 15 -> 16, of which waited for: 6 -> 7; matrix products, arithmetic and copies ran while one was open for 1% -> 2% of each run, Pallas kernels for 34% -> 53%
where the time goes in v2:
time: 330 us
  Pallas kernels  194 us (59%)
  waiting for transfers between devices  93.7 us (28%)
  starting transfers between devices  27.6 us (8%)
  local copies, waits for them, and re-layouts  9.29 us (3%)
  other arithmetic  4.55 us (1%)
    pallas_call x2, Pallas kernels, over_vertical(): pl.pallas_call(functools.partial(vertical_kernel, cfg + (self.plane, self...  122 us
    ppermute x4, waiting for transfers between devices, shifted(): return lax.ppermute(value, 'ctx', [(i, i + by) for i in range(size - by)])  48.4 us
    ppermute x12, waiting for transfers between devices, crossed(): return lax.ppermute(value, 'ctx', [(i, i ^ bits) for i in range(size)])  45.3 us
    pallas_call x2, Pallas kernels, over_slash(): pl.pallas_call(functools.partial(slash_kernel, cfg), grid_spec=pltpu.Pref...  35.9 us
    pallas_call x2, Pallas kernels, project(): pl.pallas_call(functools.partial(project_kernel, n, before is not None),...  31.3 us
    ppermute x12, starting transfers between devices, crossed(): return lax.ppermute(value, 'ctx', [(i, i ^ bits) for i in range(size)])  18.4 us
    ppermute x4, starting transfers between devices, shifted(): return lax.ppermute(value, 'ctx', [(i, i + by) for i in range(size - by)])  9.19 us
  transfers between devices with their start and end apart: 16, of which 7 were waited for; matrix products, arithmetic and copies ran while one was open for 2% of the time, Pallas kernels for 53%

profile of v2, /device:TPU:25, one launch (start us, length us, event | category | flops | bytes accessed | tf_op | source)
XLA Modules:
  0.0 329.6 jit_solution(7605098409260155431)
XLA Ops:
  0.0 1.3 constant_dynamic-slice_fusion.1
  5.4 4.6 %prepare.1 = (bf16[1024,512]{1,0:T(8,128)(2,1)}, bf16[1024,512]{1,0:T(8,128)(2,1)}, bf16[1024,256]{1,0:T(8,128)(2,1)}, bf16[1024,256]{1,0:T(8,128)(2,1)}, bf16[1...) custom-call(s32[2]{0:T(128)} %pad_add_fusion.info, s32[4,8]{1,0:T(4,128)} %constant_dynamic-slice_fusion.4.vert, ...), custom_call_target="tpu_custom_call" | custom-call | bytes 8388608 | tf_op jit(solution)/shard_map/prepare/pallas_call | solution.py:82
  11.2 1.2 collective-permute-start.2
  12.6 1.8 constant_dynamic-slice_fusion
  14.4 8.9 %collective-permute-done.1 = bf16[1024,256]{1,0:T(8,128)(2,1)S(1)} collective-permute-done((bf16[1024,256]{1,0:T(8,128)(2,1)}, bf16[1024,256]{1,0:T(8,128)(2,1)S(1)}, u32[]{:S(2)}, u32[]{:S(2)}) %collective-permute-start.1) | collective-permute-done | bytes 524320 | tf_op jit(solution)/shard_map/ppermute | solution.py:27
  24.2 11.4 %collective-permute-done.3 = bf16[1024,256]{1,0:T(8,128)(2,1)} collective-permute-done((bf16[1024,256]{1,0:T(8,128)(2,1)}, bf16[1024,256]{1,0:T(8,128)(2,1)}, u32[]{:S(2)}, u32[]{:S(2)}) %collective-permute-start.3) | collective-permute-done | bytes 524320 | tf_op jit(solution)/shard_map/ppermute | solution.py:27
  35.6 1.3 add_add_fusion
  37.0 2.2 collective-permute-start.5
  39.1 3.1 collective-permute-start.12
  42.3 1.3 collective-permute-start.4
  43.6 23.4 %collective-permute-done.12.refs_4_ = bf16[1024,512]{1,0:T(8,128)(2,1)} collective-permute-done((bf16[1024,512]{1,0:T(8,128)(2,1)}, bf16[1024,512]{1,0:T(8,128)(2,1)}, u32[]{:S(2)}, u32[]{:S(2)}) %collective-permute-start.12) | collective-permute-done | bytes 1048608 | tf_op jit(solution)/shard_map/ppermute | solution.py:22
  67.0 1.3 broadcast_select_fusion
  68.9 1.3 collective-permute-start.6
  71.6 25.0 %collective-permute-done.6 = bf16[1024,256]{1,0:T(8,128)(2,1)S(1)} collective-permute-done((bf16[1024,256]{1,0:T(8,128)(2,1)S(1)}, bf16[1024,256]{1,0:T(8,128)(2,1)S(1)}, u32[]{:S(2)}, u32[]{:S(2)}) %collective-permute-start.6) | collective-permute-done | bytes 524320 | tf_op jit(solution)/shard_map/ppermute | solution.py:22
  96.8 9.9 %collective-permute-start.10 = (bf16[1024,256]{1,0:T(8,128)(2,1)S(1)}, bf16[1024,256]{1,0:T(8,128)(2,1)S(1)}, u32[]{:S(2)}, u32[]{:S(2)}) collective-permute-start(bf16[1024,256]{1,0:T(8,128)(2,1)S(1)} %add.43), channel_id=1, source_target_pairs={{0,4},{1,5},{2,6},{3,7},{4,0},{5,1},{6,2},{7,3},{8,12},{9,13},{10,... | collective-permute-start | bytes 1572872 | tf_op jit(solution)/shard_map/ppermute | solution.py:27
  107.9 3.5 %collective-permute-start.7 = (bf16[1024,512]{1,0:T(8,128)(2,1)S(1)}, bf16[1024,512]{1,0:T(8,128)(2,1)S(1)}, u32[]{:S(2)}, u32[]{:S(2)}) collective-permute-start(bf16[1024,512]{1,0:T(8,128)(2,1)S(1)} %copy-done.5), channel_id=1, source_target_pairs={{0,4},{1,5},{2,6},{3,7},{4,8},{5,9},{6,10},{7,11},{8,12},{9,13},{1... | collective-permute-start | bytes 3145736 | tf_op jit(solution)/shard_map/ppermute | solution.py:22
  111.4 17.9 %attend_slash.3.refs_5_ = f32[2,8,512,256]{3,2,1,0:T(8,128)} custom-call(s32[2]{0:T(128)} %pad_add_fusion.info, s32[4,8]{1,0:T(4,128)} %constant_dynamic-slice_fusion.3.slash, bf16[512,4096]{1,0:T(8,128)(2,1)} %refs_0_.9, bf16[512,2048]{1,0:T(8,128)(2,1)} %collective-permute-done.5.refs_1_, bf16[1024,512]{1,0:T(8,128)(2,1)} %get-tuple-element.43.refs_2_, ...), custom_call_target="tpu_custom_call" | custom-call | flops 8589934592 | bytes 10485760 | tf_op jit(solution)/shard_map/attend_slash/pallas_call | solution.py:342
  129.3 23.0 %collective-permute-done.10 = bf16[1024,256]{1,0:T(8,128)(2,1)S(1)} collective-permute-done((bf16[1024,256]{1,0:T(8,128)(2,1)S(1)}, bf16[1024,256]{1,0:T(8,128)(2,1)S(1)}, u32[]{:S(2)}, u32[]{:S(2)}) %collective-permute-start.10) | collective-permute-done | bytes 524320 | tf_op jit(solution)/shard_map/ppermute | solution.py:27
  153.4 1.3 copy-done.9
  154.7 61.2 %attend_vertical.3 = (bf16[512,1024]{1,0:T(8,128)(2,1)}, bf16[512,1024]{1,0:T(8,128)(2,1)}) custom-call(s32[2]{0:T(128)} %pad_add_fusion.info, s32[4,8]{1,0:T(4,128)} %constant_dynamic-slice_fusion.4.vert, s32[4,8]{1,0:T(4,128)} %constant_dynamic-slice_fusion.3.slash, bf16[512,4096]{1,0:T(8,128)(2,1)} %refs_0_.9, ...), custom_call_target="tpu_custom_call" | custom-call | flops 8589934592 | bytes 10485760 | tf_op jit(solution)/shard_map/attend_vertical/pallas_call | solution.py:368
  216.9 18.1 %attend_slash.2.refs_5_ = f32[2,8,512,256]{3,2,1,0:T(8,128)} custom-call(s32[2]{0:T(128)} %pad_add_fusion.info, s32[4,8]{1,0:T(4,128)} %constant_dynamic-slice_fusion.3.slash, bf16[512,4096]{1,0:T(8,128)(2,1)} %refs_0_.9, bf16[512,2048]{1,0:T(8,128)(2,1)} %collective-permute-done.5.refs_1_, bf16[1024,512]{1,0:T(8,128)(2,1)} %get-tuple-element.41.refs_2_, ...), custom_call_target="tpu_custom_call" | custom-call | flops 8589934592 | bytes 10485760 | tf_op jit(solution)/shard_map/attend_slash/pallas_call | solution.py:342
  235.0 61.2 %attend_vertical.2 = (bf16[512,1024]{1,0:T(8,128)(2,1)}, bf16[512,1024]{1,0:T(8,128)(2,1)}) custom-call(s32[2]{0:T(128)} %pad_add_fusion.info, s32[4,8]{1,0:T(4,128)} %constant_dynamic-slice_fusion.4.vert, s32[4,8]{1,0:T(4,128)} %constant_dynamic-slice_fusion.3.slash, bf16[512,4096]{1,0:T(8,128)(2,1)} %refs_0_.9, ...), custom_call_target="tpu_custom_call" | custom-call | flops 8589934592 | bytes 10485760 | tf_op jit(solution)/shard_map/attend_vertical/pallas_call | solution.py:368
  297.2 15.1 %project.2.refs_4_ = f32[512,4096]{1,0:T(8,128)} custom-call(s32[2]{0:T(128)} %pad_add_fusion.info, bf16[512,1024]{1,0:T(8,128)(2,1)} %get-tuple-element.51.refs_0_, bf16[512,1024]{1,0:T(8,128)(2,1)} %copy-done.2, bf16[4096,4096]{1,0:T(8,128)(2,1)} %refs_3_.3, bf16[4096,4096]{1,0:T(8,128)(2,1)} %refs_3_.3), custom_call_target="tpu_custom_call" | custom-call | flops 8589934592 | bytes 35651584 | tf_op jit(solution)/shard_map/project/pallas_call | solution.py:425
  313.4 16.3 %project.3 = bf16[512,4096]{1,0:T(8,128)(2,1)} custom-call(s32[2]{0:T(128)} %pad_add_fusion.info, bf16[512,1024]{1,0:T(8,128)(2,1)} %get-tuple-element.48.refs_0_, bf16[512,1024]{1,0:T(8,128)(2,1)} %copy-done.3, bf16[4096,4096]{1,0:T(8,128)(2,1)} %refs_3_.3, bf16[4096,4096]{1,0:T(8,128)(2,1)} %refs_3_.3, f32[512,4096]{1,0:T(8,128)} %project.2.refs_4_), custom_call_target="tpu_custom_call" | custom-call | flops 8589934592 | bytes 35651584 | tf_op jit(solution)/shard_map/project/pallas_call | solution.py:425
  (56 shorter events, 13.9 us)
Async XLA Ops:
  0.0 2.8 copy-start
  1.4 3.0 collective-permute-start
  10.0 13.3 %collective-permute-start.1 = (bf16[1024,256]{1,0:T(8,128)(2,1)}, bf16[1024,256]{1,0:T(8,128)(2,1)S(1)}, u32[]{:S(2)}, u32[]{:S(2)}) collective-permute-start(bf16[1024,256]{1,0:T(8,128)(2,1)} %get-tuple-element.30), channel_id=1, source_target_pairs={{0,2},{1,3},{2,0},{3,1},{4,6},{5,7},{6,4},{7,5},{8,10},{9,11},{10,... | collective-permute-start | bytes 1572872 | tf_op jit(solution)/shard_map/ppermute | solution.py:27
  11.2 13.0 %collective-permute-start.2 = (bf16[1024,256]{1,0:T(8,128)(2,1)}, bf16[1024,256]{1,0:T(8,128)(2,1)S(1)}, u32[]{:S(2)}, u32[]{:S(2)}) collective-permute-start(bf16[1024,256]{1,0:T(8,128)(2,1)} %get-tuple-element.31), channel_id=1, source_target_pairs={{0,4},{1,5},{2,6},{3,7},{4,0},{5,1},{6,2},{7,3},{8,12},{9,13},{10,... | collective-permute-start | bytes 1572872 | tf_op jit(solution)/shard_map/ppermute | solution.py:27
  12.4 23.2 %collective-permute-start.3 = (bf16[1024,256]{1,0:T(8,128)(2,1)}, bf16[1024,256]{1,0:T(8,128)(2,1)}, u32[]{:S(2)}, u32[]{:S(2)}) collective-permute-start(bf16[1024,256]{1,0:T(8,128)(2,1)} %get-tuple-element.32), channel_id=1, source_target_pairs={{0,6},{1,7},{2,4},{3,5},{4,2},{5,3},{6,0},{7,1},{8,14},{9,15},{10,... | collective-permute-start | bytes 1572872 | tf_op jit(solution)/shard_map/ppermute | solution.py:27
  12.6 23.0 %copy-start.7 = (bf16[1024,256]{1,0:T(8,128)(2,1)S(1)}, bf16[1024,256]{1,0:T(8,128)(2,1)}, u32[]{:S(2)}) copy-start(bf16[1024,256]{1,0:T(8,128)(2,1)} %get-tuple-element.29) | copy-start | bytes 1572868
  24.2 11.5 %copy-start.8 = (bf16[1024,256]{1,0:T(8,128)(2,1)}, bf16[1024,256]{1,0:T(8,128)(2,1)S(1)}, u32[]{:S(2)}) copy-start(bf16[1024,256]{1,0:T(8,128)(2,1)S(1)} %collective-permute-done.2) | copy-start | bytes 1572868
  37.0 31.9 %collective-permute-start.5 = (bf16[512,2048]{1,0:T(8,128)(2,1)S(1)}, bf16[512,2048]{1,0:T(8,128)(2,1)}, u32[]{:S(2)}, u32[]{:S(2)}) collective-permute-start(bf16[512,2048]{1,0:T(8,128)(2,1)S(1)} %constant_dynamic-slice_fusion), channel_id=1, source_target_pairs={{0,1},{1,0},{2,3},{3,2},{4,5},{5,4},{6,7},{7,6},{8,9},{9,8},{10,11... | collective-permute-start | bytes 6291464 | tf_op jit(solution)/shard_map/ppermute | solution.py:27
  39.1 27.9 %collective-permute-start.12 = (bf16[1024,512]{1,0:T(8,128)(2,1)}, bf16[1024,512]{1,0:T(8,128)(2,1)}, u32[]{:S(2)}, u32[]{:S(2)}) collective-permute-start(bf16[1024,512]{1,0:T(8,128)(2,1)} %get-tuple-element.43.refs_2_), channel_id=1, source_target_pairs={{0,4},{1,5},{2,6},{3,7},{4,8},{5,9},{6,10},{7,11},{8,12},{9,13},{1... | collective-permute-start | bytes 3145736 | tf_op jit(solution)/shard_map/ppermute | solution.py:22
  42.3 27.9 %copy-start.10 = (s32[8,8]{1,0:T(8,128)S(1)}, s32[8,8]{1,0:T(8,128)}, u32[]{:S(2)}) copy-start(s32[8,8]{1,0:T(8,128)} %param.10) | copy-start | bytes 772
  42.3 26.4 %collective-permute-start.4 = (bf16[1024,256]{1,0:T(8,128)(2,1)S(1)}, bf16[1024,256]{1,0:T(8,128)(2,1)S(1)}, u32[]{:S(2)}, u32[]{:S(2)}) collective-permute-start(bf16[1024,256]{1,0:T(8,128)(2,1)S(1)} %add_add_fusion), channel_id=1, source_target_pairs={{0,8},{1,9},{2,10},{3,11},{4,12},{5,13},{6,14},{7,15},{8,16},{9,17... | collective-permute-start | bytes 1572872 | tf_op jit(solution)/shard_map/ppermute | solution.py:22
  68.3 39.6 %copy-start.5 = (bf16[1024,512]{1,0:T(8,128)(2,1)S(1)}, bf16[1024,512]{1,0:T(8,128)(2,1)}, u32[]{:S(2)}) copy-start(bf16[1024,512]{1,0:T(8,128)(2,1)} %get-tuple-element.41.refs_2_) | copy-start | bytes 3145732
  68.4 43.0 %collective-permute-start.13 = (bf16[1024,512]{1,0:T(8,128)(2,1)S(1)}, bf16[1024,512]{1,0:T(8,128)(2,1)}, u32[]{:S(2)}, u32[]{:S(2)}) collective-permute-start(bf16[1024,512]{1,0:T(8,128)(2,1)S(1)} %broadcast_select_fusion), channel_id=1, source_target_pairs={{0,2},{1,3},{2,0},{3,1},{4,6},{5,7},{6,4},{7,5},{8,10},{9,11},{10,... | collective-permute-start | bytes 3145736 | tf_op jit(solution)/shard_map/ppermute | solution.py:27
  68.9 27.8 %collective-permute-start.6 = (bf16[1024,256]{1,0:T(8,128)(2,1)S(1)}, bf16[1024,256]{1,0:T(8,128)(2,1)S(1)}, u32[]{:S(2)}, u32[]{:S(2)}) collective-permute-start(bf16[1024,256]{1,0:T(8,128)(2,1)S(1)} %add.42), channel_id=1, source_target_pairs={{0,16},{1,17},{2,18},{3,19},{4,20},{5,21},{6,22},{7,23},{8,24},{9,... | collective-permute-start | bytes 1572872 | tf_op jit(solution)/shard_map/ppermute | solution.py:22
  96.8 55.5 %collective-permute-start.10 = (bf16[1024,256]{1,0:T(8,128)(2,1)S(1)}, bf16[1024,256]{1,0:T(8,128)(2,1)S(1)}, u32[]{:S(2)}, u32[]{:S(2)}) collective-permute-start(bf16[1024,256]{1,0:T(8,128)(2,1)S(1)} %add.43), channel_id=1, source_target_pairs={{0,4},{1,5},{2,6},{3,7},{4,0},{5,1},{6,2},{7,3},{8,12},{9,13},{10,... | collective-permute-start | bytes 1572872 | tf_op jit(solution)/shard_map/ppermute | solution.py:27
  106.7 45.6 %collective-permute-start.11 = (bf16[1024,256]{1,0:T(8,128)(2,1)S(1)}, bf16[1024,256]{1,0:T(8,128)(2,1)S(1)}, u32[]{:S(2)}, u32[]{:S(2)}) collective-permute-start(bf16[1024,256]{1,0:T(8,128)(2,1)S(1)} %add.43), channel_id=1, source_target_pairs={{0,6},{1,7},{2,4},{3,5},{4,2},{5,3},{6,0},{7,1},{8,14},{9,15},{10,... | collective-permute-start | bytes 1572872 | tf_op jit(solution)/shard_map/ppermute | solution.py:27
  106.7 45.5 %collective-permute-start.9 = (bf16[1024,256]{1,0:T(8,128)(2,1)S(1)}, bf16[1024,256]{1,0:T(8,128)(2,1)S(1)}, u32[]{:S(2)}, u32[]{:S(2)}) collective-permute-start(bf16[1024,256]{1,0:T(8,128)(2,1)S(1)} %add.43), channel_id=1, source_target_pairs={{0,2},{1,3},{2,0},{3,1},{4,6},{5,7},{6,4},{7,5},{8,10},{9,11},{10,... | collective-permute-start | bytes 1572872 | tf_op jit(solution)/shard_map/ppermute | solution.py:27
  107.9 44.4 %collective-permute-start.7 = (bf16[1024,512]{1,0:T(8,128)(2,1)S(1)}, bf16[1024,512]{1,0:T(8,128)(2,1)S(1)}, u32[]{:S(2)}, u32[]{:S(2)}) collective-permute-start(bf16[1024,512]{1,0:T(8,128)(2,1)S(1)} %copy-done.5), channel_id=1, source_target_pairs={{0,4},{1,5},{2,6},{3,7},{4,8},{5,9},{6,10},{7,11},{8,12},{9,13},{1... | collective-permute-start | bytes 3145736 | tf_op jit(solution)/shard_map/ppermute | solution.py:22
  152.5 64.5 %collective-permute-start.8 = (bf16[1024,512]{1,0:T(8,128)(2,1)S(1)}, bf16[1024,512]{1,0:T(8,128)(2,1)}, u32[]{:S(2)}, u32[]{:S(2)}) collective-permute-start(bf16[1024,512]{1,0:T(8,128)(2,1)S(1)} %broadcast_select_fusion.1), channel_id=1, source_target_pairs={{0,2},{1,3},{2,0},{3,1},{4,6},{5,7},{6,4},{7,5},{8,10},{9,11},{10,... | collective-permute-start | bytes 3145736 | tf_op jit(solution)/shard_map/ppermute | solution.py:27
  153.4 1.3 copy-start.9
  215.9 80.3 %collective-permute-start.15 = (bf16[512,1024]{1,0:T(8,128)(2,1)}, bf16[512,1024]{1,0:T(8,128)(2,1)S(1)}, u32[]{:S(2)}, u32[]{:S(2)}) collective-permute-start(bf16[512,1024]{1,0:T(8,128)(2,1)} %get-tuple-element.52), channel_id=1, source_target_pairs={{0,1},{1,0},{2,3},{3,2},{4,5},{5,4},{6,7},{7,6},{8,9},{9,8},{10,11... | collective-permute-start | bytes 3145736 | tf_op jit(solution)/shard_map/ppermute | solution.py:27
  296.2 16.1 %collective-permute-start.14 = (bf16[512,1024]{1,0:T(8,128)(2,1)}, bf16[512,1024]{1,0:T(8,128)(2,1)S(1)}, u32[]{:S(2)}, u32[]{:S(2)}) collective-permute-start(bf16[512,1024]{1,0:T(8,128)(2,1)} %get-tuple-element.49), channel_id=1, source_target_pairs={{0,1},{1,0},{2,3},{3,2},{4,5},{5,4},{6,7},{7,6},{8,9},{9,8},{10,11... | collective-permute-start | bytes 3145736 | tf_op jit(solution)/shard_map/ppermute | solution.py:27
  312.3 1.0 copy-start.3
  313.4 16.3 %copy-start.1 = (s32[8,8]{1,0:T(8,128)S(1)}, s32[8,8]{1,0:T(8,128)}, u32[]{:S(2)}) copy-start(s32[8,8]{1,0:T(8,128)} %param.9) | copy-start | bytes 772
  (3 other events, 2.9 us)

commit v3 on v2

--- a/solution.py
+++ b/solution.py
@@ -96,14 +96,19 @@
     return list(outs[:n_chunks]), list(outs[n_chunks:])
 
 
-def onehot_rows(shape, at, dtype):
-    row = lax.broadcasted_iota(jnp.int32, shape, 0)
-    col = lax.broadcasted_iota(jnp.int32, shape, 1)
-    return jnp.where(col == at(row), 1.0, 0.0).astype(dtype)
-
-
-def exponentials(q, k, factor):
-    return jnp.exp2(jnp.dot(q, k, preferred_element_type=jnp.float32) * factor)
+def soften(q, k, bias, p_ref, group, factor):
+    s = jnp.dot(q, k, preferred_element_type=jnp.float32)
+    totals = []
+    for g in range(group):
+        rows = slice(g * BLK, (g + 1) * BLK)
+        total = None
+        for j in range(k.shape[1] // BLK):
+            cols = slice(j * BLK, (j + 1) * BLK)
+            p = jnp.exp2(s[rows, cols] * factor + bias(j))
+            p_ref[rows, cols] = p.astype(p_ref.dtype)
+            total = p if total is None else total + p
+        totals.append(total)
+    return jnp.concatenate(totals, 0)
 
 
 def pipelined(blocks, stage):
@@ -141,15 +146,11 @@
             at = pl.multiple_of((reach - back) * chip_rows + owner * dev_rows, dev_rows)
             rows = slice(slot * dev_rows, (slot + 1) * dev_rows)
             win[pl.ds(at, dev_rows), :] = w_refs[back][rows, :]
-    for vg in vgs:
-        vg[:, HD:] = jnp.ones((width, HD), vg.dtype)
-    eye = onehot_rows((BLK, HD), lambda row: row, qx.dtype)
     for i in range(chip_blocks):
         slot, b = divmod(i, local)
         for g in range(group):
             rows = slice(g * BLK, (g + 1) * BLK)
-            qx[i, rows, :HD] = q_refs[slot][b * BLK : (b + 1) * BLK, g * HD : (g + 1) * HD]
-            qx[i, rows, HD:] = eye
+            qx[i, rows, :] = q_refs[slot][b * BLK : (b + 1) * BLK, g * HD : (g + 1) * HD]
 
     def within(i):
         return (core ^ i // local) * local + i % local if pair > 1 else i
@@ -159,25 +160,27 @@
         return pl.ds(pl.multiple_of(src, BLK), BLK)
 
     def place_keys(i, at):
-        here = chip * chip_blocks + within(i)
         for j in range(n_slash):
-            off = slash[e, j]
-            cols = slice(j * BLK, (j + 1) * BLK)
-            kgs[at][:HD, cols] = win[take(i, j), :HD]
-            kgs[at][HD:, cols] = masks[jnp.where(off > here, 2, jnp.where(off == 0, 1, 0))]
+            kgs[at][:, j * BLK : (j + 1) * BLK] = win[take(i, j), :HD]
 
     def stage(i, at, ahead, behind):
         if ahead:
             place_keys(i + 1, 1 - at)
         if behind:
-            acc[i - 1] = jnp.dot(
+            acc[i - 1, :, :HD] = jnp.dot(
                 ps[1 - at][...], vgs[1 - at][...], preferred_element_type=jnp.float32
             )
         if isinstance(i, int) and i == chip_blocks:
             return
+        here = chip * chip_blocks + within(i)
+
+        def bias(j):
+            off = slash[e, j]
+            return masks[jnp.where(off > here, 2, jnp.where(off == 0, 1, 0))]
+
         for j in range(n_slash):
-            vgs[at][j * BLK : (j + 1) * BLK, :HD] = win[take(i, j), HD:]
-        ps[at][...] = exponentials(qx[i], kgs[at][...], factor).astype(ps[at].dtype)
+            vgs[at][j * BLK : (j + 1) * BLK, :] = win[take(i, j), HD:]
+        acc[i, :, HD:] = soften(qx[i], kgs[at][...], bias, ps[at], group, factor)
 
     place_keys(0, 0)
     pipelined(chip_blocks, stage)
@@ -190,13 +193,11 @@
     before, kv_vert, masks, refs = refs[0], refs[1], refs[2], refs[3:]
     out_refs, refs = refs[:pair], refs[pair:]
     ke, ve, qx, res, good = refs[:5]
-    ps, (kg, vg, sc, pg) = refs[5:7], refs[7:]
+    ps, sums, (kg, vg, sc, pg) = refs[5:7], refs[7:9], refs[9:]
     e = first + pl.program_id(0)
     chip, core = info[0], info[1]
     dev_rows = local * BLK
     chip_blocks = pair * local
-    wide = n_vert * BLK
-    step = min(2 * BLK, wide)
     factor = math.log2(math.e) / math.sqrt(HD)
 
     def within(i):
@@ -210,52 +211,46 @@
         return found
 
     per = heads * n_vert // plane
-    row = lax.broadcasted_iota(jnp.int32, (HD, BLK), 0)
     for j in range(n_vert):
         flat = e * n_vert + j
         src = pl.multiple_of(((flat // per ^ chip % plane) * per + flat % per) * BLK, BLK)
         rows = slice(j * BLK, (j + 1) * BLK)
-        ke[:HD, rows] = kv_vert[pl.ds(src, BLK), :HD]
-        ve[rows, :HD] = kv_vert[pl.ds(src, BLK), HD:]
-        bias = jnp.zeros((HD, BLK), jnp.float32)
-        for i in range(chip_blocks):
-            bias = jnp.where((row == i) & hidden(i, j), MASKED, bias)
-        ke[HD:, rows] = bias.astype(ke.dtype)
-    ve[:, HD:] = jnp.ones((wide, HD), ve.dtype)
+        ke[:, rows] = kv_vert[pl.ds(src, BLK), :HD]
+        ve[rows, :] = kv_vert[pl.ds(src, BLK), HD:]
     for i in range(chip_blocks):
         slot, b = divmod(i, local)
         for g in range(group):
             rows = slice(g * BLK, (g + 1) * BLK)
-            qx[i, rows, :HD] = q_refs[slot][b * BLK : (b + 1) * BLK, g * HD : (g + 1) * HD]
-            qx[i, rows, HD:] = onehot_rows((BLK, HD), lambda row, i=i: i, qx.dtype)
+            qx[i, rows, :] = q_refs[slot][b * BLK : (b + 1) * BLK, g * HD : (g + 1) * HD]
     good[...] = jnp.ones(good.shape, good.dtype)
 
     def stage(i, at, ahead, behind):
         if behind:
-            acc = before[i - 1] + jnp.dot(
+            attended = before[i - 1, :, :HD] + jnp.dot(
                 ps[1 - at][...], ve[...], preferred_element_type=jnp.float32
             )
-            total = acc[:, HD:]
-            res[i - 1] = (acc[:, :HD] / total).astype(res.dtype)
+            total = jnp.sum(sums[1 - at][...], axis=1, keepdims=True)
+            res[i - 1] = (attended / total).astype(res.dtype)
             fine = jnp.where((total > SMALLEST) & (total < LARGEST), 1.0, 0.0)
             good[...] = jnp.minimum(good[...], jnp.min(fine, axis=0, keepdims=True))
         if isinstance(i, int) and i == chip_blocks:
             return
-        ps[at][...] = exponentials(qx[i], ke[...], factor).astype(ps[at].dtype)
+
+        def bias(j):
+            return jnp.where(hidden(i, j), MASKED, 0.0)
+
+        sums[at][...] = before[i, :, HD:] + soften(qx[i], ke[...], bias, ps[at], group, factor)
 
     pipelined(chip_blocks, stage)
 
     @pl.when(jnp.logical_not(jnp.min(good[...]) > 0.5))
     def _():
-        vg[: n_slash * BLK, HD:] = jnp.ones((n_slash * BLK, HD), vg.dtype)
         kg[:, n_slash * BLK :] = ke[...]
         vg[n_slash * BLK :, :] = ve[...]
-        eye = onehot_rows((BLK, HD), lambda row: row, qx.dtype)
 
         def shifted_block(i, carry):
             here = chip * chip_blocks + within(i)
-            for g in range(group):
-                qx[i, g * BLK : (g + 1) * BLK, HD:] = eye
+            biases = []
             for j in range(n_slash):
                 off = slash[e, j]
                 pos = reach * chip_blocks + within(i) - off
@@ -268,25 +263,24 @@
                 for d in range(1, reach + 1):
                     found = jnp.where(back == d, w_refs[d][at, :], found)
                 rows = slice(j * BLK, (j + 1) * BLK)
-                kg[:HD, rows] = found[:, :HD]
-                vg[rows, :HD] = found[:, HD:]
-                kg[HD:, rows] = masks[jnp.where(off > here, 2, jnp.where(off == 0, 1, 0))]
+                kg[:, rows] = found[:, :HD]
+                vg[rows, :] = found[:, HD:]
+                biases.append(masks[jnp.where(off > here, 2, jnp.where(off == 0, 1, 0))])
             for j in range(n_vert):
-                rows = slice((n_slash + j) * BLK, (n_slash + j + 1) * BLK)
-                kg[HD:, rows] = masks[jnp.where(hidden(i, j), 2, 0)]
-            top = None
-            for t in range(0, kg.shape[1], step):
-                s = jnp.dot(qx[i], kg[:, t : t + step], preferred_element_type=jnp.float32)
-                sc[:, t : t + step] = s
-                for u in range(0, step, HD):
-                    piece = s[:, u : u + HD]
-                    top = piece if top is None else jnp.maximum(top, piece)
-            top = jnp.max(top, axis=1, keepdims=True)
-            for t in range(0, kg.shape[1], step):
-                p = jnp.exp2((sc[:, t : t + step] - top) * factor)
-                pg[:, t : t + step] = p.astype(pg.dtype)
+                biases.append(jnp.where(hidden(i, j), MASKED, 0.0))
+            sc[...] = jnp.dot(qx[i], kg[...], preferred_element_type=jnp.float32)
+            for g in range(group):
+                rows = slice(g * BLK, (g + 1) * BLK)
+                top = None
+                for j, bias in enumerate(biases):
+                    cols = slice(j * BLK, (j + 1) * BLK)
+                    sc[rows, cols] = sc[rows, cols] * factor + bias
+                    top = sc[rows, cols] if top is None else jnp.maximum(top, sc[rows, cols])
+                p = jnp.exp2(sc[rows, :] - jnp.max(top, axis=1, keepdims=True))
+                pg[rows, :] = p.astype(pg.dtype)
+                sums[0][rows, :] = jnp.broadcast_to(jnp.sum(p, axis=1, keepdims=True), (BLK, HD))
             acc = jnp.dot(pg[...], vg[...], preferred_element_type=jnp.float32)
-            res[i] = (acc[:, :HD] / acc[:, HD:]).astype(res.dtype)
+            res[i] = (acc / sums[0][...]).astype(res.dtype)
             return carry
 
         lax.fori_loop(0, chip_blocks, shifted_block, 0)
@@ -348,10 +342,10 @@
                 out_specs=self.acc_spec(),
                 scratch_shapes=[
                     pltpu.VMEM((sum(w.shape[0] for w in windows), 2 * HD), self.dtype),
-                    pltpu.VMEM((self.blocks, rows, 2 * HD), self.dtype),
+                    pltpu.VMEM((self.blocks, rows, HD), self.dtype),
                 ]
-                + [pltpu.VMEM((2 * HD, width), self.dtype)] * 2
-                + [pltpu.VMEM((width, 2 * HD), self.dtype)] * 2
+                + [pltpu.VMEM((HD, width), self.dtype)] * 2
+                + [pltpu.VMEM((width, HD), self.dtype)] * 2
                 + [pltpu.VMEM((rows, width), self.dtype)] * 2,
             ),
             out_shape=jax.ShapeDtypeStruct(shape, jnp.float32),
@@ -374,15 +368,17 @@
                 + [self.acc_spec(), self.whole(kv_vert), self.whole(self.masks)],
                 out_specs=[out] * self.pair,
                 scratch_shapes=[
-                    pltpu.VMEM((2 * HD, width), self.dtype),
-                    pltpu.VMEM((width, 2 * HD), self.dtype),
-                    pltpu.VMEM((self.blocks, rows, 2 * HD), self.dtype),
+                    pltpu.VMEM((HD, width), self.dtype),
+                    pltpu.VMEM((width, HD), self.dtype),
                     pltpu.VMEM((self.blocks, rows, HD), self.dtype),
-                    pltpu.VMEM((1, HD), jnp.float32),
+                    pltpu.VMEM((self.blocks, rows, HD), self.dtype),
+                    pltpu.VMEM((1, 1), jnp.float32),
                     pltpu.VMEM((rows, width), self.dtype),
                     pltpu.VMEM((rows, width), self.dtype),
-                    pltpu.VMEM((2 * HD, both), self.dtype),
-                    pltpu.VMEM((both, 2 * HD), self.dtype),
+                    pltpu.VMEM((rows, HD), jnp.float32),
+                    pltpu.VMEM((rows, HD), jnp.float32),
+                    pltpu.VMEM((HD, both), self.dtype),
+                    pltpu.VMEM((both, HD), self.dtype),
                     pltpu.VMEM((rows, both), jnp.float32),
                     pltpu.VMEM((rows, both), self.dtype),
                 ],
@@ -455,7 +451,6 @@
     pos = jnp.arange(BLK)
     causal = jnp.where(pos[:, None] < pos[None, :], MASKED, 0.0)
     masks = jnp.stack([jnp.zeros_like(causal), causal, jnp.full_like(causal, MASKED)])
-    masks = masks.astype(queries.dtype)
 
     def part(value, axis, which):
         span = value.shape[axis] // pair
@@ -477,9 +472,9 @@
     step = 1
     while step < chips // plane:
         total = total + shifted(total, step * plane * pair)
-        total, q_other = lax.optimization_barrier((total, q_other))
+        if step == 1:
+            total, q_other, own[1:] = lax.optimization_barrier((total, q_other, own[1:]))
         step *= 2
-    total, own[1:] = lax.optimization_barrier((total, own[1:]))
 
     attention = Attention(queries, q_other, info, vert, slash, masks, heads, local, plane)
     chunks = heads // per_chunk

time: 330 us -> 324 us (0.982)
  waiting for transfers between devices: 93.7 us -> 73.4 us
  starting transfers between devices: 27.6 us -> 35.7 us
  Pallas kernels: 194 us -> 200 us
    ppermute x4, waiting for transfers between devices: 48.4 us -> 36.5 us  [shifted(): return lax.ppermute(value, 'ctx', [(i, i + by) for i in range(size - by)])]
    ppermute x4, starting transfers between devices: 9.19 us -> 17.8 us  [shifted(): return lax.ppermute(value, 'ctx', [(i, i + by) for i in range(size - by)])]
    ppermute x12, waiting for transfers between devices: 45.3 us -> 36.9 us  [crossed(): return lax.ppermute(value, 'ctx', [(i, i ^ bits) for i in range(size)])]
    pallas_call x2, Pallas kernels: 122 us -> 128 us  [over_vertical(): pl.pallas_call(functools.partial(vertical_kernel, cfg + (self.plane, self...]
  transfers between devices with their start and end apart: 16 -> 16, of which waited for: 7 -> 7; matrix products, arithmetic and copies ran while one was open for 2% -> 2% of each run, Pallas kernels for 53% -> 55%
where the time goes in v3:
time: 324 us; the launch traced here: 323 us
  Pallas kernels  200 us (62%)
  waiting for transfers between devices  73.4 us (23%)
  starting transfers between devices  35.7 us (11%)
  local copies, waits for them, and re-layouts  9.23 us (3%)
  other arithmetic  4.51 us (1%)
    pallas_call x2, Pallas kernels, over_vertical(): pl.pallas_call(functools.partial(vertical_kernel, cfg + (self.plane, self...  128 us
    ppermute x12, waiting for transfers between devices, crossed(): return lax.ppermute(value, 'ctx', [(i, i ^ bits) for i in range(size)])  36.9 us
    ppermute x4, waiting for transfers between devices, shifted(): return lax.ppermute(value, 'ctx', [(i, i + by) for i in range(size - by)])  36.5 us
    pallas_call x2, Pallas kernels, over_slash(): pl.pallas_call(functools.partial(slash_kernel, cfg), grid_spec=pltpu.Pref...  35.9 us
    pallas_call x2, Pallas kernels, project(): pl.pallas_call(functools.partial(project_kernel, n, before is not None),...  31.3 us
    ppermute x12, starting transfers between devices, crossed(): return lax.ppermute(value, 'ctx', [(i, i ^ bits) for i in range(size)])  17.9 us
    ppermute x4, starting transfers between devices, shifted(): return lax.ppermute(value, 'ctx', [(i, i + by) for i in range(size - by)])  17.8 us
  transfers between devices with their start and end apart: 16, of which 7 were waited for; matrix products, arithmetic and copies ran while one was open for 2% of the time, Pallas kernels for 55%

profile of v3, /device:TPU:25, one launch (start us, length us, event | category | flops | bytes accessed | tf_op | source)
XLA Modules:
  0.0 323.2 jit_solution(15873071968941413745)
XLA Ops:
  0.0 1.3 constant_dynamic-slice_fusion.1
  5.4 4.6 %prepare.1 = (bf16[1024,512]{1,0:T(8,128)(2,1)}, bf16[1024,512]{1,0:T(8,128)(2,1)}, bf16[1024,256]{1,0:T(8,128)(2,1)}, bf16[1024,256]{1,0:T(8,128)(2,1)}, bf16[1...) custom-call(s32[2]{0:T(128)} %pad_add_fusion.info, s32[4,8]{1,0:T(4,128)} %constant_dynamic-slice_fusion.4.vert, ...), custom_call_target="tpu_custom_call" | custom-call | bytes 8388608 | tf_op jit(solution)/shard_map/prepare/pallas_call | solution.py:82
  11.2 1.2 collective-permute-start.2
  12.6 1.8 constant_dynamic-slice_fusion
  14.4 8.9 %collective-permute-done.1 = bf16[1024,256]{1,0:T(8,128)(2,1)S(1)} collective-permute-done((bf16[1024,256]{1,0:T(8,128)(2,1)}, bf16[1024,256]{1,0:T(8,128)(2,1)S(1)}, u32[]{:S(2)}, u32[]{:S(2)}) %collective-permute-start.1) | collective-permute-done | bytes 524320 | tf_op jit(solution)/shard_map/ppermute | solution.py:27
  24.2 11.4 %collective-permute-done.3 = bf16[1024,256]{1,0:T(8,128)(2,1)} collective-permute-done((bf16[1024,256]{1,0:T(8,128)(2,1)}, bf16[1024,256]{1,0:T(8,128)(2,1)}, u32[]{:S(2)}, u32[]{:S(2)}) %collective-permute-start.3) | collective-permute-done | bytes 524320 | tf_op jit(solution)/shard_map/ppermute | solution.py:27
  35.6 1.3 add_add_fusion
  37.0 2.2 collective-permute-start.5
  39.1 3.1 collective-permute-start.12
  42.3 1.4 collective-permute-start.4
  43.8 23.2 %collective-permute-done.12.refs_4_ = bf16[1024,512]{1,0:T(8,128)(2,1)} collective-permute-done((bf16[1024,512]{1,0:T(8,128)(2,1)}, bf16[1024,512]{1,0:T(8,128)(2,1)}, u32[]{:S(2)}, u32[]{:S(2)}) %collective-permute-start.12) | collective-permute-done | bytes 1048608 | tf_op jit(solution)/shard_map/ppermute | solution.py:22
  67.0 1.3 broadcast_select_fusion
  68.8 1.3 collective-permute-start.8
  71.5 11.9 %collective-permute-start.6 = (bf16[1024,512]{1,0:T(8,128)(2,1)S(1)}, bf16[1024,512]{1,0:T(8,128)(2,1)S(1)}, u32[]{:S(2)}, u32[]{:S(2)}) collective-permute-start(bf16[1024,512]{1,0:T(8,128)(2,1)S(1)} %copy-done.5), channel_id=1, source_target_pairs={{0,4},{1,5},{2,6},{3,7},{4,8},{5,9},{6,10},{7,11},{8,12},{9,13},{1... | collective-permute-start | bytes 3145736 | tf_op jit(solution)/shard_map/ppermute | solution.py:22
  83.4 13.2 %collective-permute-done.8 = bf16[1024,256]{1,0:T(8,128)(2,1)S(1)} collective-permute-done((bf16[1024,256]{1,0:T(8,128)(2,1)S(1)}, bf16[1024,256]{1,0:T(8,128)(2,1)S(1)}, u32[]{:S(2)}, u32[]{:S(2)}) %collective-permute-start.8) | collective-permute-done | bytes 524320 | tf_op jit(solution)/shard_map/ppermute | solution.py:22
  96.8 9.9 %collective-permute-start.10 = (bf16[1024,256]{1,0:T(8,128)(2,1)S(1)}, bf16[1024,256]{1,0:T(8,128)(2,1)S(1)}, u32[]{:S(2)}, u32[]{:S(2)}) collective-permute-start(bf16[1024,256]{1,0:T(8,128)(2,1)S(1)} %add.44), channel_id=1, source_target_pairs={{0,4},{1,5},{2,6},{3,7},{4,0},{5,1},{6,2},{7,3},{8,12},{9,13},{10,... | collective-permute-start | bytes 1572872 | tf_op jit(solution)/shard_map/ppermute | solution.py:27
  108.0 17.8 %attend_slash.3.refs_5_ = f32[2,8,512,256]{3,2,1,0:T(8,128)} custom-call(s32[2]{0:T(128)} %pad_add_fusion.info, s32[4,8]{1,0:T(4,128)} %constant_dynamic-slice_fusion.3.slash, bf16[512,4096]{1,0:T(8,128)(2,1)} %refs_0_.9, bf16[512,2048]{1,0:T(8,128)(2,1)} %collective-permute-done.5.refs_1_, bf16[1024,512]{1,0:T(8,128)(2,1)} %get-tuple-element.37.refs_2_, ...), custom_call_target="tpu_custom_call" | custom-call | flops 8589934592 | bytes 10485760 | tf_op jit(solution)/shard_map/attend_slash/pallas_call | solution.py:336
  125.8 14.6 %collective-permute-done.10 = bf16[1024,256]{1,0:T(8,128)(2,1)S(1)} collective-permute-done((bf16[1024,256]{1,0:T(8,128)(2,1)S(1)}, bf16[1024,256]{1,0:T(8,128)(2,1)S(1)}, u32[]{:S(2)}, u32[]{:S(2)}) %collective-permute-start.10) | collective-permute-done | bytes 524320 | tf_op jit(solution)/shard_map/ppermute | solution.py:27
  141.6 1.3 copy-done.9
  142.9 64.2 %attend_vertical.3 = (bf16[512,1024]{1,0:T(8,128)(2,1)}, bf16[512,1024]{1,0:T(8,128)(2,1)}) custom-call(s32[2]{0:T(128)} %pad_add_fusion.info, s32[4,8]{1,0:T(4,128)} %constant_dynamic-slice_fusion.4.vert, s32[4,8]{1,0:T(4,128)} %constant_dynamic-slice_fusion.3.slash, bf16[512,4096]{1,0:T(8,128)(2,1)} %refs_0_.9, ...), custom_call_target="tpu_custom_call" | custom-call | flops 8589934592 | bytes 10485760 | tf_op jit(solution)/shard_map/attend_vertical/pallas_call | solution.py:362
  207.5 18.1 %attend_slash.2.refs_5_ = f32[2,8,512,256]{3,2,1,0:T(8,128)} custom-call(s32[2]{0:T(128)} %pad_add_fusion.info, s32[4,8]{1,0:T(4,128)} %constant_dynamic-slice_fusion.3.slash, bf16[512,4096]{1,0:T(8,128)(2,1)} %refs_0_.9, bf16[512,2048]{1,0:T(8,128)(2,1)} %collective-permute-done.5.refs_1_, bf16[1024,512]{1,0:T(8,128)(2,1)} %get-tuple-element.35.refs_2_, ...), custom_call_target="tpu_custom_call" | custom-call | flops 8589934592 | bytes 10485760 | tf_op jit(solution)/shard_map/attend_slash/pallas_call | solution.py:336
  225.6 64.2 %attend_vertical.2 = (bf16[512,1024]{1,0:T(8,128)(2,1)}, bf16[512,1024]{1,0:T(8,128)(2,1)}) custom-call(s32[2]{0:T(128)} %pad_add_fusion.info, s32[4,8]{1,0:T(4,128)} %constant_dynamic-slice_fusion.4.vert, s32[4,8]{1,0:T(4,128)} %constant_dynamic-slice_fusion.3.slash, bf16[512,4096]{1,0:T(8,128)(2,1)} %refs_0_.9, ...), custom_call_target="tpu_custom_call" | custom-call | flops 8589934592 | bytes 10485760 | tf_op jit(solution)/shard_map/attend_vertical/pallas_call | solution.py:362
  290.8 15.1 %project.2.refs_4_ = f32[512,4096]{1,0:T(8,128)} custom-call(s32[2]{0:T(128)} %pad_add_fusion.info, bf16[512,1024]{1,0:T(8,128)(2,1)} %get-tuple-element.45.refs_0_, bf16[512,1024]{1,0:T(8,128)(2,1)} %copy-done.2, bf16[4096,4096]{1,0:T(8,128)(2,1)} %refs_3_.3, bf16[4096,4096]{1,0:T(8,128)(2,1)} %refs_3_.3), custom_call_target="tpu_custom_call" | custom-call | flops 8589934592 | bytes 35651584 | tf_op jit(solution)/shard_map/project/pallas_call | solution.py:421
  306.9 16.3 %project.3 = bf16[512,4096]{1,0:T(8,128)(2,1)} custom-call(s32[2]{0:T(128)} %pad_add_fusion.info, bf16[512,1024]{1,0:T(8,128)(2,1)} %get-tuple-element.42.refs_0_, bf16[512,1024]{1,0:T(8,128)(2,1)} %copy-done.3, bf16[4096,4096]{1,0:T(8,128)(2,1)} %refs_3_.3, bf16[4096,4096]{1,0:T(8,128)(2,1)} %refs_3_.3, f32[512,4096]{1,0:T(8,128)} %project.2.refs_4_), custom_call_target="tpu_custom_call" | custom-call | flops 8589934592 | bytes 35651584 | tf_op jit(solution)/shard_map/project/pallas_call | solution.py:421
  (56 shorter events, 13.3 us)
Async XLA Ops:
  0.0 2.8 copy-start
  1.4 3.0 collective-permute-start
  10.0 13.3 %collective-permute-start.1 = (bf16[1024,256]{1,0:T(8,128)(2,1)}, bf16[1024,256]{1,0:T(8,128)(2,1)S(1)}, u32[]{:S(2)}, u32[]{:S(2)}) collective-permute-start(bf16[1024,256]{1,0:T(8,128)(2,1)} %get-tuple-element.27), channel_id=1, source_target_pairs={{0,2},{1,3},{2,0},{3,1},{4,6},{5,7},{6,4},{7,5},{8,10},{9,11},{10,... | collective-permute-start | bytes 1572872 | tf_op jit(solution)/shard_map/ppermute | solution.py:27
  11.2 13.0 %collective-permute-start.2 = (bf16[1024,256]{1,0:T(8,128)(2,1)}, bf16[1024,256]{1,0:T(8,128)(2,1)S(1)}, u32[]{:S(2)}, u32[]{:S(2)}) collective-permute-start(bf16[1024,256]{1,0:T(8,128)(2,1)} %get-tuple-element.28), channel_id=1, source_target_pairs={{0,4},{1,5},{2,6},{3,7},{4,0},{5,1},{6,2},{7,3},{8,12},{9,13},{10,... | collective-permute-start | bytes 1572872 | tf_op jit(solution)/shard_map/ppermute | solution.py:27
  12.4 23.2 %collective-permute-start.3 = (bf16[1024,256]{1,0:T(8,128)(2,1)}, bf16[1024,256]{1,0:T(8,128)(2,1)}, u32[]{:S(2)}, u32[]{:S(2)}) collective-permute-start(bf16[1024,256]{1,0:T(8,128)(2,1)} %get-tuple-element.29), channel_id=1, source_target_pairs={{0,6},{1,7},{2,4},{3,5},{4,2},{5,3},{6,0},{7,1},{8,14},{9,15},{10,... | collective-permute-start | bytes 1572872 | tf_op jit(solution)/shard_map/ppermute | solution.py:27
  12.6 23.0 %copy-start.7 = (bf16[1024,256]{1,0:T(8,128)(2,1)S(1)}, bf16[1024,256]{1,0:T(8,128)(2,1)}, u32[]{:S(2)}) copy-start(bf16[1024,256]{1,0:T(8,128)(2,1)} %get-tuple-element.26) | copy-start | bytes 1572868
  24.2 11.5 %copy-start.8 = (bf16[1024,256]{1,0:T(8,128)(2,1)}, bf16[1024,256]{1,0:T(8,128)(2,1)S(1)}, u32[]{:S(2)}) copy-start(bf16[1024,256]{1,0:T(8,128)(2,1)S(1)} %collective-permute-done.2) | copy-start | bytes 1572868
  37.0 31.9 %collective-permute-start.5 = (bf16[512,2048]{1,0:T(8,128)(2,1)S(1)}, bf16[512,2048]{1,0:T(8,128)(2,1)}, u32[]{:S(2)}, u32[]{:S(2)}) collective-permute-start(bf16[512,2048]{1,0:T(8,128)(2,1)S(1)} %constant_dynamic-slice_fusion), channel_id=1, source_target_pairs={{0,1},{1,0},{2,3},{3,2},{4,5},{5,4},{6,7},{7,6},{8,9},{9,8},{10,11... | collective-permute-start | bytes 6291464 | tf_op jit(solution)/shard_map/ppermute | solution.py:27
  39.1 27.9 %collective-permute-start.12 = (bf16[1024,512]{1,0:T(8,128)(2,1)}, bf16[1024,512]{1,0:T(8,128)(2,1)}, u32[]{:S(2)}, u32[]{:S(2)}) collective-permute-start(bf16[1024,512]{1,0:T(8,128)(2,1)} %get-tuple-element.37.refs_2_), channel_id=1, source_target_pairs={{0,4},{1,5},{2,6},{3,7},{4,8},{5,9},{6,10},{7,11},{8,12},{9,13},{1... | collective-permute-start | bytes 3145736 | tf_op jit(solution)/shard_map/ppermute | solution.py:22
  42.3 27.8 %copy-start.10 = (s32[8,8]{1,0:T(8,128)S(1)}, s32[8,8]{1,0:T(8,128)}, u32[]{:S(2)}) copy-start(s32[8,8]{1,0:T(8,128)} %param.10) | copy-start | bytes 772
  42.3 29.2 %copy-start.5 = (bf16[1024,512]{1,0:T(8,128)(2,1)S(1)}, bf16[1024,512]{1,0:T(8,128)(2,1)}, u32[]{:S(2)}) copy-start(bf16[1024,512]{1,0:T(8,128)(2,1)} %get-tuple-element.35.refs_2_) | copy-start | bytes 3145732
  42.3 26.4 %collective-permute-start.4 = (bf16[1024,256]{1,0:T(8,128)(2,1)S(1)}, bf16[1024,256]{1,0:T(8,128)(2,1)S(1)}, u32[]{:S(2)}, u32[]{:S(2)}) collective-permute-start(bf16[1024,256]{1,0:T(8,128)(2,1)S(1)} %add_add_fusion), channel_id=1, source_target_pairs={{0,8},{1,9},{2,10},{3,11},{4,12},{5,13},{6,14},{7,15},{8,16},{9,17... | collective-permute-start | bytes 1572872 | tf_op jit(solution)/shard_map/ppermute | solution.py:22
  68.3 39.6 %collective-permute-start.13 = (bf16[1024,512]{1,0:T(8,128)(2,1)S(1)}, bf16[1024,512]{1,0:T(8,128)(2,1)}, u32[]{:S(2)}, u32[]{:S(2)}) collective-permute-start(bf16[1024,512]{1,0:T(8,128)(2,1)S(1)} %broadcast_select_fusion), channel_id=1, source_target_pairs={{0,2},{1,3},{2,0},{3,1},{4,6},{5,7},{6,4},{7,5},{8,10},{9,11},{10,... | collective-permute-start | bytes 3145736 | tf_op jit(solution)/shard_map/ppermute | solution.py:27
  68.8 27.8 %collective-permute-start.8 = (bf16[1024,256]{1,0:T(8,128)(2,1)S(1)}, bf16[1024,256]{1,0:T(8,128)(2,1)S(1)}, u32[]{:S(2)}, u32[]{:S(2)}) collective-permute-start(bf16[1024,256]{1,0:T(8,128)(2,1)S(1)} %add.42), channel_id=1, source_target_pairs={{0,16},{1,17},{2,18},{3,19},{4,20},{5,21},{6,22},{7,23},{8,24},{9,... | collective-permute-start | bytes 1572872 | tf_op jit(solution)/shard_map/ppermute | solution.py:22
  71.5 69.0 %collective-permute-start.6 = (bf16[1024,512]{1,0:T(8,128)(2,1)S(1)}, bf16[1024,512]{1,0:T(8,128)(2,1)S(1)}, u32[]{:S(2)}, u32[]{:S(2)}) collective-permute-start(bf16[1024,512]{1,0:T(8,128)(2,1)S(1)} %copy-done.5), channel_id=1, source_target_pairs={{0,4},{1,5},{2,6},{3,7},{4,8},{5,9},{6,10},{7,11},{8,12},{9,13},{1... | collective-permute-start | bytes 3145736 | tf_op jit(solution)/shard_map/ppermute | solution.py:22
  96.8 43.7 %collective-permute-start.10 = (bf16[1024,256]{1,0:T(8,128)(2,1)S(1)}, bf16[1024,256]{1,0:T(8,128)(2,1)S(1)}, u32[]{:S(2)}, u32[]{:S(2)}) collective-permute-start(bf16[1024,256]{1,0:T(8,128)(2,1)S(1)} %add.44), channel_id=1, source_target_pairs={{0,4},{1,5},{2,6},{3,7},{4,0},{5,1},{6,2},{7,3},{8,12},{9,13},{10,... | collective-permute-start | bytes 1572872 | tf_op jit(solution)/shard_map/ppermute | solution.py:27
  106.7 33.7 %collective-permute-start.11 = (bf16[1024,256]{1,0:T(8,128)(2,1)S(1)}, bf16[1024,256]{1,0:T(8,128)(2,1)S(1)}, u32[]{:S(2)}, u32[]{:S(2)}) collective-permute-start(bf16[1024,256]{1,0:T(8,128)(2,1)S(1)} %add.44), channel_id=1, source_target_pairs={{0,6},{1,7},{2,4},{3,5},{4,2},{5,3},{6,0},{7,1},{8,14},{9,15},{10,... | collective-permute-start | bytes 1572872 | tf_op jit(solution)/shard_map/ppermute | solution.py:27
  106.8 33.6 %collective-permute-start.9 = (bf16[1024,256]{1,0:T(8,128)(2,1)S(1)}, bf16[1024,256]{1,0:T(8,128)(2,1)S(1)}, u32[]{:S(2)}, u32[]{:S(2)}) collective-permute-start(bf16[1024,256]{1,0:T(8,128)(2,1)S(1)} %add.44), channel_id=1, source_target_pairs={{0,2},{1,3},{2,0},{3,1},{4,6},{5,7},{6,4},{7,5},{8,10},{9,11},{10,... | collective-permute-start | bytes 1572872 | tf_op jit(solution)/shard_map/ppermute | solution.py:27
  140.6 66.9 %collective-permute-start.7 = (bf16[1024,512]{1,0:T(8,128)(2,1)S(1)}, bf16[1024,512]{1,0:T(8,128)(2,1)}, u32[]{:S(2)}, u32[]{:S(2)}) collective-permute-start(bf16[1024,512]{1,0:T(8,128)(2,1)S(1)} %broadcast_select_fusion.1), channel_id=1, source_target_pairs={{0,2},{1,3},{2,0},{3,1},{4,6},{5,7},{6,4},{7,5},{8,10},{9,11},{10,... | collective-permute-start | bytes 3145736 | tf_op jit(solution)/shard_map/ppermute | solution.py:27
  141.6 1.3 copy-start.9
  207.0 82.8 %collective-permute-start.15 = (bf16[512,1024]{1,0:T(8,128)(2,1)}, bf16[512,1024]{1,0:T(8,128)(2,1)S(1)}, u32[]{:S(2)}, u32[]{:S(2)}) collective-permute-start(bf16[512,1024]{1,0:T(8,128)(2,1)} %get-tuple-element.46), channel_id=1, source_target_pairs={{0,1},{1,0},{2,3},{3,2},{4,5},{5,4},{6,7},{7,6},{8,9},{9,8},{10,11... | collective-permute-start | bytes 3145736 | tf_op jit(solution)/shard_map/ppermute | solution.py:27
  289.8 16.1 %collective-permute-start.14 = (bf16[512,1024]{1,0:T(8,128)(2,1)}, bf16[512,1024]{1,0:T(8,128)(2,1)S(1)}, u32[]{:S(2)}, u32[]{:S(2)}) collective-permute-start(bf16[512,1024]{1,0:T(8,128)(2,1)} %get-tuple-element.43), channel_id=1, source_target_pairs={{0,1},{1,0},{2,3},{3,2},{4,5},{5,4},{6,7},{7,6},{8,9},{9,8},{10,11... | collective-permute-start | bytes 3145736 | tf_op jit(solution)/shard_map/ppermute | solution.py:27
  305.9 1.0 copy-start.3
  306.9 16.3 %copy-start.1 = (s32[8,8]{1,0:T(8,128)S(1)}, s32[8,8]{1,0:T(8,128)}, u32[]{:S(2)}) copy-start(s32[8,8]{1,0:T(8,128)} %param.9) | copy-start | bytes 772
  (3 other events, 2.9 us)

commit v4 on v3

--- a/solution.py
+++ b/solution.py
@@ -104,7 +104,7 @@
         total = None
         for j in range(k.shape[1] // BLK):
             cols = slice(j * BLK, (j + 1) * BLK)
-            p = jnp.exp2(s[rows, cols] * factor + bias(j))
+            p = jnp.exp(s[rows, cols] * factor + bias(j))
             p_ref[rows, cols] = p.astype(p_ref.dtype)
             total = p if total is None else total + p
         totals.append(total)
@@ -138,7 +138,7 @@
     chip_blocks = pair * local
     chip_rows = chip_blocks * BLK
     width = n_slash * BLK
-    factor = math.log2(math.e) / math.sqrt(HD)
+    factor = 1.0 / math.sqrt(HD)
 
     for back in range(reach + 1):
         for slot in range(pair):
@@ -198,7 +198,7 @@
     chip, core = info[0], info[1]
     dev_rows = local * BLK
     chip_blocks = pair * local
-    factor = math.log2(math.e) / math.sqrt(HD)
+    factor = 1.0 / math.sqrt(HD)
 
     def within(i):
         return (core ^ i // local) * local + i % local if pair > 1 else i
@@ -276,7 +276,7 @@
                     cols = slice(j * BLK, (j + 1) * BLK)
                     sc[rows, cols] = sc[rows, cols] * factor + bias
                     top = sc[rows, cols] if top is None else jnp.maximum(top, sc[rows, cols])
-                p = jnp.exp2(sc[rows, :] - jnp.max(top, axis=1, keepdims=True))
+                p = jnp.exp(sc[rows, :] - jnp.max(top, axis=1, keepdims=True))
                 pg[rows, :] = p.astype(pg.dtype)
                 sums[0][rows, :] = jnp.broadcast_to(jnp.sum(p, axis=1, keepdims=True), (BLK, HD))
             acc = jnp.dot(pg[...], vg[...], preferred_element_type=jnp.float32)
@@ -391,49 +391,6 @@
         )(self.info, self.vert, self.slash, *self.qs, *windows, before, kv_vert, self.masks)
 
 
-def project_kernel(n, has_before, info, *refs):
-    lefts, rights, refs = refs[:n], refs[n : 2 * n], refs[2 * n :]
-    acc = refs[0][...] if has_before else None
-    for left, right in zip(lefts, rights):
-        part = jnp.dot(left[...], right[...], preferred_element_type=jnp.float32)
-        acc = part if acc is None else acc + part
-    refs[-1][...] = acc.astype(refs[-1].dtype)
-
-
-def project(pieces, before, out_weight, info, chunks, dtype):
-    rows, wide = pieces[0][2].shape
-    columns = out_weight.shape[1]
-    tile = min(1024, columns)
-    n = len(pieces)
-
-    def weight_spec(swap, c):
-        if swap:
-            return pl.BlockSpec((wide, tile), lambda i, info: ((1 - info[1]) * chunks + c, i))
-        return pl.BlockSpec((wide, tile), lambda i, info: (info[1] * chunks + c, i))
-
-    in_specs = [pl.BlockSpec((rows, wide), lambda i, info: (0, 0))] * n
-    in_specs += [weight_spec(swap, c) for swap, c, _ in pieces]
-    args = [a for _, _, a in pieces] + [out_weight] * n
-    out_spec = pl.BlockSpec((rows, tile), lambda i, info: (0, i))
-    if before is not None:
-        in_specs.append(out_spec)
-        args.append(before)
-    return pl.pallas_call(
-        functools.partial(project_kernel, n, before is not None),
-        grid_spec=pltpu.PrefetchScalarGridSpec(
-            num_scalar_prefetch=1, grid=(columns // tile,), in_specs=in_specs, out_specs=out_spec
-        ),
-        out_shape=jax.ShapeDtypeStruct((rows, columns), dtype),
-        compiler_params=pltpu.CompilerParams(vmem_limit_bytes=VMEM_LIMIT),
-        cost_estimate=pl.CostEstimate(
-            flops=2 * n * rows * wide * columns,
-            bytes_accessed=2 * n * wide * (rows + columns) + 8 * rows * columns,
-            transcendentals=0,
-        ),
-        name="project",
-    )(info, *args)
-
-
 def body(queries, keys, values, vertical_blocks, slash_offsets, out_weight):
     tokens_dev = queries.shape[0]
     kv_heads = keys.shape[1] // HD
@@ -495,18 +452,16 @@
     near, far = [], []
     for c in range(chunks):
         att = attention.over_vertical(c * per_chunk, per_chunk, all_windows[c], sums[c], kv_vert)
-        near.append((False, c, att[0]))
+        near.append(att[0])
         if pair == 2:
-            far.append((True, c, crossed(att[1], 1)))
-    if pair == 1:
-        attended = jnp.concatenate([a for _, _, a in near], 1)
-        attended = lax.all_gather(attended, "head", axis=1, tiled=True)
-        output = jnp.dot(attended, out_weight, preferred_element_type=jnp.float32)
-        return output.astype(jnp.bfloat16)
-    first = None
-    if chunks > 1:
-        first = project(near[:-1] + far[:-1], None, out_weight, info, chunks, jnp.float32)
-    return project(near[-1:] + far[-1:], first, out_weight, info, chunks, jnp.bfloat16)
+            far.append(crossed(att[1], 1))
+    attended = near
+    if pair == 2:
+        attended = [jnp.where(core == 0, a, b) for a, b in zip(near, far)]
+        attended += [jnp.where(core == 0, b, a) for a, b in zip(near, far)]
+    attended = lax.all_gather(jnp.concatenate(attended, 1), "head", axis=1, tiled=True)
+    output = jnp.dot(attended, out_weight, preferred_element_type=jnp.float32)
+    return output.astype(jnp.bfloat16)
 
 
 def solution(mesh):

time: 324 us -> 323 us (level)
  Pallas kernels: 200 us -> 174 us
  matrix products: 0 us -> 22.9 us
    pallas_call x2 -> x0, Pallas kernels: 31.3 us -> none  [project(): pl.pallas_call(functools.partial(project_kernel, n, before is not None),...]
    dot_general x0 -> x1, matrix products: none -> 22.9 us  [body(): output = jnp.dot(attended, out_weight, preferred_element_type=jnp.float32)]
    pallas_call x2, Pallas kernels: 128 us -> 132 us  [over_vertical(): pl.pallas_call(functools.partial(vertical_kernel, cfg + (self.plane, self...]
  transfers between devices with their start and end apart: 16 -> 16, of which waited for: 7 -> 8; matrix products, arithmetic and copies ran while one was open for 2% -> 2% of each run, Pallas kernels for 55% -> 52%
where the time goes in v4:
time: 323 us
  Pallas kernels  174 us (54%)
  waiting for transfers between devices  76.5 us (24%)
  starting transfers between devices  35.4 us (11%)
  matrix products  22.9 us (7%)
  local copies, waits for them, and re-layouts  7.64 us (2%)
  other arithmetic  6.19 us (2%)
    pallas_call x2, Pallas kernels, over_vertical(): pl.pallas_call(functools.partial(vertical_kernel, cfg + (self.plane, self...  132 us
    ppermute x12, waiting for transfers between devices, crossed(): return lax.ppermute(value, 'ctx', [(i, i ^ bits) for i in range(size)])  39.3 us
    ppermute x4, waiting for transfers between devices, shifted(): return lax.ppermute(value, 'ctx', [(i, i + by) for i in range(size - by)])  37.1 us
    pallas_call x2, Pallas kernels, over_slash(): pl.pallas_call(functools.partial(slash_kernel, cfg), grid_spec=pltpu.Pref...  36.9 us
    dot_general x1, matrix products, body(): output = jnp.dot(attended, out_weight, preferred_element_type=jnp.float32)  22.9 us
    ppermute x12, starting transfers between devices, crossed(): return lax.ppermute(value, 'ctx', [(i, i ^ bits) for i in range(size)])  18.4 us
    ppermute x4, starting transfers between devices, shifted(): return lax.ppermute(value, 'ctx', [(i, i + by) for i in range(size - by)])  17.1 us
  transfers between devices with their start and end apart: 16, of which 8 were waited for; matrix products, arithmetic and copies ran while one was open for 2% of the time, Pallas kernels for 52%

profile of v4, /device:TPU:25, one launch (start us, length us, event | category | flops | bytes accessed | tf_op | source)
XLA Modules:
  0.0 322.5 jit_solution(17927141830433281068)
XLA Ops:
  0.0 1.3 constant_dynamic-slice_fusion.1
  5.4 4.5 %prepare.1 = (bf16[1024,512]{1,0:T(8,128)(2,1)}, bf16[1024,512]{1,0:T(8,128)(2,1)}, bf16[1024,256]{1,0:T(8,128)(2,1)}, bf16[1024,256]{1,0:T(8,128)(2,1)}, bf16[1...) custom-call(s32[2]{0:T(128)} %pad_add_fusion.info, s32[4,8]{1,0:T(4,128)} %constant_dynamic-slice_fusion.4.vert, ...), custom_call_target="tpu_custom_call" | custom-call | bytes 8388608 | tf_op jit(solution)/shard_map/prepare/pallas_call | solution.py:82
  12.6 1.7 constant_dynamic-slice_fusion
  14.3 9.0 %collective-permute-done.1 = bf16[1024,256]{1,0:T(8,128)(2,1)S(1)} collective-permute-done((bf16[1024,256]{1,0:T(8,128)(2,1)}, bf16[1024,256]{1,0:T(8,128)(2,1)S(1)}, u32[]{:S(2)}, u32[]{:S(2)}) %collective-permute-start.1) | collective-permute-done | bytes 524320 | tf_op jit(solution)/shard_map/ppermute | solution.py:27
  24.3 11.3 %collective-permute-done.3 = bf16[1024,256]{1,0:T(8,128)(2,1)} collective-permute-done((bf16[1024,256]{1,0:T(8,128)(2,1)}, bf16[1024,256]{1,0:T(8,128)(2,1)}, u32[]{:S(2)}, u32[]{:S(2)}) %collective-permute-start.3) | collective-permute-done | bytes 524320 | tf_op jit(solution)/shard_map/ppermute | solution.py:27
  35.6 1.5 add_add_fusion
  37.1 1.5 collective-permute-start.5
  38.6 3.1 collective-permute-start.6
  41.8 1.4 collective-permute-start.4
  43.2 23.3 %collective-permute-done.6.refs_4_ = bf16[1024,512]{1,0:T(8,128)(2,1)} collective-permute-done((bf16[1024,512]{1,0:T(8,128)(2,1)}, bf16[1024,512]{1,0:T(8,128)(2,1)}, u32[]{:S(2)}, u32[]{:S(2)}) %collective-permute-start.6) | collective-permute-done | bytes 1048608 | tf_op jit(solution)/shard_map/ppermute | solution.py:22
  66.5 1.3 broadcast_select_fusion.1
  69.0 1.3 collective-permute-start.8
  71.7 11.2 %collective-permute-start.13 = (bf16[1024,512]{1,0:T(8,128)(2,1)S(1)}, bf16[1024,512]{1,0:T(8,128)(2,1)S(1)}, u32[]{:S(2)}, u32[]{:S(2)}) collective-permute-start(bf16[1024,512]{1,0:T(8,128)(2,1)S(1)} %copy-done.5), channel_id=1, source_target_pairs={{0,4},{1,5},{2,6},{3,7},{4,8},{5,9},{6,10},{7,11},{8,12},{9,13},{1... | collective-permute-start | bytes 3145736 | tf_op jit(solution)/shard_map/ppermute | solution.py:22
  82.9 13.9 %collective-permute-done.8 = bf16[1024,256]{1,0:T(8,128)(2,1)S(1)} collective-permute-done((bf16[1024,256]{1,0:T(8,128)(2,1)S(1)}, bf16[1024,256]{1,0:T(8,128)(2,1)S(1)}, u32[]{:S(2)}, u32[]{:S(2)}) %collective-permute-start.8) | collective-permute-done | bytes 524320 | tf_op jit(solution)/shard_map/ppermute | solution.py:22
  96.9 9.3 %collective-permute-start.10 = (bf16[1024,256]{1,0:T(8,128)(2,1)S(1)}, bf16[1024,256]{1,0:T(8,128)(2,1)S(1)}, u32[]{:S(2)}, u32[]{:S(2)}) collective-permute-start(bf16[1024,256]{1,0:T(8,128)(2,1)S(1)} %add.44), channel_id=1, source_target_pairs={{0,4},{1,5},{2,6},{3,7},{4,0},{5,1},{6,2},{7,3},{8,12},{9,13},{10,... | collective-permute-start | bytes 1572872 | tf_op jit(solution)/shard_map/ppermute | solution.py:27
  107.5 18.3 %attend_slash.2.refs_5_ = f32[2,8,512,256]{3,2,1,0:T(8,128)} custom-call(s32[2]{0:T(128)} %pad_add_fusion.info, s32[4,8]{1,0:T(4,128)} %constant_dynamic-slice_fusion.3.slash, bf16[512,4096]{1,0:T(8,128)(2,1)} %refs_0_.9, bf16[512,2048]{1,0:T(8,128)(2,1)} %collective-permute-done.5.refs_1_, bf16[1024,512]{1,0:T(8,128)(2,1)} %get-tuple-element.35.refs_2_, ...), custom_call_target="tpu_custom_call" | custom-call | flops 8589934592 | bytes 10485760 | tf_op jit(solution)/shard_map/attend_slash/pallas_call | solution.py:336
  125.8 14.1 %collective-permute-done.10 = bf16[1024,256]{1,0:T(8,128)(2,1)S(1)} collective-permute-done((bf16[1024,256]{1,0:T(8,128)(2,1)S(1)}, bf16[1024,256]{1,0:T(8,128)(2,1)S(1)}, u32[]{:S(2)}, u32[]{:S(2)}) %collective-permute-start.10) | collective-permute-done | bytes 524320 | tf_op jit(solution)/shard_map/ppermute | solution.py:27
  141.3 1.3 copy-done.9
  142.6 66.0 %attend_vertical.2 = (bf16[512,1024]{1,0:T(8,128)(2,1)}, bf16[512,1024]{1,0:T(8,128)(2,1)}) custom-call(s32[2]{0:T(128)} %pad_add_fusion.info, s32[4,8]{1,0:T(4,128)} %constant_dynamic-slice_fusion.4.vert, s32[4,8]{1,0:T(4,128)} %constant_dynamic-slice_fusion.3.slash, bf16[512,4096]{1,0:T(8,128)(2,1)} %refs_0_.9, ...), custom_call_target="tpu_custom_call" | custom-call | flops 8589934592 | bytes 10485760 | tf_op jit(solution)/shard_map/attend_vertical/pallas_call | solution.py:362
  210.4 18.6 %attend_slash.3.refs_5_ = f32[2,8,512,256]{3,2,1,0:T(8,128)} custom-call(s32[2]{0:T(128)} %pad_add_fusion.info, s32[4,8]{1,0:T(4,128)} %constant_dynamic-slice_fusion.3.slash, bf16[512,4096]{1,0:T(8,128)(2,1)} %refs_0_.9, bf16[512,2048]{1,0:T(8,128)(2,1)} %collective-permute-done.5.refs_1_, bf16[1024,512]{1,0:T(8,128)(2,1)} %get-tuple-element.44.refs_2_, ...), custom_call_target="tpu_custom_call" | custom-call | flops 8589934592 | bytes 10485760 | tf_op jit(solution)/shard_map/attend_slash/pallas_call | solution.py:336
  229.0 66.2 %attend_vertical.3 = (bf16[512,1024]{1,0:T(8,128)(2,1)}, bf16[512,1024]{1,0:T(8,128)(2,1)}) custom-call(s32[2]{0:T(128)} %pad_add_fusion.info, s32[4,8]{1,0:T(4,128)} %constant_dynamic-slice_fusion.4.vert, s32[4,8]{1,0:T(4,128)} %constant_dynamic-slice_fusion.3.slash, bf16[512,4096]{1,0:T(8,128)(2,1)} %refs_0_.9, ...), custom_call_target="tpu_custom_call" | custom-call | flops 8589934592 | bytes 10485760 | tf_op jit(solution)/shard_map/attend_vertical/pallas_call | solution.py:362
  295.5 2.8 collective-permute-done.15
  298.3 1.4 broadcast_select_fusion.4
  299.7 22.9 %convolution_convert_fusion = bf16[512,4096]{1,0:T(8,128)(2,1)} fusion(bf16[4096,4096]{1,0:T(8,128)(2,1)} %param.11, bf16[512,1024]{1,0:T(8,128)(2,1)S(1)} %get-tuple-element.50, bf16[512,1024]{1,0:T(8,128)(2,1)S(1)} %get-tuple-element.48, bf16[512,1024]{1,0:T(8,128)(2,1)S(1)} %get-tuple-element.49, bf16[512,1024]{1,0:T(8,128)(2,1)S(1)} %get-tuple-element.47), kind=kOutput, calls=%fused_computation | convolution fusion | flops 17198743552 | bytes 41943040 | tf_op jit(solution)/shard_map/dot_general | solution.py:463
  (59 shorter events, 14.9 us)
Async XLA Ops:
  1.4 3.0 collective-permute-start
  9.9 25.7 %copy-start.7 = (bf16[1024,256]{1,0:T(8,128)(2,1)S(1)}, bf16[1024,256]{1,0:T(8,128)(2,1)}, u32[]{:S(2)}) copy-start(bf16[1024,256]{1,0:T(8,128)(2,1)} %get-tuple-element.26) | copy-start | bytes 1572868
  9.9 13.4 %collective-permute-start.1 = (bf16[1024,256]{1,0:T(8,128)(2,1)}, bf16[1024,256]{1,0:T(8,128)(2,1)S(1)}, u32[]{:S(2)}, u32[]{:S(2)}) collective-permute-start(bf16[1024,256]{1,0:T(8,128)(2,1)} %get-tuple-element.27), channel_id=1, source_target_pairs={{0,2},{1,3},{2,0},{3,1},{4,6},{5,7},{6,4},{7,5},{8,10},{9,11},{10,... | collective-permute-start | bytes 1572872 | tf_op jit(solution)/shard_map/ppermute | solution.py:27
  11.1 13.1 %collective-permute-start.2 = (bf16[1024,256]{1,0:T(8,128)(2,1)}, bf16[1024,256]{1,0:T(8,128)(2,1)}, u32[]{:S(2)}, u32[]{:S(2)}) collective-permute-start(bf16[1024,256]{1,0:T(8,128)(2,1)} %get-tuple-element.28), channel_id=1, source_target_pairs={{0,4},{1,5},{2,6},{3,7},{4,0},{5,1},{6,2},{7,3},{8,12},{9,13},{10,... | collective-permute-start | bytes 1572872 | tf_op jit(solution)/shard_map/ppermute | solution.py:27
  12.4 23.2 %collective-permute-start.3 = (bf16[1024,256]{1,0:T(8,128)(2,1)}, bf16[1024,256]{1,0:T(8,128)(2,1)}, u32[]{:S(2)}, u32[]{:S(2)}) collective-permute-start(bf16[1024,256]{1,0:T(8,128)(2,1)} %get-tuple-element.29), channel_id=1, source_target_pairs={{0,6},{1,7},{2,4},{3,5},{4,2},{5,3},{6,0},{7,1},{8,14},{9,15},{10,... | collective-permute-start | bytes 1572872 | tf_op jit(solution)/shard_map/ppermute | solution.py:27
  14.3 56.0 %copy-start.10 = (s32[8,8]{1,0:T(8,128)S(1)}, s32[8,8]{1,0:T(8,128)}, u32[]{:S(2)}) copy-start(s32[8,8]{1,0:T(8,128)} %param.10) | copy-start | bytes 772
  23.4 12.2 %copy-start.8 = (bf16[1024,256]{1,0:T(8,128)(2,1)}, bf16[1024,256]{1,0:T(8,128)(2,1)S(1)}, u32[]{:S(2)}) copy-start(bf16[1024,256]{1,0:T(8,128)(2,1)S(1)} %collective-permute-done.1) | copy-start | bytes 1572868
  37.1 31.9 %collective-permute-start.5 = (bf16[512,2048]{1,0:T(8,128)(2,1)S(1)}, bf16[512,2048]{1,0:T(8,128)(2,1)}, u32[]{:S(2)}, u32[]{:S(2)}) collective-permute-start(bf16[512,2048]{1,0:T(8,128)(2,1)S(1)} %constant_dynamic-slice_fusion), channel_id=1, source_target_pairs={{0,1},{1,0},{2,3},{3,2},{4,5},{5,4},{6,7},{7,6},{8,9},{9,8},{10,11... | collective-permute-start | bytes 6291464 | tf_op jit(solution)/shard_map/ppermute | solution.py:27
  38.6 27.9 %collective-permute-start.6 = (bf16[1024,512]{1,0:T(8,128)(2,1)}, bf16[1024,512]{1,0:T(8,128)(2,1)}, u32[]{:S(2)}, u32[]{:S(2)}) collective-permute-start(bf16[1024,512]{1,0:T(8,128)(2,1)} %get-tuple-element.35.refs_2_), channel_id=1, source_target_pairs={{0,4},{1,5},{2,6},{3,7},{4,8},{5,9},{6,10},{7,11},{8,12},{9,13},{1... | collective-permute-start | bytes 3145736 | tf_op jit(solution)/shard_map/ppermute | solution.py:22
  41.8 29.9 %copy-start.5 = (bf16[1024,512]{1,0:T(8,128)(2,1)S(1)}, bf16[1024,512]{1,0:T(8,128)(2,1)}, u32[]{:S(2)}) copy-start(bf16[1024,512]{1,0:T(8,128)(2,1)} %get-tuple-element.44.refs_2_) | copy-start | bytes 3145732
  41.8 27.0 %collective-permute-start.4 = (bf16[1024,256]{1,0:T(8,128)(2,1)S(1)}, bf16[1024,256]{1,0:T(8,128)(2,1)S(1)}, u32[]{:S(2)}, u32[]{:S(2)}) collective-permute-start(bf16[1024,256]{1,0:T(8,128)(2,1)S(1)} %add_add_fusion), channel_id=1, source_target_pairs={{0,8},{1,9},{2,10},{3,11},{4,12},{5,13},{6,14},{7,15},{8,16},{9,17... | collective-permute-start | bytes 1572872 | tf_op jit(solution)/shard_map/ppermute | solution.py:22
  67.8 39.6 %collective-permute-start.7 = (bf16[1024,512]{1,0:T(8,128)(2,1)S(1)}, bf16[1024,512]{1,0:T(8,128)(2,1)}, u32[]{:S(2)}, u32[]{:S(2)}) collective-permute-start(bf16[1024,512]{1,0:T(8,128)(2,1)S(1)} %broadcast_select_fusion.1), channel_id=1, source_target_pairs={{0,2},{1,3},{2,0},{3,1},{4,6},{5,7},{6,4},{7,5},{8,10},{9,11},{10,... | collective-permute-start | bytes 3145736 | tf_op jit(solution)/shard_map/ppermute | solution.py:27
  69.0 27.8 %collective-permute-start.8 = (bf16[1024,256]{1,0:T(8,128)(2,1)S(1)}, bf16[1024,256]{1,0:T(8,128)(2,1)S(1)}, u32[]{:S(2)}, u32[]{:S(2)}) collective-permute-start(bf16[1024,256]{1,0:T(8,128)(2,1)S(1)} %add.42), channel_id=1, source_target_pairs={{0,16},{1,17},{2,18},{3,19},{4,20},{5,21},{6,22},{7,23},{8,24},{9,... | collective-permute-start | bytes 1572872 | tf_op jit(solution)/shard_map/ppermute | solution.py:22
  71.7 68.3 %collective-permute-start.13 = (bf16[1024,512]{1,0:T(8,128)(2,1)S(1)}, bf16[1024,512]{1,0:T(8,128)(2,1)S(1)}, u32[]{:S(2)}, u32[]{:S(2)}) collective-permute-start(bf16[1024,512]{1,0:T(8,128)(2,1)S(1)} %copy-done.5), channel_id=1, source_target_pairs={{0,4},{1,5},{2,6},{3,7},{4,8},{5,9},{6,10},{7,11},{8,12},{9,13},{1... | collective-permute-start | bytes 3145736 | tf_op jit(solution)/shard_map/ppermute | solution.py:22
  96.9 43.0 %collective-permute-start.10 = (bf16[1024,256]{1,0:T(8,128)(2,1)S(1)}, bf16[1024,256]{1,0:T(8,128)(2,1)S(1)}, u32[]{:S(2)}, u32[]{:S(2)}) collective-permute-start(bf16[1024,256]{1,0:T(8,128)(2,1)S(1)} %add.44), channel_id=1, source_target_pairs={{0,4},{1,5},{2,6},{3,7},{4,0},{5,1},{6,2},{7,3},{8,12},{9,13},{10,... | collective-permute-start | bytes 1572872 | tf_op jit(solution)/shard_map/ppermute | solution.py:27
  106.2 33.7 %collective-permute-start.11 = (bf16[1024,256]{1,0:T(8,128)(2,1)S(1)}, bf16[1024,256]{1,0:T(8,128)(2,1)S(1)}, u32[]{:S(2)}, u32[]{:S(2)}) collective-permute-start(bf16[1024,256]{1,0:T(8,128)(2,1)S(1)} %add.44), channel_id=1, source_target_pairs={{0,6},{1,7},{2,4},{3,5},{4,2},{5,3},{6,0},{7,1},{8,14},{9,15},{10,... | collective-permute-start | bytes 1572872 | tf_op jit(solution)/shard_map/ppermute | solution.py:27
  106.9 33.0 %collective-permute-start.9 = (bf16[1024,256]{1,0:T(8,128)(2,1)S(1)}, bf16[1024,256]{1,0:T(8,128)(2,1)S(1)}, u32[]{:S(2)}, u32[]{:S(2)}) collective-permute-start(bf16[1024,256]{1,0:T(8,128)(2,1)S(1)} %add.44), channel_id=1, source_target_pairs={{0,2},{1,3},{2,0},{3,1},{4,6},{5,7},{6,4},{7,5},{8,10},{9,11},{10,... | collective-permute-start | bytes 1572872 | tf_op jit(solution)/shard_map/ppermute | solution.py:27
  140.0 68.6 %copy-start.6 = (bf16[1024,512]{1,0:T(8,128)(2,1)}, bf16[1024,512]{1,0:T(8,128)(2,1)S(1)}, u32[]{:S(2)}) copy-start(bf16[1024,512]{1,0:T(8,128)(2,1)S(1)} %collective-permute-done.13.refs_4_) | copy-start | bytes 3145732
  140.2 69.3 %collective-permute-start.14 = (bf16[1024,512]{1,0:T(8,128)(2,1)S(1)}, bf16[1024,512]{1,0:T(8,128)(2,1)S(1)}, u32[]{:S(2)}, u32[]{:S(2)}) collective-permute-start(bf16[1024,512]{1,0:T(8,128)(2,1)S(1)} %broadcast_select_fusion), channel_id=1, source_target_pairs={{0,2},{1,3},{2,0},{3,1},{4,6},{5,7},{6,4},{7,5},{8,10},{9,11},{10,... | collective-permute-start | bytes 3145736 | tf_op jit(solution)/shard_map/ppermute | solution.py:27
  208.6 86.7 %collective-permute-start.12 = (bf16[512,1024]{1,0:T(8,128)(2,1)}, bf16[512,1024]{1,0:T(8,128)(2,1)S(1)}, u32[]{:S(2)}, u32[]{:S(2)}) collective-permute-start(bf16[512,1024]{1,0:T(8,128)(2,1)} %get-tuple-element.43), channel_id=1, source_target_pairs={{0,1},{1,0},{2,3},{3,2},{4,5},{5,4},{6,7},{7,6},{8,9},{9,8},{10,11... | collective-permute-start | bytes 3145736 | tf_op jit(solution)/shard_map/ppermute | solution.py:27
  229.0 66.3 %copy-start.3 = (bf16[512,1024]{1,0:T(8,128)(2,1)S(1)}, bf16[512,1024]{1,0:T(8,128)(2,1)}, u32[]{:S(2)}) copy-start(bf16[512,1024]{1,0:T(8,128)(2,1)} %get-tuple-element.42) | copy-start | bytes 3145732
  295.2 3.1 copy-start.4
  295.2 3.1 collective-permute-start.15
  299.6 22.9 %copy-start.1 = (s32[8,8]{1,0:T(8,128)S(1)}, s32[8,8]{1,0:T(8,128)}, u32[]{:S(2)}) copy-start(s32[8,8]{1,0:T(8,128)} %param.9) | copy-start | bytes 772
  (4 other events, 6.0 us)

commit v5 on v2

--- a/solution.py
+++ b/solution.py
@@ -13,7 +13,7 @@
 MAXOFF = 16
 PLANE = 4
 MASKED = -1e30
-SMALLEST, LARGEST = 2.0**-60, 2.0**100
+SMALLEST, LARGEST = 2.0**-30, 2.0**30
 VMEM_LIMIT = 56 * 1024 * 1024
 
 
@@ -103,7 +103,10 @@
 
 
 def exponentials(q, k, factor):
-    return jnp.exp2(jnp.dot(q, k, preferred_element_type=jnp.float32) * factor)
+    x = jnp.dot(q, k, preferred_element_type=jnp.float32) * factor
+    high = x.astype(jnp.bfloat16)
+    low = x - high.astype(jnp.float32)
+    return jnp.exp2(high) * (low * math.log(2.0) + 1.0).astype(jnp.bfloat16)
 
 
 def pipelined(blocks, stage):
@@ -395,49 +398,6 @@
         )(self.info, self.vert, self.slash, *self.qs, *windows, before, kv_vert, self.masks)
 
 
-def project_kernel(n, has_before, info, *refs):
-    lefts, rights, refs = refs[:n], refs[n : 2 * n], refs[2 * n :]
-    acc = refs[0][...] if has_before else None
-    for left, right in zip(lefts, rights):
-        part = jnp.dot(left[...], right[...], preferred_element_type=jnp.float32)
-        acc = part if acc is None else acc + part
-    refs[-1][...] = acc.astype(refs[-1].dtype)
-
-
-def project(pieces, before, out_weight, info, chunks, dtype):
-    rows, wide = pieces[0][2].shape
-    columns = out_weight.shape[1]
-    tile = min(1024, columns)
-    n = len(pieces)
-
-    def weight_spec(swap, c):
-        if swap:
-            return pl.BlockSpec((wide, tile), lambda i, info: ((1 - info[1]) * chunks + c, i))
-        return pl.BlockSpec((wide, tile), lambda i, info: (info[1] * chunks + c, i))
-
-    in_specs = [pl.BlockSpec((rows, wide), lambda i, info: (0, 0))] * n
-    in_specs += [weight_spec(swap, c) for swap, c, _ in pieces]
-    args = [a for _, _, a in pieces] + [out_weight] * n
-    out_spec = pl.BlockSpec((rows, tile), lambda i, info: (0, i))
-    if before is not None:
-        in_specs.append(out_spec)
-        args.append(before)
-    return pl.pallas_call(
-        functools.partial(project_kernel, n, before is not None),
-        grid_spec=pltpu.PrefetchScalarGridSpec(
-            num_scalar_prefetch=1, grid=(columns // tile,), in_specs=in_specs, out_specs=out_spec
-        ),
-        out_shape=jax.ShapeDtypeStruct((rows, columns), dtype),
-        compiler_params=pltpu.CompilerParams(vmem_limit_bytes=VMEM_LIMIT),
-        cost_estimate=pl.CostEstimate(
-            flops=2 * n * rows * wide * columns,
-            bytes_accessed=2 * n * wide * (rows + columns) + 8 * rows * columns,
-            transcendentals=0,
-        ),
-        name="project",
-    )(info, *args)
-
-
 def body(queries, keys, values, vertical_blocks, slash_offsets, out_weight):
     tokens_dev = queries.shape[0]
     kv_heads = keys.shape[1] // HD
@@ -477,9 +437,9 @@
     step = 1
     while step < chips // plane:
         total = total + shifted(total, step * plane * pair)
-        total, q_other = lax.optimization_barrier((total, q_other))
+        if step == 1:
+            total, q_other, own[1:] = lax.optimization_barrier((total, q_other, own[1:]))
         step *= 2
-    total, own[1:] = lax.optimization_barrier((total, own[1:]))
 
     attention = Attention(queries, q_other, info, vert, slash, masks, heads, local, plane)
     chunks = heads // per_chunk
@@ -500,18 +460,16 @@
     near, far = [], []
     for c in range(chunks):
         att = attention.over_vertical(c * per_chunk, per_chunk, all_windows[c], sums[c], kv_vert)
-        near.append((False, c, att[0]))
+        near.append(att[0])
         if pair == 2:
-            far.append((True, c, crossed(att[1], 1)))
-    if pair == 1:
-        attended = jnp.concatenate([a for _, _, a in near], 1)
-        attended = lax.all_gather(attended, "head", axis=1, tiled=True)
-        output = jnp.dot(attended, out_weight, preferred_element_type=jnp.float32)
-        return output.astype(jnp.bfloat16)
-    first = None
-    if chunks > 1:
-        first = project(near[:-1] + far[:-1], None, out_weight, info, chunks, jnp.float32)
-    return project(near[-1:] + far[-1:], first, out_weight, info, chunks, jnp.bfloat16)
+            far.append(crossed(att[1], 1))
+    attended = near
+    if pair == 2:
+        attended = [jnp.where(core == 0, a, b) for a, b in zip(near, far)]
+        attended += [jnp.where(core == 0, b, a) for a, b in zip(near, far)]
+    attended = lax.all_gather(jnp.concatenate(attended, 1), "head", axis=1, tiled=True)
+    output = jnp.dot(attended, out_weight, preferred_element_type=jnp.float32)
+    return output.astype(jnp.bfloat16)
 
 
 def solution(mesh):

time: 330 us -> 318 us (0.964)
  Pallas kernels: 194 us -> 169 us
  matrix products: 0 us -> 22.9 us
  waiting for transfers between devices: 93.7 us -> 76 us
  starting transfers between devices: 27.6 us -> 35.4 us
    pallas_call x2 -> x0, Pallas kernels: 31.3 us -> none  [project(): pl.pallas_call(functools.partial(project_kernel, n, before is not None),...]
    dot_general x0 -> x1, matrix products: none -> 22.9 us  [body(): output = jnp.dot(attended, out_weight, preferred_element_type=jnp.float32)]
    ppermute x4, waiting for transfers between devices: 48.4 us -> 37.1 us  [shifted(): return lax.ppermute(value, 'ctx', [(i, i + by) for i in range(size - by)])]
    ppermute x4, starting transfers between devices: 9.19 us -> 17.1 us  [shifted(): return lax.ppermute(value, 'ctx', [(i, i + by) for i in range(size - by)])]
    ppermute x12, waiting for transfers between devices: 45.3 us -> 38.9 us  [crossed(): return lax.ppermute(value, 'ctx', [(i, i ^ bits) for i in range(size)])]
    pallas_call x2, Pallas kernels: 122 us -> 126 us  [over_vertical(): pl.pallas_call(functools.partial(vertical_kernel, cfg + (self.plane, self...]
  transfers between devices with their start and end apart: 16 -> 16, of which waited for: 7 -> 8; matrix products, arithmetic and copies ran while one was open for 2% -> 2% of each run, Pallas kernels for 53% -> 52%
where the time goes in v5:
time: 318 us; the launch traced here: 317 us
  Pallas kernels  169 us (53%)
  waiting for transfers between devices  76 us (24%)
  starting transfers between devices  35.4 us (11%)
  matrix products  22.9 us (7%)
  local copies, waits for them, and re-layouts  7.69 us (2%)
  other arithmetic  6.28 us (2%)
    pallas_call x2, Pallas kernels, over_vertical(): pl.pallas_call(functools.partial(vertical_kernel, cfg + (self.plane, self...  126 us
    ppermute x12, waiting for transfers between devices, crossed(): return lax.ppermute(value, 'ctx', [(i, i ^ bits) for i in range(size)])  38.9 us
    pallas_call x2, Pallas kernels, over_slash(): pl.pallas_call(functools.partial(slash_kernel, cfg), grid_spec=pltpu.Pref...  37.7 us
    ppermute x4, waiting for transfers between devices, shifted(): return lax.ppermute(value, 'ctx', [(i, i + by) for i in range(size - by)])  37.1 us
    dot_general x1, matrix products, body(): output = jnp.dot(attended, out_weight, preferred_element_type=jnp.float32)  22.9 us
    ppermute x12, starting transfers between devices, crossed(): return lax.ppermute(value, 'ctx', [(i, i ^ bits) for i in range(size)])  18.3 us
    ppermute x4, starting transfers between devices, shifted(): return lax.ppermute(value, 'ctx', [(i, i + by) for i in range(size - by)])  17.1 us
  transfers between devices with their start and end apart: 16, of which 8 were waited for; matrix products, arithmetic and copies ran while one was open for 2% of the time, Pallas kernels for 52%

profile of v5, /device:TPU:25, one launch (start us, length us, event | category | flops | bytes accessed | tf_op | source)
XLA Modules:
  0.0 317.1 jit_solution(15140413690870944891)
XLA Ops:
  0.0 1.3 constant_dynamic-slice_fusion.1
  5.4 4.5 %prepare.1 = (bf16[1024,512]{1,0:T(8,128)(2,1)}, bf16[1024,512]{1,0:T(8,128)(2,1)}, bf16[1024,256]{1,0:T(8,128)(2,1)}, bf16[1024,256]{1,0:T(8,128)(2,1)}, bf16[1...) custom-call(s32[2]{0:T(128)} %pad_add_fusion.info, s32[4,8]{1,0:T(4,128)} %constant_dynamic-slice_fusion.4.vert, ...), custom_call_target="tpu_custom_call" | custom-call | bytes 8388608 | tf_op jit(solution)/shard_map/prepare/pallas_call | solution.py:82
  12.6 1.7 constant_dynamic-slice_fusion
  14.3 9.0 %collective-permute-done.1 = bf16[1024,256]{1,0:T(8,128)(2,1)S(1)} collective-permute-done((bf16[1024,256]{1,0:T(8,128)(2,1)}, bf16[1024,256]{1,0:T(8,128)(2,1)S(1)}, u32[]{:S(2)}, u32[]{:S(2)}) %collective-permute-start.1) | collective-permute-done | bytes 524320 | tf_op jit(solution)/shard_map/ppermute | solution.py:27
  24.3 11.3 %collective-permute-done.3 = bf16[1024,256]{1,0:T(8,128)(2,1)} collective-permute-done((bf16[1024,256]{1,0:T(8,128)(2,1)}, bf16[1024,256]{1,0:T(8,128)(2,1)}, u32[]{:S(2)}, u32[]{:S(2)}) %collective-permute-start.3) | collective-permute-done | bytes 524320 | tf_op jit(solution)/shard_map/ppermute | solution.py:27
  35.6 1.5 add_add_fusion
  37.1 1.5 collective-permute-start.5
  38.6 3.1 collective-permute-start.6
  41.8 1.4 collective-permute-start.4
  43.2 23.3 %collective-permute-done.6.refs_4_ = bf16[1024,512]{1,0:T(8,128)(2,1)} collective-permute-done((bf16[1024,512]{1,0:T(8,128)(2,1)}, bf16[1024,512]{1,0:T(8,128)(2,1)}, u32[]{:S(2)}, u32[]{:S(2)}) %collective-permute-start.6) | collective-permute-done | bytes 1048608 | tf_op jit(solution)/shard_map/ppermute | solution.py:22
  66.5 1.3 broadcast_select_fusion.1
  69.0 1.3 collective-permute-start.8
  71.7 11.2 %collective-permute-start.13 = (bf16[1024,512]{1,0:T(8,128)(2,1)S(1)}, bf16[1024,512]{1,0:T(8,128)(2,1)S(1)}, u32[]{:S(2)}, u32[]{:S(2)}) collective-permute-start(bf16[1024,512]{1,0:T(8,128)(2,1)S(1)} %copy-done.5), channel_id=1, source_target_pairs={{0,4},{1,5},{2,6},{3,7},{4,8},{5,9},{6,10},{7,11},{8,12},{9,13},{1... | collective-permute-start | bytes 3145736 | tf_op jit(solution)/shard_map/ppermute | solution.py:22
  83.0 13.8 %collective-permute-done.8 = bf16[1024,256]{1,0:T(8,128)(2,1)S(1)} collective-permute-done((bf16[1024,256]{1,0:T(8,128)(2,1)S(1)}, bf16[1024,256]{1,0:T(8,128)(2,1)S(1)}, u32[]{:S(2)}, u32[]{:S(2)}) %collective-permute-start.8) | collective-permute-done | bytes 524320 | tf_op jit(solution)/shard_map/ppermute | solution.py:22
  96.9 9.3 %collective-permute-start.10 = (bf16[1024,256]{1,0:T(8,128)(2,1)S(1)}, bf16[1024,256]{1,0:T(8,128)(2,1)S(1)}, u32[]{:S(2)}, u32[]{:S(2)}) collective-permute-start(bf16[1024,256]{1,0:T(8,128)(2,1)S(1)} %add.44), channel_id=1, source_target_pairs={{0,4},{1,5},{2,6},{3,7},{4,0},{5,1},{6,2},{7,3},{8,12},{9,13},{10,... | collective-permute-start | bytes 1572872 | tf_op jit(solution)/shard_map/ppermute | solution.py:27
  107.5 18.7 %attend_slash.2.refs_5_ = f32[2,8,512,256]{3,2,1,0:T(8,128)} custom-call(s32[2]{0:T(128)} %pad_add_fusion.info, s32[4,8]{1,0:T(4,128)} %constant_dynamic-slice_fusion.3.slash, bf16[512,4096]{1,0:T(8,128)(2,1)} %refs_0_.9, bf16[512,2048]{1,0:T(8,128)(2,1)} %collective-permute-done.5.refs_1_, bf16[1024,512]{1,0:T(8,128)(2,1)} %get-tuple-element.35.refs_2_, ...), custom_call_target="tpu_custom_call" | custom-call | flops 8589934592 | bytes 10485760 | tf_op jit(solution)/shard_map/attend_slash/pallas_call | solution.py:345
  126.2 13.8 %collective-permute-done.10 = bf16[1024,256]{1,0:T(8,128)(2,1)S(1)} collective-permute-done((bf16[1024,256]{1,0:T(8,128)(2,1)S(1)}, bf16[1024,256]{1,0:T(8,128)(2,1)S(1)}, u32[]{:S(2)}, u32[]{:S(2)}) %collective-permute-start.10) | collective-permute-done | bytes 524320 | tf_op jit(solution)/shard_map/ppermute | solution.py:27
  141.3 1.3 copy-done.9
  142.6 63.1 %attend_vertical.2 = (bf16[512,1024]{1,0:T(8,128)(2,1)}, bf16[512,1024]{1,0:T(8,128)(2,1)}) custom-call(s32[2]{0:T(128)} %pad_add_fusion.info, s32[4,8]{1,0:T(4,128)} %constant_dynamic-slice_fusion.4.vert, s32[4,8]{1,0:T(4,128)} %constant_dynamic-slice_fusion.3.slash, bf16[512,4096]{1,0:T(8,128)(2,1)} %refs_0_.9, ...), custom_call_target="tpu_custom_call" | custom-call | flops 8589934592 | bytes 10485760 | tf_op jit(solution)/shard_map/attend_vertical/pallas_call | solution.py:371
  207.5 18.9 %attend_slash.3.refs_5_ = f32[2,8,512,256]{3,2,1,0:T(8,128)} custom-call(s32[2]{0:T(128)} %pad_add_fusion.info, s32[4,8]{1,0:T(4,128)} %constant_dynamic-slice_fusion.3.slash, bf16[512,4096]{1,0:T(8,128)(2,1)} %refs_0_.9, bf16[512,2048]{1,0:T(8,128)(2,1)} %collective-permute-done.5.refs_1_, bf16[1024,512]{1,0:T(8,128)(2,1)} %get-tuple-element.44.refs_2_, ...), custom_call_target="tpu_custom_call" | custom-call | flops 8589934592 | bytes 10485760 | tf_op jit(solution)/shard_map/attend_slash/pallas_call | solution.py:345
  226.5 63.3 %attend_vertical.3 = (bf16[512,1024]{1,0:T(8,128)(2,1)}, bf16[512,1024]{1,0:T(8,128)(2,1)}) custom-call(s32[2]{0:T(128)} %pad_add_fusion.info, s32[4,8]{1,0:T(4,128)} %constant_dynamic-slice_fusion.4.vert, s32[4,8]{1,0:T(4,128)} %constant_dynamic-slice_fusion.3.slash, bf16[512,4096]{1,0:T(8,128)(2,1)} %refs_0_.9, ...), custom_call_target="tpu_custom_call" | custom-call | flops 8589934592 | bytes 10485760 | tf_op jit(solution)/shard_map/attend_vertical/pallas_call | solution.py:371
  290.1 2.8 collective-permute-done.15
  292.9 1.4 broadcast_select_fusion.4
  294.3 22.9 %convolution_convert_fusion = bf16[512,4096]{1,0:T(8,128)(2,1)} fusion(bf16[4096,4096]{1,0:T(8,128)(2,1)} %param.11, bf16[512,1024]{1,0:T(8,128)(2,1)S(1)} %get-tuple-element.50, bf16[512,1024]{1,0:T(8,128)(2,1)S(1)} %get-tuple-element.48, bf16[512,1024]{1,0:T(8,128)(2,1)S(1)} %get-tuple-element.49, bf16[512,1024]{1,0:T(8,128)(2,1)S(1)} %get-tuple-element.47), kind=kOutput, calls=%fused_computation | convolution fusion | flops 17198743552 | bytes 41943040 | tf_op jit(solution)/shard_map/dot_general | solution.py:471
  (59 shorter events, 15.0 us)
Async XLA Ops:
  1.4 3.0 collective-permute-start
  9.9 25.7 %copy-start.7 = (bf16[1024,256]{1,0:T(8,128)(2,1)S(1)}, bf16[1024,256]{1,0:T(8,128)(2,1)}, u32[]{:S(2)}) copy-start(bf16[1024,256]{1,0:T(8,128)(2,1)} %get-tuple-element.26) | copy-start | bytes 1572868
  9.9 13.4 %collective-permute-start.1 = (bf16[1024,256]{1,0:T(8,128)(2,1)}, bf16[1024,256]{1,0:T(8,128)(2,1)S(1)}, u32[]{:S(2)}, u32[]{:S(2)}) collective-permute-start(bf16[1024,256]{1,0:T(8,128)(2,1)} %get-tuple-element.27), channel_id=1, source_target_pairs={{0,2},{1,3},{2,0},{3,1},{4,6},{5,7},{6,4},{7,5},{8,10},{9,11},{10,... | collective-permute-start | bytes 1572872 | tf_op jit(solution)/shard_map/ppermute | solution.py:27
  11.1 13.1 %collective-permute-start.2 = (bf16[1024,256]{1,0:T(8,128)(2,1)}, bf16[1024,256]{1,0:T(8,128)(2,1)}, u32[]{:S(2)}, u32[]{:S(2)}) collective-permute-start(bf16[1024,256]{1,0:T(8,128)(2,1)} %get-tuple-element.28), channel_id=1, source_target_pairs={{0,4},{1,5},{2,6},{3,7},{4,0},{5,1},{6,2},{7,3},{8,12},{9,13},{10,... | collective-permute-start | bytes 1572872 | tf_op jit(solution)/shard_map/ppermute | solution.py:27
  12.4 23.2 %collective-permute-start.3 = (bf16[1024,256]{1,0:T(8,128)(2,1)}, bf16[1024,256]{1,0:T(8,128)(2,1)}, u32[]{:S(2)}, u32[]{:S(2)}) collective-permute-start(bf16[1024,256]{1,0:T(8,128)(2,1)} %get-tuple-element.29), channel_id=1, source_target_pairs={{0,6},{1,7},{2,4},{3,5},{4,2},{5,3},{6,0},{7,1},{8,14},{9,15},{10,... | collective-permute-start | bytes 1572872 | tf_op jit(solution)/shard_map/ppermute | solution.py:27
  14.3 56.1 %copy-start.10 = (s32[8,8]{1,0:T(8,128)S(1)}, s32[8,8]{1,0:T(8,128)}, u32[]{:S(2)}) copy-start(s32[8,8]{1,0:T(8,128)} %param.10) | copy-start | bytes 772
  23.4 12.2 %copy-start.8 = (bf16[1024,256]{1,0:T(8,128)(2,1)}, bf16[1024,256]{1,0:T(8,128)(2,1)S(1)}, u32[]{:S(2)}) copy-start(bf16[1024,256]{1,0:T(8,128)(2,1)S(1)} %collective-permute-done.1) | copy-start | bytes 1572868
  37.1 31.9 %collective-permute-start.5 = (bf16[512,2048]{1,0:T(8,128)(2,1)S(1)}, bf16[512,2048]{1,0:T(8,128)(2,1)}, u32[]{:S(2)}, u32[]{:S(2)}) collective-permute-start(bf16[512,2048]{1,0:T(8,128)(2,1)S(1)} %constant_dynamic-slice_fusion), channel_id=1, source_target_pairs={{0,1},{1,0},{2,3},{3,2},{4,5},{5,4},{6,7},{7,6},{8,9},{9,8},{10,11... | collective-permute-start | bytes 6291464 | tf_op jit(solution)/shard_map/ppermute | solution.py:27
  38.6 27.9 %collective-permute-start.6 = (bf16[1024,512]{1,0:T(8,128)(2,1)}, bf16[1024,512]{1,0:T(8,128)(2,1)}, u32[]{:S(2)}, u32[]{:S(2)}) collective-permute-start(bf16[1024,512]{1,0:T(8,128)(2,1)} %get-tuple-element.35.refs_2_), channel_id=1, source_target_pairs={{0,4},{1,5},{2,6},{3,7},{4,8},{5,9},{6,10},{7,11},{8,12},{9,13},{1... | collective-permute-start | bytes 3145736 | tf_op jit(solution)/shard_map/ppermute | solution.py:22
  41.8 29.9 %copy-start.5 = (bf16[1024,512]{1,0:T(8,128)(2,1)S(1)}, bf16[1024,512]{1,0:T(8,128)(2,1)}, u32[]{:S(2)}) copy-start(bf16[1024,512]{1,0:T(8,128)(2,1)} %get-tuple-element.44.refs_2_) | copy-start | bytes 3145732
  41.8 27.0 %collective-permute-start.4 = (bf16[1024,256]{1,0:T(8,128)(2,1)S(1)}, bf16[1024,256]{1,0:T(8,128)(2,1)S(1)}, u32[]{:S(2)}, u32[]{:S(2)}) collective-permute-start(bf16[1024,256]{1,0:T(8,128)(2,1)S(1)} %add_add_fusion), channel_id=1, source_target_pairs={{0,8},{1,9},{2,10},{3,11},{4,12},{5,13},{6,14},{7,15},{8,16},{9,17... | collective-permute-start | bytes 1572872 | tf_op jit(solution)/shard_map/ppermute | solution.py:22
  67.8 39.6 %collective-permute-start.7 = (bf16[1024,512]{1,0:T(8,128)(2,1)S(1)}, bf16[1024,512]{1,0:T(8,128)(2,1)}, u32[]{:S(2)}, u32[]{:S(2)}) collective-permute-start(bf16[1024,512]{1,0:T(8,128)(2,1)S(1)} %broadcast_select_fusion.1), channel_id=1, source_target_pairs={{0,2},{1,3},{2,0},{3,1},{4,6},{5,7},{6,4},{7,5},{8,10},{9,11},{10,... | collective-permute-start | bytes 3145736 | tf_op jit(solution)/shard_map/ppermute | solution.py:27
  69.0 27.8 %collective-permute-start.8 = (bf16[1024,256]{1,0:T(8,128)(2,1)S(1)}, bf16[1024,256]{1,0:T(8,128)(2,1)S(1)}, u32[]{:S(2)}, u32[]{:S(2)}) collective-permute-start(bf16[1024,256]{1,0:T(8,128)(2,1)S(1)} %add.42), channel_id=1, source_target_pairs={{0,16},{1,17},{2,18},{3,19},{4,20},{5,21},{6,22},{7,23},{8,24},{9,... | collective-permute-start | bytes 1572872 | tf_op jit(solution)/shard_map/ppermute | solution.py:22
  71.7 68.3 %collective-permute-start.13 = (bf16[1024,512]{1,0:T(8,128)(2,1)S(1)}, bf16[1024,512]{1,0:T(8,128)(2,1)S(1)}, u32[]{:S(2)}, u32[]{:S(2)}) collective-permute-start(bf16[1024,512]{1,0:T(8,128)(2,1)S(1)} %copy-done.5), channel_id=1, source_target_pairs={{0,4},{1,5},{2,6},{3,7},{4,8},{5,9},{6,10},{7,11},{8,12},{9,13},{1... | collective-permute-start | bytes 3145736 | tf_op jit(solution)/shard_map/ppermute | solution.py:22
  96.9 43.0 %collective-permute-start.10 = (bf16[1024,256]{1,0:T(8,128)(2,1)S(1)}, bf16[1024,256]{1,0:T(8,128)(2,1)S(1)}, u32[]{:S(2)}, u32[]{:S(2)}) collective-permute-start(bf16[1024,256]{1,0:T(8,128)(2,1)S(1)} %add.44), channel_id=1, source_target_pairs={{0,4},{1,5},{2,6},{3,7},{4,0},{5,1},{6,2},{7,3},{8,12},{9,13},{10,... | collective-permute-start | bytes 1572872 | tf_op jit(solution)/shard_map/ppermute | solution.py:27
  106.2 33.8 %collective-permute-start.11 = (bf16[1024,256]{1,0:T(8,128)(2,1)S(1)}, bf16[1024,256]{1,0:T(8,128)(2,1)S(1)}, u32[]{:S(2)}, u32[]{:S(2)}) collective-permute-start(bf16[1024,256]{1,0:T(8,128)(2,1)S(1)} %add.44), channel_id=1, source_target_pairs={{0,6},{1,7},{2,4},{3,5},{4,2},{5,3},{6,0},{7,1},{8,14},{9,15},{10,... | collective-permute-start | bytes 1572872 | tf_op jit(solution)/shard_map/ppermute | solution.py:27
  106.9 33.0 %collective-permute-start.9 = (bf16[1024,256]{1,0:T(8,128)(2,1)S(1)}, bf16[1024,256]{1,0:T(8,128)(2,1)S(1)}, u32[]{:S(2)}, u32[]{:S(2)}) collective-permute-start(bf16[1024,256]{1,0:T(8,128)(2,1)S(1)} %add.44), channel_id=1, source_target_pairs={{0,2},{1,3},{2,0},{3,1},{4,6},{5,7},{6,4},{7,5},{8,10},{9,11},{10,... | collective-permute-start | bytes 1572872 | tf_op jit(solution)/shard_map/ppermute | solution.py:27
  140.1 65.7 %copy-start.6 = (bf16[1024,512]{1,0:T(8,128)(2,1)}, bf16[1024,512]{1,0:T(8,128)(2,1)S(1)}, u32[]{:S(2)}) copy-start(bf16[1024,512]{1,0:T(8,128)(2,1)S(1)} %collective-permute-done.13.refs_4_) | copy-start | bytes 3145732
  140.2 66.4 %collective-permute-start.14 = (bf16[1024,512]{1,0:T(8,128)(2,1)S(1)}, bf16[1024,512]{1,0:T(8,128)(2,1)S(1)}, u32[]{:S(2)}, u32[]{:S(2)}) collective-permute-start(bf16[1024,512]{1,0:T(8,128)(2,1)S(1)} %broadcast_select_fusion), channel_id=1, source_target_pairs={{0,2},{1,3},{2,0},{3,1},{4,6},{5,7},{6,4},{7,5},{8,10},{9,11},{10,... | collective-permute-start | bytes 3145736 | tf_op jit(solution)/shard_map/ppermute | solution.py:27
  205.7 84.2 %collective-permute-start.12 = (bf16[512,1024]{1,0:T(8,128)(2,1)}, bf16[512,1024]{1,0:T(8,128)(2,1)S(1)}, u32[]{:S(2)}, u32[]{:S(2)}) collective-permute-start(bf16[512,1024]{1,0:T(8,128)(2,1)} %get-tuple-element.43), channel_id=1, source_target_pairs={{0,1},{1,0},{2,3},{3,2},{4,5},{5,4},{6,7},{7,6},{8,9},{9,8},{10,11... | collective-permute-start | bytes 3145736 | tf_op jit(solution)/shard_map/ppermute | solution.py:27
  226.5 63.4 %copy-start.3 = (bf16[512,1024]{1,0:T(8,128)(2,1)S(1)}, bf16[512,1024]{1,0:T(8,128)(2,1)}, u32[]{:S(2)}) copy-start(bf16[512,1024]{1,0:T(8,128)(2,1)} %get-tuple-element.42) | copy-start | bytes 3145732
  289.8 3.1 copy-start.4
  289.8 3.1 collective-permute-start.15
  294.2 22.9 %copy-start.1 = (s32[8,8]{1,0:T(8,128)S(1)}, s32[8,8]{1,0:T(8,128)}, u32[]{:S(2)}) copy-start(s32[8,8]{1,0:T(8,128)} %param.9) | copy-start | bytes 772
  (4 other events, 6.1 us)

commit v6 on v5

--- a/solution.py
+++ b/solution.py
@@ -13,7 +13,7 @@
 MAXOFF = 16
 PLANE = 4
 MASKED = -1e30
-SMALLEST, LARGEST = 2.0**-30, 2.0**30
+SMALLEST, LARGEST = 2.0**-60, 2.0**100
 VMEM_LIMIT = 56 * 1024 * 1024
 
 
@@ -103,10 +103,7 @@
 
 
 def exponentials(q, k, factor):
-    x = jnp.dot(q, k, preferred_element_type=jnp.float32) * factor
-    high = x.astype(jnp.bfloat16)
-    low = x - high.astype(jnp.float32)
-    return jnp.exp2(high) * (low * math.log(2.0) + 1.0).astype(jnp.bfloat16)
+    return jnp.exp2(jnp.dot(q, k, preferred_element_type=jnp.float32) * factor)
 
 
 def pipelined(blocks, stage):
@@ -192,8 +189,8 @@
     w_refs, refs = refs[: reach + 1], refs[reach + 1 :]
     before, kv_vert, masks, refs = refs[0], refs[1], refs[2], refs[3:]
     out_refs, refs = refs[:pair], refs[pair:]
-    ke, ve, qx, res, good = refs[:5]
-    ps, (kg, vg, sc, pg) = refs[5:7], refs[7:]
+    ke, ve, qx, res, good, acc = refs[:6]
+    ps, (kg, vg, sc, pg) = refs[6:8], refs[8:]
     e = first + pl.program_id(0)
     chip, core = info[0], info[1]
     dev_rows = local * BLK
@@ -225,28 +222,42 @@
             bias = jnp.where((row == i) & hidden(i, j), MASKED, bias)
         ke[HD:, rows] = bias.astype(ke.dtype)
     ve[:, HD:] = jnp.ones((wide, HD), ve.dtype)
+    block_rows = group * BLK
     for i in range(chip_blocks):
         slot, b = divmod(i, local)
+        mark = onehot_rows((BLK, HD), lambda row, i=i: i, qx.dtype)
         for g in range(group):
-            rows = slice(g * BLK, (g + 1) * BLK)
-            qx[i, rows, :HD] = q_refs[slot][b * BLK : (b + 1) * BLK, g * HD : (g + 1) * HD]
-            qx[i, rows, HD:] = onehot_rows((BLK, HD), lambda row, i=i: i, qx.dtype)
+            rows = slice(i * block_rows + g * BLK, i * block_rows + (g + 1) * BLK)
+            qx[rows, :HD] = q_refs[slot][b * BLK : (b + 1) * BLK, g * HD : (g + 1) * HD]
+            qx[rows, HD:] = mark
+
+    def stage(t, at, ahead, behind):
+        last = isinstance(t, int) and t == tiles
+        if behind:
+            rows = slice((t - 1) * step, t * step)
+            if not isinstance(t, int):
+                rows = pl.ds(pl.multiple_of((t - 1) * step, step), step)
+            part = jnp.dot(ps[1 - at][...], ve[rows, :], preferred_element_type=jnp.float32)
+            acc[...] = acc[...] + part
+        else:
+            for i in range(chip_blocks):
+                acc[i * block_rows : (i + 1) * block_rows, :] = before[i]
+        if last:
+            return
+        cols = slice(t * step, (t + 1) * step)
+        if not isinstance(t, int):
+            cols = pl.ds(pl.multiple_of(t * step, step), step)
+        ps[at][...] = exponentials(qx[...], ke[:, cols], factor).astype(ps[at].dtype)
+
+    tiles = wide // step
+    pipelined(tiles, stage)
     good[...] = jnp.ones(good.shape, good.dtype)
-
-    def stage(i, at, ahead, behind):
-        if behind:
-            acc = before[i - 1] + jnp.dot(
-                ps[1 - at][...], ve[...], preferred_element_type=jnp.float32
-            )
-            total = acc[:, HD:]
-            res[i - 1] = (acc[:, :HD] / total).astype(res.dtype)
-            fine = jnp.where((total > SMALLEST) & (total < LARGEST), 1.0, 0.0)
-            good[...] = jnp.minimum(good[...], jnp.min(fine, axis=0, keepdims=True))
-        if isinstance(i, int) and i == chip_blocks:
-            return
-        ps[at][...] = exponentials(qx[i], ke[...], factor).astype(ps[at].dtype)
-
-    pipelined(chip_blocks, stage)
+    for i in range(chip_blocks):
+        rows = slice(i * block_rows, (i + 1) * block_rows)
+        total = acc[rows, HD:]
+        res[i] = (acc[rows, :HD] / total).astype(res.dtype)
+        fine = jnp.where((total > SMALLEST) & (total < LARGEST), 1.0, 0.0)
+        good[...] = jnp.minimum(good[...], jnp.min(fine, axis=0, keepdims=True))
 
     @pl.when(jnp.logical_not(jnp.min(good[...]) > 0.5))
     def _():
@@ -257,8 +268,10 @@
 
         def shifted_block(i, carry):
             here = chip * chip_blocks + within(i)
+            q_rows = pl.ds(pl.multiple_of(i * block_rows, block_rows), block_rows)
             for g in range(group):
-                qx[i, g * BLK : (g + 1) * BLK, HD:] = eye
+                at = pl.ds(pl.multiple_of(i * block_rows + g * BLK, BLK), BLK)
+                qx[at, HD:] = eye
             for j in range(n_slash):
                 off = slash[e, j]
                 pos = reach * chip_blocks + within(i) - off
@@ -279,7 +292,7 @@
                 kg[HD:, rows] = masks[jnp.where(hidden(i, j), 2, 0)]
             top = None
             for t in range(0, kg.shape[1], step):
-                s = jnp.dot(qx[i], kg[:, t : t + step], preferred_element_type=jnp.float32)
+                s = jnp.dot(qx[q_rows, :], kg[:, t : t + step], preferred_element_type=jnp.float32)
                 sc[:, t : t + step] = s
                 for u in range(0, step, HD):
                     piece = s[:, u : u + HD]
@@ -288,8 +301,8 @@
             for t in range(0, kg.shape[1], step):
                 p = jnp.exp2((sc[:, t : t + step] - top) * factor)
                 pg[:, t : t + step] = p.astype(pg.dtype)
-            acc = jnp.dot(pg[...], vg[...], preferred_element_type=jnp.float32)
-            res[i] = (acc[:, :HD] / acc[:, HD:]).astype(res.dtype)
+            sums = jnp.dot(pg[...], vg[...], preferred_element_type=jnp.float32)
+            res[i] = (sums[:, :HD] / sums[:, HD:]).astype(res.dtype)
             return carry
 
         lax.fori_loop(0, chip_blocks, shifted_block, 0)
@@ -379,11 +392,12 @@
                 scratch_shapes=[
                     pltpu.VMEM((2 * HD, width), self.dtype),
                     pltpu.VMEM((width, 2 * HD), self.dtype),
-                    pltpu.VMEM((self.blocks, rows, 2 * HD), self.dtype),
+                    pltpu.VMEM((self.blocks * rows, 2 * HD), self.dtype),
                     pltpu.VMEM((self.blocks, rows, HD), self.dtype),
                     pltpu.VMEM((1, HD), jnp.float32),
-                    pltpu.VMEM((rows, width), self.dtype),
-                    pltpu.VMEM((rows, width), self.dtype),
+                    pltpu.VMEM((self.blocks * rows, 2 * HD), jnp.float32),
+                    pltpu.VMEM((self.blocks * rows, 2 * BLK), self.dtype),
+                    pltpu.VMEM((self.blocks * rows, 2 * BLK), self.dtype),
                     pltpu.VMEM((2 * HD, both), self.dtype),
                     pltpu.VMEM((both, 2 * HD), self.dtype),
                     pltpu.VMEM((rows, both), jnp.float32),

time: 318 us -> 309 us (0.972)
  Pallas kernels: 169 us -> 159 us
    pallas_call x2, Pallas kernels: 126 us -> 118 us  [over_vertical(): pl.pallas_call(functools.partial(vertical_kernel, cfg + (self.plane, self...]
  transfers between devices with their start and end apart: 16 -> 16, of which waited for: 8 -> 8; matrix products, arithmetic and copies ran while one was open for 2% -> 2% of each run, Pallas kernels for 52% -> 50%
where the time goes in v6:
time: 309 us; the launch traced here: 308 us
  Pallas kernels  159 us (51%)
  waiting for transfers between devices  76.9 us (25%)
  starting transfers between devices  35.4 us (11%)
  matrix products  22.9 us (7%)
  local copies, waits for them, and re-layouts  7.69 us (2%)
  other arithmetic  6.28 us (2%)
    pallas_call x2, Pallas kernels, over_vertical(): pl.pallas_call(functools.partial(vertical_kernel, cfg + (self.plane, self...  118 us
    ppermute x12, waiting for transfers between devices, crossed(): return lax.ppermute(value, 'ctx', [(i, i ^ bits) for i in range(size)])  39.8 us
    ppermute x4, waiting for transfers between devices, shifted(): return lax.ppermute(value, 'ctx', [(i, i + by) for i in range(size - by)])  37.1 us
    pallas_call x2, Pallas kernels, over_slash(): pl.pallas_call(functools.partial(slash_kernel, cfg), grid_spec=pltpu.Pref...  35.9 us
    dot_general x1, matrix products, body(): output = jnp.dot(attended, out_weight, preferred_element_type=jnp.float32)  22.9 us
    ppermute x12, starting transfers between devices, crossed(): return lax.ppermute(value, 'ctx', [(i, i ^ bits) for i in range(size)])  18.3 us
    ppermute x4, starting transfers between devices, shifted(): return lax.ppermute(value, 'ctx', [(i, i + by) for i in range(size - by)])  17.1 us
  transfers between devices with their start and end apart: 16, of which 8 were waited for; matrix products, arithmetic and copies ran while one was open for 2% of the time, Pallas kernels for 50%

profile of v6, /device:TPU:25, one launch (start us, length us, event | category | flops | bytes accessed | tf_op | source)
XLA Modules:
  0.0 308.2 jit_solution(4958001156046829729)
XLA Ops:
  0.0 1.3 constant_dynamic-slice_fusion.1
  5.4 4.5 %prepare.1 = (bf16[1024,512]{1,0:T(8,128)(2,1)}, bf16[1024,512]{1,0:T(8,128)(2,1)}, bf16[1024,256]{1,0:T(8,128)(2,1)}, bf16[1024,256]{1,0:T(8,128)(2,1)}, bf16[1...) custom-call(s32[2]{0:T(128)} %pad_add_fusion.info, s32[4,8]{1,0:T(4,128)} %constant_dynamic-slice_fusion.4.vert, ...), custom_call_target="tpu_custom_call" | custom-call | bytes 8388608 | tf_op jit(solution)/shard_map/prepare/pallas_call | solution.py:82
  12.6 1.7 constant_dynamic-slice_fusion
  14.3 9.0 %collective-permute-done.1 = bf16[1024,256]{1,0:T(8,128)(2,1)S(1)} collective-permute-done((bf16[1024,256]{1,0:T(8,128)(2,1)}, bf16[1024,256]{1,0:T(8,128)(2,1)S(1)}, u32[]{:S(2)}, u32[]{:S(2)}) %collective-permute-start.1) | collective-permute-done | bytes 524320 | tf_op jit(solution)/shard_map/ppermute | solution.py:27
  24.3 11.3 %collective-permute-done.3 = bf16[1024,256]{1,0:T(8,128)(2,1)} collective-permute-done((bf16[1024,256]{1,0:T(8,128)(2,1)}, bf16[1024,256]{1,0:T(8,128)(2,1)}, u32[]{:S(2)}, u32[]{:S(2)}) %collective-permute-start.3) | collective-permute-done | bytes 524320 | tf_op jit(solution)/shard_map/ppermute | solution.py:27
  35.6 1.5 add_add_fusion
  37.1 1.5 collective-permute-start.5
  38.6 3.1 %collective-permute-start.6 = (bf16[1024,512]{1,0:T(8,128)(2,1)}, bf16[1024,512]{1,0:T(8,128)(2,1)}, u32[]{:S(2)}, u32[]{:S(2)}) collective-permute-start(bf16[1024,512]{1,0:T(8,128)(2,1)} %get-tuple-element.35.refs_2_), channel_id=1, source_target_pairs={{0,4},{1,5},{2,6},{3,7},{4,8},{5,9},{6,10},{7,11},{8,12},{9,13},{1... | collective-permute-start | bytes 3145736 | tf_op jit(solution)/shard_map/ppermute | solution.py:22
  41.8 1.4 collective-permute-start.4
  43.2 23.3 %collective-permute-done.6.refs_4_ = bf16[1024,512]{1,0:T(8,128)(2,1)} collective-permute-done((bf16[1024,512]{1,0:T(8,128)(2,1)}, bf16[1024,512]{1,0:T(8,128)(2,1)}, u32[]{:S(2)}, u32[]{:S(2)}) %collective-permute-start.6) | collective-permute-done | bytes 1048608 | tf_op jit(solution)/shard_map/ppermute | solution.py:22
  66.5 1.3 broadcast_select_fusion.1
  69.0 1.3 collective-permute-start.8
  71.7 11.2 %collective-permute-start.13 = (bf16[1024,512]{1,0:T(8,128)(2,1)S(1)}, bf16[1024,512]{1,0:T(8,128)(2,1)S(1)}, u32[]{:S(2)}, u32[]{:S(2)}) collective-permute-start(bf16[1024,512]{1,0:T(8,128)(2,1)S(1)} %copy-done.5), channel_id=1, source_target_pairs={{0,4},{1,5},{2,6},{3,7},{4,8},{5,9},{6,10},{7,11},{8,12},{9,13},{1... | collective-permute-start | bytes 3145736 | tf_op jit(solution)/shard_map/ppermute | solution.py:22
  83.0 13.8 %collective-permute-done.8 = bf16[1024,256]{1,0:T(8,128)(2,1)S(1)} collective-permute-done((bf16[1024,256]{1,0:T(8,128)(2,1)S(1)}, bf16[1024,256]{1,0:T(8,128)(2,1)S(1)}, u32[]{:S(2)}, u32[]{:S(2)}) %collective-permute-start.8) | collective-permute-done | bytes 524320 | tf_op jit(solution)/shard_map/ppermute | solution.py:22
  96.9 9.3 %collective-permute-start.10 = (bf16[1024,256]{1,0:T(8,128)(2,1)S(1)}, bf16[1024,256]{1,0:T(8,128)(2,1)S(1)}, u32[]{:S(2)}, u32[]{:S(2)}) collective-permute-start(bf16[1024,256]{1,0:T(8,128)(2,1)S(1)} %add.44), channel_id=1, source_target_pairs={{0,4},{1,5},{2,6},{3,7},{4,0},{5,1},{6,2},{7,3},{8,12},{9,13},{10,... | collective-permute-start | bytes 1572872 | tf_op jit(solution)/shard_map/ppermute | solution.py:27
  107.5 17.8 %attend_slash.2.refs_5_ = f32[2,8,512,256]{3,2,1,0:T(8,128)} custom-call(s32[2]{0:T(128)} %pad_add_fusion.info, s32[4,8]{1,0:T(4,128)} %constant_dynamic-slice_fusion.3.slash, bf16[512,4096]{1,0:T(8,128)(2,1)} %refs_0_.9, bf16[512,2048]{1,0:T(8,128)(2,1)} %collective-permute-done.5.refs_1_, bf16[1024,512]{1,0:T(8,128)(2,1)} %get-tuple-element.35.refs_2_, ...), custom_call_target="tpu_custom_call" | custom-call | flops 8589934592 | bytes 10485760 | tf_op jit(solution)/shard_map/attend_slash/pallas_call | solution.py:358
  125.3 14.7 %collective-permute-done.10 = bf16[1024,256]{1,0:T(8,128)(2,1)S(1)} collective-permute-done((bf16[1024,256]{1,0:T(8,128)(2,1)S(1)}, bf16[1024,256]{1,0:T(8,128)(2,1)S(1)}, u32[]{:S(2)}, u32[]{:S(2)}) %collective-permute-start.10) | collective-permute-done | bytes 524320 | tf_op jit(solution)/shard_map/ppermute | solution.py:27
  141.3 1.3 copy-done.9
  142.6 59.1 %attend_vertical.2 = (bf16[512,1024]{1,0:T(8,128)(2,1)}, bf16[512,1024]{1,0:T(8,128)(2,1)}) custom-call(s32[2]{0:T(128)} %pad_add_fusion.info, s32[4,8]{1,0:T(4,128)} %constant_dynamic-slice_fusion.4.vert, s32[4,8]{1,0:T(4,128)} %constant_dynamic-slice_fusion.3.slash, bf16[512,4096]{1,0:T(8,128)(2,1)} %refs_0_.9, ...), custom_call_target="tpu_custom_call" | custom-call | flops 8589934592 | bytes 10485760 | tf_op jit(solution)/shard_map/attend_vertical/pallas_call | solution.py:384
  203.5 18.1 %attend_slash.3.refs_5_ = f32[2,8,512,256]{3,2,1,0:T(8,128)} custom-call(s32[2]{0:T(128)} %pad_add_fusion.info, s32[4,8]{1,0:T(4,128)} %constant_dynamic-slice_fusion.3.slash, bf16[512,4096]{1,0:T(8,128)(2,1)} %refs_0_.9, bf16[512,2048]{1,0:T(8,128)(2,1)} %collective-permute-done.5.refs_1_, bf16[1024,512]{1,0:T(8,128)(2,1)} %get-tuple-element.44.refs_2_, ...), custom_call_target="tpu_custom_call" | custom-call | flops 8589934592 | bytes 10485760 | tf_op jit(solution)/shard_map/attend_slash/pallas_call | solution.py:358
  221.6 59.3 %attend_vertical.3 = (bf16[512,1024]{1,0:T(8,128)(2,1)}, bf16[512,1024]{1,0:T(8,128)(2,1)}) custom-call(s32[2]{0:T(128)} %pad_add_fusion.info, s32[4,8]{1,0:T(4,128)} %constant_dynamic-slice_fusion.4.vert, s32[4,8]{1,0:T(4,128)} %constant_dynamic-slice_fusion.3.slash, bf16[512,4096]{1,0:T(8,128)(2,1)} %refs_0_.9, ...), custom_call_target="tpu_custom_call" | custom-call | flops 8589934592 | bytes 10485760 | tf_op jit(solution)/shard_map/attend_vertical/pallas_call | solution.py:384
  281.1 2.8 collective-permute-done.15
  283.9 1.4 broadcast_select_fusion.4
  285.3 22.9 %convolution_convert_fusion = bf16[512,4096]{1,0:T(8,128)(2,1)} fusion(bf16[4096,4096]{1,0:T(8,128)(2,1)} %param.11, bf16[512,1024]{1,0:T(8,128)(2,1)S(1)} %get-tuple-element.50, bf16[512,1024]{1,0:T(8,128)(2,1)S(1)} %get-tuple-element.48, bf16[512,1024]{1,0:T(8,128)(2,1)S(1)} %get-tuple-element.49, bf16[512,1024]{1,0:T(8,128)(2,1)S(1)} %get-tuple-element.47), kind=kOutput, calls=%fused_computation | convolution fusion | flops 17198743552 | bytes 41943040 | tf_op jit(solution)/shard_map/dot_general | solution.py:485
  (59 shorter events, 15.0 us)
Async XLA Ops:
  1.4 3.0 collective-permute-start
  9.9 25.7 %copy-start.7 = (bf16[1024,256]{1,0:T(8,128)(2,1)S(1)}, bf16[1024,256]{1,0:T(8,128)(2,1)}, u32[]{:S(2)}) copy-start(bf16[1024,256]{1,0:T(8,128)(2,1)} %get-tuple-element.26) | copy-start | bytes 1572868
  9.9 13.4 %collective-permute-start.1 = (bf16[1024,256]{1,0:T(8,128)(2,1)}, bf16[1024,256]{1,0:T(8,128)(2,1)S(1)}, u32[]{:S(2)}, u32[]{:S(2)}) collective-permute-start(bf16[1024,256]{1,0:T(8,128)(2,1)} %get-tuple-element.27), channel_id=1, source_target_pairs={{0,2},{1,3},{2,0},{3,1},{4,6},{5,7},{6,4},{7,5},{8,10},{9,11},{10,... | collective-permute-start | bytes 1572872 | tf_op jit(solution)/shard_map/ppermute | solution.py:27
  11.1 13.1 %collective-permute-start.2 = (bf16[1024,256]{1,0:T(8,128)(2,1)}, bf16[1024,256]{1,0:T(8,128)(2,1)}, u32[]{:S(2)}, u32[]{:S(2)}) collective-permute-start(bf16[1024,256]{1,0:T(8,128)(2,1)} %get-tuple-element.28), channel_id=1, source_target_pairs={{0,4},{1,5},{2,6},{3,7},{4,0},{5,1},{6,2},{7,3},{8,12},{9,13},{10,... | collective-permute-start | bytes 1572872 | tf_op jit(solution)/shard_map/ppermute | solution.py:27
  12.4 23.2 %collective-permute-start.3 = (bf16[1024,256]{1,0:T(8,128)(2,1)}, bf16[1024,256]{1,0:T(8,128)(2,1)}, u32[]{:S(2)}, u32[]{:S(2)}) collective-permute-start(bf16[1024,256]{1,0:T(8,128)(2,1)} %get-tuple-element.29), channel_id=1, source_target_pairs={{0,6},{1,7},{2,4},{3,5},{4,2},{5,3},{6,0},{7,1},{8,14},{9,15},{10,... | collective-permute-start | bytes 1572872 | tf_op jit(solution)/shard_map/ppermute | solution.py:27
  14.3 56.1 %copy-start.10 = (s32[8,8]{1,0:T(8,128)S(1)}, s32[8,8]{1,0:T(8,128)}, u32[]{:S(2)}) copy-start(s32[8,8]{1,0:T(8,128)} %param.10) | copy-start | bytes 772
  23.4 12.2 %copy-start.8 = (bf16[1024,256]{1,0:T(8,128)(2,1)}, bf16[1024,256]{1,0:T(8,128)(2,1)S(1)}, u32[]{:S(2)}) copy-start(bf16[1024,256]{1,0:T(8,128)(2,1)S(1)} %collective-permute-done.1) | copy-start | bytes 1572868
  37.1 31.9 %collective-permute-start.5 = (bf16[512,2048]{1,0:T(8,128)(2,1)S(1)}, bf16[512,2048]{1,0:T(8,128)(2,1)}, u32[]{:S(2)}, u32[]{:S(2)}) collective-permute-start(bf16[512,2048]{1,0:T(8,128)(2,1)S(1)} %constant_dynamic-slice_fusion), channel_id=1, source_target_pairs={{0,1},{1,0},{2,3},{3,2},{4,5},{5,4},{6,7},{7,6},{8,9},{9,8},{10,11... | collective-permute-start | bytes 6291464 | tf_op jit(solution)/shard_map/ppermute | solution.py:27
  38.6 27.9 %collective-permute-start.6 = (bf16[1024,512]{1,0:T(8,128)(2,1)}, bf16[1024,512]{1,0:T(8,128)(2,1)}, u32[]{:S(2)}, u32[]{:S(2)}) collective-permute-start(bf16[1024,512]{1,0:T(8,128)(2,1)} %get-tuple-element.35.refs_2_), channel_id=1, source_target_pairs={{0,4},{1,5},{2,6},{3,7},{4,8},{5,9},{6,10},{7,11},{8,12},{9,13},{1... | collective-permute-start | bytes 3145736 | tf_op jit(solution)/shard_map/ppermute | solution.py:22
  41.8 29.9 %copy-start.5 = (bf16[1024,512]{1,0:T(8,128)(2,1)S(1)}, bf16[1024,512]{1,0:T(8,128)(2,1)}, u32[]{:S(2)}) copy-start(bf16[1024,512]{1,0:T(8,128)(2,1)} %get-tuple-element.44.refs_2_) | copy-start | bytes 3145732
  41.8 27.0 %collective-permute-start.4 = (bf16[1024,256]{1,0:T(8,128)(2,1)S(1)}, bf16[1024,256]{1,0:T(8,128)(2,1)S(1)}, u32[]{:S(2)}, u32[]{:S(2)}) collective-permute-start(bf16[1024,256]{1,0:T(8,128)(2,1)S(1)} %add_add_fusion), channel_id=1, source_target_pairs={{0,8},{1,9},{2,10},{3,11},{4,12},{5,13},{6,14},{7,15},{8,16},{9,17... | collective-permute-start | bytes 1572872 | tf_op jit(solution)/shard_map/ppermute | solution.py:22
  67.8 39.6 %collective-permute-start.7 = (bf16[1024,512]{1,0:T(8,128)(2,1)S(1)}, bf16[1024,512]{1,0:T(8,128)(2,1)}, u32[]{:S(2)}, u32[]{:S(2)}) collective-permute-start(bf16[1024,512]{1,0:T(8,128)(2,1)S(1)} %broadcast_select_fusion.1), channel_id=1, source_target_pairs={{0,2},{1,3},{2,0},{3,1},{4,6},{5,7},{6,4},{7,5},{8,10},{9,11},{10,... | collective-permute-start | bytes 3145736 | tf_op jit(solution)/shard_map/ppermute | solution.py:27
  69.0 27.8 %collective-permute-start.8 = (bf16[1024,256]{1,0:T(8,128)(2,1)S(1)}, bf16[1024,256]{1,0:T(8,128)(2,1)S(1)}, u32[]{:S(2)}, u32[]{:S(2)}) collective-permute-start(bf16[1024,256]{1,0:T(8,128)(2,1)S(1)} %add.42), channel_id=1, source_target_pairs={{0,16},{1,17},{2,18},{3,19},{4,20},{5,21},{6,22},{7,23},{8,24},{9,... | collective-permute-start | bytes 1572872 | tf_op jit(solution)/shard_map/ppermute | solution.py:22
  71.7 68.3 %collective-permute-start.13 = (bf16[1024,512]{1,0:T(8,128)(2,1)S(1)}, bf16[1024,512]{1,0:T(8,128)(2,1)S(1)}, u32[]{:S(2)}, u32[]{:S(2)}) collective-permute-start(bf16[1024,512]{1,0:T(8,128)(2,1)S(1)} %copy-done.5), channel_id=1, source_target_pairs={{0,4},{1,5},{2,6},{3,7},{4,8},{5,9},{6,10},{7,11},{8,12},{9,13},{1... | collective-permute-start | bytes 3145736 | tf_op jit(solution)/shard_map/ppermute | solution.py:22
  96.9 43.0 %collective-permute-start.10 = (bf16[1024,256]{1,0:T(8,128)(2,1)S(1)}, bf16[1024,256]{1,0:T(8,128)(2,1)S(1)}, u32[]{:S(2)}, u32[]{:S(2)}) collective-permute-start(bf16[1024,256]{1,0:T(8,128)(2,1)S(1)} %add.44), channel_id=1, source_target_pairs={{0,4},{1,5},{2,6},{3,7},{4,0},{5,1},{6,2},{7,3},{8,12},{9,13},{10,... | collective-permute-start | bytes 1572872 | tf_op jit(solution)/shard_map/ppermute | solution.py:27
  106.2 33.8 %collective-permute-start.11 = (bf16[1024,256]{1,0:T(8,128)(2,1)S(1)}, bf16[1024,256]{1,0:T(8,128)(2,1)S(1)}, u32[]{:S(2)}, u32[]{:S(2)}) collective-permute-start(bf16[1024,256]{1,0:T(8,128)(2,1)S(1)} %add.44), channel_id=1, source_target_pairs={{0,6},{1,7},{2,4},{3,5},{4,2},{5,3},{6,0},{7,1},{8,14},{9,15},{10,... | collective-permute-start | bytes 1572872 | tf_op jit(solution)/shard_map/ppermute | solution.py:27
  106.9 33.0 %collective-permute-start.9 = (bf16[1024,256]{1,0:T(8,128)(2,1)S(1)}, bf16[1024,256]{1,0:T(8,128)(2,1)S(1)}, u32[]{:S(2)}, u32[]{:S(2)}) collective-permute-start(bf16[1024,256]{1,0:T(8,128)(2,1)S(1)} %add.44), channel_id=1, source_target_pairs={{0,2},{1,3},{2,0},{3,1},{4,6},{5,7},{6,4},{7,5},{8,10},{9,11},{10,... | collective-permute-start | bytes 1572872 | tf_op jit(solution)/shard_map/ppermute | solution.py:27
  140.1 61.6 %copy-start.6 = (bf16[1024,512]{1,0:T(8,128)(2,1)}, bf16[1024,512]{1,0:T(8,128)(2,1)S(1)}, u32[]{:S(2)}) copy-start(bf16[1024,512]{1,0:T(8,128)(2,1)S(1)} %collective-permute-done.13.refs_4_) | copy-start | bytes 3145732
  140.2 62.3 %collective-permute-start.14 = (bf16[1024,512]{1,0:T(8,128)(2,1)S(1)}, bf16[1024,512]{1,0:T(8,128)(2,1)S(1)}, u32[]{:S(2)}, u32[]{:S(2)}) collective-permute-start(bf16[1024,512]{1,0:T(8,128)(2,1)S(1)} %broadcast_select_fusion), channel_id=1, source_target_pairs={{0,2},{1,3},{2,0},{3,1},{4,6},{5,7},{6,4},{7,5},{8,10},{9,11},{10,... | collective-permute-start | bytes 3145736 | tf_op jit(solution)/shard_map/ppermute | solution.py:27
  201.7 79.2 %collective-permute-start.12 = (bf16[512,1024]{1,0:T(8,128)(2,1)}, bf16[512,1024]{1,0:T(8,128)(2,1)S(1)}, u32[]{:S(2)}, u32[]{:S(2)}) collective-permute-start(bf16[512,1024]{1,0:T(8,128)(2,1)} %get-tuple-element.43), channel_id=1, source_target_pairs={{0,1},{1,0},{2,3},{3,2},{4,5},{5,4},{6,7},{7,6},{8,9},{9,8},{10,11... | collective-permute-start | bytes 3145736 | tf_op jit(solution)/shard_map/ppermute | solution.py:27
  221.6 59.4 %copy-start.3 = (bf16[512,1024]{1,0:T(8,128)(2,1)S(1)}, bf16[512,1024]{1,0:T(8,128)(2,1)}, u32[]{:S(2)}) copy-start(bf16[512,1024]{1,0:T(8,128)(2,1)} %get-tuple-element.42) | copy-start | bytes 3145732
  280.8 3.1 copy-start.4
  280.8 3.1 collective-permute-start.15
  285.3 22.9 %copy-start.1 = (s32[8,8]{1,0:T(8,128)S(1)}, s32[8,8]{1,0:T(8,128)}, u32[]{:S(2)}) copy-start(s32[8,8]{1,0:T(8,128)} %param.9) | copy-start | bytes 772
  (4 other events, 6.1 us)

commit v7 on v6

--- a/solution.py
+++ b/solution.py
@@ -445,14 +445,16 @@
     total = listed[0]
     for k in range(1, plane):
         total = total + crossed(listed[k], k * pair)
-    q_sent = part(queries, 1, 1 - core) if pair == 2 else None
-    total, own[0], q_sent = lax.optimization_barrier((total, own[0], q_sent))
-    q_other = crossed(q_sent, 1) if pair == 2 else None
+    two_back = [None] * len(own)
+    passes_on = pair == 2 and reach == 2 and chips % 2 == 0
+    if passes_on:
+        two_back[0] = shifted(own[0], 2 * pair)
+        two_back[0], own[1:], total = lax.optimization_barrier((two_back[0], own[1:], total))
+        two_back[1:] = [shifted(w, 2 * pair) for w in own[1:]]
+    q_other = crossed(part(queries, 1, 1 - core), 1) if pair == 2 else None
     step = 1
     while step < chips // plane:
         total = total + shifted(total, step * plane * pair)
-        if step == 1:
-            total, q_other, own[1:] = lax.optimization_barrier((total, q_other, own[1:]))
         step *= 2
 
     attention = Attention(queries, q_other, info, vert, slash, masks, heads, local, plane)
@@ -460,16 +462,15 @@
     all_windows, sums = [], []
     for c in range(chunks):
         windows = [own[c]]
-        if pair == 2 and reach == 2 and chips % 2 == 0:
-            two_back = shifted(own[c], 2 * pair)
-            passed = jnp.where(chip % 2 == 0, own[c], two_back)
-            windows += [crossed(passed, pair), two_back]
+        if passes_on:
+            passed = jnp.where(chip % 2 == 0, own[c], two_back[c])
+            windows += [crossed(passed, pair), two_back[c]]
         else:
             windows += [shifted(own[c], pair * d) for d in range(1, reach + 1)]
         all_windows.append(windows)
         sums.append(attention.over_slash(c * per_chunk, per_chunk, windows))
     gathered = [total] + [crossed(total, k * pair) for k in range(1, plane)]
-    gathered, sums[0] = lax.optimization_barrier((gathered, sums[0]))
+    gathered, sums = lax.optimization_barrier((gathered, sums))
     kv_vert = jnp.concatenate(gathered, 0)
     near, far = [], []
     for c in range(chunks):

time: 309 us -> 302 us (0.977)
  starting transfers between devices: 35.4 us -> 25.3 us
    ppermute x12, waiting for transfers between devices: 39.8 us -> 50.8 us  [crossed(): return lax.ppermute(value, 'ctx', [(i, i ^ bits) for i in range(size)])]
    ppermute x4, starting transfers between devices: 17.1 us -> 7.77 us  [shifted(): return lax.ppermute(value, 'ctx', [(i, i + by) for i in range(size - by)])]
    ppermute x4, waiting for transfers between devices: 37.1 us -> 29 us  [shifted(): return lax.ppermute(value, 'ctx', [(i, i + by) for i in range(size - by)])]
  transfers between devices with their start and end apart: 16 -> 16, of which waited for: 8 -> 7; matrix products, arithmetic and copies ran while one was open for 2% -> 3% of each run, Pallas kernels for 50% -> 31%
where the time goes in v7:
time: 302 us
  Pallas kernels  159 us (53%)
  waiting for transfers between devices  79.8 us (26%)
  starting transfers between devices  25.3 us (8%)
  matrix products  22.6 us (7%)
  local copies, waits for them, and re-layouts  7.73 us (3%)
  other arithmetic  7.47 us (2%)
    pallas_call x2, Pallas kernels, over_vertical(): pl.pallas_call(functools.partial(vertical_kernel, cfg + (self.plane, self...  119 us
    ppermute x12, waiting for transfers between devices, crossed(): return lax.ppermute(value, 'ctx', [(i, i ^ bits) for i in range(size)])  50.8 us
    pallas_call x2, Pallas kernels, over_slash(): pl.pallas_call(functools.partial(slash_kernel, cfg), grid_spec=pltpu.Pref...  35.6 us
    ppermute x4, waiting for transfers between devices, shifted(): return lax.ppermute(value, 'ctx', [(i, i + by) for i in range(size - by)])  29 us
    dot_general x1, matrix products, body(): output = jnp.dot(attended, out_weight, preferred_element_type=jnp.float32)  22.6 us
    ppermute x12, starting transfers between devices, crossed(): return lax.ppermute(value, 'ctx', [(i, i ^ bits) for i in range(size)])  17.5 us
    ppermute x4, starting transfers between devices, shifted(): return lax.ppermute(value, 'ctx', [(i, i + by) for i in range(size - by)])  7.77 us
  transfers between devices with their start and end apart: 16, of which 7 were waited for; matrix products, arithmetic and copies ran while one was open for 3% of the time, Pallas kernels for 31%

profile of v7, /device:TPU:25, one launch (start us, length us, event | category | flops | bytes accessed | tf_op | source)
XLA Modules:
  0.0 301.8 jit_solution(12249534670948428516)
XLA Ops:
  5.4 4.5 %prepare.1 = (bf16[1024,512]{1,0:T(8,128)(2,1)}, bf16[1024,512]{1,0:T(8,128)(2,1)}, bf16[1024,256]{1,0:T(8,128)(2,1)}, bf16[1024,256]{1,0:T(8,128)(2,1)}, bf16[1...) custom-call(s32[2]{0:T(128)} %pad_add_fusion.info, s32[4,8]{1,0:T(4,128)} %constant_dynamic-slice_fusion.4.vert, ...), custom_call_target="tpu_custom_call" | custom-call | bytes 8388608 | tf_op jit(solution)/shard_map/prepare/pallas_call | solution.py:82
  9.9 3.3 %collective-permute-start.2 = (bf16[1024,512]{1,0:T(8,128)(2,1)}, bf16[1024,512]{1,0:T(8,128)(2,1)}, u32[]{:S(2)}, u32[]{:S(2)}) collective-permute-start(bf16[1024,512]{1,0:T(8,128)(2,1)} %get-tuple-element.24.refs_2_), channel_id=1, source_target_pairs={{0,4},{1,5},{2,6},{3,7},{4,8},{5,9},{6,10},{7,11},{8,12},{9,13},{1... | collective-permute-start | bytes 3145736 | tf_op jit(solution)/shard_map/ppermute | solution.py:22
  14.4 1.4 collective-permute-start.5
  15.9 1.7 constant_dynamic-slice_fusion.2
  17.6 1.6 collective-permute-start
  19.2 7.2 %collective-permute-done.3 = bf16[1024,256]{1,0:T(8,128)(2,1)S(1)} collective-permute-done((bf16[1024,256]{1,0:T(8,128)(2,1)}, bf16[1024,256]{1,0:T(8,128)(2,1)S(1)}, u32[]{:S(2)}, u32[]{:S(2)}) %collective-permute-start.3) | collective-permute-done | bytes 524320 | tf_op jit(solution)/shard_map/ppermute | solution.py:27
  26.3 34.3 %collective-permute-done.4 = bf16[1024,256]{1,0:T(8,128)(2,1)} collective-permute-done((bf16[1024,256]{1,0:T(8,128)(2,1)}, bf16[1024,256]{1,0:T(8,128)(2,1)}, u32[]{:S(2)}, u32[]{:S(2)}) %collective-permute-start.4) | collective-permute-done | bytes 524320 | tf_op jit(solution)/shard_map/ppermute | solution.py:27
  60.7 1.5 add_add_fusion
  62.2 1.9 collective-permute-start.12
  64.2 1.3 broadcast_select_fusion.1
  68.1 21.5 %collective-permute-done.12.refs_4_ = bf16[1024,512]{1,0:T(8,128)(2,1)} collective-permute-done((bf16[1024,512]{1,0:T(8,128)(2,1)}, bf16[1024,512]{1,0:T(8,128)(2,1)}, u32[]{:S(2)}, u32[]{:S(2)}) %collective-permute-start.12) | collective-permute-done | bytes 1048608 | tf_op jit(solution)/shard_map/ppermute | solution.py:22
  89.6 1.3 broadcast_select_fusion
  93.7 1.3 collective-permute-start.8
  96.1 17.8 %attend_slash.2.refs_5_ = f32[2,8,512,256]{3,2,1,0:T(8,128)} custom-call(s32[2]{0:T(128)} %pad_add_fusion.info, s32[4,8]{1,0:T(4,128)} %constant_dynamic-slice_fusion.3.slash, bf16[512,4096]{1,0:T(8,128)(2,1)} %refs_0_.9, bf16[512,2048]{1,0:T(8,128)(2,1)} %collective-permute-done.refs_1_, bf16[1024,512]{1,0:T(8,128)(2,1)} %get-tuple-element.24.refs_2_, ...), custom_call_target="tpu_custom_call" | custom-call | flops 8589934592 | bytes 10485760 | tf_op jit(solution)/shard_map/attend_slash/pallas_call | solution.py:358
  113.9 7.5 %collective-permute-done.8 = bf16[1024,256]{1,0:T(8,128)(2,1)S(1)} collective-permute-done((bf16[1024,256]{1,0:T(8,128)(2,1)S(1)}, bf16[1024,256]{1,0:T(8,128)(2,1)S(1)}, u32[]{:S(2)}, u32[]{:S(2)}) %collective-permute-start.8) | collective-permute-done | bytes 524320 | tf_op jit(solution)/shard_map/ppermute | solution.py:22
  121.6 8.5 %collective-permute-start.11 = (bf16[1024,256]{1,0:T(8,128)(2,1)S(1)}, bf16[1024,256]{1,0:T(8,128)(2,1)S(1)}, u32[]{:S(2)}, u32[]{:S(2)}) collective-permute-start(bf16[1024,256]{1,0:T(8,128)(2,1)S(1)} %add.44), channel_id=1, source_target_pairs={{0,6},{1,7},{2,4},{3,5},{4,2},{5,3},{6,0},{7,1},{8,14},{9,15},{10,... | collective-permute-start | bytes 1572872 | tf_op jit(solution)/shard_map/ppermute | solution.py:27
  130.5 17.8 %attend_slash.3.refs_5_ = f32[2,8,512,256]{3,2,1,0:T(8,128)} custom-call(s32[2]{0:T(128)} %pad_add_fusion.info, s32[4,8]{1,0:T(4,128)} %constant_dynamic-slice_fusion.3.slash, bf16[512,4096]{1,0:T(8,128)(2,1)} %refs_0_.9, bf16[512,2048]{1,0:T(8,128)(2,1)} %collective-permute-done.refs_1_, bf16[1024,512]{1,0:T(8,128)(2,1)} %get-tuple-element.32.refs_2_, ...), custom_call_target="tpu_custom_call" | custom-call | flops 8589934592 | bytes 10485760 | tf_op jit(solution)/shard_map/attend_slash/pallas_call | solution.py:358
  148.3 5.5 %collective-permute-done.10 = bf16[1024,256]{1,0:T(8,128)(2,1)S(1)} collective-permute-done((bf16[1024,256]{1,0:T(8,128)(2,1)S(1)}, bf16[1024,256]{1,0:T(8,128)(2,1)S(1)}, u32[]{:S(2)}, u32[]{:S(2)}) %collective-permute-start.10) | collective-permute-done | bytes 524320 | tf_op jit(solution)/shard_map/ppermute | solution.py:27
  153.9 1.3 copy-done.7
  155.3 59.3 %attend_vertical.3 = (bf16[512,1024]{1,0:T(8,128)(2,1)}, bf16[512,1024]{1,0:T(8,128)(2,1)}) custom-call(s32[2]{0:T(128)} %pad_add_fusion.info, s32[4,8]{1,0:T(4,128)} %constant_dynamic-slice_fusion.4.vert, s32[4,8]{1,0:T(4,128)} %constant_dynamic-slice_fusion.3.slash, bf16[512,4096]{1,0:T(8,128)(2,1)} %refs_0_.9, ...), custom_call_target="tpu_custom_call" | custom-call | flops 8589934592 | bytes 10485760 | tf_op jit(solution)/shard_map/attend_vertical/pallas_call | solution.py:384
  215.4 59.3 %attend_vertical.2 = (bf16[512,1024]{1,0:T(8,128)(2,1)}, bf16[512,1024]{1,0:T(8,128)(2,1)}) custom-call(s32[2]{0:T(128)} %pad_add_fusion.info, s32[4,8]{1,0:T(4,128)} %constant_dynamic-slice_fusion.4.vert, s32[4,8]{1,0:T(4,128)} %constant_dynamic-slice_fusion.3.slash, bf16[512,4096]{1,0:T(8,128)(2,1)} %refs_0_.9, ...), custom_call_target="tpu_custom_call" | custom-call | flops 8589934592 | bytes 10485760 | tf_op jit(solution)/shard_map/attend_vertical/pallas_call | solution.py:384
  275.1 2.7 collective-permute-done.14
  277.8 1.4 broadcast_select_fusion.5
  279.2 22.6 %convolution_convert_fusion = bf16[512,4096]{1,0:T(8,128)(2,1)} fusion(bf16[4096,4096]{1,0:T(8,128)(2,1)} %param.11, bf16[512,1024]{1,0:T(8,128)(2,1)S(1)} %get-tuple-element.46, bf16[512,1024]{1,0:T(8,128)(2,1)S(1)} %get-tuple-element.44, bf16[512,1024]{1,0:T(8,128)(2,1)S(1)} %get-tuple-element.45, bf16[512,1024]{1,0:T(8,128)(2,1)S(1)} %get-tuple-element.43), kind=kOutput, calls=%fused_computation | convolution fusion | flops 17198743552 | bytes 41943040 | tf_op jit(solution)/shard_map/dot_general | solution.py:486
  (55 shorter events, 15.0 us)
Async XLA Ops:
  0.0 2.8 copy-start
  1.4 3.0 %collective-permute-start.1 = (bf16[512,1024]{1,0:T(8,128)(2,1)S(1)}, bf16[512,1024]{1,0:T(8,128)(2,1)S(1)}, u32[]{:S(2)}, u32[]{:S(2)}) collective-permute-start(bf16[512,1024]{1,0:T(8,128)(2,1)S(1)} %pad_maximum_fusion), channel_id=1, source_target_pairs={{0,1},{1,0},{2,3},{3,2},{4,5},{5,4},{6,7},{7,6},{8,9},{9,8},{10,11... | collective-permute-start | bytes 3145736 | tf_op jit(solution)/shard_map/ppermute | solution.py:27
  9.9 50.8 %copy-start.5 = (bf16[1024,256]{1,0:T(8,128)(2,1)S(1)}, bf16[1024,256]{1,0:T(8,128)(2,1)}, u32[]{:S(2)}) copy-start(bf16[1024,256]{1,0:T(8,128)(2,1)} %get-tuple-element.26) | copy-start | bytes 1572868
  9.9 52.3 %collective-permute-start.2 = (bf16[1024,512]{1,0:T(8,128)(2,1)}, bf16[1024,512]{1,0:T(8,128)(2,1)}, u32[]{:S(2)}, u32[]{:S(2)}) collective-permute-start(bf16[1024,512]{1,0:T(8,128)(2,1)} %get-tuple-element.24.refs_2_), channel_id=1, source_target_pairs={{0,4},{1,5},{2,6},{3,7},{4,8},{5,9},{6,10},{7,11},{8,12},{9,13},{1... | collective-permute-start | bytes 3145736 | tf_op jit(solution)/shard_map/ppermute | solution.py:22
  13.2 13.2 %collective-permute-start.3 = (bf16[1024,256]{1,0:T(8,128)(2,1)}, bf16[1024,256]{1,0:T(8,128)(2,1)S(1)}, u32[]{:S(2)}, u32[]{:S(2)}) collective-permute-start(bf16[1024,256]{1,0:T(8,128)(2,1)} %get-tuple-element.27), channel_id=1, source_target_pairs={{0,2},{1,3},{2,0},{3,1},{4,6},{5,7},{6,4},{7,5},{8,10},{9,11},{10,... | collective-permute-start | bytes 1572872 | tf_op jit(solution)/shard_map/ppermute | solution.py:27
  14.4 46.2 %collective-permute-start.4 = (bf16[1024,256]{1,0:T(8,128)(2,1)}, bf16[1024,256]{1,0:T(8,128)(2,1)}, u32[]{:S(2)}, u32[]{:S(2)}) collective-permute-start(bf16[1024,256]{1,0:T(8,128)(2,1)} %get-tuple-element.28), channel_id=1, source_target_pairs={{0,4},{1,5},{2,6},{3,7},{4,0},{5,1},{6,2},{7,3},{8,12},{9,13},{10,... | collective-permute-start | bytes 1572872 | tf_op jit(solution)/shard_map/ppermute | solution.py:27
  14.4 46.2 %collective-permute-start.5 = (bf16[1024,256]{1,0:T(8,128)(2,1)}, bf16[1024,256]{1,0:T(8,128)(2,1)}, u32[]{:S(2)}, u32[]{:S(2)}) collective-permute-start(bf16[1024,256]{1,0:T(8,128)(2,1)} %get-tuple-element.29), channel_id=1, source_target_pairs={{0,6},{1,7},{2,4},{3,5},{4,2},{5,3},{6,0},{7,1},{8,14},{9,15},{10,... | collective-permute-start | bytes 1572872 | tf_op jit(solution)/shard_map/ppermute | solution.py:27
  17.6 77.4 %collective-permute-start = (bf16[512,2048]{1,0:T(8,128)(2,1)S(1)}, bf16[512,2048]{1,0:T(8,128)(2,1)}, u32[]{:S(2)}, u32[]{:S(2)}) collective-permute-start(bf16[512,2048]{1,0:T(8,128)(2,1)S(1)} %constant_dynamic-slice_fusion.2), channel_id=1, source_target_pairs={{0,1},{1,0},{2,3},{3,2},{4,5},{5,4},{6,7},{7,6},{8,9},{9,8},{10,11... | collective-permute-start | bytes 6291464 | tf_op jit(solution)/shard_map/ppermute | solution.py:27
  26.3 34.3 %copy-start.6 = (bf16[1024,256]{1,0:T(8,128)(2,1)}, bf16[1024,256]{1,0:T(8,128)(2,1)S(1)}, u32[]{:S(2)}) copy-start(bf16[1024,256]{1,0:T(8,128)(2,1)S(1)} %collective-permute-done.3) | copy-start | bytes 1572868
  60.7 31.5 %copy-start.8 = (s32[8,8]{1,0:T(8,128)S(1)}, s32[8,8]{1,0:T(8,128)}, u32[]{:S(2)}) copy-start(s32[8,8]{1,0:T(8,128)} %param.10) | copy-start | bytes 772
  62.2 27.3 %collective-permute-start.12 = (bf16[1024,512]{1,0:T(8,128)(2,1)}, bf16[1024,512]{1,0:T(8,128)(2,1)}, u32[]{:S(2)}, u32[]{:S(2)}) collective-permute-start(bf16[1024,512]{1,0:T(8,128)(2,1)} %get-tuple-element.32.refs_2_), channel_id=1, source_target_pairs={{0,4},{1,5},{2,6},{3,7},{4,8},{5,9},{6,10},{7,11},{8,12},{9,13},{1... | collective-permute-start | bytes 3145736 | tf_op jit(solution)/shard_map/ppermute | solution.py:22
  65.5 29.5 %collective-permute-start.6 = (bf16[1024,512]{1,0:T(8,128)(2,1)S(1)}, bf16[1024,512]{1,0:T(8,128)(2,1)S(1)}, u32[]{:S(2)}, u32[]{:S(2)}) collective-permute-start(bf16[1024,512]{1,0:T(8,128)(2,1)S(1)} %broadcast_select_fusion.1), channel_id=1, source_target_pairs={{0,2},{1,3},{2,0},{3,1},{4,6},{5,7},{6,4},{7,5},{8,10},{9,11},{10,... | collective-permute-start | bytes 3145736 | tf_op jit(solution)/shard_map/ppermute | solution.py:27
  66.8 26.7 %collective-permute-start.7 = (bf16[1024,256]{1,0:T(8,128)(2,1)S(1)}, bf16[1024,256]{1,0:T(8,128)(2,1)S(1)}, u32[]{:S(2)}, u32[]{:S(2)}) collective-permute-start(bf16[1024,256]{1,0:T(8,128)(2,1)S(1)} %add_add_fusion), channel_id=1, source_target_pairs={{0,8},{1,9},{2,10},{3,11},{4,12},{5,13},{6,14},{7,15},{8,16},{9,17... | collective-permute-start | bytes 1572872 | tf_op jit(solution)/shard_map/ppermute | solution.py:22
  90.9 39.6 %collective-permute-start.13 = (bf16[1024,512]{1,0:T(8,128)(2,1)S(1)}, bf16[1024,512]{1,0:T(8,128)(2,1)}, u32[]{:S(2)}, u32[]{:S(2)}) collective-permute-start(bf16[1024,512]{1,0:T(8,128)(2,1)S(1)} %broadcast_select_fusion), channel_id=1, source_target_pairs={{0,2},{1,3},{2,0},{3,1},{4,6},{5,7},{6,4},{7,5},{8,10},{9,11},{10,... | collective-permute-start | bytes 3145736 | tf_op jit(solution)/shard_map/ppermute | solution.py:27
  93.7 27.8 %collective-permute-start.8 = (bf16[1024,256]{1,0:T(8,128)(2,1)S(1)}, bf16[1024,256]{1,0:T(8,128)(2,1)S(1)}, u32[]{:S(2)}, u32[]{:S(2)}) collective-permute-start(bf16[1024,256]{1,0:T(8,128)(2,1)S(1)} %add.43), channel_id=1, source_target_pairs={{0,16},{1,17},{2,18},{3,19},{4,20},{5,21},{6,22},{7,23},{8,24},{9,... | collective-permute-start | bytes 1572872 | tf_op jit(solution)/shard_map/ppermute | solution.py:22
  121.6 26.7 %collective-permute-start.11 = (bf16[1024,256]{1,0:T(8,128)(2,1)S(1)}, bf16[1024,256]{1,0:T(8,128)(2,1)S(1)}, u32[]{:S(2)}, u32[]{:S(2)}) collective-permute-start(bf16[1024,256]{1,0:T(8,128)(2,1)S(1)} %add.44), channel_id=1, source_target_pairs={{0,6},{1,7},{2,4},{3,5},{4,2},{5,3},{6,0},{7,1},{8,14},{9,15},{10,... | collective-permute-start | bytes 1572872 | tf_op jit(solution)/shard_map/ppermute | solution.py:27
  130.1 23.6 %collective-permute-start.10 = (bf16[1024,256]{1,0:T(8,128)(2,1)S(1)}, bf16[1024,256]{1,0:T(8,128)(2,1)S(1)}, u32[]{:S(2)}, u32[]{:S(2)}) collective-permute-start(bf16[1024,256]{1,0:T(8,128)(2,1)S(1)} %add.44), channel_id=1, source_target_pairs={{0,4},{1,5},{2,6},{3,7},{4,0},{5,1},{6,2},{7,3},{8,12},{9,13},{10,... | collective-permute-start | bytes 1572872 | tf_op jit(solution)/shard_map/ppermute | solution.py:27
  130.1 23.6 %collective-permute-start.9 = (bf16[1024,256]{1,0:T(8,128)(2,1)S(1)}, bf16[1024,256]{1,0:T(8,128)(2,1)S(1)}, u32[]{:S(2)}, u32[]{:S(2)}) collective-permute-start(bf16[1024,256]{1,0:T(8,128)(2,1)S(1)} %add.44), channel_id=1, source_target_pairs={{0,2},{1,3},{2,0},{3,1},{4,6},{5,7},{6,4},{7,5},{8,10},{9,11},{10,... | collective-permute-start | bytes 1572872 | tf_op jit(solution)/shard_map/ppermute | solution.py:27
  153.9 1.3 copy-start.7
  214.5 60.4 %copy-start.3 = (bf16[512,1024]{1,0:T(8,128)(2,1)S(1)}, bf16[512,1024]{1,0:T(8,128)(2,1)}, u32[]{:S(2)}) copy-start(bf16[512,1024]{1,0:T(8,128)(2,1)} %get-tuple-element.41) | copy-start | bytes 3145732
  214.5 60.4 %collective-permute-start.15 = (bf16[512,1024]{1,0:T(8,128)(2,1)}, bf16[512,1024]{1,0:T(8,128)(2,1)S(1)}, u32[]{:S(2)}, u32[]{:S(2)}) collective-permute-start(bf16[512,1024]{1,0:T(8,128)(2,1)} %get-tuple-element.42), channel_id=1, source_target_pairs={{0,1},{1,0},{2,3},{3,2},{4,5},{5,4},{6,7},{7,6},{8,9},{9,8},{10,11... | collective-permute-start | bytes 3145736 | tf_op jit(solution)/shard_map/ppermute | solution.py:27
  274.7 3.1 %copy-start.4 = (bf16[512,1024]{1,0:T(8,128)(2,1)S(1)}, bf16[512,1024]{1,0:T(8,128)(2,1)}, u32[]{:S(2)}) copy-start(bf16[512,1024]{1,0:T(8,128)(2,1)} %get-tuple-element.38) | copy-start | bytes 3145732
  274.7 3.1 %collective-permute-start.14 = (bf16[512,1024]{1,0:T(8,128)(2,1)}, bf16[512,1024]{1,0:T(8,128)(2,1)}, u32[]{:S(2)}, u32[]{:S(2)}) collective-permute-start(bf16[512,1024]{1,0:T(8,128)(2,1)} %get-tuple-element.39), channel_id=1, source_target_pairs={{0,1},{1,0},{2,3},{3,2},{4,5},{5,4},{6,7},{7,6},{8,9},{9,8},{10,11... | collective-permute-start | bytes 3145736 | tf_op jit(solution)/shard_map/ppermute | solution.py:27
  279.2 22.6 %copy-start.1 = (s32[8,8]{1,0:T(8,128)S(1)}, s32[8,8]{1,0:T(8,128)}, u32[]{:S(2)}) copy-start(s32[8,8]{1,0:T(8,128)} %param.9) | copy-start | bytes 772
  (2 other events, 2.0 us)

commit v8 on v7

--- a/solution.py
+++ b/solution.py
@@ -446,11 +446,16 @@
     for k in range(1, plane):
         total = total + crossed(listed[k], k * pair)
     two_back = [None] * len(own)
-    passes_on = pair == 2 and reach == 2 and chips % 2 == 0
+    passes_on = pair == 2 and reach == 2 and plane == 4
     if passes_on:
+        upper = chip % plane >= 2
+        stride = plane * pair
+        pairs = [(i, i + stride) for i in range(size - stride) if i // pair % plane >= 2]
+        risen = [lax.ppermute(w, "ctx", pairs) for w in own[1:]]
         two_back[0] = shifted(own[0], 2 * pair)
-        two_back[0], own[1:], total = lax.optimization_barrier((two_back[0], own[1:], total))
-        two_back[1:] = [shifted(w, 2 * pair) for w in own[1:]]
+        two_back[0], risen, total = lax.optimization_barrier((two_back[0], risen, total))
+        for c, w in enumerate(risen, 1):
+            two_back[c] = crossed(jnp.where(upper, w, own[c]), 2 * pair)
     q_other = crossed(part(queries, 1, 1 - core), 1) if pair == 2 else None
     step = 1
     while step < chips // plane:

time: 302 us -> 300 us (level)
  waiting for transfers between devices: 79.8 us -> 71.1 us
  starting transfers between devices: 25.3 us -> 30.3 us
    ppermute x4 -> x3, waiting for transfers between devices: 29 us -> 6.63 us  [shifted(): return lax.ppermute(value, 'ctx', [(i, i + by) for i in range(size - by)])]
    ppermute x12 -> x13, waiting for transfers between devices: 50.8 us -> 64.5 us  [crossed(): return lax.ppermute(value, 'ctx', [(i, i ^ bits) for i in range(size)])]
    ppermute x12 -> x13, starting transfers between devices: 17.5 us -> 22.8 us  [crossed(): return lax.ppermute(value, 'ctx', [(i, i ^ bits) for i in range(size)])]
    ppermute x4 -> x3, starting transfers between devices: 7.77 us -> 5.86 us  [shifted(): return lax.ppermute(value, 'ctx', [(i, i + by) for i in range(size - by)])]
  transfers between devices with their start and end apart: 16 -> 17, of which waited for: 7 -> 7; matrix products, arithmetic and copies ran while one was open for 3% -> 3% of each run, Pallas kernels for 31% -> 32%
where the time goes in v8:
time: 300 us; the launch traced here: 299 us
  Pallas kernels  159 us (53%)
  waiting for transfers between devices  71.1 us (24%)
  starting transfers between devices  30.3 us (10%)
  matrix products  22.6 us (8%)
  local copies, waits for them, and re-layouts  10.3 us (3%)
  other arithmetic  6.16 us (2%)
    pallas_call x2, Pallas kernels, over_vertical(): pl.pallas_call(functools.partial(vertical_kernel, cfg + (self.plane, self...  119 us
    ppermute x13, waiting for transfers between devices, crossed(): return lax.ppermute(value, 'ctx', [(i, i ^ bits) for i in range(size)])  64.5 us
    pallas_call x2, Pallas kernels, over_slash(): pl.pallas_call(functools.partial(slash_kernel, cfg), grid_spec=pltpu.Pref...  35.6 us
    ppermute x13, starting transfers between devices, crossed(): return lax.ppermute(value, 'ctx', [(i, i ^ bits) for i in range(size)])  22.8 us
    dot_general x1, matrix products, body(): output = jnp.dot(attended, out_weight, preferred_element_type=jnp.float32)  22.6 us
    ppermute x3, waiting for transfers between devices, shifted(): return lax.ppermute(value, 'ctx', [(i, i + by) for i in range(size - by)])  6.63 us
  transfers between devices with their start and end apart: 17, of which 7 were waited for; matrix products, arithmetic and copies ran while one was open for 3% of the time, Pallas kernels for 32%

profile of v8, /device:TPU:25, one launch (start us, length us, event | category | flops | bytes accessed | tf_op | source)
XLA Modules:
  0.0 299.4 jit_solution(12398885093003540176)
XLA Ops:
  5.4 4.5 %prepare.1 = (bf16[1024,512]{1,0:T(8,128)(2,1)}, bf16[1024,512]{1,0:T(8,128)(2,1)}, bf16[1024,256]{1,0:T(8,128)(2,1)}, bf16[1024,256]{1,0:T(8,128)(2,1)}, bf16[1...) custom-call(s32[2]{0:T(128)} %pad_add_fusion.info, s32[4,8]{1,0:T(4,128)} %constant_dynamic-slice_fusion.4.vert, ...), custom_call_target="tpu_custom_call" | custom-call | bytes 8388608 | tf_op jit(solution)/shard_map/prepare/pallas_call | solution.py:82
  10.0 3.3 %collective-permute-start.2 = (bf16[1024,512]{1,0:T(8,128)(2,1)}, bf16[1024,512]{1,0:T(8,128)(2,1)}, u32[]{:S(2)}, u32[]{:S(2)}) collective-permute-start(bf16[1024,512]{1,0:T(8,128)(2,1)} %get-tuple-element.24.refs_2_), channel_id=1, source_target_pairs={{0,4},{1,5},{2,6},{3,7},{4,8},{5,9},{6,10},{7,11},{8,12},{9,13},{1... | collective-permute-start | bytes 3145736 | tf_op jit(solution)/shard_map/ppermute | solution.py:22
  13.2 1.7 collective-permute-start.3
  16.1 1.4 collective-permute-start.6
  17.5 3.2 %constant_dynamic-slice_fusion.2 = bf16[512,2048]{1,0:T(8,128)(2,1)} fusion(bf16[512,4096]{1,0:T(8,128)(2,1)} %refs_0_.9, s32[]{:T(128)S(6)} %select_n.85), kind=kLoop, calls=%fused_computation.26 | loop fusion | bytes 4194308 | tf_op jit(solution)/shard_map/dynamic_slice | solution.py:436
  20.8 7.2 %collective-permute-done.4 = bf16[1024,256]{1,0:T(8,128)(2,1)S(1)} collective-permute-done((bf16[1024,256]{1,0:T(8,128)(2,1)}, bf16[1024,256]{1,0:T(8,128)(2,1)S(1)}, u32[]{:S(2)}, u32[]{:S(2)}) %collective-permute-start.4) | collective-permute-done | bytes 524320 | tf_op jit(solution)/shard_map/ppermute | solution.py:27
  28.0 2.6 collective-permute-start
  30.6 30.2 %collective-permute-done.5 = bf16[1024,256]{1,0:T(8,128)(2,1)} collective-permute-done((bf16[1024,256]{1,0:T(8,128)(2,1)}, bf16[1024,256]{1,0:T(8,128)(2,1)}, u32[]{:S(2)}, u32[]{:S(2)}) %collective-permute-start.5) | collective-permute-done | bytes 524320 | tf_op jit(solution)/shard_map/ppermute | solution.py:27
  60.8 1.5 add_add_fusion
  63.5 8.3 %collective-permute-start.13 = (bf16[1024,512]{1,0:T(8,128)(2,1)}, bf16[1024,512]{1,0:T(8,128)(2,1)}, u32[]{:S(2)}, u32[]{:S(2)}) collective-permute-start(bf16[1024,512]{1,0:T(8,128)(2,1)} %broadcast_select_fusion), channel_id=1, source_target_pairs={{0,4},{1,5},{2,6},{3,7},{4,0},{5,1},{6,2},{7,3},{8,12},{9,13},{10,... | collective-permute-start | bytes 3145736 | tf_op jit(solution)/shard_map/ppermute | solution.py:27
  71.9 2.5 collective-permute-start.7
  75.7 18.6 %collective-permute-done.13.refs_4_ = bf16[1024,512]{1,0:T(8,128)(2,1)} collective-permute-done((bf16[1024,512]{1,0:T(8,128)(2,1)}, bf16[1024,512]{1,0:T(8,128)(2,1)}, u32[]{:S(2)}, u32[]{:S(2)}) %collective-permute-start.13) | collective-permute-done | bytes 1048608 | tf_op jit(solution)/shard_map/ppermute | solution.py:27
  94.5 2.5 collective-permute-start.14
  100.9 17.8 %attend_slash.2.refs_5_ = f32[2,8,512,256]{3,2,1,0:T(8,128)} custom-call(s32[2]{0:T(128)} %pad_add_fusion.info, s32[4,8]{1,0:T(4,128)} %constant_dynamic-slice_fusion.3.slash, bf16[512,4096]{1,0:T(8,128)(2,1)} %refs_0_.9, bf16[512,2048]{1,0:T(8,128)(2,1)} %collective-permute-done.refs_1_, bf16[1024,512]{1,0:T(8,128)(2,1)} %get-tuple-element.24.refs_2_, ...), custom_call_target="tpu_custom_call" | custom-call | flops 8589934592 | bytes 10485760 | tf_op jit(solution)/shard_map/attend_slash/pallas_call | solution.py:358
  118.8 6.6 %collective-permute-done.9 = bf16[1024,256]{1,0:T(8,128)(2,1)S(1)} collective-permute-done((bf16[1024,256]{1,0:T(8,128)(2,1)S(1)}, bf16[1024,256]{1,0:T(8,128)(2,1)S(1)}, u32[]{:S(2)}, u32[]{:S(2)}) %collective-permute-start.9) | collective-permute-done | bytes 524320 | tf_op jit(solution)/shard_map/ppermute | solution.py:22
  126.9 1.4 collective-permute-start.10
  129.3 17.8 %attend_slash.3.refs_5_ = f32[2,8,512,256]{3,2,1,0:T(8,128)} custom-call(s32[2]{0:T(128)} %pad_add_fusion.info, s32[4,8]{1,0:T(4,128)} %constant_dynamic-slice_fusion.3.slash, bf16[512,4096]{1,0:T(8,128)(2,1)} %refs_0_.9, bf16[512,2048]{1,0:T(8,128)(2,1)} %collective-permute-done.refs_1_, bf16[1024,512]{1,0:T(8,128)(2,1)} %get-tuple-element.25.refs_2_, ...), custom_call_target="tpu_custom_call" | custom-call | flops 8589934592 | bytes 10485760 | tf_op jit(solution)/shard_map/attend_slash/pallas_call | solution.py:358
  147.0 4.6 %collective-permute-done.11 = bf16[1024,256]{1,0:T(8,128)(2,1)S(1)} collective-permute-done((bf16[1024,256]{1,0:T(8,128)(2,1)S(1)}, bf16[1024,256]{1,0:T(8,128)(2,1)S(1)}, u32[]{:S(2)}, u32[]{:S(2)}) %collective-permute-start.11) | collective-permute-done | bytes 524320 | tf_op jit(solution)/shard_map/ppermute | solution.py:27
  151.8 1.3 copy-done.9
  153.1 59.3 %attend_vertical.3 = (bf16[512,1024]{1,0:T(8,128)(2,1)}, bf16[512,1024]{1,0:T(8,128)(2,1)}) custom-call(s32[2]{0:T(128)} %pad_add_fusion.info, s32[4,8]{1,0:T(4,128)} %constant_dynamic-slice_fusion.4.vert, s32[4,8]{1,0:T(4,128)} %constant_dynamic-slice_fusion.3.slash, bf16[512,4096]{1,0:T(8,128)(2,1)} %refs_0_.9, ...), custom_call_target="tpu_custom_call" | custom-call | flops 8589934592 | bytes 10485760 | tf_op jit(solution)/shard_map/attend_vertical/pallas_call | solution.py:384
  213.0 59.3 %attend_vertical.2 = (bf16[512,1024]{1,0:T(8,128)(2,1)}, bf16[512,1024]{1,0:T(8,128)(2,1)}) custom-call(s32[2]{0:T(128)} %pad_add_fusion.info, s32[4,8]{1,0:T(4,128)} %constant_dynamic-slice_fusion.4.vert, s32[4,8]{1,0:T(4,128)} %constant_dynamic-slice_fusion.3.slash, bf16[512,4096]{1,0:T(8,128)(2,1)} %refs_0_.9, ...), custom_call_target="tpu_custom_call" | custom-call | flops 8589934592 | bytes 10485760 | tf_op jit(solution)/shard_map/attend_vertical/pallas_call | solution.py:384
  272.7 2.7 collective-permute-done.15
  275.4 1.4 broadcast_select_fusion.6
  276.7 22.6 %convolution_convert_fusion = bf16[512,4096]{1,0:T(8,128)(2,1)} fusion(bf16[4096,4096]{1,0:T(8,128)(2,1)} %param.11, bf16[512,1024]{1,0:T(8,128)(2,1)S(1)} %get-tuple-element.46, bf16[512,1024]{1,0:T(8,128)(2,1)S(1)} %get-tuple-element.44, bf16[512,1024]{1,0:T(8,128)(2,1)S(1)} %get-tuple-element.45, bf16[512,1024]{1,0:T(8,128)(2,1)S(1)} %get-tuple-element.43), kind=kOutput, calls=%fused_computation | convolution fusion | flops 17198743552 | bytes 41943040 | tf_op jit(solution)/shard_map/dot_general | solution.py:491
  (64 shorter events, 16.9 us)
Async XLA Ops:
  1.4 3.0 %collective-permute-start.1 = (bf16[512,1024]{1,0:T(8,128)(2,1)S(1)}, bf16[512,1024]{1,0:T(8,128)(2,1)S(1)}, u32[]{:S(2)}, u32[]{:S(2)}) collective-permute-start(bf16[512,1024]{1,0:T(8,128)(2,1)S(1)} %pad_maximum_fusion), channel_id=1, source_target_pairs={{0,1},{1,0},{2,3},{3,2},{4,5},{5,4},{6,7},{7,6},{8,9},{9,8},{10,11... | collective-permute-start | bytes 3145736 | tf_op jit(solution)/shard_map/ppermute | solution.py:27
  10.0 50.8 %copy-start.7 = (bf16[1024,256]{1,0:T(8,128)(2,1)S(1)}, bf16[1024,256]{1,0:T(8,128)(2,1)}, u32[]{:S(2)}) copy-start(bf16[1024,256]{1,0:T(8,128)(2,1)} %get-tuple-element.26) | copy-start | bytes 1572868
  10.0 52.4 %copy-start.2 = (bf16[1024,512]{1,0:T(8,128)(2,1)S(1)}, bf16[1024,512]{1,0:T(8,128)(2,1)}, u32[]{:S(2)}) copy-start(bf16[1024,512]{1,0:T(8,128)(2,1)} %get-tuple-element.25.refs_2_) | copy-start | bytes 3145732
  10.0 52.3 %collective-permute-start.2 = (bf16[1024,512]{1,0:T(8,128)(2,1)}, bf16[1024,512]{1,0:T(8,128)(2,1)}, u32[]{:S(2)}, u32[]{:S(2)}) collective-permute-start(bf16[1024,512]{1,0:T(8,128)(2,1)} %get-tuple-element.24.refs_2_), channel_id=1, source_target_pairs={{0,4},{1,5},{2,6},{3,7},{4,8},{5,9},{6,10},{7,11},{8,12},{9,13},{1... | collective-permute-start | bytes 3145736 | tf_op jit(solution)/shard_map/ppermute | solution.py:22
  13.2 49.1 %collective-permute-start.3 = (bf16[1024,512]{1,0:T(8,128)(2,1)}, bf16[1024,512]{1,0:T(8,128)(2,1)}, u32[]{:S(2)}, u32[]{:S(2)}) collective-permute-start(bf16[1024,512]{1,0:T(8,128)(2,1)} %get-tuple-element.25.refs_2_), channel_id=1, source_target_pairs={{4,12},{5,13},{6,14},{7,15},{12,20},{13,21},{14,22},{15,23},{20,28... | collective-permute-start | bytes 3145736 | tf_op jit(solution)/shard_map/ppermute | solution.py:454
  14.9 13.1 %collective-permute-start.4 = (bf16[1024,256]{1,0:T(8,128)(2,1)}, bf16[1024,256]{1,0:T(8,128)(2,1)S(1)}, u32[]{:S(2)}, u32[]{:S(2)}) collective-permute-start(bf16[1024,256]{1,0:T(8,128)(2,1)} %get-tuple-element.27), channel_id=1, source_target_pairs={{0,2},{1,3},{2,0},{3,1},{4,6},{5,7},{6,4},{7,5},{8,10},{9,11},{10,... | collective-permute-start | bytes 1572872 | tf_op jit(solution)/shard_map/ppermute | solution.py:27
  16.1 44.6 %collective-permute-start.5 = (bf16[1024,256]{1,0:T(8,128)(2,1)}, bf16[1024,256]{1,0:T(8,128)(2,1)}, u32[]{:S(2)}, u32[]{:S(2)}) collective-permute-start(bf16[1024,256]{1,0:T(8,128)(2,1)} %get-tuple-element.28), channel_id=1, source_target_pairs={{0,4},{1,5},{2,6},{3,7},{4,0},{5,1},{6,2},{7,3},{8,12},{9,13},{10,... | collective-permute-start | bytes 1572872 | tf_op jit(solution)/shard_map/ppermute | solution.py:27
  16.1 44.6 %collective-permute-start.6 = (bf16[1024,256]{1,0:T(8,128)(2,1)}, bf16[1024,256]{1,0:T(8,128)(2,1)}, u32[]{:S(2)}, u32[]{:S(2)}) collective-permute-start(bf16[1024,256]{1,0:T(8,128)(2,1)} %get-tuple-element.29), channel_id=1, source_target_pairs={{0,6},{1,7},{2,4},{3,5},{4,2},{5,3},{6,0},{7,1},{8,14},{9,15},{10,... | collective-permute-start | bytes 1572872 | tf_op jit(solution)/shard_map/ppermute | solution.py:27
  17.5 54.3 %copy-start.6 = (bf16[1024,512]{1,0:T(8,128)(2,1)S(1)}, bf16[1024,512]{1,0:T(8,128)(2,1)}, u32[]{:S(2)}) copy-start(bf16[1024,512]{1,0:T(8,128)(2,1)} %get-tuple-element.24.refs_2_) | copy-start | bytes 3145732
  28.0 32.7 %copy-start.8 = (bf16[1024,256]{1,0:T(8,128)(2,1)}, bf16[1024,256]{1,0:T(8,128)(2,1)S(1)}, u32[]{:S(2)}) copy-start(bf16[1024,256]{1,0:T(8,128)(2,1)S(1)} %collective-permute-done.4) | copy-start | bytes 1572868
  28.0 71.8 %collective-permute-start = (bf16[512,2048]{1,0:T(8,128)(2,1)}, bf16[512,2048]{1,0:T(8,128)(2,1)}, u32[]{:S(2)}, u32[]{:S(2)}) collective-permute-start(bf16[512,2048]{1,0:T(8,128)(2,1)} %constant_dynamic-slice_fusion.2), channel_id=1, source_target_pairs={{0,1},{1,0},{2,3},{3,2},{4,5},{5,4},{6,7},{7,6},{8,9},{9,8},{10,11... | collective-permute-start | bytes 6291464 | tf_op jit(solution)/shard_map/ppermute | solution.py:27
  62.3 34.7 %copy-start.10 = (s32[8,8]{1,0:T(8,128)S(1)}, s32[8,8]{1,0:T(8,128)}, u32[]{:S(2)}) copy-start(s32[8,8]{1,0:T(8,128)} %param.10) | copy-start | bytes 772
  63.5 30.9 %collective-permute-start.13 = (bf16[1024,512]{1,0:T(8,128)(2,1)}, bf16[1024,512]{1,0:T(8,128)(2,1)}, u32[]{:S(2)}, u32[]{:S(2)}) collective-permute-start(bf16[1024,512]{1,0:T(8,128)(2,1)} %broadcast_select_fusion), channel_id=1, source_target_pairs={{0,4},{1,5},{2,6},{3,7},{4,0},{5,1},{6,2},{7,3},{8,12},{9,13},{10,... | collective-permute-start | bytes 3145736 | tf_op jit(solution)/shard_map/ppermute | solution.py:27
  71.9 27.9 %collective-permute-start.7 = (bf16[1024,512]{1,0:T(8,128)(2,1)S(1)}, bf16[1024,512]{1,0:T(8,128)(2,1)S(1)}, u32[]{:S(2)}, u32[]{:S(2)}) collective-permute-start(bf16[1024,512]{1,0:T(8,128)(2,1)S(1)} %broadcast_select_fusion.2), channel_id=1, source_target_pairs={{0,2},{1,3},{2,0},{3,1},{4,6},{5,7},{6,4},{7,5},{8,10},{9,11},{10,... | collective-permute-start | bytes 3145736 | tf_op jit(solution)/shard_map/ppermute | solution.py:27
  74.4 24.0 %collective-permute-start.8 = (bf16[1024,256]{1,0:T(8,128)(2,1)S(1)}, bf16[1024,256]{1,0:T(8,128)(2,1)S(1)}, u32[]{:S(2)}, u32[]{:S(2)}) collective-permute-start(bf16[1024,256]{1,0:T(8,128)(2,1)S(1)} %add_add_fusion), channel_id=1, source_target_pairs={{0,8},{1,9},{2,10},{3,11},{4,12},{5,13},{6,14},{7,15},{8,16},{9,17... | collective-permute-start | bytes 1572872 | tf_op jit(solution)/shard_map/ppermute | solution.py:22
  94.5 33.8 %collective-permute-start.14 = (bf16[1024,512]{1,0:T(8,128)(2,1)S(1)}, bf16[1024,512]{1,0:T(8,128)(2,1)S(1)}, u32[]{:S(2)}, u32[]{:S(2)}) collective-permute-start(bf16[1024,512]{1,0:T(8,128)(2,1)S(1)} %broadcast_select_fusion.1), channel_id=1, source_target_pairs={{0,2},{1,3},{2,0},{3,1},{4,6},{5,7},{6,4},{7,5},{8,10},{9,11},{10,... | collective-permute-start | bytes 3145736 | tf_op jit(solution)/shard_map/ppermute | solution.py:27
  98.6 26.9 %collective-permute-start.9 = (bf16[1024,256]{1,0:T(8,128)(2,1)S(1)}, bf16[1024,256]{1,0:T(8,128)(2,1)S(1)}, u32[]{:S(2)}, u32[]{:S(2)}) collective-permute-start(bf16[1024,256]{1,0:T(8,128)(2,1)S(1)} %add.46), channel_id=1, source_target_pairs={{0,16},{1,17},{2,18},{3,19},{4,20},{5,21},{6,22},{7,23},{8,24},{9,... | collective-permute-start | bytes 1572872 | tf_op jit(solution)/shard_map/ppermute | solution.py:22
  125.6 21.5 %collective-permute-start.12 = (bf16[1024,256]{1,0:T(8,128)(2,1)S(1)}, bf16[1024,256]{1,0:T(8,128)(2,1)S(1)}, u32[]{:S(2)}, u32[]{:S(2)}) collective-permute-start(bf16[1024,256]{1,0:T(8,128)(2,1)S(1)} %add.47), channel_id=1, source_target_pairs={{0,6},{1,7},{2,4},{3,5},{4,2},{5,3},{6,0},{7,1},{8,14},{9,15},{10,... | collective-permute-start | bytes 1572872 | tf_op jit(solution)/shard_map/ppermute | solution.py:27
  126.5 25.1 %collective-permute-start.11 = (bf16[1024,256]{1,0:T(8,128)(2,1)S(1)}, bf16[1024,256]{1,0:T(8,128)(2,1)S(1)}, u32[]{:S(2)}, u32[]{:S(2)}) collective-permute-start(bf16[1024,256]{1,0:T(8,128)(2,1)S(1)} %add.47), channel_id=1, source_target_pairs={{0,4},{1,5},{2,6},{3,7},{4,0},{5,1},{6,2},{7,3},{8,12},{9,13},{10,... | collective-permute-start | bytes 1572872 | tf_op jit(solution)/shard_map/ppermute | solution.py:27
  126.9 24.7 %collective-permute-start.10 = (bf16[1024,256]{1,0:T(8,128)(2,1)S(1)}, bf16[1024,256]{1,0:T(8,128)(2,1)S(1)}, u32[]{:S(2)}, u32[]{:S(2)}) collective-permute-start(bf16[1024,256]{1,0:T(8,128)(2,1)S(1)} %add.47), channel_id=1, source_target_pairs={{0,2},{1,3},{2,0},{3,1},{4,6},{5,7},{6,4},{7,5},{8,10},{9,11},{10,... | collective-permute-start | bytes 1572872 | tf_op jit(solution)/shard_map/ppermute | solution.py:27
  212.4 60.1 %copy-start.4 = (bf16[512,1024]{1,0:T(8,128)(2,1)S(1)}, bf16[512,1024]{1,0:T(8,128)(2,1)}, u32[]{:S(2)}) copy-start(bf16[512,1024]{1,0:T(8,128)(2,1)} %get-tuple-element.41) | copy-start | bytes 3145732
  212.4 60.1 %collective-permute-start.16 = (bf16[512,1024]{1,0:T(8,128)(2,1)}, bf16[512,1024]{1,0:T(8,128)(2,1)S(1)}, u32[]{:S(2)}, u32[]{:S(2)}) collective-permute-start(bf16[512,1024]{1,0:T(8,128)(2,1)} %get-tuple-element.42), channel_id=1, source_target_pairs={{0,1},{1,0},{2,3},{3,2},{4,5},{5,4},{6,7},{7,6},{8,9},{9,8},{10,11... | collective-permute-start | bytes 3145736 | tf_op jit(solution)/shard_map/ppermute | solution.py:27
  272.3 3.1 %collective-permute-start.15 = (bf16[512,1024]{1,0:T(8,128)(2,1)}, bf16[512,1024]{1,0:T(8,128)(2,1)}, u32[]{:S(2)}, u32[]{:S(2)}) collective-permute-start(bf16[512,1024]{1,0:T(8,128)(2,1)} %get-tuple-element.39), channel_id=1, source_target_pairs={{0,1},{1,0},{2,3},{3,2},{4,5},{5,4},{6,7},{7,6},{8,9},{9,8},{10,11... | collective-permute-start | bytes 3145736 | tf_op jit(solution)/shard_map/ppermute | solution.py:27
  276.7 22.6 %copy-start.1 = (s32[8,8]{1,0:T(8,128)S(1)}, s32[8,8]{1,0:T(8,128)}, u32[]{:S(2)}) copy-start(s32[8,8]{1,0:T(8,128)} %param.9) | copy-start | bytes 772
  (6 other events, 10.1 us)

commit v9 on v8

--- a/solution.py
+++ b/solution.py
@@ -25,6 +25,10 @@
 def crossed(value, bits):
     size = lax.axis_size("ctx")
     return lax.ppermute(value, "ctx", [(i, i ^ bits) for i in range(size)])
+
+
+def after(value, other):
+    return lax.optimization_barrier((value, other))[0]
 
 
 def prepare_kernel(cfg, info, vert, *refs):
@@ -451,11 +455,12 @@
         upper = chip % plane >= 2
         stride = plane * pair
         pairs = [(i, i + stride) for i in range(size - stride) if i // pair % plane >= 2]
-        risen = [lax.ppermute(w, "ctx", pairs) for w in own[1:]]
-        two_back[0] = shifted(own[0], 2 * pair)
-        two_back[0], risen, total = lax.optimization_barrier((two_back[0], risen, total))
-        for c, w in enumerate(risen, 1):
-            two_back[c] = crossed(jnp.where(upper, w, own[c]), 2 * pair)
+        before, risen = total, None
+        first_step = total + shifted(total, stride)
+        for c, w in enumerate(own):
+            risen = lax.ppermute(w if risen is None else after(w, risen), "ctx", pairs)
+            two_back[c] = crossed(after(jnp.where(upper, risen, w), before), 2 * pair)
+            before = (two_back[c], first_step)
     q_other = crossed(part(queries, 1, 1 - core), 1) if pair == 2 else None
     step = 1
     while step < chips // plane:

time: 300 us -> 299 us (level)
  waiting for transfers between devices: 71.1 us -> 64.8 us
  other arithmetic: 6.16 us -> 9.2 us
    ppermute x13 -> x14, waiting for transfers between devices: 64.5 us -> 52.4 us  [crossed(): return lax.ppermute(value, 'ctx', [(i, i ^ bits) for i in range(size)])]
    ppermute x3 -> x2, waiting for transfers between devices: 6.63 us -> 12.4 us  [shifted(): return lax.ppermute(value, 'ctx', [(i, i + by) for i in range(size - by)])]
    ppermute x13 -> x14, starting transfers between devices: 22.8 us -> 27.6 us  [crossed(): return lax.ppermute(value, 'ctx', [(i, i ^ bits) for i in range(size)])]
    ppermute x3 -> x2, starting transfers between devices: 5.86 us -> 2.57 us  [shifted(): return lax.ppermute(value, 'ctx', [(i, i + by) for i in range(size - by)])]
  transfers between devices with their start and end apart: 17 -> 18, of which waited for: 7 -> 9; matrix products, arithmetic and copies ran while one was open for 3% -> 4% of each run, Pallas kernels for 32% -> 32%
where the time goes in v9:
time: 299 us; the launch traced here: 298 us
  Pallas kernels  159 us (53%)
  waiting for transfers between devices  64.8 us (22%)
  starting transfers between devices  32.6 us (11%)
  matrix products  22.6 us (8%)
  local copies, waits for them, and re-layouts  10.3 us (3%)
  other arithmetic  9.2 us (3%)
    pallas_call x2, Pallas kernels, over_vertical(): pl.pallas_call(functools.partial(vertical_kernel, cfg + (self.plane, self...  119 us
    ppermute x14, waiting for transfers between devices, crossed(): return lax.ppermute(value, 'ctx', [(i, i ^ bits) for i in range(size)])  52.4 us
    pallas_call x2, Pallas kernels, over_slash(): pl.pallas_call(functools.partial(slash_kernel, cfg), grid_spec=pltpu.Pref...  35.6 us
    ppermute x14, starting transfers between devices, crossed(): return lax.ppermute(value, 'ctx', [(i, i ^ bits) for i in range(size)])  27.6 us
    dot_general x1, matrix products, body(): output = jnp.dot(attended, out_weight, preferred_element_type=jnp.float32)  22.6 us
    ppermute x2, waiting for transfers between devices, shifted(): return lax.ppermute(value, 'ctx', [(i, i + by) for i in range(size - by)])  12.4 us
  transfers between devices with their start and end apart: 18, of which 9 were waited for; matrix products, arithmetic and copies ran while one was open for 4% of the time, Pallas kernels for 32%

profile of v9, /device:TPU:25, one launch (start us, length us, event | category | flops | bytes accessed | tf_op | source)
XLA Modules:
  0.0 298.3 jit_solution(2425262783797347767)
XLA Ops:
  5.4 4.5 %prepare.1 = (bf16[1024,512]{1,0:T(8,128)(2,1)}, bf16[1024,512]{1,0:T(8,128)(2,1)}, bf16[1024,256]{1,0:T(8,128)(2,1)}, bf16[1024,256]{1,0:T(8,128)(2,1)}, bf16[1...) custom-call(s32[2]{0:T(128)} %pad_add_fusion.info, s32[4,8]{1,0:T(4,128)} %constant_dynamic-slice_fusion.4.vert, ...), custom_call_target="tpu_custom_call" | custom-call | bytes 8388608 | tf_op jit(solution)/shard_map/prepare/pallas_call | solution.py:86
  11.9 1.8 collective-permute-start.4
  13.7 10.3 %collective-permute-done.3 = bf16[1024,256]{1,0:T(8,128)(2,1)S(1)} collective-permute-done((bf16[1024,256]{1,0:T(8,128)(2,1)}, bf16[1024,256]{1,0:T(8,128)(2,1)S(1)}, u32[]{:S(2)}, u32[]{:S(2)}) %collective-permute-start.3) | collective-permute-done | bytes 524320 | tf_op jit(solution)/shard_map/ppermute | solution.py:27
  24.0 11.7 %collective-permute-done.4 = bf16[1024,256]{1,0:T(8,128)(2,1)S(1)} collective-permute-done((bf16[1024,256]{1,0:T(8,128)(2,1)}, bf16[1024,256]{1,0:T(8,128)(2,1)S(1)}, u32[]{:S(2)}, u32[]{:S(2)}) %collective-permute-start.4) | collective-permute-done | bytes 524320 | tf_op jit(solution)/shard_map/ppermute | solution.py:27
  37.9 1.8 collective-permute-start.13
  39.7 2.3 broadcast_select_fusion.1
  43.3 3.3 %constant_dynamic-slice_fusion.2 = bf16[512,2048]{1,0:T(8,128)(2,1)} fusion(bf16[512,4096]{1,0:T(8,128)(2,1)} %refs_0_.9, s32[]{:T(128)S(6)} %select_n.89), kind=kLoop, calls=%fused_computation.27 | loop fusion | bytes 4194308 | tf_op jit(solution)/shard_map/dynamic_slice | solution.py:440
  46.6 1.4 collective-permute-start
  48.0 8.1 %collective-permute-done.8 = bf16[1024,256]{1,0:T(8,128)(2,1)} collective-permute-done((bf16[1024,256]{1,0:T(8,128)(2,1)S(1)}, bf16[1024,256]{1,0:T(8,128)(2,1)}, u32[]{:S(2)}, u32[]{:S(2)}) %collective-permute-start.8) | collective-permute-done | bytes 524320 | tf_op jit(solution)/shard_map/ppermute | solution.py:22
  58.5 7.2 %collective-permute-done.6.refs_4_ = bf16[1024,512]{1,0:T(8,128)(2,1)} collective-permute-done((bf16[1024,512]{1,0:T(8,128)(2,1)}, bf16[1024,512]{1,0:T(8,128)(2,1)}, u32[]{:S(2)}, u32[]{:S(2)}) %collective-permute-start.6) | collective-permute-done | bytes 1048608 | tf_op jit(solution)/shard_map/ppermute | solution.py:27
  65.7 13.9 %collective-permute-start.14 = (bf16[1024,512]{1,0:T(8,128)(2,1)}, bf16[1024,512]{1,0:T(8,128)(2,1)}, u32[]{:S(2)}, u32[]{:S(2)}) collective-permute-start(bf16[1024,512]{1,0:T(8,128)(2,1)} %broadcast_select_fusion), channel_id=1, source_target_pairs={{0,4},{1,5},{2,6},{3,7},{4,0},{5,1},{6,2},{7,3},{8,12},{9,13},{10,... | collective-permute-start | bytes 3145736 | tf_op jit(solution)/shard_map/ppermute | solution.py:27
  79.8 1.5 collective-permute-start.7
  82.7 18.3 %collective-permute-done.14.refs_4_ = bf16[1024,512]{1,0:T(8,128)(2,1)} collective-permute-done((bf16[1024,512]{1,0:T(8,128)(2,1)}, bf16[1024,512]{1,0:T(8,128)(2,1)}, u32[]{:S(2)}, u32[]{:S(2)}) %collective-permute-start.14) | collective-permute-done | bytes 1048608 | tf_op jit(solution)/shard_map/ppermute | solution.py:27
  101.1 1.5 collective-permute-start.15
  104.0 4.3 %collective-permute-done.9 = bf16[1024,256]{1,0:T(8,128)(2,1)S(1)} collective-permute-done((bf16[1024,256]{1,0:T(8,128)(2,1)S(1)}, bf16[1024,256]{1,0:T(8,128)(2,1)S(1)}, u32[]{:S(2)}, u32[]{:S(2)}) %collective-permute-start.9) | collective-permute-done | bytes 524320 | tf_op jit(solution)/shard_map/ppermute | solution.py:22
  109.7 1.4 collective-permute-start.10
  112.2 17.8 %attend_slash.2.refs_5_ = f32[2,8,512,256]{3,2,1,0:T(8,128)} custom-call(s32[2]{0:T(128)} %pad_add_fusion.info, s32[4,8]{1,0:T(4,128)} %constant_dynamic-slice_fusion.3.slash, bf16[512,4096]{1,0:T(8,128)(2,1)} %refs_0_.9, bf16[512,2048]{1,0:T(8,128)(2,1)} %collective-permute-done.refs_1_, bf16[1024,512]{1,0:T(8,128)(2,1)} %get-tuple-element.24.refs_2_, ...), custom_call_target="tpu_custom_call" | custom-call | flops 8589934592 | bytes 10485760 | tf_op jit(solution)/shard_map/attend_slash/pallas_call | solution.py:362
  131.1 17.8 %attend_slash.3.refs_5_ = f32[2,8,512,256]{3,2,1,0:T(8,128)} custom-call(s32[2]{0:T(128)} %pad_add_fusion.info, s32[4,8]{1,0:T(4,128)} %constant_dynamic-slice_fusion.3.slash, bf16[512,4096]{1,0:T(8,128)(2,1)} %refs_0_.9, bf16[512,2048]{1,0:T(8,128)(2,1)} %collective-permute-done.refs_1_, bf16[1024,512]{1,0:T(8,128)(2,1)} %get-tuple-element.31.refs_2_, ...), custom_call_target="tpu_custom_call" | custom-call | flops 8589934592 | bytes 10485760 | tf_op jit(solution)/shard_map/attend_slash/pallas_call | solution.py:362
  150.4 59.3 %attend_vertical.3 = (bf16[512,1024]{1,0:T(8,128)(2,1)}, bf16[512,1024]{1,0:T(8,128)(2,1)}) custom-call(s32[2]{0:T(128)} %pad_add_fusion.info, s32[4,8]{1,0:T(4,128)} %constant_dynamic-slice_fusion.4.vert, s32[4,8]{1,0:T(4,128)} %constant_dynamic-slice_fusion.3.slash, bf16[512,4096]{1,0:T(8,128)(2,1)} %refs_0_.9, ...), custom_call_target="tpu_custom_call" | custom-call | flops 8589934592 | bytes 10485760 | tf_op jit(solution)/shard_map/attend_vertical/pallas_call | solution.py:388
  209.6 2.4 collective-permute-start.17
  212.0 59.3 %attend_vertical.2 = (bf16[512,1024]{1,0:T(8,128)(2,1)}, bf16[512,1024]{1,0:T(8,128)(2,1)}) custom-call(s32[2]{0:T(128)} %pad_add_fusion.info, s32[4,8]{1,0:T(4,128)} %constant_dynamic-slice_fusion.4.vert, s32[4,8]{1,0:T(4,128)} %constant_dynamic-slice_fusion.3.slash, bf16[512,4096]{1,0:T(8,128)(2,1)} %refs_0_.9, ...), custom_call_target="tpu_custom_call" | custom-call | flops 8589934592 | bytes 10485760 | tf_op jit(solution)/shard_map/attend_vertical/pallas_call | solution.py:388
  271.6 2.7 collective-permute-done.16
  274.3 1.4 broadcast_select_fusion.7
  275.7 22.6 %convolution_convert_fusion = bf16[512,4096]{1,0:T(8,128)(2,1)} fusion(bf16[4096,4096]{1,0:T(8,128)(2,1)} %param.11, bf16[512,1024]{1,0:T(8,128)(2,1)S(1)} %get-tuple-element.46, bf16[512,1024]{1,0:T(8,128)(2,1)S(1)} %get-tuple-element.44, bf16[512,1024]{1,0:T(8,128)(2,1)S(1)} %get-tuple-element.45, bf16[512,1024]{1,0:T(8,128)(2,1)S(1)} %get-tuple-element.43), kind=kOutput, calls=%fused_computation | convolution fusion | flops 17198743552 | bytes 41943040 | tf_op jit(solution)/shard_map/dot_general | solution.py:496
  (63 shorter events, 21.5 us)
Async XLA Ops:
  1.4 3.0 %collective-permute-start.1 = (bf16[512,1024]{1,0:T(8,128)(2,1)S(1)}, bf16[512,1024]{1,0:T(8,128)(2,1)S(1)}, u32[]{:S(2)}, u32[]{:S(2)}) collective-permute-start(bf16[512,1024]{1,0:T(8,128)(2,1)S(1)} %pad_maximum_fusion), channel_id=1, source_target_pairs={{0,1},{1,0},{2,3},{3,2},{4,5},{5,4},{6,7},{7,6},{8,9},{9,8},{10,11... | collective-permute-start | bytes 3145736 | tf_op jit(solution)/shard_map/ppermute | solution.py:27
  9.9 28.0 %collective-permute-start.2 = (bf16[1024,512]{1,0:T(8,128)(2,1)}, bf16[1024,512]{1,0:T(8,128)(2,1)S(1)}, u32[]{:S(2)}, u32[]{:S(2)}) collective-permute-start(bf16[1024,512]{1,0:T(8,128)(2,1)} %get-tuple-element.24.refs_2_), channel_id=1, source_target_pairs={{4,12},{5,13},{6,14},{7,15},{12,20},{13,21},{14,22},{15,23},{20,28... | collective-permute-start | bytes 3145736 | tf_op jit(solution)/shard_map/ppermute | solution.py:461
  10.6 13.4 %collective-permute-start.3 = (bf16[1024,256]{1,0:T(8,128)(2,1)}, bf16[1024,256]{1,0:T(8,128)(2,1)S(1)}, u32[]{:S(2)}, u32[]{:S(2)}) collective-permute-start(bf16[1024,256]{1,0:T(8,128)(2,1)} %get-tuple-element.26), channel_id=1, source_target_pairs={{0,2},{1,3},{2,0},{3,1},{4,6},{5,7},{6,4},{7,5},{8,10},{9,11},{10,... | collective-permute-start | bytes 1572872 | tf_op jit(solution)/shard_map/ppermute | solution.py:27
  11.9 23.8 %collective-permute-start.4 = (bf16[1024,256]{1,0:T(8,128)(2,1)}, bf16[1024,256]{1,0:T(8,128)(2,1)S(1)}, u32[]{:S(2)}, u32[]{:S(2)}) collective-permute-start(bf16[1024,256]{1,0:T(8,128)(2,1)} %get-tuple-element.27), channel_id=1, source_target_pairs={{0,4},{1,5},{2,6},{3,7},{4,0},{5,1},{6,2},{7,3},{8,12},{9,13},{10,... | collective-permute-start | bytes 1572872 | tf_op jit(solution)/shard_map/ppermute | solution.py:27
  13.7 23.1 %collective-permute-start.5 = (bf16[1024,256]{1,0:T(8,128)(2,1)}, bf16[1024,256]{1,0:T(8,128)(2,1)S(1)}, u32[]{:S(2)}, u32[]{:S(2)}) collective-permute-start(bf16[1024,256]{1,0:T(8,128)(2,1)} %get-tuple-element.28), channel_id=1, source_target_pairs={{0,6},{1,7},{2,4},{3,5},{4,2},{5,3},{6,0},{7,1},{8,14},{9,15},{10,... | collective-permute-start | bytes 1572872 | tf_op jit(solution)/shard_map/ppermute | solution.py:27
  37.9 19.4 %copy-start.3 = (bf16[1024,512]{1,0:T(8,128)(2,1)S(1)}, bf16[1024,512]{1,0:T(8,128)(2,1)}, u32[]{:S(2)}) copy-start(bf16[1024,512]{1,0:T(8,128)(2,1)} %get-tuple-element.31.refs_2_) | copy-start | bytes 3145732
  37.9 19.4 %collective-permute-start.13 = (bf16[1024,512]{1,0:T(8,128)(2,1)}, bf16[1024,512]{1,0:T(8,128)(2,1)}, u32[]{:S(2)}, u32[]{:S(2)}) collective-permute-start(bf16[1024,512]{1,0:T(8,128)(2,1)} %get-tuple-element.31.refs_2_), channel_id=1, source_target_pairs={{4,12},{5,13},{6,14},{7,15},{12,20},{13,21},{14,22},{15,23},{20,28... | collective-permute-start | bytes 3145736 | tf_op jit(solution)/shard_map/ppermute | solution.py:461
  42.0 23.7 %collective-permute-start.6 = (bf16[1024,512]{1,0:T(8,128)(2,1)}, bf16[1024,512]{1,0:T(8,128)(2,1)}, u32[]{:S(2)}, u32[]{:S(2)}) collective-permute-start(bf16[1024,512]{1,0:T(8,128)(2,1)} %broadcast_select_fusion.1), channel_id=1, source_target_pairs={{0,4},{1,5},{2,6},{3,7},{4,0},{5,1},{6,2},{7,3},{8,12},{9,13},{10,... | collective-permute-start | bytes 3145736 | tf_op jit(solution)/shard_map/ppermute | solution.py:27
  42.0 14.1 %collective-permute-start.8 = (bf16[1024,256]{1,0:T(8,128)(2,1)S(1)}, bf16[1024,256]{1,0:T(8,128)(2,1)}, u32[]{:S(2)}, u32[]{:S(2)}) collective-permute-start(bf16[1024,256]{1,0:T(8,128)(2,1)S(1)} %add_add_fusion), channel_id=1, source_target_pairs={{0,8},{1,9},{2,10},{3,11},{4,12},{5,13},{6,14},{7,15},{8,16},{9,17... | collective-permute-start | bytes 1572872 | tf_op jit(solution)/shard_map/ppermute | solution.py:22
  43.3 36.4 %copy-start.2 = (bf16[1024,512]{1,0:T(8,128)(2,1)S(1)}, bf16[1024,512]{1,0:T(8,128)(2,1)}, u32[]{:S(2)}) copy-start(bf16[1024,512]{1,0:T(8,128)(2,1)} %get-tuple-element.24.refs_2_) | copy-start | bytes 3145732
  46.6 63.1 %collective-permute-start = (bf16[512,2048]{1,0:T(8,128)(2,1)}, bf16[512,2048]{1,0:T(8,128)(2,1)}, u32[]{:S(2)}, u32[]{:S(2)}) collective-permute-start(bf16[512,2048]{1,0:T(8,128)(2,1)} %constant_dynamic-slice_fusion.2), channel_id=1, source_target_pairs={{0,1},{1,0},{2,3},{3,2},{4,5},{5,4},{6,7},{7,6},{8,9},{9,8},{10,11... | collective-permute-start | bytes 6291464 | tf_op jit(solution)/shard_map/ppermute | solution.py:27
  57.3 45.3 %copy-start.8 = (s32[8,8]{1,0:T(8,128)S(1)}, s32[8,8]{1,0:T(8,128)}, u32[]{:S(2)}) copy-start(s32[8,8]{1,0:T(8,128)} %param.10) | copy-start | bytes 772
  65.7 35.2 %collective-permute-start.14 = (bf16[1024,512]{1,0:T(8,128)(2,1)}, bf16[1024,512]{1,0:T(8,128)(2,1)}, u32[]{:S(2)}, u32[]{:S(2)}) collective-permute-start(bf16[1024,512]{1,0:T(8,128)(2,1)} %broadcast_select_fusion), channel_id=1, source_target_pairs={{0,4},{1,5},{2,6},{3,7},{4,0},{5,1},{6,2},{7,3},{8,12},{9,13},{10,... | collective-permute-start | bytes 3145736 | tf_op jit(solution)/shard_map/ppermute | solution.py:27
  79.8 31.3 %collective-permute-start.7 = (bf16[1024,512]{1,0:T(8,128)(2,1)S(1)}, bf16[1024,512]{1,0:T(8,128)(2,1)S(1)}, u32[]{:S(2)}, u32[]{:S(2)}) collective-permute-start(bf16[1024,512]{1,0:T(8,128)(2,1)S(1)} %broadcast_select_fusion.3), channel_id=1, source_target_pairs={{0,2},{1,3},{2,0},{3,1},{4,6},{5,7},{6,4},{7,5},{8,10},{9,11},{10,... | collective-permute-start | bytes 3145736 | tf_op jit(solution)/shard_map/ppermute | solution.py:27
  81.4 26.9 %collective-permute-start.9 = (bf16[1024,256]{1,0:T(8,128)(2,1)S(1)}, bf16[1024,256]{1,0:T(8,128)(2,1)S(1)}, u32[]{:S(2)}, u32[]{:S(2)}) collective-permute-start(bf16[1024,256]{1,0:T(8,128)(2,1)S(1)} %add.48), channel_id=1, source_target_pairs={{0,16},{1,17},{2,18},{3,19},{4,20},{5,21},{6,22},{7,23},{8,24},{9,... | collective-permute-start | bytes 1572872 | tf_op jit(solution)/shard_map/ppermute | solution.py:22
  101.1 29.0 %collective-permute-start.15 = (bf16[1024,512]{1,0:T(8,128)(2,1)S(1)}, bf16[1024,512]{1,0:T(8,128)(2,1)S(1)}, u32[]{:S(2)}, u32[]{:S(2)}) collective-permute-start(bf16[1024,512]{1,0:T(8,128)(2,1)S(1)} %broadcast_select_fusion.2), channel_id=1, source_target_pairs={{0,2},{1,3},{2,0},{3,1},{4,6},{5,7},{6,4},{7,5},{8,10},{9,11},{10,... | collective-permute-start | bytes 3145736 | tf_op jit(solution)/shard_map/ppermute | solution.py:27
  108.4 40.4 %collective-permute-start.12 = (bf16[1024,256]{1,0:T(8,128)(2,1)S(1)}, bf16[1024,256]{1,0:T(8,128)(2,1)S(1)}, u32[]{:S(2)}, u32[]{:S(2)}) collective-permute-start(bf16[1024,256]{1,0:T(8,128)(2,1)S(1)} %add.49), channel_id=1, source_target_pairs={{0,6},{1,7},{2,4},{3,5},{4,2},{5,3},{6,0},{7,1},{8,14},{9,15},{10,... | collective-permute-start | bytes 1572872 | tf_op jit(solution)/shard_map/ppermute | solution.py:27
  108.5 40.3 %collective-permute-start.11 = (bf16[1024,256]{1,0:T(8,128)(2,1)S(1)}, bf16[1024,256]{1,0:T(8,128)(2,1)S(1)}, u32[]{:S(2)}, u32[]{:S(2)}) collective-permute-start(bf16[1024,256]{1,0:T(8,128)(2,1)S(1)} %add.49), channel_id=1, source_target_pairs={{0,4},{1,5},{2,6},{3,7},{4,0},{5,1},{6,2},{7,3},{8,12},{9,13},{10,... | collective-permute-start | bytes 1572872 | tf_op jit(solution)/shard_map/ppermute | solution.py:27
  109.7 39.2 %collective-permute-start.10 = (bf16[1024,256]{1,0:T(8,128)(2,1)S(1)}, bf16[1024,256]{1,0:T(8,128)(2,1)S(1)}, u32[]{:S(2)}, u32[]{:S(2)}) collective-permute-start(bf16[1024,256]{1,0:T(8,128)(2,1)S(1)} %add.49), channel_id=1, source_target_pairs={{0,2},{1,3},{2,0},{3,1},{4,6},{5,7},{6,4},{7,5},{8,10},{9,11},{10,... | collective-permute-start | bytes 1572872 | tf_op jit(solution)/shard_map/ppermute | solution.py:27
  209.6 61.9 %copy-start.5 = (bf16[512,1024]{1,0:T(8,128)(2,1)S(1)}, bf16[512,1024]{1,0:T(8,128)(2,1)}, u32[]{:S(2)}) copy-start(bf16[512,1024]{1,0:T(8,128)(2,1)} %get-tuple-element.41) | copy-start | bytes 3145732
  209.6 61.9 %collective-permute-start.17 = (bf16[512,1024]{1,0:T(8,128)(2,1)}, bf16[512,1024]{1,0:T(8,128)(2,1)S(1)}, u32[]{:S(2)}, u32[]{:S(2)}) collective-permute-start(bf16[512,1024]{1,0:T(8,128)(2,1)} %get-tuple-element.42), channel_id=1, source_target_pairs={{0,1},{1,0},{2,3},{3,2},{4,5},{5,4},{6,7},{7,6},{8,9},{9,8},{10,11... | collective-permute-start | bytes 3145736 | tf_op jit(solution)/shard_map/ppermute | solution.py:27
  271.3 3.1 %copy-start.6 = (bf16[512,1024]{1,0:T(8,128)(2,1)S(1)}, bf16[512,1024]{1,0:T(8,128)(2,1)}, u32[]{:S(2)}) copy-start(bf16[512,1024]{1,0:T(8,128)(2,1)} %get-tuple-element.38) | copy-start | bytes 3145732
  271.3 3.1 %collective-permute-start.16 = (bf16[512,1024]{1,0:T(8,128)(2,1)}, bf16[512,1024]{1,0:T(8,128)(2,1)}, u32[]{:S(2)}, u32[]{:S(2)}) collective-permute-start(bf16[512,1024]{1,0:T(8,128)(2,1)} %get-tuple-element.39), channel_id=1, source_target_pairs={{0,1},{1,0},{2,3},{3,2},{4,5},{5,4},{6,7},{7,6},{8,9},{9,8},{10,11... | collective-permute-start | bytes 3145736 | tf_op jit(solution)/shard_map/ppermute | solution.py:27
  275.7 22.6 %copy-start.1 = (s32[8,8]{1,0:T(8,128)S(1)}, s32[8,8]{1,0:T(8,128)}, u32[]{:S(2)}) copy-start(s32[8,8]{1,0:T(8,128)} %param.9) | copy-start | bytes 772
  (5 other events, 7.2 us)

commit v10 on v9

--- a/solution.py
+++ b/solution.py
@@ -454,13 +454,17 @@
     if passes_on:
         upper = chip % plane >= 2
         stride = plane * pair
-        pairs = [(i, i + stride) for i in range(size - stride) if i // pair % plane >= 2]
-        before, risen = total, None
-        first_step = total + shifted(total, stride)
-        for c, w in enumerate(own):
-            risen = lax.ppermute(w if risen is None else after(w, risen), "ctx", pairs)
-            two_back[c] = crossed(after(jnp.where(upper, risen, w), before), 2 * pair)
-            before = (two_back[c], first_step)
+
+        def sent_on(value, half):
+            pairs = [(i, i + stride) for i in range(size - stride) if i // pair % plane // 2 == half]
+            return lax.ppermute(value, "ctx", pairs)
+
+        risen = sent_on(own[0], 1)
+        two_back[0] = crossed(after(jnp.where(upper, risen, own[0]), total), 2 * pair)
+        met = (two_back[0], total + shifted(total, stride))
+        for c in range(1, len(own)):
+            met = crossed(after(own[c], met), 2 * pair)
+            two_back[c] = jnp.where(upper, met, sent_on(met, 0))
     q_other = crossed(part(queries, 1, 1 - core), 1) if pair == 2 else None
     step = 1
     while step < chips // plane:
@@ -474,13 +478,16 @@
         windows = [own[c]]
         if passes_on:
             passed = jnp.where(chip % 2 == 0, own[c], two_back[c])
-            windows += [crossed(passed, pair), two_back[c]]
+            one_back = crossed(passed, pair)
+            if c == 0:
+                one_back = after(one_back, met)
+            windows += [one_back, two_back[c]]
         else:
             windows += [shifted(own[c], pair * d) for d in range(1, reach + 1)]
         all_windows.append(windows)
         sums.append(attention.over_slash(c * per_chunk, per_chunk, windows))
     gathered = [total] + [crossed(total, k * pair) for k in range(1, plane)]
-    gathered, sums = lax.optimization_barrier((gathered, sums))
+    gathered = after(gathered, (sums[0], two_back[1:]))
     kv_vert = jnp.concatenate(gathered, 0)
     near, far = [], []
     for c in range(chunks):

time: 299 us -> 288 us (0.963)
  starting transfers between devices: 32.6 us -> 15.4 us
  waiting for transfers between devices: 64.8 us -> 69.7 us
    ppermute x14, starting transfers between devices: 27.6 us -> 10.9 us  [crossed(): return lax.ppermute(value, 'ctx', [(i, i ^ bits) for i in range(size)])]
    ppermute x2, waiting for transfers between devices: 12.4 us -> 17.8 us  [shifted(): return lax.ppermute(value, 'ctx', [(i, i + by) for i in range(size - by)])]
  transfers between devices with their start and end apart: 18 -> 18, of which waited for: 9 -> 11; matrix products, arithmetic and copies ran while one was open for 4% -> 4% of each run, Pallas kernels for 32% -> 54%
where the time goes in v10:
time: 288 us; the launch traced here: 286 us
  Pallas kernels  159 us (55%)
  waiting for transfers between devices  69.7 us (24%)
  matrix products  22.9 us (8%)
  starting transfers between devices  15.4 us (5%)
  other arithmetic  9.42 us (3%)
  local copies, waits for them, and re-layouts  9.16 us (3%)
    pallas_call x2, Pallas kernels, over_vertical(): pl.pallas_call(functools.partial(vertical_kernel, cfg + (self.plane, self...  118 us
    ppermute x14, waiting for transfers between devices, crossed(): return lax.ppermute(value, 'ctx', [(i, i ^ bits) for i in range(size)])  50.6 us
    pallas_call x2, Pallas kernels, over_slash(): pl.pallas_call(functools.partial(slash_kernel, cfg), grid_spec=pltpu.Pref...  36.1 us
    dot_general x1, matrix products, body(): output = jnp.dot(attended, out_weight, preferred_element_type=jnp.float32)  22.9 us
    ppermute x2, waiting for transfers between devices, shifted(): return lax.ppermute(value, 'ctx', [(i, i + by) for i in range(size - by)])  17.8 us
    ppermute x14, starting transfers between devices, crossed(): return lax.ppermute(value, 'ctx', [(i, i ^ bits) for i in range(size)])  10.9 us
  transfers between devices with their start and end apart: 18, of which 11 were waited for; matrix products, arithmetic and copies ran while one was open for 4% of the time, Pallas kernels for 54%

profile of v10, /device:TPU:25, one launch (start us, length us, event | category | flops | bytes accessed | tf_op | source)
XLA Modules:
  0.0 285.8 jit_solution(716054014555872153)
XLA Ops:
  5.4 4.5 %prepare.1 = (bf16[1024,512]{1,0:T(8,128)(2,1)}, bf16[1024,512]{1,0:T(8,128)(2,1)}, bf16[1024,256]{1,0:T(8,128)(2,1)}, bf16[1024,256]{1,0:T(8,128)(2,1)}, bf16[1...) custom-call(s32[2]{0:T(128)} %pad_add_fusion.info, s32[4,8]{1,0:T(4,128)} %constant_dynamic-slice_fusion.4.vert, ...), custom_call_target="tpu_custom_call" | custom-call | bytes 8388608 | tf_op jit(solution)/shard_map/prepare/pallas_call | solution.py:86
  11.9 1.8 collective-permute-start.4
  13.7 10.3 %collective-permute-done.3 = bf16[1024,256]{1,0:T(8,128)(2,1)S(1)} collective-permute-done((bf16[1024,256]{1,0:T(8,128)(2,1)}, bf16[1024,256]{1,0:T(8,128)(2,1)S(1)}, u32[]{:S(2)}, u32[]{:S(2)}) %collective-permute-start.3) | collective-permute-done | bytes 524320 | tf_op jit(solution)/shard_map/ppermute | solution.py:27
  24.1 11.7 %collective-permute-done.4 = bf16[1024,256]{1,0:T(8,128)(2,1)S(1)} collective-permute-done((bf16[1024,256]{1,0:T(8,128)(2,1)}, bf16[1024,256]{1,0:T(8,128)(2,1)S(1)}, u32[]{:S(2)}, u32[]{:S(2)}) %collective-permute-start.4) | collective-permute-done | bytes 524320 | tf_op jit(solution)/shard_map/ppermute | solution.py:27
  38.0 2.4 broadcast_select_fusion.1
  40.4 3.2 %constant_dynamic-slice_fusion.2 = bf16[512,2048]{1,0:T(8,128)(2,1)} fusion(bf16[512,4096]{1,0:T(8,128)(2,1)} %refs_0_.9, s32[]{:T(128)S(6)} %select_n.89), kind=kLoop, calls=%fused_computation.27 | loop fusion | bytes 4194308 | tf_op jit(solution)/shard_map/dynamic_slice | solution.py:440
  43.6 1.7 collective-permute-start
  46.6 15.0 %collective-permute-done.8 = bf16[1024,256]{1,0:T(8,128)(2,1)S(1)} collective-permute-done((bf16[1024,256]{1,0:T(8,128)(2,1)S(1)}, bf16[1024,256]{1,0:T(8,128)(2,1)S(1)}, u32[]{:S(2)}, u32[]{:S(2)}) %collective-permute-start.8) | collective-permute-done | bytes 524320 | tf_op jit(solution)/shard_map/ppermute | solution.py:22
  61.7 2.3 collective-permute-done.6.refs_4_
  64.2 1.6 collective-permute-start.7
  67.1 19.8 %collective-permute-done.9 = bf16[1024,512]{1,0:T(8,128)(2,1)} collective-permute-done((bf16[1024,512]{1,0:T(8,128)(2,1)}, bf16[1024,512]{1,0:T(8,128)(2,1)}, u32[]{:S(2)}, u32[]{:S(2)}) %collective-permute-start.9) | collective-permute-done | bytes 1048608 | tf_op jit(solution)/shard_map/ppermute | solution.py:27
  89.5 2.9 %collective-permute-done.10 = bf16[1024,256]{1,0:T(8,128)(2,1)S(1)} collective-permute-done((bf16[1024,256]{1,0:T(8,128)(2,1)S(1)}, bf16[1024,256]{1,0:T(8,128)(2,1)S(1)}, u32[]{:S(2)}, u32[]{:S(2)}) %collective-permute-start.10) | collective-permute-done | bytes 524320 | tf_op jit(solution)/shard_map/ppermute | solution.py:22
  93.9 1.4 collective-permute-start.11
  95.3 18.0 %attend_slash.2.refs_5_ = f32[2,8,512,256]{3,2,1,0:T(8,128)} custom-call(s32[2]{0:T(128)} %pad_add_fusion.info, s32[4,8]{1,0:T(4,128)} %constant_dynamic-slice_fusion.3.slash, bf16[512,4096]{1,0:T(8,128)(2,1)} %refs_0_.9, bf16[512,2048]{1,0:T(8,128)(2,1)} %collective-permute-done.refs_1_, bf16[1024,512]{1,0:T(8,128)(2,1)} %get-tuple-element.22.refs_2_, ...), custom_call_target="tpu_custom_call" | custom-call | flops 8589934592 | bytes 10485760 | tf_op jit(solution)/shard_map/attend_slash/pallas_call | solution.py:362
  113.3 1.3 collective-permute-done.14
  114.6 2.5 broadcast_select_fusion.2
  117.1 1.5 collective-permute-done.12
  118.8 1.3 copy-done.7
  120.1 59.1 %attend_vertical.2 = (bf16[512,1024]{1,0:T(8,128)(2,1)}, bf16[512,1024]{1,0:T(8,128)(2,1)}) custom-call(s32[2]{0:T(128)} %pad_add_fusion.info, s32[4,8]{1,0:T(4,128)} %constant_dynamic-slice_fusion.4.vert, s32[4,8]{1,0:T(4,128)} %constant_dynamic-slice_fusion.3.slash, bf16[512,4096]{1,0:T(8,128)(2,1)} %refs_0_.9, ...), custom_call_target="tpu_custom_call" | custom-call | flops 8589934592 | bytes 10485760 | tf_op jit(solution)/shard_map/attend_vertical/pallas_call | solution.py:388
  181.1 18.1 %attend_slash.3.refs_5_ = f32[2,8,512,256]{3,2,1,0:T(8,128)} custom-call(s32[2]{0:T(128)} %pad_add_fusion.info, s32[4,8]{1,0:T(4,128)} %constant_dynamic-slice_fusion.3.slash, bf16[512,4096]{1,0:T(8,128)(2,1)} %refs_0_.9, bf16[512,2048]{1,0:T(8,128)(2,1)} %collective-permute-done.refs_1_, bf16[1024,512]{1,0:T(8,128)(2,1)} %get-tuple-element.29.refs_2_, ...), custom_call_target="tpu_custom_call" | custom-call | flops 8589934592 | bytes 10485760 | tf_op jit(solution)/shard_map/attend_slash/pallas_call | solution.py:362
  199.2 59.3 %attend_vertical.3 = (bf16[512,1024]{1,0:T(8,128)(2,1)}, bf16[512,1024]{1,0:T(8,128)(2,1)}) custom-call(s32[2]{0:T(128)} %pad_add_fusion.info, s32[4,8]{1,0:T(4,128)} %constant_dynamic-slice_fusion.4.vert, s32[4,8]{1,0:T(4,128)} %constant_dynamic-slice_fusion.3.slash, bf16[512,4096]{1,0:T(8,128)(2,1)} %refs_0_.9, ...), custom_call_target="tpu_custom_call" | custom-call | flops 8589934592 | bytes 10485760 | tf_op jit(solution)/shard_map/attend_vertical/pallas_call | solution.py:388
  258.7 2.8 collective-permute-done.17
  261.5 1.4 broadcast_select_fusion.6
  262.9 22.9 %convolution_convert_fusion = bf16[512,4096]{1,0:T(8,128)(2,1)} fusion(bf16[4096,4096]{1,0:T(8,128)(2,1)} %param.11, bf16[512,1024]{1,0:T(8,128)(2,1)S(1)} %get-tuple-element.44, bf16[512,1024]{1,0:T(8,128)(2,1)S(1)} %get-tuple-element.42, bf16[512,1024]{1,0:T(8,128)(2,1)S(1)} %get-tuple-element.43, bf16[512,1024]{1,0:T(8,128)(2,1)S(1)} %get-tuple-element.41), kind=kOutput, calls=%fused_computation | convolution fusion | flops 17198743552 | bytes 41943040 | tf_op jit(solution)/shard_map/dot_general | solution.py:503
  (62 shorter events, 18.9 us)
Async XLA Ops:
  1.4 3.0 %collective-permute-start.1 = (bf16[512,1024]{1,0:T(8,128)(2,1)S(1)}, bf16[512,1024]{1,0:T(8,128)(2,1)S(1)}, u32[]{:S(2)}, u32[]{:S(2)}) collective-permute-start(bf16[512,1024]{1,0:T(8,128)(2,1)S(1)} %pad_maximum_fusion), channel_id=1, source_target_pairs={{0,1},{1,0},{2,3},{3,2},{4,5},{5,4},{6,7},{7,6},{8,9},{9,8},{10,11... | collective-permute-start | bytes 3145736 | tf_op jit(solution)/shard_map/ppermute | solution.py:27
  9.9 28.0 %collective-permute-start.2 = (bf16[1024,512]{1,0:T(8,128)(2,1)}, bf16[1024,512]{1,0:T(8,128)(2,1)S(1)}, u32[]{:S(2)}, u32[]{:S(2)}) collective-permute-start(bf16[1024,512]{1,0:T(8,128)(2,1)} %get-tuple-element.22.refs_2_), channel_id=1, source_target_pairs={{4,12},{5,13},{6,14},{7,15},{12,20},{13,21},{14,22},{15,23},{20,28... | collective-permute-start | bytes 3145736 | tf_op jit(solution)/shard_map/ppermute | solution.py:460
  10.7 13.4 %collective-permute-start.3 = (bf16[1024,256]{1,0:T(8,128)(2,1)}, bf16[1024,256]{1,0:T(8,128)(2,1)S(1)}, u32[]{:S(2)}, u32[]{:S(2)}) collective-permute-start(bf16[1024,256]{1,0:T(8,128)(2,1)} %get-tuple-element.24), channel_id=1, source_target_pairs={{0,2},{1,3},{2,0},{3,1},{4,6},{5,7},{6,4},{7,5},{8,10},{9,11},{10,... | collective-permute-start | bytes 1572872 | tf_op jit(solution)/shard_map/ppermute | solution.py:27
  11.9 23.8 %collective-permute-start.4 = (bf16[1024,256]{1,0:T(8,128)(2,1)}, bf16[1024,256]{1,0:T(8,128)(2,1)S(1)}, u32[]{:S(2)}, u32[]{:S(2)}) collective-permute-start(bf16[1024,256]{1,0:T(8,128)(2,1)} %get-tuple-element.25), channel_id=1, source_target_pairs={{0,4},{1,5},{2,6},{3,7},{4,0},{5,1},{6,2},{7,3},{8,12},{9,13},{10,... | collective-permute-start | bytes 1572872 | tf_op jit(solution)/shard_map/ppermute | solution.py:27
  13.7 23.1 %collective-permute-start.5 = (bf16[1024,256]{1,0:T(8,128)(2,1)}, bf16[1024,256]{1,0:T(8,128)(2,1)S(1)}, u32[]{:S(2)}, u32[]{:S(2)}) collective-permute-start(bf16[1024,256]{1,0:T(8,128)(2,1)} %get-tuple-element.26), channel_id=1, source_target_pairs={{0,6},{1,7},{2,4},{3,5},{4,2},{5,3},{6,0},{7,1},{8,14},{9,15},{10,... | collective-permute-start | bytes 1572872 | tf_op jit(solution)/shard_map/ppermute | solution.py:27
  38.0 26.1 %copy-start.2 = (bf16[1024,512]{1,0:T(8,128)(2,1)S(1)}, bf16[1024,512]{1,0:T(8,128)(2,1)}, u32[]{:S(2)}) copy-start(bf16[1024,512]{1,0:T(8,128)(2,1)} %get-tuple-element.22.refs_2_) | copy-start | bytes 3145732
  40.4 23.6 %collective-permute-start.6 = (bf16[1024,512]{1,0:T(8,128)(2,1)}, bf16[1024,512]{1,0:T(8,128)(2,1)S(1)}, u32[]{:S(2)}, u32[]{:S(2)}) collective-permute-start(bf16[1024,512]{1,0:T(8,128)(2,1)} %broadcast_select_fusion.1), channel_id=1, source_target_pairs={{0,4},{1,5},{2,6},{3,7},{4,0},{5,1},{6,2},{7,3},{8,12},{9,13},{10,... | collective-permute-start | bytes 3145736 | tf_op jit(solution)/shard_map/ppermute | solution.py:27
  40.4 47.7 %copy-start.8 = (s32[8,8]{1,0:T(8,128)S(1)}, s32[8,8]{1,0:T(8,128)}, u32[]{:S(2)}) copy-start(s32[8,8]{1,0:T(8,128)} %param.10) | copy-start | bytes 772
  43.6 51.7 %collective-permute-start = (bf16[512,2048]{1,0:T(8,128)(2,1)}, bf16[512,2048]{1,0:T(8,128)(2,1)}, u32[]{:S(2)}, u32[]{:S(2)}) collective-permute-start(bf16[512,2048]{1,0:T(8,128)(2,1)} %constant_dynamic-slice_fusion.2), channel_id=1, source_target_pairs={{0,1},{1,0},{2,3},{3,2},{4,5},{5,4},{6,7},{7,6},{8,9},{9,8},{10,11... | collective-permute-start | bytes 6291464 | tf_op jit(solution)/shard_map/ppermute | solution.py:27
  45.3 16.3 %collective-permute-start.8 = (bf16[1024,256]{1,0:T(8,128)(2,1)S(1)}, bf16[1024,256]{1,0:T(8,128)(2,1)S(1)}, u32[]{:S(2)}, u32[]{:S(2)}) collective-permute-start(bf16[1024,256]{1,0:T(8,128)(2,1)S(1)} %add_add_fusion), channel_id=1, source_target_pairs={{0,8},{1,9},{2,10},{3,11},{4,12},{5,13},{6,14},{7,15},{8,16},{9,17... | collective-permute-start | bytes 1572872 | tf_op jit(solution)/shard_map/ppermute | solution.py:22
  64.0 31.2 %copy-start.6 = (bf16[1024,512]{1,0:T(8,128)(2,1)}, bf16[1024,512]{1,0:T(8,128)(2,1)S(1)}, u32[]{:S(2)}) copy-start(bf16[1024,512]{1,0:T(8,128)(2,1)S(1)} %collective-permute-done.6.refs_4_) | copy-start | bytes 3145732
  64.0 22.8 %collective-permute-start.9 = (bf16[1024,512]{1,0:T(8,128)(2,1)}, bf16[1024,512]{1,0:T(8,128)(2,1)}, u32[]{:S(2)}, u32[]{:S(2)}) collective-permute-start(bf16[1024,512]{1,0:T(8,128)(2,1)} %get-tuple-element.29.refs_2_), channel_id=1, source_target_pairs={{0,4},{1,5},{2,6},{3,7},{4,0},{5,1},{6,2},{7,3},{8,12},{9,13},{10,... | collective-permute-start | bytes 3145736 | tf_op jit(solution)/shard_map/ppermute | solution.py:27
  64.2 29.7 %collective-permute-start.7 = (bf16[1024,512]{1,0:T(8,128)(2,1)S(1)}, bf16[1024,512]{1,0:T(8,128)(2,1)S(1)}, u32[]{:S(2)}, u32[]{:S(2)}) collective-permute-start(bf16[1024,512]{1,0:T(8,128)(2,1)S(1)} %broadcast_select_fusion.3), channel_id=1, source_target_pairs={{0,2},{1,3},{2,0},{3,1},{4,6},{5,7},{6,4},{7,5},{8,10},{9,11},{10,... | collective-permute-start | bytes 3145736 | tf_op jit(solution)/shard_map/ppermute | solution.py:27
  65.8 26.6 %collective-permute-start.10 = (bf16[1024,256]{1,0:T(8,128)(2,1)S(1)}, bf16[1024,256]{1,0:T(8,128)(2,1)S(1)}, u32[]{:S(2)}, u32[]{:S(2)}) collective-permute-start(bf16[1024,256]{1,0:T(8,128)(2,1)S(1)} %add.48), channel_id=1, source_target_pairs={{0,16},{1,17},{2,18},{3,19},{4,20},{5,21},{6,22},{7,23},{8,24},{9,... | collective-permute-start | bytes 1572872 | tf_op jit(solution)/shard_map/ppermute | solution.py:22
  86.8 27.8 %collective-permute-start.14 = (bf16[1024,512]{1,0:T(8,128)(2,1)}, bf16[1024,512]{1,0:T(8,128)(2,1)S(1)}, u32[]{:S(2)}, u32[]{:S(2)}) collective-permute-start(bf16[1024,512]{1,0:T(8,128)(2,1)} %collective-permute-done.9), channel_id=1, source_target_pairs={{0,8},{1,9},{2,10},{3,11},{8,16},{9,17},{10,18},{11,19},{16,24},{1... | collective-permute-start | bytes 3145736 | tf_op jit(solution)/shard_map/ppermute | solution.py:460
  92.6 24.6 %collective-permute-start.13 = (bf16[1024,256]{1,0:T(8,128)(2,1)S(1)}, bf16[1024,256]{1,0:T(8,128)(2,1)S(1)}, u32[]{:S(2)}, u32[]{:S(2)}) collective-permute-start(bf16[1024,256]{1,0:T(8,128)(2,1)S(1)} %add.49), channel_id=1, source_target_pairs={{0,6},{1,7},{2,4},{3,5},{4,2},{5,3},{6,0},{7,1},{8,14},{9,15},{10,... | collective-permute-start | bytes 1572872 | tf_op jit(solution)/shard_map/ppermute | solution.py:27
  93.7 24.9 %collective-permute-start.12 = (bf16[1024,256]{1,0:T(8,128)(2,1)S(1)}, bf16[1024,256]{1,0:T(8,128)(2,1)S(1)}, u32[]{:S(2)}, u32[]{:S(2)}) collective-permute-start(bf16[1024,256]{1,0:T(8,128)(2,1)S(1)} %add.49), channel_id=1, source_target_pairs={{0,4},{1,5},{2,6},{3,7},{4,0},{5,1},{6,2},{7,3},{8,12},{9,13},{10,... | collective-permute-start | bytes 1572872 | tf_op jit(solution)/shard_map/ppermute | solution.py:27
  93.9 24.7 %collective-permute-start.11 = (bf16[1024,256]{1,0:T(8,128)(2,1)S(1)}, bf16[1024,256]{1,0:T(8,128)(2,1)S(1)}, u32[]{:S(2)}, u32[]{:S(2)}) collective-permute-start(bf16[1024,256]{1,0:T(8,128)(2,1)S(1)} %add.49), channel_id=1, source_target_pairs={{0,2},{1,3},{2,0},{3,1},{4,6},{5,7},{6,4},{7,5},{8,10},{9,11},{10,... | collective-permute-start | bytes 1572872 | tf_op jit(solution)/shard_map/ppermute | solution.py:27
  117.1 63.0 %collective-permute-start.16 = (bf16[1024,512]{1,0:T(8,128)(2,1)S(1)}, bf16[1024,512]{1,0:T(8,128)(2,1)S(1)}, u32[]{:S(2)}, u32[]{:S(2)}) collective-permute-start(bf16[1024,512]{1,0:T(8,128)(2,1)S(1)} %get-tuple-element.39), channel_id=1, source_target_pairs={{0,2},{1,3},{2,0},{3,1},{4,6},{5,7},{6,4},{7,5},{8,10},{9,11},{10,... | collective-permute-start | bytes 3145736 | tf_op jit(solution)/shard_map/ppermute | solution.py:27
  179.2 79.4 %collective-permute-start.15 = (bf16[512,1024]{1,0:T(8,128)(2,1)}, bf16[512,1024]{1,0:T(8,128)(2,1)S(1)}, u32[]{:S(2)}, u32[]{:S(2)}) collective-permute-start(bf16[512,1024]{1,0:T(8,128)(2,1)} %get-tuple-element.36), channel_id=1, source_target_pairs={{0,1},{1,0},{2,3},{3,2},{4,5},{5,4},{6,7},{7,6},{8,9},{9,8},{10,11... | collective-permute-start | bytes 3145736 | tf_op jit(solution)/shard_map/ppermute | solution.py:27
  199.2 59.4 %copy-start.4 = (bf16[512,1024]{1,0:T(8,128)(2,1)S(1)}, bf16[512,1024]{1,0:T(8,128)(2,1)}, u32[]{:S(2)}) copy-start(bf16[512,1024]{1,0:T(8,128)(2,1)} %get-tuple-element.35) | copy-start | bytes 3145732
  258.4 3.1 %copy-start.5 = (bf16[512,1024]{1,0:T(8,128)(2,1)S(1)}, bf16[512,1024]{1,0:T(8,128)(2,1)}, u32[]{:S(2)}) copy-start(bf16[512,1024]{1,0:T(8,128)(2,1)} %get-tuple-element.37) | copy-start | bytes 3145732
  258.4 3.1 %collective-permute-start.17 = (bf16[512,1024]{1,0:T(8,128)(2,1)}, bf16[512,1024]{1,0:T(8,128)(2,1)}, u32[]{:S(2)}, u32[]{:S(2)}) collective-permute-start(bf16[512,1024]{1,0:T(8,128)(2,1)} %get-tuple-element.38), channel_id=1, source_target_pairs={{0,1},{1,0},{2,3},{3,2},{4,5},{5,4},{6,7},{7,6},{8,9},{9,8},{10,11... | collective-permute-start | bytes 3145736 | tf_op jit(solution)/shard_map/ppermute | solution.py:27
  262.9 22.9 %copy-start.1 = (s32[8,8]{1,0:T(8,128)S(1)}, s32[8,8]{1,0:T(8,128)}, u32[]{:S(2)}) copy-start(s32[8,8]{1,0:T(8,128)} %param.9) | copy-start | bytes 772
  (5 other events, 7.4 us)

commit v11 on v10

--- a/solution.py
+++ b/solution.py
@@ -193,8 +193,8 @@
     w_refs, refs = refs[: reach + 1], refs[reach + 1 :]
     before, kv_vert, masks, refs = refs[0], refs[1], refs[2], refs[3:]
     out_refs, refs = refs[:pair], refs[pair:]
-    ke, ve, qx, res, good, acc = refs[:6]
-    ps, (kg, vg, sc, pg) = refs[6:8], refs[8:]
+    ke, ve, qx, res, good = refs[:5]
+    ps, (kg, vg, sc, pg) = refs[5:7], refs[7:]
     e = first + pl.program_id(0)
     chip, core = info[0], info[1]
     dev_rows = local * BLK
@@ -235,33 +235,28 @@
             qx[rows, :HD] = q_refs[slot][b * BLK : (b + 1) * BLK, g * HD : (g + 1) * HD]
             qx[rows, HD:] = mark
 
-    def stage(t, at, ahead, behind):
-        last = isinstance(t, int) and t == tiles
+    n_rows = ps[0].shape[0]
+
+    def stage(t, at, behind):
         if behind:
-            rows = slice((t - 1) * step, t * step)
-            if not isinstance(t, int):
-                rows = pl.ds(pl.multiple_of((t - 1) * step, step), step)
-            part = jnp.dot(ps[1 - at][...], ve[rows, :], preferred_element_type=jnp.float32)
-            acc[...] = acc[...] + part
-        else:
-            for i in range(chip_blocks):
-                acc[i * block_rows : (i + 1) * block_rows, :] = before[i]
-        if last:
+            part = jnp.dot(ps[1 - at][...], ve[...], preferred_element_type=jnp.float32)
+            for u in range(n_rows // block_rows):
+                i = (t - 1) * (n_rows // block_rows) + u
+                finish(i, before[i] + part[u * block_rows : (u + 1) * block_rows, :])
+        if t * n_rows == qx.shape[0]:
             return
-        cols = slice(t * step, (t + 1) * step)
-        if not isinstance(t, int):
-            cols = pl.ds(pl.multiple_of(t * step, step), step)
-        ps[at][...] = exponentials(qx[...], ke[:, cols], factor).astype(ps[at].dtype)
-
-    tiles = wide // step
-    pipelined(tiles, stage)
-    good[...] = jnp.ones(good.shape, good.dtype)
-    for i in range(chip_blocks):
-        rows = slice(i * block_rows, (i + 1) * block_rows)
-        total = acc[rows, HD:]
-        res[i] = (acc[rows, :HD] / total).astype(res.dtype)
+        q = qx[t * n_rows : (t + 1) * n_rows, :]
+        ps[at][...] = exponentials(q, ke[...], factor).astype(ps[at].dtype)
+
+    def finish(i, acc):
+        total = acc[:, HD:]
+        res[i] = (acc[:, :HD] / total).astype(res.dtype)
         fine = jnp.where((total > SMALLEST) & (total < LARGEST), 1.0, 0.0)
         good[...] = jnp.minimum(good[...], jnp.min(fine, axis=0, keepdims=True))
+
+    good[...] = jnp.ones(good.shape, good.dtype)
+    for t in range(qx.shape[0] // n_rows + 1):
+        stage(t, t % 2, t > 0)
 
     @pl.when(jnp.logical_not(jnp.min(good[...]) > 0.5))
     def _():
@@ -399,9 +394,8 @@
                     pltpu.VMEM((self.blocks * rows, 2 * HD), self.dtype),
                     pltpu.VMEM((self.blocks, rows, HD), self.dtype),
                     pltpu.VMEM((1, HD), jnp.float32),
-                    pltpu.VMEM((self.blocks * rows, 2 * HD), jnp.float32),
-                    pltpu.VMEM((self.blocks * rows, 2 * BLK), self.dtype),
-                    pltpu.VMEM((self.blocks * rows, 2 * BLK), self.dtype),
+                    pltpu.VMEM((self.blocks // 2 * rows, width), self.dtype),
+                    pltpu.VMEM((self.blocks // 2 * rows, width), self.dtype),
                     pltpu.VMEM((2 * HD, both), self.dtype),
                     pltpu.VMEM((both, 2 * HD), self.dtype),
                     pltpu.VMEM((rows, both), jnp.float32),
@@ -449,6 +443,10 @@
     total = listed[0]
     for k in range(1, plane):
         total = total + crossed(listed[k], k * pair)
+    q_other = None
+    if pair == 2:
+        q_other = crossed(after(part(queries, 1, 1 - core), own[0]), 1)
+        total = after(total, q_other)
     two_back = [None] * len(own)
     passes_on = pair == 2 and reach == 2 and plane == 4
     if passes_on:
@@ -465,7 +463,6 @@
         for c in range(1, len(own)):
             met = crossed(after(own[c], met), 2 * pair)
             two_back[c] = jnp.where(upper, met, sent_on(met, 0))
-    q_other = crossed(part(queries, 1, 1 - core), 1) if pair == 2 else None
     step = 1
     while step < chips // plane:
         total = total + shifted(total, step * plane * pair)

time: 288 us -> 289 us (level)
  transfers between devices with their start and end apart: 18 -> 18, of which waited for: 11 -> 9; matrix products, arithmetic and copies ran while one was open for 4% -> 4% of each run, Pallas kernels for 54% -> 54%
where the time goes in v11:
time: 289 us; the launch traced here: 286 us
  Pallas kernels  159 us (55%)
  waiting for transfers between devices  70.2 us (24%)
  matrix products  22.9 us (8%)
  starting transfers between devices  17.2 us (6%)
  other arithmetic  8.83 us (3%)
  local copies, waits for them, and re-layouts  7.72 us (3%)
    pallas_call x2, Pallas kernels, over_vertical(): pl.pallas_call(functools.partial(vertical_kernel, cfg + (self.plane, self...  118 us
    ppermute x14, waiting for transfers between devices, crossed(): return lax.ppermute(value, 'ctx', [(i, i ^ bits) for i in range(size)])  52.3 us
    pallas_call x2, Pallas kernels, over_slash(): pl.pallas_call(functools.partial(slash_kernel, cfg), grid_spec=pltpu.Pref...  36.1 us
    dot_general x1, matrix products, body(): output = jnp.dot(attended, out_weight, preferred_element_type=jnp.float32)  22.9 us
    ppermute x2, waiting for transfers between devices, shifted(): return lax.ppermute(value, 'ctx', [(i, i + by) for i in range(size - by)])  17.5 us
    ppermute x14, starting transfers between devices, crossed(): return lax.ppermute(value, 'ctx', [(i, i ^ bits) for i in range(size)])  11.6 us
  transfers between devices with their start and end apart: 18, of which 9 were waited for; matrix products, arithmetic and copies ran while one was open for 4% of the time, Pallas kernels for 54%

profile of v11, /device:TPU:25, one launch (start us, length us, event | category | flops | bytes accessed | tf_op | source)
XLA Modules:
  0.0 286.1 jit_solution(17135015390218641715)
XLA Ops:
  0.0 1.3 constant_dynamic-slice_fusion
  3.4 1.7 constant_dynamic-slice_fusion.2
  5.1 4.5 %prepare.1 = (bf16[1024,512]{1,0:T(8,128)(2,1)}, bf16[1024,512]{1,0:T(8,128)(2,1)}, bf16[1024,256]{1,0:T(8,128)(2,1)}, bf16[1024,256]{1,0:T(8,128)(2,1)}, bf16[1...) custom-call(s32[2]{0:T(128)} %pad_add_fusion.info, s32[4,8]{1,0:T(4,128)} %constant_dynamic-slice_fusion.4.vert, ...), custom_call_target="tpu_custom_call" | custom-call | bytes 8388608 | tf_op jit(solution)/shard_map/prepare/pallas_call | solution.py:86
  9.6 1.8 collective-permute-start.2
  14.1 10.9 %collective-permute-done.3 = bf16[1024,256]{1,0:T(8,128)(2,1)} collective-permute-done((bf16[1024,256]{1,0:T(8,128)(2,1)}, bf16[1024,256]{1,0:T(8,128)(2,1)}, u32[]{:S(2)}, u32[]{:S(2)}) %collective-permute-start.3) | collective-permute-done | bytes 524320 | tf_op jit(solution)/shard_map/ppermute | solution.py:27
  26.0 10.8 %collective-permute-done.5 = bf16[1024,256]{1,0:T(8,128)(2,1)} collective-permute-done((bf16[1024,256]{1,0:T(8,128)(2,1)}, bf16[1024,256]{1,0:T(8,128)(2,1)}, u32[]{:S(2)}, u32[]{:S(2)}) %collective-permute-start.5) | collective-permute-done | bytes 524320 | tf_op jit(solution)/shard_map/ppermute | solution.py:27
  36.9 1.6 add_add_fusion
  38.5 1.4 broadcast_select_fusion.1
  41.7 13.2 %collective-permute-done.8 = bf16[1024,256]{1,0:T(8,128)(2,1)S(1)} collective-permute-done((bf16[1024,256]{1,0:T(8,128)(2,1)S(1)}, bf16[1024,256]{1,0:T(8,128)(2,1)S(1)}, u32[]{:S(2)}, u32[]{:S(2)}) %collective-permute-start.8) | collective-permute-done | bytes 524320 | tf_op jit(solution)/shard_map/ppermute | solution.py:22
  55.0 7.9 %collective-permute-done.6.refs_4_ = bf16[1024,512]{1,0:T(8,128)(2,1)S(1)} collective-permute-done((bf16[1024,512]{1,0:T(8,128)(2,1)S(1)}, bf16[1024,512]{1,0:T(8,128)(2,1)S(1)}, u32[]{:S(2)}, u32[]{:S(2)}) %collective-permute-start.6) | collective-permute-done | bytes 1048608 | tf_op jit(solution)/shard_map/ppermute | solution.py:27
  63.1 2.1 collective-permute-start.7
  66.6 18.7 %collective-permute-done.9 = bf16[1024,512]{1,0:T(8,128)(2,1)} collective-permute-done((bf16[1024,512]{1,0:T(8,128)(2,1)}, bf16[1024,512]{1,0:T(8,128)(2,1)}, u32[]{:S(2)}, u32[]{:S(2)}) %collective-permute-start.9) | collective-permute-done | bytes 1048608 | tf_op jit(solution)/shard_map/ppermute | solution.py:27
  88.0 4.4 %collective-permute-done.10 = bf16[1024,256]{1,0:T(8,128)(2,1)S(1)} collective-permute-done((bf16[1024,256]{1,0:T(8,128)(2,1)S(1)}, bf16[1024,256]{1,0:T(8,128)(2,1)S(1)}, u32[]{:S(2)}, u32[]{:S(2)}) %collective-permute-start.10) | collective-permute-done | bytes 524320 | tf_op jit(solution)/shard_map/ppermute | solution.py:22
  93.2 2.1 collective-permute-start.11
  96.3 18.0 %attend_slash.2.refs_5_ = f32[2,8,512,256]{3,2,1,0:T(8,128)} custom-call(s32[2]{0:T(128)} %pad_add_fusion.info, s32[4,8]{1,0:T(4,128)} %constant_dynamic-slice_fusion.3.slash, bf16[512,4096]{1,0:T(8,128)(2,1)} %refs_0_.9, bf16[512,2048]{1,0:T(8,128)(2,1)} %collective-permute-done.1.refs_1_, bf16[1024,512]{1,0:T(8,128)(2,1)} %get-tuple-element.24.refs_2_, ...), custom_call_target="tpu_custom_call" | custom-call | flops 8589934592 | bytes 10485760 | tf_op jit(solution)/shard_map/attend_slash/pallas_call | solution.py:357
  114.7 2.5 broadcast_select_fusion.2
  117.4 1.3 copy-done.6
  118.7 59.2 %attend_vertical.2 = (bf16[512,1024]{1,0:T(8,128)(2,1)}, bf16[512,1024]{1,0:T(8,128)(2,1)}) custom-call(s32[2]{0:T(128)} %pad_add_fusion.info, s32[4,8]{1,0:T(4,128)} %constant_dynamic-slice_fusion.4.vert, s32[4,8]{1,0:T(4,128)} %constant_dynamic-slice_fusion.3.slash, bf16[512,4096]{1,0:T(8,128)(2,1)} %refs_0_.9, ...), custom_call_target="tpu_custom_call" | custom-call | flops 8589934592 | bytes 10485760 | tf_op jit(solution)/shard_map/attend_vertical/pallas_call | solution.py:383
  177.8 2.6 collective-permute-start.15
  181.4 18.1 %attend_slash.3.refs_5_ = f32[2,8,512,256]{3,2,1,0:T(8,128)} custom-call(s32[2]{0:T(128)} %pad_add_fusion.info, s32[4,8]{1,0:T(4,128)} %constant_dynamic-slice_fusion.3.slash, bf16[512,4096]{1,0:T(8,128)(2,1)} %refs_0_.9, bf16[512,2048]{1,0:T(8,128)(2,1)} %collective-permute-done.1.refs_1_, bf16[1024,512]{1,0:T(8,128)(2,1)} %get-tuple-element.33.refs_2_, ...), custom_call_target="tpu_custom_call" | custom-call | flops 8589934592 | bytes 10485760 | tf_op jit(solution)/shard_map/attend_slash/pallas_call | solution.py:357
  199.5 59.3 %attend_vertical.3 = (bf16[512,1024]{1,0:T(8,128)(2,1)}, bf16[512,1024]{1,0:T(8,128)(2,1)}) custom-call(s32[2]{0:T(128)} %pad_add_fusion.info, s32[4,8]{1,0:T(4,128)} %constant_dynamic-slice_fusion.4.vert, s32[4,8]{1,0:T(4,128)} %constant_dynamic-slice_fusion.3.slash, bf16[512,4096]{1,0:T(8,128)(2,1)} %refs_0_.9, ...), custom_call_target="tpu_custom_call" | custom-call | flops 8589934592 | bytes 10485760 | tf_op jit(solution)/shard_map/attend_vertical/pallas_call | solution.py:383
  259.0 2.8 collective-permute-done.17
  261.8 1.4 broadcast_select_fusion.6
  263.2 22.9 %convolution_convert_fusion = bf16[512,4096]{1,0:T(8,128)(2,1)} fusion(bf16[4096,4096]{1,0:T(8,128)(2,1)} %param.11, bf16[512,1024]{1,0:T(8,128)(2,1)S(1)} %get-tuple-element.48, bf16[512,1024]{1,0:T(8,128)(2,1)S(1)} %get-tuple-element.46, bf16[512,1024]{1,0:T(8,128)(2,1)S(1)} %get-tuple-element.47, bf16[512,1024]{1,0:T(8,128)(2,1)S(1)} %get-tuple-element.45), kind=kOutput, calls=%fused_computation | convolution fusion | flops 17198743552 | bytes 41943040 | tf_op jit(solution)/shard_map/dot_general | solution.py:500
  (60 shorter events, 15.6 us)
Async XLA Ops:
  1.4 3.7 %collective-permute-start = (bf16[512,1024]{1,0:T(8,128)(2,1)S(1)}, bf16[512,1024]{1,0:T(8,128)(2,1)}, u32[]{:S(2)}, u32[]{:S(2)}) collective-permute-start(bf16[512,1024]{1,0:T(8,128)(2,1)S(1)} %pad_maximum_fusion), channel_id=1, source_target_pairs={{0,1},{1,0},{2,3},{3,2},{4,5},{5,4},{6,7},{7,6},{8,9},{9,8},{10,11... | collective-permute-start | bytes 3145736 | tf_op jit(solution)/shard_map/ppermute | solution.py:27
  9.6 53.4 %copy-start.2 = (bf16[1024,512]{1,0:T(8,128)(2,1)S(1)}, bf16[1024,512]{1,0:T(8,128)(2,1)}, u32[]{:S(2)}) copy-start(bf16[1024,512]{1,0:T(8,128)(2,1)} %get-tuple-element.24.refs_2_) | copy-start | bytes 3145732
  9.6 30.3 %collective-permute-start.1 = (bf16[512,2048]{1,0:T(8,128)(2,1)S(1)}, bf16[512,2048]{1,0:T(8,128)(2,1)}, u32[]{:S(2)}, u32[]{:S(2)}) collective-permute-start(bf16[512,2048]{1,0:T(8,128)(2,1)S(1)} %constant_dynamic-slice_fusion.2), channel_id=1, source_target_pairs={{0,1},{1,0},{2,3},{3,2},{4,5},{5,4},{6,7},{7,6},{8,9},{9,8},{10,11... | collective-permute-start | bytes 6291464 | tf_op jit(solution)/shard_map/ppermute | solution.py:27
  9.6 28.9 %collective-permute-start.2 = (bf16[1024,512]{1,0:T(8,128)(2,1)}, bf16[1024,512]{1,0:T(8,128)(2,1)}, u32[]{:S(2)}, u32[]{:S(2)}) collective-permute-start(bf16[1024,512]{1,0:T(8,128)(2,1)} %get-tuple-element.24.refs_2_), channel_id=1, source_target_pairs={{4,12},{5,13},{6,14},{7,15},{12,20},{13,21},{14,22},{15,23},{20,28... | collective-permute-start | bytes 3145736 | tf_op jit(solution)/shard_map/ppermute | solution.py:458
  11.4 13.5 %collective-permute-start.3 = (bf16[1024,256]{1,0:T(8,128)(2,1)}, bf16[1024,256]{1,0:T(8,128)(2,1)}, u32[]{:S(2)}, u32[]{:S(2)}) collective-permute-start(bf16[1024,256]{1,0:T(8,128)(2,1)} %get-tuple-element.27), channel_id=1, source_target_pairs={{0,2},{1,3},{2,0},{3,1},{4,6},{5,7},{6,4},{7,5},{8,10},{9,11},{10,... | collective-permute-start | bytes 1572872 | tf_op jit(solution)/shard_map/ppermute | solution.py:27
  12.6 13.4 %collective-permute-start.4 = (bf16[1024,256]{1,0:T(8,128)(2,1)}, bf16[1024,256]{1,0:T(8,128)(2,1)}, u32[]{:S(2)}, u32[]{:S(2)}) collective-permute-start(bf16[1024,256]{1,0:T(8,128)(2,1)} %get-tuple-element.28), channel_id=1, source_target_pairs={{0,4},{1,5},{2,6},{3,7},{4,0},{5,1},{6,2},{7,3},{8,12},{9,13},{10,... | collective-permute-start | bytes 1572872 | tf_op jit(solution)/shard_map/ppermute | solution.py:27
  13.6 23.3 %collective-permute-start.5 = (bf16[1024,256]{1,0:T(8,128)(2,1)}, bf16[1024,256]{1,0:T(8,128)(2,1)}, u32[]{:S(2)}, u32[]{:S(2)}) collective-permute-start(bf16[1024,256]{1,0:T(8,128)(2,1)} %get-tuple-element.29), channel_id=1, source_target_pairs={{0,6},{1,7},{2,4},{3,5},{4,2},{5,3},{6,0},{7,1},{8,14},{9,15},{10,... | collective-permute-start | bytes 1572872 | tf_op jit(solution)/shard_map/ppermute | solution.py:27
  38.5 48.1 %copy-start.7 = (s32[8,8]{1,0:T(8,128)S(1)}, s32[8,8]{1,0:T(8,128)}, u32[]{:S(2)}) copy-start(s32[8,8]{1,0:T(8,128)} %param.10) | copy-start | bytes 772
  39.9 23.1 %collective-permute-start.6 = (bf16[1024,512]{1,0:T(8,128)(2,1)S(1)}, bf16[1024,512]{1,0:T(8,128)(2,1)S(1)}, u32[]{:S(2)}, u32[]{:S(2)}) collective-permute-start(bf16[1024,512]{1,0:T(8,128)(2,1)S(1)} %broadcast_select_fusion.1), channel_id=1, source_target_pairs={{0,4},{1,5},{2,6},{3,7},{4,0},{5,1},{6,2},{7,3},{8,12},{9,13},{10,... | collective-permute-start | bytes 3145736 | tf_op jit(solution)/shard_map/ppermute | solution.py:27
  40.5 14.4 %collective-permute-start.8 = (bf16[1024,256]{1,0:T(8,128)(2,1)S(1)}, bf16[1024,256]{1,0:T(8,128)(2,1)S(1)}, u32[]{:S(2)}, u32[]{:S(2)}) collective-permute-start(bf16[1024,256]{1,0:T(8,128)(2,1)S(1)} %add_add_fusion), channel_id=1, source_target_pairs={{0,8},{1,9},{2,10},{3,11},{4,12},{5,13},{6,14},{7,15},{8,16},{9,17... | collective-permute-start | bytes 1572872 | tf_op jit(solution)/shard_map/ppermute | solution.py:22
  62.9 32.4 %copy-start.5 = (bf16[1024,512]{1,0:T(8,128)(2,1)}, bf16[1024,512]{1,0:T(8,128)(2,1)S(1)}, u32[]{:S(2)}) copy-start(bf16[1024,512]{1,0:T(8,128)(2,1)S(1)} %collective-permute-done.6.refs_4_) | copy-start | bytes 3145732
  62.9 22.4 %collective-permute-start.9 = (bf16[1024,512]{1,0:T(8,128)(2,1)}, bf16[1024,512]{1,0:T(8,128)(2,1)}, u32[]{:S(2)}, u32[]{:S(2)}) collective-permute-start(bf16[1024,512]{1,0:T(8,128)(2,1)} %get-tuple-element.33.refs_2_), channel_id=1, source_target_pairs={{0,4},{1,5},{2,6},{3,7},{4,0},{5,1},{6,2},{7,3},{8,12},{9,13},{10,... | collective-permute-start | bytes 3145736 | tf_op jit(solution)/shard_map/ppermute | solution.py:27
  63.1 32.1 %collective-permute-start.7 = (bf16[1024,512]{1,0:T(8,128)(2,1)S(1)}, bf16[1024,512]{1,0:T(8,128)(2,1)S(1)}, u32[]{:S(2)}, u32[]{:S(2)}) collective-permute-start(bf16[1024,512]{1,0:T(8,128)(2,1)S(1)} %broadcast_select_fusion.3), channel_id=1, source_target_pairs={{0,2},{1,3},{2,0},{3,1},{4,6},{5,7},{6,4},{7,5},{8,10},{9,11},{10,... | collective-permute-start | bytes 3145736 | tf_op jit(solution)/shard_map/ppermute | solution.py:27
  65.3 27.1 %collective-permute-start.10 = (bf16[1024,256]{1,0:T(8,128)(2,1)S(1)}, bf16[1024,256]{1,0:T(8,128)(2,1)S(1)}, u32[]{:S(2)}, u32[]{:S(2)}) collective-permute-start(bf16[1024,256]{1,0:T(8,128)(2,1)S(1)} %add.48), channel_id=1, source_target_pairs={{0,16},{1,17},{2,18},{3,19},{4,20},{5,21},{6,22},{7,23},{8,24},{9,... | collective-permute-start | bytes 1572872 | tf_op jit(solution)/shard_map/ppermute | solution.py:22
  85.3 29.3 %collective-permute-start.14 = (bf16[1024,512]{1,0:T(8,128)(2,1)}, bf16[1024,512]{1,0:T(8,128)(2,1)S(1)}, u32[]{:S(2)}, u32[]{:S(2)}) collective-permute-start(bf16[1024,512]{1,0:T(8,128)(2,1)} %collective-permute-done.9), channel_id=1, source_target_pairs={{0,8},{1,9},{2,10},{3,11},{8,16},{9,17},{10,18},{11,19},{16,24},{1... | collective-permute-start | bytes 3145736 | tf_op jit(solution)/shard_map/ppermute | solution.py:458
  92.6 24.6 %collective-permute-start.13 = (bf16[1024,256]{1,0:T(8,128)(2,1)S(1)}, bf16[1024,256]{1,0:T(8,128)(2,1)S(1)}, u32[]{:S(2)}, u32[]{:S(2)}) collective-permute-start(bf16[1024,256]{1,0:T(8,128)(2,1)S(1)} %add.49), channel_id=1, source_target_pairs={{0,6},{1,7},{2,4},{3,5},{4,2},{5,3},{6,0},{7,1},{8,14},{9,15},{10,... | collective-permute-start | bytes 1572872 | tf_op jit(solution)/shard_map/ppermute | solution.py:27
  92.7 24.5 %collective-permute-start.12 = (bf16[1024,256]{1,0:T(8,128)(2,1)S(1)}, bf16[1024,256]{1,0:T(8,128)(2,1)S(1)}, u32[]{:S(2)}, u32[]{:S(2)}) collective-permute-start(bf16[1024,256]{1,0:T(8,128)(2,1)S(1)} %add.49), channel_id=1, source_target_pairs={{0,4},{1,5},{2,6},{3,7},{4,0},{5,1},{6,2},{7,3},{8,12},{9,13},{10,... | collective-permute-start | bytes 1572872 | tf_op jit(solution)/shard_map/ppermute | solution.py:27
  93.2 24.0 %collective-permute-start.11 = (bf16[1024,256]{1,0:T(8,128)(2,1)S(1)}, bf16[1024,256]{1,0:T(8,128)(2,1)S(1)}, u32[]{:S(2)}, u32[]{:S(2)}) collective-permute-start(bf16[1024,256]{1,0:T(8,128)(2,1)S(1)} %add.49), channel_id=1, source_target_pairs={{0,2},{1,3},{2,0},{3,1},{4,6},{5,7},{6,4},{7,5},{8,10},{9,11},{10,... | collective-permute-start | bytes 1572872 | tf_op jit(solution)/shard_map/ppermute | solution.py:27
  117.2 63.2 %collective-permute-start.16 = (bf16[1024,512]{1,0:T(8,128)(2,1)S(1)}, bf16[1024,512]{1,0:T(8,128)(2,1)S(1)}, u32[]{:S(2)}, u32[]{:S(2)}) collective-permute-start(bf16[1024,512]{1,0:T(8,128)(2,1)S(1)} %get-tuple-element.43), channel_id=1, source_target_pairs={{0,2},{1,3},{2,0},{3,1},{4,6},{5,7},{6,4},{7,5},{8,10},{9,11},{10,... | collective-permute-start | bytes 3145736 | tf_op jit(solution)/shard_map/ppermute | solution.py:27
  177.8 81.0 %collective-permute-start.15 = (bf16[512,1024]{1,0:T(8,128)(2,1)}, bf16[512,1024]{1,0:T(8,128)(2,1)S(1)}, u32[]{:S(2)}, u32[]{:S(2)}) collective-permute-start(bf16[512,1024]{1,0:T(8,128)(2,1)} %get-tuple-element.40), channel_id=1, source_target_pairs={{0,1},{1,0},{2,3},{3,2},{4,5},{5,4},{6,7},{7,6},{8,9},{9,8},{10,11... | collective-permute-start | bytes 3145736 | tf_op jit(solution)/shard_map/ppermute | solution.py:27
  199.5 59.4 %copy-start.3 = (bf16[512,1024]{1,0:T(8,128)(2,1)S(1)}, bf16[512,1024]{1,0:T(8,128)(2,1)}, u32[]{:S(2)}) copy-start(bf16[512,1024]{1,0:T(8,128)(2,1)} %get-tuple-element.39) | copy-start | bytes 3145732
  258.7 3.1 %copy-start.4 = (bf16[512,1024]{1,0:T(8,128)(2,1)S(1)}, bf16[512,1024]{1,0:T(8,128)(2,1)}, u32[]{:S(2)}) copy-start(bf16[512,1024]{1,0:T(8,128)(2,1)} %get-tuple-element.41) | copy-start | bytes 3145732
  258.7 3.1 %collective-permute-start.17 = (bf16[512,1024]{1,0:T(8,128)(2,1)}, bf16[512,1024]{1,0:T(8,128)(2,1)}, u32[]{:S(2)}, u32[]{:S(2)}) collective-permute-start(bf16[512,1024]{1,0:T(8,128)(2,1)} %get-tuple-element.42), channel_id=1, source_target_pairs={{0,1},{1,0},{2,3},{3,2},{4,5},{5,4},{6,7},{7,6},{8,9},{9,8},{10,11... | collective-permute-start | bytes 3145736 | tf_op jit(solution)/shard_map/ppermute | solution.py:27
  263.2 22.9 %copy-start.1 = (s32[8,8]{1,0:T(8,128)S(1)}, s32[8,8]{1,0:T(8,128)}, u32[]{:S(2)}) copy-start(s32[8,8]{1,0:T(8,128)} %param.9) | copy-start | bytes 772
  (4 other events, 6.1 us)

commit v12 on v11

--- a/solution.py
+++ b/solution.py
@@ -447,6 +447,7 @@
     if pair == 2:
         q_other = crossed(after(part(queries, 1, 1 - core), own[0]), 1)
         total = after(total, q_other)
+    steps = [2**n for n in reversed(range((chips // plane - 1).bit_length()))]
     two_back = [None] * len(own)
     passes_on = pair == 2 and reach == 2 and plane == 4
     if passes_on:
@@ -459,14 +460,13 @@
 
         risen = sent_on(own[0], 1)
         two_back[0] = crossed(after(jnp.where(upper, risen, own[0]), total), 2 * pair)
-        met = (two_back[0], total + shifted(total, stride))
+        first_step = total + shifted(total, steps[0] * stride) if steps else total
+        met = two_back[0]
         for c in range(1, len(own)):
             met = crossed(after(own[c], met), 2 * pair)
             two_back[c] = jnp.where(upper, met, sent_on(met, 0))
-    step = 1
-    while step < chips // plane:
-        total = total + shifted(total, step * plane * pair)
-        step *= 2
+    for n in steps:
+        total = total + shifted(total, n * plane * pair)
 
     attention = Attention(queries, q_other, info, vert, slash, masks, heads, local, plane)
     chunks = heads // per_chunk
@@ -475,6 +475,8 @@
         windows = [own[c]]
         if passes_on:
             passed = jnp.where(chip % 2 == 0, own[c], two_back[c])
+            if c == 0:
+                passed = after(passed, first_step)
             one_back = crossed(passed, pair)
             if c == 0:
                 one_back = after(one_back, met)

time: 289 us -> 291 us (level)
    ppermute x2, waiting for transfers between devices: 17.5 us -> 3.13 us  [shifted(): return lax.ppermute(value, 'ctx', [(i, i + by) for i in range(size - by)])]
    ppermute x14, waiting for transfers between devices: 52.3 us -> 64.6 us  [crossed(): return lax.ppermute(value, 'ctx', [(i, i ^ bits) for i in range(size)])]
where the time goes in v12:
time: 291 us; the launch traced here: 286 us
  Pallas kernels  159 us (55%)
  waiting for transfers between devices  67.7 us (23%)
  matrix products  22.9 us (8%)
  starting transfers between devices  16.5 us (6%)
  local copies, waits for them, and re-layouts  10.1 us (3%)
  other arithmetic  9.75 us (3%)
    pallas_call x2, Pallas kernels, over_vertical(): pl.pallas_call(functools.partial(vertical_kernel, cfg + (self.plane, self...  118 us
    ppermute x14, waiting for transfers between devices, crossed(): return lax.ppermute(value, 'ctx', [(i, i ^ bits) for i in range(size)])  64.6 us
    pallas_call x2, Pallas kernels, over_slash(): pl.pallas_call(functools.partial(slash_kernel, cfg), grid_spec=pltpu.Pref...  36.1 us
    dot_general x1, matrix products, body(): output = jnp.dot(attended, out_weight, preferred_element_type=jnp.float32)  22.9 us
    ppermute x14, starting transfers between devices, crossed(): return lax.ppermute(value, 'ctx', [(i, i ^ bits) for i in range(size)])  11.8 us
  transfers between devices with their start and end apart: 18, of which 9 were waited for; matrix products, arithmetic and copies ran while one was open for 4% of the time, Pallas kernels for 54%

profile of v12, /device:TPU:25, one launch (start us, length us, event | category | flops | bytes accessed | tf_op | source)
XLA Modules:
  0.0 286.1 jit_solution(13374985577639588576)
XLA Ops:
  0.0 1.3 constant_dynamic-slice_fusion
  3.3 3.2 %constant_dynamic-slice_fusion.2 = bf16[512,2048]{1,0:T(8,128)(2,1)} fusion(bf16[512,4096]{1,0:T(8,128)(2,1)} %refs_0_.9, s32[]{:T(128)S(6)} %select_n.89), kind=kLoop, calls=%fused_computation.27 | loop fusion | bytes 4194308 | tf_op jit(solution)/shard_map/dynamic_slice | solution.py:434
  7.5 4.5 %prepare.1 = (bf16[1024,512]{1,0:T(8,128)(2,1)}, bf16[1024,512]{1,0:T(8,128)(2,1)}, bf16[1024,256]{1,0:T(8,128)(2,1)}, bf16[1024,256]{1,0:T(8,128)(2,1)}, bf16[1...) custom-call(s32[2]{0:T(128)} %pad_add_fusion.info, s32[4,8]{1,0:T(4,128)} %constant_dynamic-slice_fusion.4.vert, ...), custom_call_target="tpu_custom_call" | custom-call | bytes 8388608 | tf_op jit(solution)/shard_map/prepare/pallas_call | solution.py:86
  14.1 1.8 collective-permute-start.4
  15.9 10.4 %collective-permute-done.3 = bf16[1024,256]{1,0:T(8,128)(2,1)S(1)} collective-permute-done((bf16[1024,256]{1,0:T(8,128)(2,1)}, bf16[1024,256]{1,0:T(8,128)(2,1)S(1)}, u32[]{:S(2)}, u32[]{:S(2)}) %collective-permute-start.3) | collective-permute-done | bytes 524320 | tf_op jit(solution)/shard_map/ppermute | solution.py:27
  26.3 11.7 %collective-permute-done.4 = bf16[1024,256]{1,0:T(8,128)(2,1)S(1)} collective-permute-done((bf16[1024,256]{1,0:T(8,128)(2,1)}, bf16[1024,256]{1,0:T(8,128)(2,1)S(1)}, u32[]{:S(2)}, u32[]{:S(2)}) %collective-permute-start.4) | collective-permute-done | bytes 524320 | tf_op jit(solution)/shard_map/ppermute | solution.py:27
  39.2 1.5 add_add_fusion
  40.7 1.4 broadcast_select_fusion.1
  42.8 1.3 collective-permute-start.7
  44.1 21.6 %collective-permute-done.6.refs_4_ = bf16[1024,512]{1,0:T(8,128)(2,1)S(1)} collective-permute-done((bf16[1024,512]{1,0:T(8,128)(2,1)S(1)}, bf16[1024,512]{1,0:T(8,128)(2,1)S(1)}, u32[]{:S(2)}, u32[]{:S(2)}) %collective-permute-start.6) | collective-permute-done | bytes 1048608 | tf_op jit(solution)/shard_map/ppermute | solution.py:27
  66.1 3.1 %collective-permute-done.7 = bf16[1024,256]{1,0:T(8,128)(2,1)} collective-permute-done((bf16[1024,256]{1,0:T(8,128)(2,1)S(1)}, bf16[1024,256]{1,0:T(8,128)(2,1)}, u32[]{:S(2)}, u32[]{:S(2)}) %collective-permute-start.7) | collective-permute-done | bytes 524320 | tf_op jit(solution)/shard_map/ppermute | solution.py:22
  72.5 16.1 %collective-permute-done.9 = bf16[1024,512]{1,0:T(8,128)(2,1)} collective-permute-done((bf16[1024,512]{1,0:T(8,128)(2,1)}, bf16[1024,512]{1,0:T(8,128)(2,1)}, u32[]{:S(2)}, u32[]{:S(2)}) %collective-permute-start.9) | collective-permute-done | bytes 1048608 | tf_op jit(solution)/shard_map/ppermute | solution.py:27
  88.6 1.3 collective-permute-start.14
  92.0 2.0 collective-permute-start.12
  95.1 18.0 %attend_slash.2.refs_5_ = f32[2,8,512,256]{3,2,1,0:T(8,128)} custom-call(s32[2]{0:T(128)} %pad_add_fusion.info, s32[4,8]{1,0:T(4,128)} %constant_dynamic-slice_fusion.3.slash, bf16[512,4096]{1,0:T(8,128)(2,1)} %refs_0_.9, bf16[512,2048]{1,0:T(8,128)(2,1)} %collective-permute-done.1.refs_1_, bf16[1024,512]{1,0:T(8,128)(2,1)} %get-tuple-element.25.refs_2_, ...), custom_call_target="tpu_custom_call" | custom-call | flops 8589934592 | bytes 10485760 | tf_op jit(solution)/shard_map/attend_slash/pallas_call | solution.py:357
  113.1 2.5 broadcast_select_fusion.2
  116.8 1.3 copy-done.8
  118.2 59.2 %attend_vertical.2 = (bf16[512,1024]{1,0:T(8,128)(2,1)}, bf16[512,1024]{1,0:T(8,128)(2,1)}) custom-call(s32[2]{0:T(128)} %pad_add_fusion.info, s32[4,8]{1,0:T(4,128)} %constant_dynamic-slice_fusion.4.vert, s32[4,8]{1,0:T(4,128)} %constant_dynamic-slice_fusion.3.slash, bf16[512,4096]{1,0:T(8,128)(2,1)} %refs_0_.9, ...), custom_call_target="tpu_custom_call" | custom-call | flops 8589934592 | bytes 10485760 | tf_op jit(solution)/shard_map/attend_vertical/pallas_call | solution.py:383
  177.3 3.1 %collective-permute-start.15 = (bf16[512,1024]{1,0:T(8,128)(2,1)}, bf16[512,1024]{1,0:T(8,128)(2,1)S(1)}, u32[]{:S(2)}, u32[]{:S(2)}) collective-permute-start(bf16[512,1024]{1,0:T(8,128)(2,1)} %get-tuple-element.42), channel_id=1, source_target_pairs={{0,1},{1,0},{2,3},{3,2},{4,5},{5,4},{6,7},{7,6},{8,9},{9,8},{10,11... | collective-permute-start | bytes 3145736 | tf_op jit(solution)/shard_map/ppermute | solution.py:27
  181.4 18.1 %attend_slash.3.refs_5_ = f32[2,8,512,256]{3,2,1,0:T(8,128)} custom-call(s32[2]{0:T(128)} %pad_add_fusion.info, s32[4,8]{1,0:T(4,128)} %constant_dynamic-slice_fusion.3.slash, bf16[512,4096]{1,0:T(8,128)(2,1)} %refs_0_.9, bf16[512,2048]{1,0:T(8,128)(2,1)} %collective-permute-done.1.refs_1_, bf16[1024,512]{1,0:T(8,128)(2,1)} %get-tuple-element.35.refs_2_, ...), custom_call_target="tpu_custom_call" | custom-call | flops 8589934592 | bytes 10485760 | tf_op jit(solution)/shard_map/attend_slash/pallas_call | solution.py:357
  199.5 59.3 %attend_vertical.3 = (bf16[512,1024]{1,0:T(8,128)(2,1)}, bf16[512,1024]{1,0:T(8,128)(2,1)}) custom-call(s32[2]{0:T(128)} %pad_add_fusion.info, s32[4,8]{1,0:T(4,128)} %constant_dynamic-slice_fusion.4.vert, s32[4,8]{1,0:T(4,128)} %constant_dynamic-slice_fusion.3.slash, bf16[512,4096]{1,0:T(8,128)(2,1)} %refs_0_.9, ...), custom_call_target="tpu_custom_call" | custom-call | flops 8589934592 | bytes 10485760 | tf_op jit(solution)/shard_map/attend_vertical/pallas_call | solution.py:383
  259.0 2.8 collective-permute-done.17
  261.9 1.4 broadcast_select_fusion.6
  263.2 22.9 %convolution_convert_fusion = bf16[512,4096]{1,0:T(8,128)(2,1)} fusion(bf16[4096,4096]{1,0:T(8,128)(2,1)} %param.11, bf16[512,1024]{1,0:T(8,128)(2,1)S(1)} %get-tuple-element.50, bf16[512,1024]{1,0:T(8,128)(2,1)S(1)} %get-tuple-element.48, bf16[512,1024]{1,0:T(8,128)(2,1)S(1)} %get-tuple-element.49, bf16[512,1024]{1,0:T(8,128)(2,1)S(1)} %get-tuple-element.47), kind=kOutput, calls=%fused_computation | convolution fusion | flops 17198743552 | bytes 41943040 | tf_op jit(solution)/shard_map/dot_general | solution.py:502
  (64 shorter events, 16.4 us)
Async XLA Ops:
  1.4 5.1 %collective-permute-start = (bf16[512,1024]{1,0:T(8,128)(2,1)S(1)}, bf16[512,1024]{1,0:T(8,128)(2,1)S(1)}, u32[]{:S(2)}, u32[]{:S(2)}) collective-permute-start(bf16[512,1024]{1,0:T(8,128)(2,1)S(1)} %pad_maximum_fusion), channel_id=1, source_target_pairs={{0,1},{1,0},{2,3},{3,2},{4,5},{5,4},{6,7},{7,6},{8,9},{9,8},{10,11... | collective-permute-start | bytes 3145736 | tf_op jit(solution)/shard_map/ppermute | solution.py:27
  11.9 58.5 %copy-start.2 = (bf16[1024,512]{1,0:T(8,128)(2,1)S(1)}, bf16[1024,512]{1,0:T(8,128)(2,1)}, u32[]{:S(2)}) copy-start(bf16[1024,512]{1,0:T(8,128)(2,1)} %get-tuple-element.25.refs_2_) | copy-start | bytes 3145732
  11.9 30.1 %collective-permute-start.1 = (bf16[512,2048]{1,0:T(8,128)(2,1)}, bf16[512,2048]{1,0:T(8,128)(2,1)}, u32[]{:S(2)}, u32[]{:S(2)}) collective-permute-start(bf16[512,2048]{1,0:T(8,128)(2,1)} %constant_dynamic-slice_fusion.2), channel_id=1, source_target_pairs={{0,1},{1,0},{2,3},{3,2},{4,5},{5,4},{6,7},{7,6},{8,9},{9,8},{10,11... | collective-permute-start | bytes 6291464 | tf_op jit(solution)/shard_map/ppermute | solution.py:27
  12.0 28.7 %collective-permute-start.2 = (bf16[1024,512]{1,0:T(8,128)(2,1)}, bf16[1024,512]{1,0:T(8,128)(2,1)S(1)}, u32[]{:S(2)}, u32[]{:S(2)}) collective-permute-start(bf16[1024,512]{1,0:T(8,128)(2,1)} %get-tuple-element.25.refs_2_), channel_id=1, source_target_pairs={{4,12},{5,13},{6,14},{7,15},{12,20},{13,21},{14,22},{15,23},{20,28... | collective-permute-start | bytes 3145736 | tf_op jit(solution)/shard_map/ppermute | solution.py:459
  12.8 13.5 %collective-permute-start.3 = (bf16[1024,256]{1,0:T(8,128)(2,1)}, bf16[1024,256]{1,0:T(8,128)(2,1)S(1)}, u32[]{:S(2)}, u32[]{:S(2)}) collective-permute-start(bf16[1024,256]{1,0:T(8,128)(2,1)} %get-tuple-element.28), channel_id=1, source_target_pairs={{0,2},{1,3},{2,0},{3,1},{4,6},{5,7},{6,4},{7,5},{8,10},{9,11},{10,... | collective-permute-start | bytes 1572872 | tf_op jit(solution)/shard_map/ppermute | solution.py:27
  14.1 23.9 %collective-permute-start.4 = (bf16[1024,256]{1,0:T(8,128)(2,1)}, bf16[1024,256]{1,0:T(8,128)(2,1)S(1)}, u32[]{:S(2)}, u32[]{:S(2)}) collective-permute-start(bf16[1024,256]{1,0:T(8,128)(2,1)} %get-tuple-element.29), channel_id=1, source_target_pairs={{0,4},{1,5},{2,6},{3,7},{4,0},{5,1},{6,2},{7,3},{8,12},{9,13},{10,... | collective-permute-start | bytes 1572872 | tf_op jit(solution)/shard_map/ppermute | solution.py:27
  15.9 23.2 %collective-permute-start.5 = (bf16[1024,256]{1,0:T(8,128)(2,1)}, bf16[1024,256]{1,0:T(8,128)(2,1)}, u32[]{:S(2)}, u32[]{:S(2)}) collective-permute-start(bf16[1024,256]{1,0:T(8,128)(2,1)} %get-tuple-element.30), channel_id=1, source_target_pairs={{0,6},{1,7},{2,4},{3,5},{4,2},{5,3},{6,0},{7,1},{8,14},{9,15},{10,... | collective-permute-start | bytes 1572872 | tf_op jit(solution)/shard_map/ppermute | solution.py:27
  40.7 49.2 %copy-start.9 = (s32[8,8]{1,0:T(8,128)S(1)}, s32[8,8]{1,0:T(8,128)}, u32[]{:S(2)}) copy-start(s32[8,8]{1,0:T(8,128)} %param.10) | copy-start | bytes 772
  42.1 23.6 %collective-permute-start.6 = (bf16[1024,512]{1,0:T(8,128)(2,1)S(1)}, bf16[1024,512]{1,0:T(8,128)(2,1)S(1)}, u32[]{:S(2)}, u32[]{:S(2)}) collective-permute-start(bf16[1024,512]{1,0:T(8,128)(2,1)S(1)} %broadcast_select_fusion.1), channel_id=1, source_target_pairs={{0,4},{1,5},{2,6},{3,7},{4,0},{5,1},{6,2},{7,3},{8,12},{9,13},{10,... | collective-permute-start | bytes 3145736 | tf_op jit(solution)/shard_map/ppermute | solution.py:27
  42.8 26.4 %collective-permute-start.7 = (bf16[1024,256]{1,0:T(8,128)(2,1)S(1)}, bf16[1024,256]{1,0:T(8,128)(2,1)}, u32[]{:S(2)}, u32[]{:S(2)}) collective-permute-start(bf16[1024,256]{1,0:T(8,128)(2,1)S(1)} %add_add_fusion), channel_id=1, source_target_pairs={{0,16},{1,17},{2,18},{3,19},{4,20},{5,21},{6,22},{7,23},{8,24},{9,... | collective-permute-start | bytes 1572872 | tf_op jit(solution)/shard_map/ppermute | solution.py:22
  65.7 28.4 %copy-start.6 = (bf16[1024,512]{1,0:T(8,128)(2,1)}, bf16[1024,512]{1,0:T(8,128)(2,1)S(1)}, u32[]{:S(2)}) copy-start(bf16[1024,512]{1,0:T(8,128)(2,1)S(1)} %collective-permute-done.6.refs_4_) | copy-start | bytes 3145732
  65.7 22.9 %collective-permute-start.9 = (bf16[1024,512]{1,0:T(8,128)(2,1)}, bf16[1024,512]{1,0:T(8,128)(2,1)}, u32[]{:S(2)}, u32[]{:S(2)}) collective-permute-start(bf16[1024,512]{1,0:T(8,128)(2,1)} %get-tuple-element.35.refs_2_), channel_id=1, source_target_pairs={{0,4},{1,5},{2,6},{3,7},{4,0},{5,1},{6,2},{7,3},{8,12},{9,13},{10,... | collective-permute-start | bytes 3145736 | tf_op jit(solution)/shard_map/ppermute | solution.py:27
  70.5 23.5 %collective-permute-start.8 = (bf16[1024,512]{1,0:T(8,128)(2,1)S(1)}, bf16[1024,512]{1,0:T(8,128)(2,1)S(1)}, u32[]{:S(2)}, u32[]{:S(2)}) collective-permute-start(bf16[1024,512]{1,0:T(8,128)(2,1)S(1)} %broadcast_select_fusion.3), channel_id=1, source_target_pairs={{0,2},{1,3},{2,0},{3,1},{4,6},{5,7},{6,4},{7,5},{8,10},{9,11},{10,... | collective-permute-start | bytes 3145736 | tf_op jit(solution)/shard_map/ppermute | solution.py:27
  71.2 20.0 %collective-permute-start.10 = (bf16[1024,256]{1,0:T(8,128)(2,1)S(1)}, bf16[1024,256]{1,0:T(8,128)(2,1)S(1)}, u32[]{:S(2)}, u32[]{:S(2)}) collective-permute-start(bf16[1024,256]{1,0:T(8,128)(2,1)S(1)} %add.48), channel_id=1, source_target_pairs={{0,8},{1,9},{2,10},{3,11},{4,12},{5,13},{6,14},{7,15},{8,16},{9,17... | collective-permute-start | bytes 1572872 | tf_op jit(solution)/shard_map/ppermute | solution.py:22
  88.6 24.5 %collective-permute-start.14 = (bf16[1024,512]{1,0:T(8,128)(2,1)}, bf16[1024,512]{1,0:T(8,128)(2,1)S(1)}, u32[]{:S(2)}, u32[]{:S(2)}) collective-permute-start(bf16[1024,512]{1,0:T(8,128)(2,1)} %collective-permute-done.9), channel_id=1, source_target_pairs={{0,8},{1,9},{2,10},{3,11},{8,16},{9,17},{10,18},{11,19},{16,24},{1... | collective-permute-start | bytes 3145736 | tf_op jit(solution)/shard_map/ppermute | solution.py:459
  91.4 24.4 %collective-permute-start.13 = (bf16[1024,256]{1,0:T(8,128)(2,1)S(1)}, bf16[1024,256]{1,0:T(8,128)(2,1)S(1)}, u32[]{:S(2)}, u32[]{:S(2)}) collective-permute-start(bf16[1024,256]{1,0:T(8,128)(2,1)S(1)} %add.49), channel_id=1, source_target_pairs={{0,6},{1,7},{2,4},{3,5},{4,2},{5,3},{6,0},{7,1},{8,14},{9,15},{10,... | collective-permute-start | bytes 1572872 | tf_op jit(solution)/shard_map/ppermute | solution.py:27
  92.0 24.4 %collective-permute-start.12 = (bf16[1024,256]{1,0:T(8,128)(2,1)S(1)}, bf16[1024,256]{1,0:T(8,128)(2,1)S(1)}, u32[]{:S(2)}, u32[]{:S(2)}) collective-permute-start(bf16[1024,256]{1,0:T(8,128)(2,1)S(1)} %add.49), channel_id=1, source_target_pairs={{0,4},{1,5},{2,6},{3,7},{4,0},{5,1},{6,2},{7,3},{8,12},{9,13},{10,... | collective-permute-start | bytes 1572872 | tf_op jit(solution)/shard_map/ppermute | solution.py:27
  94.0 22.6 %collective-permute-start.11 = (bf16[1024,256]{1,0:T(8,128)(2,1)S(1)}, bf16[1024,256]{1,0:T(8,128)(2,1)S(1)}, u32[]{:S(2)}, u32[]{:S(2)}) collective-permute-start(bf16[1024,256]{1,0:T(8,128)(2,1)S(1)} %add.49), channel_id=1, source_target_pairs={{0,2},{1,3},{2,0},{3,1},{4,6},{5,7},{6,4},{7,5},{8,10},{9,11},{10,... | collective-permute-start | bytes 1572872 | tf_op jit(solution)/shard_map/ppermute | solution.py:27
  115.6 64.9 %collective-permute-start.16 = (bf16[1024,512]{1,0:T(8,128)(2,1)S(1)}, bf16[1024,512]{1,0:T(8,128)(2,1)S(1)}, u32[]{:S(2)}, u32[]{:S(2)}) collective-permute-start(bf16[1024,512]{1,0:T(8,128)(2,1)S(1)} %get-tuple-element.45), channel_id=1, source_target_pairs={{0,2},{1,3},{2,0},{3,1},{4,6},{5,7},{6,4},{7,5},{8,10},{9,11},{10,... | collective-permute-start | bytes 3145736 | tf_op jit(solution)/shard_map/ppermute | solution.py:27
  177.3 81.6 %collective-permute-start.15 = (bf16[512,1024]{1,0:T(8,128)(2,1)}, bf16[512,1024]{1,0:T(8,128)(2,1)S(1)}, u32[]{:S(2)}, u32[]{:S(2)}) collective-permute-start(bf16[512,1024]{1,0:T(8,128)(2,1)} %get-tuple-element.42), channel_id=1, source_target_pairs={{0,1},{1,0},{2,3},{3,2},{4,5},{5,4},{6,7},{7,6},{8,9},{9,8},{10,11... | collective-permute-start | bytes 3145736 | tf_op jit(solution)/shard_map/ppermute | solution.py:27
  199.5 59.4 %copy-start.4 = (bf16[512,1024]{1,0:T(8,128)(2,1)S(1)}, bf16[512,1024]{1,0:T(8,128)(2,1)}, u32[]{:S(2)}) copy-start(bf16[512,1024]{1,0:T(8,128)(2,1)} %get-tuple-element.41) | copy-start | bytes 3145732
  258.8 3.1 %copy-start.5 = (bf16[512,1024]{1,0:T(8,128)(2,1)S(1)}, bf16[512,1024]{1,0:T(8,128)(2,1)}, u32[]{:S(2)}) copy-start(bf16[512,1024]{1,0:T(8,128)(2,1)} %get-tuple-element.43) | copy-start | bytes 3145732
  258.8 3.1 %collective-permute-start.17 = (bf16[512,1024]{1,0:T(8,128)(2,1)}, bf16[512,1024]{1,0:T(8,128)(2,1)}, u32[]{:S(2)}, u32[]{:S(2)}) collective-permute-start(bf16[512,1024]{1,0:T(8,128)(2,1)} %get-tuple-element.44), channel_id=1, source_target_pairs={{0,1},{1,0},{2,3},{3,2},{4,5},{5,4},{6,7},{7,6},{8,9},{9,8},{10,11... | collective-permute-start | bytes 3145736 | tf_op jit(solution)/shard_map/ppermute | solution.py:27
  263.2 22.9 %copy-start.1 = (s32[8,8]{1,0:T(8,128)S(1)}, s32[8,8]{1,0:T(8,128)}, u32[]{:S(2)}) copy-start(s32[8,8]{1,0:T(8,128)} %param.9) | copy-start | bytes 772
  (6 other events, 8.2 us)

commit v13 on v11

--- a/solution.py
+++ b/solution.py
@@ -129,8 +129,9 @@
     first, pair, local, group, reach, n_slash = cfg
     q_refs, refs = refs[:pair], refs[pair:]
     w_refs, refs = refs[: reach + 1], refs[reach + 1 :]
-    masks, acc, win, qx = refs[:4]
-    kgs, vgs, ps = refs[4:6], refs[6:8], refs[8:10]
+    masks, acc, sums, win, qx = refs[:5]
+    kgs, vgs, ps = refs[5:7], refs[7:9], refs[9:11]
+    lane = lax.broadcasted_iota(jnp.int32, sums.shape, 1)
     e = first + pl.program_id(0)
     chip, core = info[0], info[1]
     dev_rows = local * BLK
@@ -174,15 +175,16 @@
         if ahead:
             place_keys(i + 1, 1 - at)
         if behind:
-            acc[i - 1] = jnp.dot(
-                ps[1 - at][...], vgs[1 - at][...], preferred_element_type=jnp.float32
-            )
+            part = jnp.dot(ps[1 - at][...], vgs[1 - at][...], preferred_element_type=jnp.float32)
+            acc[i - 1] = part[:, :HD]
+            sums[...] = jnp.where(lane == i - 1, part[:, HD:], sums[...])
         if isinstance(i, int) and i == chip_blocks:
             return
         for j in range(n_slash):
             vgs[at][j * BLK : (j + 1) * BLK, :HD] = win[take(i, j), HD:]
         ps[at][...] = exponentials(qx[i], kgs[at][...], factor).astype(ps[at].dtype)
 
+    sums[...] = jnp.zeros(sums.shape, sums.dtype)
     place_keys(0, 0)
     pipelined(chip_blocks, stage)
 
@@ -191,7 +193,8 @@
     first, pair, local, group, reach, n_slash, n_vert, plane, heads = cfg
     q_refs, refs = refs[:pair], refs[pair:]
     w_refs, refs = refs[: reach + 1], refs[reach + 1 :]
-    before, kv_vert, masks, refs = refs[0], refs[1], refs[2], refs[3:]
+    before, sums, kv_vert, masks, refs = refs[0], refs[1], refs[2], refs[3], refs[4:]
+    lane = lax.broadcasted_iota(jnp.int32, sums.shape, 1)
     out_refs, refs = refs[:pair], refs[pair:]
     ke, ve, qx, res, good = refs[:5]
     ps, (kg, vg, sc, pg) = refs[5:7], refs[7:]
@@ -217,7 +220,9 @@
     row = lax.broadcasted_iota(jnp.int32, (HD, BLK), 0)
     for j in range(n_vert):
         flat = e * n_vert + j
-        src = pl.multiple_of(((flat // per ^ chip % plane) * per + flat % per) * BLK, BLK)
+        src = j * BLK
+        if heads != plane:
+            src = pl.multiple_of(((flat // per ^ chip % plane) * per + flat % per) * BLK, BLK)
         rows = slice(j * BLK, (j + 1) * BLK)
         ke[:HD, rows] = kv_vert[pl.ds(src, BLK), :HD]
         ve[rows, :HD] = kv_vert[pl.ds(src, BLK), HD:]
@@ -242,15 +247,16 @@
             part = jnp.dot(ps[1 - at][...], ve[...], preferred_element_type=jnp.float32)
             for u in range(n_rows // block_rows):
                 i = (t - 1) * (n_rows // block_rows) + u
-                finish(i, before[i] + part[u * block_rows : (u + 1) * block_rows, :])
+                finish(i, part[u * block_rows : (u + 1) * block_rows, :])
         if t * n_rows == qx.shape[0]:
             return
         q = qx[t * n_rows : (t + 1) * n_rows, :]
         ps[at][...] = exponentials(q, ke[...], factor).astype(ps[at].dtype)
 
     def finish(i, acc):
-        total = acc[:, HD:]
-        res[i] = (acc[:, :HD] / total).astype(res.dtype)
+        mine = jnp.sum(jnp.where(lane == i, sums[...], 0.0), axis=1, keepdims=True)
+        total = acc[:, HD:] + mine
+        res[i] = ((acc[:, :HD] + before[i]) / total).astype(res.dtype)
         fine = jnp.where((total > SMALLEST) & (total < LARGEST), 1.0, 0.0)
         good[...] = jnp.minimum(good[...], jnp.min(fine, axis=0, keepdims=True))
 
@@ -346,13 +352,16 @@
         )
 
     def acc_spec(self):
-        shape = (self.blocks, self.group * BLK, 2 * HD)
-        return pl.BlockSpec((None, *shape), lambda i, *_: (i, 0, 0, 0))
+        rows = self.group * BLK
+        return [
+            pl.BlockSpec((None, self.blocks, rows, HD), lambda i, *_: (i, 0, 0, 0)),
+            pl.BlockSpec((None, rows, HD), lambda i, *_: (i, 0, 0)),
+        ]
 
     def over_slash(self, first, n, windows):
         n_slash = self.slash.shape[1]
         width, rows = n_slash * BLK, self.group * BLK
-        shape = (n, self.blocks, rows, 2 * HD)
+        shape = (n, self.blocks, rows, HD)
         cfg = (first, self.pair, self.local, self.group, len(windows) - 1, n_slash)
         return pl.pallas_call(
             functools.partial(slash_kernel, cfg),
@@ -369,7 +378,10 @@
                 + [pltpu.VMEM((width, 2 * HD), self.dtype)] * 2
                 + [pltpu.VMEM((rows, width), self.dtype)] * 2,
             ),
-            out_shape=jax.ShapeDtypeStruct(shape, jnp.float32),
+            out_shape=[
+                jax.ShapeDtypeStruct(shape, jnp.float32),
+                jax.ShapeDtypeStruct((n, rows, HD), jnp.float32),
+            ],
             compiler_params=pltpu.CompilerParams(vmem_limit_bytes=VMEM_LIMIT),
             cost_estimate=self.cost(n, width, 4 * math.prod(shape)),
             name="attend_slash",
@@ -380,13 +392,19 @@
         width, both, rows = n_vert * BLK, (n_slash + n_vert) * BLK, self.group * BLK
         cfg = (first, self.pair, self.local, self.group, len(windows) - 1, n_slash, n_vert)
         out = pl.BlockSpec((self.dev_rows, self.wide), lambda i, *_: (0, i))
+        kv_spec, plane = self.whole(kv_vert), self.plane
+        if self.heads == plane:
+            kv_spec = pl.BlockSpec(
+                (width, 2 * HD), lambda i, info, *_: ((first + i) ^ info[0] % plane, 0)
+            )
         return pl.pallas_call(
             functools.partial(vertical_kernel, cfg + (self.plane, self.heads)),
             grid_spec=pltpu.PrefetchScalarGridSpec(
                 num_scalar_prefetch=3,
                 grid=(n,),
                 in_specs=self.specs(first, windows)
-                + [self.acc_spec(), self.whole(kv_vert), self.whole(self.masks)],
+                + self.acc_spec()
+                + [kv_spec, self.whole(self.masks)],
                 out_specs=[out] * self.pair,
                 scratch_shapes=[
                     pltpu.VMEM((2 * HD, width), self.dtype),
@@ -405,9 +423,9 @@
             out_shape=[jax.ShapeDtypeStruct((self.dev_rows, n * self.wide), self.dtype)]
             * self.pair,
             compiler_params=pltpu.CompilerParams(vmem_limit_bytes=VMEM_LIMIT),
-            cost_estimate=self.cost(n, width, 4 * math.prod(before.shape)),
+            cost_estimate=self.cost(n, width, 4 * math.prod(before[0].shape)),
             name="attend_vertical",
-        )(self.info, self.vert, self.slash, *self.qs, *windows, before, kv_vert, self.masks)
+        )(self.info, self.vert, self.slash, *self.qs, *windows, *before, kv_vert, self.masks)
 
 
 def body(queries, keys, values, vertical_blocks, slash_offsets, out_weight):

time: 289 us -> 287 us (level)
  no operation moved by 1% of the time
where the time goes in v13:
time: 287 us; the launch traced here: 285 us
  Pallas kernels  157 us (55%)
  waiting for transfers between devices  71 us (25%)
  matrix products  22.9 us (8%)
  starting transfers between devices  17.5 us (6%)
  other arithmetic  8.84 us (3%)
  local copies, waits for them, and re-layouts  7.63 us (3%)
    pallas_call x2, Pallas kernels, over_vertical(): pl.pallas_call(functools.partial(vertical_kernel, cfg + (self.plane, self...  118 us
    ppermute x14, waiting for transfers between devices, crossed(): return lax.ppermute(value, 'ctx', [(i, i ^ bits) for i in range(size)])  52.3 us
    pallas_call x2, Pallas kernels, over_slash(): pl.pallas_call(functools.partial(slash_kernel, cfg), grid_spec=pltpu.Pref...  34.6 us
    dot_general x1, matrix products, body(): output = jnp.dot(attended, out_weight, preferred_element_type=jnp.float32)  22.9 us
    ppermute x2, waiting for transfers between devices, shifted(): return lax.ppermute(value, 'ctx', [(i, i + by) for i in range(size - by)])  17.6 us
    ppermute x14, starting transfers between devices, crossed(): return lax.ppermute(value, 'ctx', [(i, i ^ bits) for i in range(size)])  11.8 us
  transfers between devices with their start and end apart: 18, of which 9 were waited for; matrix products, arithmetic and copies ran while one was open for 4% of the time, Pallas kernels for 54%

profile of v13, /device:TPU:25, one launch (start us, length us, event | category | flops | bytes accessed | tf_op | source)
XLA Modules:
  0.0 284.9 jit_solution(2697895997607237022)
XLA Ops:
  3.3 1.7 constant_dynamic-slice_fusion.2
  5.0 4.5 %prepare.1 = (bf16[1024,512]{1,0:T(8,128)(2,1)}, bf16[1024,512]{1,0:T(8,128)(2,1)}, bf16[1024,256]{1,0:T(8,128)(2,1)}, bf16[1024,256]{1,0:T(8,128)(2,1)}, bf16[1...) custom-call(s32[2]{0:T(128)} %pad_add_fusion.info, s32[4,8]{1,0:T(4,128)} %constant_dynamic-slice_fusion.4.vert, ...), custom_call_target="tpu_custom_call" | custom-call | bytes 8388608 | tf_op jit(solution)/shard_map/prepare/pallas_call | solution.py:86
  9.6 1.8 collective-permute-start.2
  14.0 10.9 %collective-permute-done.3 = bf16[1024,256]{1,0:T(8,128)(2,1)} collective-permute-done((bf16[1024,256]{1,0:T(8,128)(2,1)}, bf16[1024,256]{1,0:T(8,128)(2,1)}, u32[]{:S(2)}, u32[]{:S(2)}) %collective-permute-start.3) | collective-permute-done | bytes 524320 | tf_op jit(solution)/shard_map/ppermute | solution.py:27
  26.0 10.8 %collective-permute-done.5 = bf16[1024,256]{1,0:T(8,128)(2,1)} collective-permute-done((bf16[1024,256]{1,0:T(8,128)(2,1)}, bf16[1024,256]{1,0:T(8,128)(2,1)}, u32[]{:S(2)}, u32[]{:S(2)}) %collective-permute-start.5) | collective-permute-done | bytes 524320 | tf_op jit(solution)/shard_map/ppermute | solution.py:27
  36.8 1.6 add_add_fusion
  38.5 1.4 broadcast_select_fusion.1
  41.7 13.2 %collective-permute-done.8 = bf16[1024,256]{1,0:T(8,128)(2,1)S(1)} collective-permute-done((bf16[1024,256]{1,0:T(8,128)(2,1)S(1)}, bf16[1024,256]{1,0:T(8,128)(2,1)S(1)}, u32[]{:S(2)}, u32[]{:S(2)}) %collective-permute-start.8) | collective-permute-done | bytes 524320 | tf_op jit(solution)/shard_map/ppermute | solution.py:22
  55.0 7.9 %collective-permute-done.6.refs_4_ = bf16[1024,512]{1,0:T(8,128)(2,1)S(1)} collective-permute-done((bf16[1024,512]{1,0:T(8,128)(2,1)S(1)}, bf16[1024,512]{1,0:T(8,128)(2,1)S(1)}, u32[]{:S(2)}, u32[]{:S(2)}) %collective-permute-start.6) | collective-permute-done | bytes 1048608 | tf_op jit(solution)/shard_map/ppermute | solution.py:27
  63.1 2.1 collective-permute-start.7
  66.5 18.7 %collective-permute-done.9 = bf16[1024,512]{1,0:T(8,128)(2,1)} collective-permute-done((bf16[1024,512]{1,0:T(8,128)(2,1)}, bf16[1024,512]{1,0:T(8,128)(2,1)}, u32[]{:S(2)}, u32[]{:S(2)}) %collective-permute-start.9) | collective-permute-done | bytes 1048608 | tf_op jit(solution)/shard_map/ppermute | solution.py:27
  85.3 1.3 collective-permute-start.14
  87.9 4.4 %collective-permute-done.10 = bf16[1024,256]{1,0:T(8,128)(2,1)S(1)} collective-permute-done((bf16[1024,256]{1,0:T(8,128)(2,1)S(1)}, bf16[1024,256]{1,0:T(8,128)(2,1)S(1)}, u32[]{:S(2)}, u32[]{:S(2)}) %collective-permute-start.10) | collective-permute-done | bytes 524320 | tf_op jit(solution)/shard_map/ppermute | solution.py:22
  93.1 2.1 collective-permute-start.13
  96.2 17.3 %attend_slash.2 = (f32[2,8,512,128]{3,2,1,0:T(8,128)}, f32[2,512,128]{2,1,0:T(8,128)}) custom-call(s32[2]{0:T(128)} %pad_add_fusion.info, s32[4,8]{1,0:T(4,128)} %constant_dynamic-slice_fusion.3.slash, bf16[512,4096]{1,0:T(8,128)(2,1)} %refs_0_.9, bf16[512,2048]{1,0:T(8,128)(2,1)} %collective-permute-done.1.refs_1_, ...), custom_call_target="tpu_custom_call" | custom-call | flops 8589934592 | bytes 6291456 | tf_op jit(solution)/shard_map/attend_slash/pallas_call | solution.py:366
  114.6 2.5 broadcast_select_fusion.2
  117.4 1.3 copy-done.6
  118.7 58.8 %attend_vertical.2 = (bf16[512,1024]{1,0:T(8,128)(2,1)}, bf16[512,1024]{1,0:T(8,128)(2,1)}) custom-call(s32[2]{0:T(128)} %pad_add_fusion.info, s32[4,8]{1,0:T(4,128)} %constant_dynamic-slice_fusion.4.vert, s32[4,8]{1,0:T(4,128)} %constant_dynamic-slice_fusion.3.slash, bf16[512,4096]{1,0:T(8,128)(2,1)} %refs_0_.9, ...), custom_call_target="tpu_custom_call" | custom-call | flops 8589934592 | bytes 6291456 | tf_op jit(solution)/shard_map/attend_vertical/pallas_call | solution.py:400
  177.5 2.7 collective-permute-start.15
  181.3 17.3 %attend_slash.3 = (f32[2,8,512,128]{3,2,1,0:T(8,128)}, f32[2,512,128]{2,1,0:T(8,128)}) custom-call(s32[2]{0:T(128)} %pad_add_fusion.info, s32[4,8]{1,0:T(4,128)} %constant_dynamic-slice_fusion.3.slash, bf16[512,4096]{1,0:T(8,128)(2,1)} %refs_0_.9, bf16[512,2048]{1,0:T(8,128)(2,1)} %collective-permute-done.1.refs_1_, ...), custom_call_target="tpu_custom_call" | custom-call | flops 8589934592 | bytes 6291456 | tf_op jit(solution)/shard_map/attend_slash/pallas_call | solution.py:366
  198.6 59.0 %attend_vertical.3 = (bf16[512,1024]{1,0:T(8,128)(2,1)}, bf16[512,1024]{1,0:T(8,128)(2,1)}) custom-call(s32[2]{0:T(128)} %pad_add_fusion.info, s32[4,8]{1,0:T(4,128)} %constant_dynamic-slice_fusion.4.vert, s32[4,8]{1,0:T(4,128)} %constant_dynamic-slice_fusion.3.slash, bf16[512,4096]{1,0:T(8,128)(2,1)} %refs_0_.9, ...), custom_call_target="tpu_custom_call" | custom-call | flops 8589934592 | bytes 6291456 | tf_op jit(solution)/shard_map/attend_vertical/pallas_call | solution.py:400
  257.9 2.8 collective-permute-done.17
  260.7 1.4 broadcast_select_fusion.6
  262.1 22.9 %convolution_convert_fusion = bf16[512,4096]{1,0:T(8,128)(2,1)} fusion(bf16[4096,4096]{1,0:T(8,128)(2,1)} %param.11, bf16[512,1024]{1,0:T(8,128)(2,1)S(1)} %get-tuple-element.56, bf16[512,1024]{1,0:T(8,128)(2,1)S(1)} %get-tuple-element.54, bf16[512,1024]{1,0:T(8,128)(2,1)S(1)} %get-tuple-element.55, bf16[512,1024]{1,0:T(8,128)(2,1)S(1)} %get-tuple-element.53), kind=kOutput, calls=%fused_computation | convolution fusion | flops 17198743552 | bytes 41943040 | tf_op jit(solution)/shard_map/dot_general | solution.py:518
  (60 shorter events, 16.3 us)
Async XLA Ops:
  1.4 3.6 %collective-permute-start = (bf16[512,1024]{1,0:T(8,128)(2,1)S(1)}, bf16[512,1024]{1,0:T(8,128)(2,1)}, u32[]{:S(2)}, u32[]{:S(2)}) collective-permute-start(bf16[512,1024]{1,0:T(8,128)(2,1)S(1)} %pad_maximum_fusion), channel_id=1, source_target_pairs={{0,1},{1,0},{2,3},{3,2},{4,5},{5,4},{6,7},{7,6},{8,9},{9,8},{10,11... | collective-permute-start | bytes 3145736 | tf_op jit(solution)/shard_map/ppermute | solution.py:27
  9.5 53.4 %copy-start.2 = (bf16[1024,512]{1,0:T(8,128)(2,1)S(1)}, bf16[1024,512]{1,0:T(8,128)(2,1)}, u32[]{:S(2)}) copy-start(bf16[1024,512]{1,0:T(8,128)(2,1)} %get-tuple-element.28.refs_2_) | copy-start | bytes 3145732
  9.5 30.3 %collective-permute-start.1 = (bf16[512,2048]{1,0:T(8,128)(2,1)S(1)}, bf16[512,2048]{1,0:T(8,128)(2,1)}, u32[]{:S(2)}, u32[]{:S(2)}) collective-permute-start(bf16[512,2048]{1,0:T(8,128)(2,1)S(1)} %constant_dynamic-slice_fusion.2), channel_id=1, source_target_pairs={{0,1},{1,0},{2,3},{3,2},{4,5},{5,4},{6,7},{7,6},{8,9},{9,8},{10,11... | collective-permute-start | bytes 6291464 | tf_op jit(solution)/shard_map/ppermute | solution.py:27
  9.6 28.9 %collective-permute-start.2 = (bf16[1024,512]{1,0:T(8,128)(2,1)}, bf16[1024,512]{1,0:T(8,128)(2,1)}, u32[]{:S(2)}, u32[]{:S(2)}) collective-permute-start(bf16[1024,512]{1,0:T(8,128)(2,1)} %get-tuple-element.28.refs_2_), channel_id=1, source_target_pairs={{4,12},{5,13},{6,14},{7,15},{12,20},{13,21},{14,22},{15,23},{20,28... | collective-permute-start | bytes 3145736 | tf_op jit(solution)/shard_map/ppermute | solution.py:476
  11.4 13.5 %collective-permute-start.3 = (bf16[1024,256]{1,0:T(8,128)(2,1)}, bf16[1024,256]{1,0:T(8,128)(2,1)}, u32[]{:S(2)}, u32[]{:S(2)}) collective-permute-start(bf16[1024,256]{1,0:T(8,128)(2,1)} %get-tuple-element.31), channel_id=1, source_target_pairs={{0,2},{1,3},{2,0},{3,1},{4,6},{5,7},{6,4},{7,5},{8,10},{9,11},{10,... | collective-permute-start | bytes 1572872 | tf_op jit(solution)/shard_map/ppermute | solution.py:27
  12.6 13.4 %collective-permute-start.4 = (bf16[1024,256]{1,0:T(8,128)(2,1)}, bf16[1024,256]{1,0:T(8,128)(2,1)}, u32[]{:S(2)}, u32[]{:S(2)}) collective-permute-start(bf16[1024,256]{1,0:T(8,128)(2,1)} %get-tuple-element.32), channel_id=1, source_target_pairs={{0,4},{1,5},{2,6},{3,7},{4,0},{5,1},{6,2},{7,3},{8,12},{9,13},{10,... | collective-permute-start | bytes 1572872 | tf_op jit(solution)/shard_map/ppermute | solution.py:27
  13.5 23.3 %collective-permute-start.5 = (bf16[1024,256]{1,0:T(8,128)(2,1)}, bf16[1024,256]{1,0:T(8,128)(2,1)}, u32[]{:S(2)}, u32[]{:S(2)}) collective-permute-start(bf16[1024,256]{1,0:T(8,128)(2,1)} %get-tuple-element.33), channel_id=1, source_target_pairs={{0,6},{1,7},{2,4},{3,5},{4,2},{5,3},{6,0},{7,1},{8,14},{9,15},{10,... | collective-permute-start | bytes 1572872 | tf_op jit(solution)/shard_map/ppermute | solution.py:27
  38.4 48.1 %copy-start.7 = (s32[8,8]{1,0:T(8,128)S(1)}, s32[8,8]{1,0:T(8,128)}, u32[]{:S(2)}) copy-start(s32[8,8]{1,0:T(8,128)} %param.10) | copy-start | bytes 772
  39.8 23.1 %collective-permute-start.6 = (bf16[1024,512]{1,0:T(8,128)(2,1)S(1)}, bf16[1024,512]{1,0:T(8,128)(2,1)S(1)}, u32[]{:S(2)}, u32[]{:S(2)}) collective-permute-start(bf16[1024,512]{1,0:T(8,128)(2,1)S(1)} %broadcast_select_fusion.1), channel_id=1, source_target_pairs={{0,4},{1,5},{2,6},{3,7},{4,0},{5,1},{6,2},{7,3},{8,12},{9,13},{10,... | collective-permute-start | bytes 3145736 | tf_op jit(solution)/shard_map/ppermute | solution.py:27
  40.4 14.4 %collective-permute-start.8 = (bf16[1024,256]{1,0:T(8,128)(2,1)S(1)}, bf16[1024,256]{1,0:T(8,128)(2,1)S(1)}, u32[]{:S(2)}, u32[]{:S(2)}) collective-permute-start(bf16[1024,256]{1,0:T(8,128)(2,1)S(1)} %add_add_fusion), channel_id=1, source_target_pairs={{0,8},{1,9},{2,10},{3,11},{4,12},{5,13},{6,14},{7,15},{8,16},{9,17... | collective-permute-start | bytes 1572872 | tf_op jit(solution)/shard_map/ppermute | solution.py:22
  62.9 32.3 %copy-start.5 = (bf16[1024,512]{1,0:T(8,128)(2,1)}, bf16[1024,512]{1,0:T(8,128)(2,1)S(1)}, u32[]{:S(2)}) copy-start(bf16[1024,512]{1,0:T(8,128)(2,1)S(1)} %collective-permute-done.6.refs_4_) | copy-start | bytes 3145732
  62.9 22.4 %collective-permute-start.9 = (bf16[1024,512]{1,0:T(8,128)(2,1)}, bf16[1024,512]{1,0:T(8,128)(2,1)}, u32[]{:S(2)}, u32[]{:S(2)}) collective-permute-start(bf16[1024,512]{1,0:T(8,128)(2,1)} %get-tuple-element.37.refs_2_), channel_id=1, source_target_pairs={{0,4},{1,5},{2,6},{3,7},{4,0},{5,1},{6,2},{7,3},{8,12},{9,13},{10,... | collective-permute-start | bytes 3145736 | tf_op jit(solution)/shard_map/ppermute | solution.py:27
  63.1 32.1 %collective-permute-start.7 = (bf16[1024,512]{1,0:T(8,128)(2,1)S(1)}, bf16[1024,512]{1,0:T(8,128)(2,1)S(1)}, u32[]{:S(2)}, u32[]{:S(2)}) collective-permute-start(bf16[1024,512]{1,0:T(8,128)(2,1)S(1)} %broadcast_select_fusion.3), channel_id=1, source_target_pairs={{0,2},{1,3},{2,0},{3,1},{4,6},{5,7},{6,4},{7,5},{8,10},{9,11},{10,... | collective-permute-start | bytes 3145736 | tf_op jit(solution)/shard_map/ppermute | solution.py:27
  65.2 27.1 %collective-permute-start.10 = (bf16[1024,256]{1,0:T(8,128)(2,1)S(1)}, bf16[1024,256]{1,0:T(8,128)(2,1)S(1)}, u32[]{:S(2)}, u32[]{:S(2)}) collective-permute-start(bf16[1024,256]{1,0:T(8,128)(2,1)S(1)} %add.48), channel_id=1, source_target_pairs={{0,16},{1,17},{2,18},{3,19},{4,20},{5,21},{6,22},{7,23},{8,24},{9,... | collective-permute-start | bytes 1572872 | tf_op jit(solution)/shard_map/ppermute | solution.py:22
  85.3 29.3 %collective-permute-start.14 = (bf16[1024,512]{1,0:T(8,128)(2,1)}, bf16[1024,512]{1,0:T(8,128)(2,1)S(1)}, u32[]{:S(2)}, u32[]{:S(2)}) collective-permute-start(bf16[1024,512]{1,0:T(8,128)(2,1)} %collective-permute-done.9), channel_id=1, source_target_pairs={{0,8},{1,9},{2,10},{3,11},{8,16},{9,17},{10,18},{11,19},{16,24},{1... | collective-permute-start | bytes 3145736 | tf_op jit(solution)/shard_map/ppermute | solution.py:476
  92.5 24.6 %collective-permute-start.11 = (bf16[1024,256]{1,0:T(8,128)(2,1)S(1)}, bf16[1024,256]{1,0:T(8,128)(2,1)S(1)}, u32[]{:S(2)}, u32[]{:S(2)}) collective-permute-start(bf16[1024,256]{1,0:T(8,128)(2,1)S(1)} %add.49), channel_id=1, source_target_pairs={{0,2},{1,3},{2,0},{3,1},{4,6},{5,7},{6,4},{7,5},{8,10},{9,11},{10,... | collective-permute-start | bytes 1572872 | tf_op jit(solution)/shard_map/ppermute | solution.py:27
  92.6 24.5 %collective-permute-start.12 = (bf16[1024,256]{1,0:T(8,128)(2,1)S(1)}, bf16[1024,256]{1,0:T(8,128)(2,1)S(1)}, u32[]{:S(2)}, u32[]{:S(2)}) collective-permute-start(bf16[1024,256]{1,0:T(8,128)(2,1)S(1)} %add.49), channel_id=1, source_target_pairs={{0,4},{1,5},{2,6},{3,7},{4,0},{5,1},{6,2},{7,3},{8,12},{9,13},{10,... | collective-permute-start | bytes 1572872 | tf_op jit(solution)/shard_map/ppermute | solution.py:27
  93.1 24.0 %collective-permute-start.13 = (bf16[1024,256]{1,0:T(8,128)(2,1)S(1)}, bf16[1024,256]{1,0:T(8,128)(2,1)S(1)}, u32[]{:S(2)}, u32[]{:S(2)}) collective-permute-start(bf16[1024,256]{1,0:T(8,128)(2,1)S(1)} %add.49), channel_id=1, source_target_pairs={{0,6},{1,7},{2,4},{3,5},{4,2},{5,3},{6,0},{7,1},{8,14},{9,15},{10,... | collective-permute-start | bytes 1572872 | tf_op jit(solution)/shard_map/ppermute | solution.py:27
  117.2 63.1 %collective-permute-start.16 = (bf16[1024,512]{1,0:T(8,128)(2,1)S(1)}, bf16[1024,512]{1,0:T(8,128)(2,1)S(1)}, u32[]{:S(2)}, u32[]{:S(2)}) collective-permute-start(bf16[1024,512]{1,0:T(8,128)(2,1)S(1)} %get-tuple-element.51), channel_id=1, source_target_pairs={{0,2},{1,3},{2,0},{3,1},{4,6},{5,7},{6,4},{7,5},{8,10},{9,11},{10,... | collective-permute-start | bytes 3145736 | tf_op jit(solution)/shard_map/ppermute | solution.py:27
  177.5 80.2 %collective-permute-start.15 = (bf16[512,1024]{1,0:T(8,128)(2,1)}, bf16[512,1024]{1,0:T(8,128)(2,1)S(1)}, u32[]{:S(2)}, u32[]{:S(2)}) collective-permute-start(bf16[512,1024]{1,0:T(8,128)(2,1)} %get-tuple-element.46), channel_id=1, source_target_pairs={{0,1},{1,0},{2,3},{3,2},{4,5},{5,4},{6,7},{7,6},{8,9},{9,8},{10,11... | collective-permute-start | bytes 3145736 | tf_op jit(solution)/shard_map/ppermute | solution.py:27
  198.6 59.1 %copy-start.3 = (bf16[512,1024]{1,0:T(8,128)(2,1)S(1)}, bf16[512,1024]{1,0:T(8,128)(2,1)}, u32[]{:S(2)}) copy-start(bf16[512,1024]{1,0:T(8,128)(2,1)} %get-tuple-element.45) | copy-start | bytes 3145732
  257.6 3.1 %copy-start.4 = (bf16[512,1024]{1,0:T(8,128)(2,1)S(1)}, bf16[512,1024]{1,0:T(8,128)(2,1)}, u32[]{:S(2)}) copy-start(bf16[512,1024]{1,0:T(8,128)(2,1)} %get-tuple-element.49) | copy-start | bytes 3145732
  257.6 3.1 %collective-permute-start.17 = (bf16[512,1024]{1,0:T(8,128)(2,1)}, bf16[512,1024]{1,0:T(8,128)(2,1)}, u32[]{:S(2)}, u32[]{:S(2)}) collective-permute-start(bf16[512,1024]{1,0:T(8,128)(2,1)} %get-tuple-element.50), channel_id=1, source_target_pairs={{0,1},{1,0},{2,3},{3,2},{4,5},{5,4},{6,7},{7,6},{8,9},{9,8},{10,11... | collective-permute-start | bytes 3145736 | tf_op jit(solution)/shard_map/ppermute | solution.py:27
  262.0 22.9 %copy-start.1 = (s32[8,8]{1,0:T(8,128)S(1)}, s32[8,8]{1,0:T(8,128)}, u32[]{:S(2)}) copy-start(s32[8,8]{1,0:T(8,128)} %param.9) | copy-start | bytes 772
  (4 other events, 6.0 us)
